TPU v7x, 32 devices: a whole 2x2x4 slice. The times are simulated.
32 devices in a mesh: dp: 8 (over z, y), mp: 4 (over x, core).
Axes of the slice: x: 2, y: 2, z: 4, core: 2. Of those that a mesh axis runs over, the one named last changes fastest.
Arguments:
- inputs: float32 [12288, 768], P('dp'), may hold values from -6 to 6
- cotangent: float32 [12288, 768], P('dp'), may hold values from -6 to 6
- word_lengths: int32 [24, 170], P('dp'), may hold values from 1 to 3
- word_count: int32 [24], P('dp'), may hold values from 20 to 170, as said below
- attn_in: float32 [2, 3, 768, 768], P(None, None, 'dp', 'mp'), may hold values from -0.3125 to 0.3125
- attn_out: float32 [2, 768, 768], P(None, 'dp', 'mp'), may hold values from -0.3125 to 0.3125
- ffn_up: float32 [2, 768, 3072], P(None, 'dp', 'mp'), may hold values from -0.21875 to 0.21875
- ffn_down: float32 [2, 768, 3072], P(None, 'dp', 'mp'), may hold values from -0.109375 to 0.109375
- head_bias: float32 [2, 2, 768], P(None, None, 'mp'), may hold values from -3 to 3
- ffn_bias: float32 [2, 3072], P(None, 'mp'), may hold values from -3 to 3
- row_params: float32 [2, 6, 768], replicated
- attn_in_mom: float32 [2, 3, 768, 768], P(None, None, 'dp', 'mp'), may hold values from -192 to 192
- attn_out_mom: float32 [2, 768, 768], P(None, 'dp', 'mp'), may hold values from -96 to 96
- ffn_up_mom: float32 [2, 768, 3072], P(None, 'dp', 'mp'), may hold values from -128 to 128
- ffn_down_mom: float32 [2, 768, 3072], P(None, 'dp', 'mp'), may hold values from -160 to 160
- head_bias_mom: float32 [2, 2, 768], P(None, None, 'mp'), may hold values from -256 to 256
- ffn_bias_mom: float32 [2, 3072], P(None, 'mp'), may hold values from -128 to 128
- row_params_mom: float32 [2, 6, 768], replicated, may hold values from -256 to 256
- attn_in_var: float32 [2, 3, 768, 768], P(None, None, 'dp', 'mp'), may hold values from 1105.92 to 4423.68
- attn_out_var: float32 [2, 768, 768], P(None, 'dp', 'mp'), may hold values from 276.48 to 1105.92
- ffn_up_var: float32 [2, 768, 3072], P(None, 'dp', 'mp'), may hold values from 491.52 to 1966.08
- ffn_down_var: float32 [2, 768, 3072], P(None, 'dp', 'mp'), may hold values from 768 to 3072
- head_bias_var: float32 [2, 2, 768], P(None, None, 'mp'), may hold values from 1966.08 to 7864.32
- ffn_bias_var: float32 [2, 3072], P(None, 'mp'), may hold values from 122.88 to 491.52
- row_params_var: float32 [2, 6, 768], replicated, may hold values from 1966.08 to 7864.32
Outputs:
- encoded: float32 [12288, 768], P('dp')
- input_grad: float32 [12288, 768], P('dp')
- attn_in_new: float32 [2, 3, 768, 768], P(None, None, 'dp', 'mp')
- attn_out_new: float32 [2, 768, 768], P(None, 'dp', 'mp')
- ffn_up_new: float32 [2, 768, 3072], P(None, 'dp', 'mp')
- ffn_down_new: float32 [2, 768, 3072], P(None, 'dp', 'mp')
- head_bias_new: float32 [2, 2, 768], P(None, None, 'mp')
- ffn_bias_new: float32 [2, 3072], P(None, 'mp')
- row_params_new: float32 [2, 6, 768], replicated
- attn_in_mom_new: float32 [2, 3, 768, 768], P(None, None, 'dp', 'mp')
- attn_out_mom_new: float32 [2, 768, 768], P(None, 'dp', 'mp')
- ffn_up_mom_new: float32 [2, 768, 3072], P(None, 'dp', 'mp')
- ffn_down_mom_new: float32 [2, 768, 3072], P(None, 'dp', 'mp')
- head_bias_mom_new: float32 [2, 2, 768], P(None, None, 'mp')
- ffn_bias_mom_new: float32 [2, 3072], P(None, 'mp')
- row_params_mom_new: float32 [2, 6, 768], replicated
- attn_in_var_new: float32 [2, 3, 768, 768], P(None, None, 'dp', 'mp')
- attn_out_var_new: float32 [2, 768, 768], P(None, 'dp', 'mp')
- ffn_up_var_new: float32 [2, 768, 3072], P(None, 'dp', 'mp')
- ffn_down_var_new: float32 [2, 768, 3072], P(None, 'dp', 'mp')
- head_bias_var_new: float32 [2, 2, 768], P(None, None, 'mp')
- ffn_bias_var_new: float32 [2, 3072], P(None, 'mp')
- row_params_var_new: float32 [2, 6, 768], replicated
- attn_in_copy: bfloat16 [2, 3, 768, 768], P(None, None, 'dp', 'mp')
- attn_out_copy: bfloat16 [2, 768, 768], P(None, 'dp', 'mp')
- ffn_up_copy: bfloat16 [2, 768, 3072], P(None, 'dp', 'mp')
- ffn_down_copy: bfloat16 [2, 768, 3072], P(None, 'dp', 'mp')
Inputs may be any that keep to these rules, and one draw needn't show every extreme that they name: `word_count`: how many word slots at the head of each sequence hold text; the rest of the sequence is padding.
All inputs are finite; a program needn't handle non-finite values.
Results may differ from a plain program's by a relative error of at most 0.04.
The roundings to bfloat16 on the way count: a program that leaves them out, or rounds other values in their place, can miss the bound.
Values may be sent and summed in bfloat16 or wider, within the bound.
No kernel may reach another device: no remote copies, remote signals or barrier semaphores. Data moves between devices by JAX's collectives and lax.ppermute only.
A program may use at most 256 MiB of HBM per device.

v0:
```python
import jax
import jax.numpy as jnp
from jax import lax
from jax.sharding import PartitionSpec as P

HEAD_DIM = 64
LAYERS = 2
ADAM_STEP = 10


EPS_NORM = 1e-12
EPS_ADAM = 1e-08
RATE_MATRIX = 0.04
RATE_VECTOR = 0.3
DECAY_MATRIX = 0.01


def norm_parts(residual, gain_row, shift_row):
    center = residual - jnp.mean(residual, axis=-1, keepdims=True)
    inv_std = lax.rsqrt(jnp.mean(center * center, axis=-1, keepdims=True) + EPS_NORM)
    scaled = center * inv_std
    return (scaled * gain_row + shift_row, scaled, inv_std)


def norm_back(grad_output, scaled, inv_std, gain_row):
    upstream = grad_output * gain_row
    mean_up = jnp.mean(upstream, axis=-1, keepdims=True)
    mean_cross = jnp.mean(upstream * scaled, axis=-1, keepdims=True)
    return inv_std * (upstream - mean_up - scaled * mean_cross)


def masked_scores(query_heads, key_heads, key_mask):
    scores = jnp.einsum(
        "sqhe,skhe->shqk", query_heads, key_heads, preferred_element_type=jnp.float32
    )
    return jnp.where(key_mask[:, None, None, :], scores, -1000000000.0)


def forward_layer(hidden, weights, head_b, ffn_b, rows, key_mask, head_shape):
    weight_in, weight_out, weight_up, weight_down = weights
    tokens = hidden.shape[0]
    width_dev = weight_in.shape[2]
    in_low = hidden.astype(jnp.bfloat16)
    projected = jnp.einsum("td,kdc->ktc", in_low, weight_in, preferred_element_type=jnp.float32)
    queries = ((projected[0] + head_b[0]) * 0.125).astype(jnp.bfloat16)
    key_rows = projected[1].astype(jnp.bfloat16)
    value_rows = (projected[2] + head_b[1]).astype(jnp.bfloat16)
    scores = masked_scores(queries.reshape(head_shape), key_rows.reshape(head_shape), key_mask)
    row_peak = jnp.max(scores, axis=-1, keepdims=True)
    shifted = jnp.exp(scores - row_peak)
    row_total = jnp.sum(shifted, axis=-1, keepdims=True)
    log_total = row_peak + jnp.log(row_total)
    probs_low = (shifted / row_total).astype(jnp.bfloat16)
    context = jnp.einsum(
        "shqk,skhe->sqhe",
        probs_low,
        value_rows.reshape(head_shape),
        preferred_element_type=jnp.float32,
    )
    context = context.reshape(tokens, width_dev).astype(jnp.bfloat16)
    partial_attn = jnp.einsum("tc,oc->to", context, weight_out, preferred_element_type=jnp.float32)
    attended = lax.psum(partial_attn, "mp") + rows[0]
    normed, scaled_one, inv_one = norm_parts(hidden + attended, rows[2], rows[3])
    normed_low = normed.astype(jnp.bfloat16)
    pre_act = jnp.dot(normed_low, weight_up, preferred_element_type=jnp.float32) + ffn_b
    activated = jax.nn.gelu(pre_act, approximate=False).astype(jnp.bfloat16)
    partial_ffn = jnp.einsum(
        "tf,of->to", activated, weight_down, preferred_element_type=jnp.float32
    )
    ffn_result = lax.psum(partial_ffn.astype(jnp.bfloat16), "mp").astype(jnp.float32) + rows[1]
    result, scaled_two, inv_two = norm_parts(normed + ffn_result, rows[4], rows[5])
    record = (
        in_low,
        queries,
        key_rows,
        value_rows,
        log_total,
        context,
        scaled_one,
        inv_one,
        normed_low,
        pre_act,
        activated,
        scaled_two,
        inv_two,
    )
    return (result, record)


def backward_layer(grad_output, record, weights, rows, key_mask, head_shape):
    (
        in_low,
        queries,
        key_rows,
        value_rows,
        log_total,
        context,
        scaled_one,
        inv_one,
        normed_low,
        pre_act,
        activated,
        scaled_two,
        inv_two,
    ) = record
    weight_in, weight_out, weight_up, weight_down = weights
    tokens = in_low.shape[0]
    width_dev = weight_in.shape[2]
    gain_two = jnp.sum(grad_output * scaled_two, axis=0)
    shift_two = jnp.sum(grad_output, axis=0)
    upper_grad = norm_back(grad_output, scaled_two, inv_two, rows[4])
    upper_low = upper_grad.astype(jnp.bfloat16)
    grad_down = jnp.einsum("to,tf->of", upper_low, activated, preferred_element_type=jnp.float32)
    grad_act = jnp.dot(upper_low, weight_down, preferred_element_type=jnp.float32)
    unused_value, gelu_back = jax.vjp(
        lambda value_in: jax.nn.gelu(value_in, approximate=False), pre_act
    )
    grad_pre = gelu_back(grad_act)[0].astype(jnp.bfloat16)
    grad_up = jnp.einsum("td,tf->df", normed_low, grad_pre, preferred_element_type=jnp.float32)
    partial_up = jnp.einsum("tf,df->td", grad_pre, weight_up, preferred_element_type=jnp.float32)
    grad_normed = upper_grad + lax.psum(partial_up.astype(jnp.bfloat16), "mp").astype(jnp.float32)
    gain_one = jnp.sum(grad_normed * scaled_one, axis=0)
    shift_one = jnp.sum(grad_normed, axis=0)
    lower_grad = norm_back(grad_normed, scaled_one, inv_one, rows[2])
    lower_low = lower_grad.astype(jnp.bfloat16)
    grad_out_weight = jnp.einsum(
        "to,tc->oc", lower_low, context, preferred_element_type=jnp.float32
    )
    grad_context = (
        jnp.dot(lower_low, weight_out, preferred_element_type=jnp.float32)
        .astype(jnp.bfloat16)
        .reshape(head_shape)
    )
    query_heads = queries.reshape(head_shape)
    key_heads = key_rows.reshape(head_shape)
    value_heads = value_rows.reshape(head_shape)
    scores = masked_scores(query_heads, key_heads, key_mask)
    attn_probs = jnp.exp(scores - log_total)
    probs_low = attn_probs.astype(jnp.bfloat16)
    grad_value = jnp.einsum(
        "shqk,sqhe->skhe", probs_low, grad_context, preferred_element_type=jnp.float32
    ).astype(jnp.bfloat16)
    grad_probs = jnp.einsum(
        "sqhe,skhe->shqk", grad_context, value_heads, preferred_element_type=jnp.float32
    )
    row_inner = jnp.sum(attn_probs * grad_probs, axis=-1, keepdims=True)
    grad_scores = (attn_probs * (grad_probs - row_inner)).astype(jnp.bfloat16)
    grad_query = (
        jnp.einsum(
            "shqk,skhe->sqhe", grad_scores, key_heads, preferred_element_type=jnp.float32
        ).astype(jnp.bfloat16)
        * 0.125
    )
    grad_key = jnp.einsum(
        "shqk,sqhe->skhe", grad_scores, query_heads, preferred_element_type=jnp.float32
    ).astype(jnp.bfloat16)
    grad_qkv = jnp.stack(
        [
            grad_query.reshape(tokens, width_dev),
            grad_key.reshape(tokens, width_dev),
            grad_value.reshape(tokens, width_dev),
        ]
    )
    grad_in_weight = jnp.einsum("td,ktc->kdc", in_low, grad_qkv, preferred_element_type=jnp.float32)
    partial_in = jnp.einsum("ktc,kdc->td", grad_qkv, weight_in, preferred_element_type=jnp.float32)
    grad_hidden = lower_grad + lax.psum(partial_in.astype(jnp.bfloat16), "mp").astype(jnp.float32)
    head_grads = jnp.stack(
        [
            jnp.sum(grad_qkv[0].astype(jnp.float32), axis=0),
            jnp.sum(grad_qkv[2].astype(jnp.float32), axis=0),
        ]
    )
    ffn_grads = jnp.sum(grad_pre.astype(jnp.float32), axis=0)
    row_grads = jnp.stack(
        [
            jnp.sum(lower_grad, axis=0),
            jnp.sum(upper_grad, axis=0),
            gain_one,
            shift_one,
            gain_two,
            shift_two,
        ]
    )
    return (
        grad_hidden,
        (grad_in_weight, grad_out_weight, grad_up, grad_down),
        (head_grads, ffn_grads, row_grads),
    )


def adam_step(master, moment, second, gradient, step_rate, decay_rate):
    correction = 1.0 - 0.5**ADAM_STEP
    moment_new = 0.5 * moment + 0.5 * gradient
    second_new = 0.5 * second + 0.5 * gradient * gradient
    update = (
        moment_new / correction / (jnp.sqrt(second_new / correction) + EPS_ADAM)
        + decay_rate * master
    )
    return (master - step_rate * update, moment_new, second_new)


def local(
    inputs,
    cotangent,
    word_lengths,
    word_count,
    attn_in,
    attn_out,
    ffn_up,
    ffn_down,
    head_bias,
    ffn_bias,
    row_params,
    attn_in_mom,
    attn_out_mom,
    ffn_up_mom,
    ffn_down_mom,
    head_bias_mom,
    ffn_bias_mom,
    row_params_mom,
    attn_in_var,
    attn_out_var,
    ffn_up_var,
    ffn_down_var,
    head_bias_var,
    ffn_bias_var,
    row_params_var,
):
    tokens = inputs.shape[0]
    seq_count = word_count.shape[0]
    seq_len = tokens // seq_count
    width_dev = attn_in.shape[3]
    head_shape = (seq_count, seq_len, width_dev // HEAD_DIM, HEAD_DIM)
    word_slots = jnp.arange(word_lengths.shape[1], dtype=jnp.int32)
    used_tokens = jnp.sum(
        jnp.where(word_slots[None, :] < word_count[:, None], word_lengths, 0), axis=1
    )
    key_mask = jnp.arange(seq_len, dtype=jnp.int32)[None, :] < used_tokens[:, None]
    row_mask = key_mask.reshape(tokens, 1).astype(jnp.float32)
    gathered = (
        lax.all_gather(attn_in.astype(jnp.bfloat16), "dp", axis=2, tiled=True),
        lax.all_gather(attn_out.astype(jnp.bfloat16), "dp", axis=1, tiled=True),
        lax.all_gather(ffn_up.astype(jnp.bfloat16), "dp", axis=1, tiled=True),
        lax.all_gather(ffn_down.astype(jnp.bfloat16), "dp", axis=1, tiled=True),
    )
    hidden = inputs
    records = []
    for layer_index in range(LAYERS):
        layer_weights = tuple((stacked[layer_index] for stacked in gathered))
        hidden, record = forward_layer(
            hidden,
            layer_weights,
            head_bias[layer_index],
            ffn_bias[layer_index],
            row_params[layer_index],
            key_mask,
            head_shape,
        )
        records.append(record)
    back_weights = (
        lax.all_gather(attn_in.astype(jnp.bfloat16), "dp", axis=2, tiled=True),
        lax.all_gather(attn_out.astype(jnp.bfloat16), "dp", axis=1, tiled=True),
        lax.all_gather(ffn_up.astype(jnp.bfloat16), "dp", axis=1, tiled=True),
        lax.all_gather(ffn_down.astype(jnp.bfloat16), "dp", axis=1, tiled=True),
    )
    grad_hidden = cotangent * row_mask
    matrix_grads = [None] * LAYERS
    vector_grads = [None] * LAYERS
    for layer_index in reversed(range(LAYERS)):
        layer_weights = tuple((stacked[layer_index] for stacked in back_weights))
        grad_hidden, layer_mats, layer_vecs = backward_layer(
            grad_hidden,
            records[layer_index],
            layer_weights,
            row_params[layer_index],
            key_mask,
            head_shape,
        )
        matrix_grads[layer_index] = layer_mats
        vector_grads[layer_index] = layer_vecs
    stacked_mats = tuple(
        (
            jnp.stack([matrix_grads[layer_index][member] for layer_index in range(LAYERS)])
            for member in range(4)
        )
    )
    stacked_mats = (
        lax.psum_scatter(stacked_mats[0], "dp", scatter_dimension=2, tiled=True),
        lax.psum_scatter(stacked_mats[1], "dp", scatter_dimension=1, tiled=True),
        lax.psum_scatter(stacked_mats[2], "dp", scatter_dimension=1, tiled=True),
        lax.psum_scatter(stacked_mats[3], "dp", scatter_dimension=1, tiled=True),
    )
    stacked_vecs = tuple(
        (
            jnp.stack([vector_grads[layer_index][member] for layer_index in range(LAYERS)])
            for member in range(3)
        )
    )
    summed_vecs = lax.psum((stacked_vecs[0], stacked_vecs[1], stacked_vecs[2]), "dp")
    params = (attn_in, attn_out, ffn_up, ffn_down, head_bias, ffn_bias, row_params)
    moments = (
        attn_in_mom,
        attn_out_mom,
        ffn_up_mom,
        ffn_down_mom,
        head_bias_mom,
        ffn_bias_mom,
        row_params_mom,
    )
    seconds = (
        attn_in_var,
        attn_out_var,
        ffn_up_var,
        ffn_down_var,
        head_bias_var,
        ffn_bias_var,
        row_params_var,
    )
    gradients = (
        stacked_mats[0],
        stacked_mats[1],
        stacked_mats[2],
        stacked_mats[3],
        summed_vecs[0],
        summed_vecs[1],
        summed_vecs[2],
    )
    new_params = []
    new_moments = []
    new_seconds = []
    for index in range(7):
        step_rate = RATE_MATRIX if index < 4 else RATE_VECTOR
        decay_rate = DECAY_MATRIX if index < 4 else 0.0
        master_new, moment_new, second_new = adam_step(
            params[index], moments[index], seconds[index], gradients[index], step_rate, decay_rate
        )
        new_params.append(master_new)
        new_moments.append(moment_new)
        new_seconds.append(second_new)
    return (
        hidden,
        grad_hidden,
        new_params[0],
        new_params[1],
        new_params[2],
        new_params[3],
        new_params[4],
        new_params[5],
        new_params[6],
        new_moments[0],
        new_moments[1],
        new_moments[2],
        new_moments[3],
        new_moments[4],
        new_moments[5],
        new_moments[6],
        new_seconds[0],
        new_seconds[1],
        new_seconds[2],
        new_seconds[3],
        new_seconds[4],
        new_seconds[5],
        new_seconds[6],
        new_params[0].astype(jnp.bfloat16),
        new_params[1].astype(jnp.bfloat16),
        new_params[2].astype(jnp.bfloat16),
        new_params[3].astype(jnp.bfloat16),
    )


def solution(mesh):
    placed = (
        P("dp", None),
        P("dp", None),
        P("dp", None),
        P("dp"),
        P(None, None, "dp", "mp"),
        P(None, "dp", "mp"),
        P(None, "dp", "mp"),
        P(None, "dp", "mp"),
        P(None, None, "mp"),
        P(None, "mp"),
        P(),
        P(None, None, "dp", "mp"),
        P(None, "dp", "mp"),
        P(None, "dp", "mp"),
        P(None, "dp", "mp"),
        P(None, None, "mp"),
        P(None, "mp"),
        P(),
        P(None, None, "dp", "mp"),
        P(None, "dp", "mp"),
        P(None, "dp", "mp"),
        P(None, "dp", "mp"),
        P(None, None, "mp"),
        P(None, "mp"),
        P(),
    )
    return jax.shard_map(
        local,
        mesh=mesh,
        in_specs=placed,
        out_specs=(
            P("dp", None),
            P("dp", None),
            P(None, None, "dp", "mp"),
            P(None, "dp", "mp"),
            P(None, "dp", "mp"),
            P(None, "dp", "mp"),
            P(None, None, "mp"),
            P(None, "mp"),
            P(),
            P(None, None, "dp", "mp"),
            P(None, "dp", "mp"),
            P(None, "dp", "mp"),
            P(None, "dp", "mp"),
            P(None, None, "mp"),
            P(None, "mp"),
            P(),
            P(None, None, "dp", "mp"),
            P(None, "dp", "mp"),
            P(None, "dp", "mp"),
            P(None, "dp", "mp"),
            P(None, None, "mp"),
            P(None, "mp"),
            P(),
            P(None, None, "dp", "mp"),
            P(None, "dp", "mp"),
            P(None, "dp", "mp"),
            P(None, "dp", "mp"),
        ),
        check_vma=False,
    )
```

profile of v0, /device:TPU:0, one launch (start us, length us, event | category | flops | bytes accessed | tf_op | source)
XLA Modules:
  0.0 1296.4 jit_solution(13648326050801212566)
XLA Ops:
  13.0 35.5 %all_gather.17 = bf16[2,768,192]{2,1,0:T(8,128)(2,1)S(1)} all-gather(bf16[2,96,192]{2,1,0:T(8,128)(2,1)S(1)} %convert_element_type.246), channel_id=1, replica_groups=mesh['dp'=8,'mp'=4] {'dp'}, dimensions={1}, use_global_device_ids=true | all-gather | bytes 663552 | tf_op jit(solution)/shard_map/all_gather | solution.py:242
  48.5 20.1 %all-gather.4.cloned.1.call-done = bf16[2,3,768,192]{3,0,1,2:T(2,128)(2,1)} async-done(((bf16[2,3,96,192]{3,0,1,2:T(2,128)(2,1)}), bf16[2,3,768,192]{3,0,1,2:T(2,128)(2,1)}) %all-gather.4.cloned.1.call-update) | async-done | bytes 1769488 | tf_op jit(solution)/shard_map/all_gather | solution.py:241
  68.6 7.8 fusion.148
  109.7 91.0 %all-reduce.10.cloned.1.call-done = f32[1536,768]{1,0:T(8,128)} async-done(((f32[1536,768]{1,0:T(8,128)}), f32[1536,768]{1,0:T(8,128)}) %all-reduce.10.cloned.1.call-update) | async-done | bytes 4718608 | tf_op jit(solution)/shard_map/psum | solution.py:62
  208.6 47.2 %all-gather.6.cloned.1.call-done = bf16[2,768,768]{2,1,0:T(8,128)(2,1)} async-done(((bf16[2,96,768]{2,1,0:T(8,128)(2,1)}), bf16[2,768,768]{2,1,0:T(8,128)(2,1)}) %all-gather.6.cloned.1.call-update) | async-done | bytes 2359312 | tf_op jit(solution)/shard_map/all_gather | solution.py:243
  255.8 14.5 %multiply_convert_fusion.3 = (bf16[1536,768]{1,0:T(8,128)(2,1)}, f32[1536,768]{1,0:T(8,128)}, f32[1536,768]{1,0:T(8,128)}) fusion(f32[768]{0:T(1024)S(1)} %get-tuple-element.167, bf16[1536,768]{1,0:T(8,128)(2,1)S(1)} %fusion.28, bf16[2,768,768]{2,1,0:T(8,128)(2,1)} %all-gather.6.cloned.1.call-done), kind=kOutput, calls=%fused_computation.70 | convolution fusion | flops 1889796096 | bytes 15338496 | tf_op jit(solution)/shard_map/dot_general | solution.py:65
  270.3 38.8 %all-gather.8.cloned.1.call-done = bf16[2,768,768]{2,1,0:T(8,128)(2,1)} async-done(((bf16[2,96,768]{2,1,0:T(8,128)(2,1)}), bf16[2,768,768]{2,1,0:T(8,128)(2,1)}) %all-gather.8.cloned.1.call-update) | async-done | bytes 2359312 | tf_op jit(solution)/shard_map/all_gather | solution.py:244
  319.7 49.3 %all-reduce.12.cloned.1.call-done = bf16[1536,768]{1,0:T(8,128)(2,1)} async-done(((bf16[1536,768]{1,0:T(8,128)(2,1)}), bf16[1536,768]{1,0:T(8,128)(2,1)}) %all-reduce.12.cloned.1.call-update) | async-done | bytes 2359312 | tf_op jit(solution)/shard_map/psum | solution.py:70
  398.2 94.2 %all-reduce.14.cloned.1.call-done = f32[1536,768]{1,0:T(8,128)} async-done(((f32[1536,768]{1,0:T(8,128)}), f32[1536,768]{1,0:T(8,128)}) %all-reduce.14.cloned.1.call-update) | async-done | bytes 4718608 | tf_op jit(solution)/shard_map/psum | solution.py:62
  501.1 14.0 %multiply_convert_fusion.2 = (bf16[1536,768]{1,0:T(8,128)(2,1)S(1)}, f32[1536,768]{1,0:T(8,128)}, f32[1536,768]{1,0:T(8,128)}) fusion(f32[768]{0:T(1024)S(1)} %get-tuple-element.166, bf16[1536,768]{1,0:T(8,128)(2,1)S(1)} %fusion.30, bf16[2,768,768]{2,1,0:T(8,128)(2,1)S(1)} %copy-done.97), kind=kOutput, calls=%fused_computation.51 | convolution fusion | flops 1889796096 | bytes 15339520 | tf_op jit(solution)/shard_map/dot_general | solution.py:65
  520.2 55.9 %all-reduce.16.cloned.1.call-done = bf16[1536,768]{1,0:T(8,128)(2,1)} async-done(((bf16[1536,768]{1,0:T(8,128)(2,1)}), bf16[1536,768]{1,0:T(8,128)(2,1)}) %all-reduce.16.cloned.1.call-update) | async-done | bytes 2359312 | tf_op jit(solution)/shard_map/psum | solution.py:70
  598.0 55.8 %all-reduce.18.cloned.1.call-done = bf16[1536,768]{1,0:T(8,128)(2,1)} async-done(((bf16[1536,768]{1,0:T(8,128)(2,1)}), bf16[1536,768]{1,0:T(8,128)(2,1)}) %all-reduce.18.cloned.1.call-update) | async-done | bytes 2359312 | tf_op jit(solution)/shard_map/psum | solution.py:121
  653.8 7.0 multiply_reduce_fusion.3
  669.8 6.8 convert_reduce_fusion.2
  703.1 55.8 %all-reduce.20.cloned.1.call-done = bf16[1536,768]{1,0:T(8,128)(2,1)} async-done(((bf16[1536,768]{1,0:T(8,128)(2,1)}), bf16[1536,768]{1,0:T(8,128)(2,1)}) %all-reduce.20.cloned.1.call-update) | async-done | bytes 2359312 | tf_op jit(solution)/shard_map/psum | solution.py:166
  759.0 7.3 multiply_reduce_fusion.4
  781.3 55.8 %all-reduce.22.cloned.1.call-done = bf16[1536,768]{1,0:T(8,128)(2,1)} async-done(((bf16[1536,768]{1,0:T(8,128)(2,1)}), bf16[1536,768]{1,0:T(8,128)(2,1)}) %all-reduce.22.cloned.1.call-update) | async-done | bytes 2359312 | tf_op jit(solution)/shard_map/psum | solution.py:121
  837.1 7.6 multiply_reduce_fusion.5
  906.6 8.0 reshape.293
  940.6 38.2 %all-reduce = (f32[2,2,192]{2,1,0:T(2,128)S(1)}, f32[2,768]{1,0:T(2,128)S(1)}, f32[2,6,768]{2,1,0:T(8,128)S(1)}) all-reduce(f32[2,2,192]{2,1,0:T(2,128)S(1)} %pad_maximum_fusion.6, f32[2,768]{1,0:T(2,128)S(1)} %pad_maximum_fusion.5, f32[2,6,768]{2,1,0:T(8,128)S(1)} %pad_maximum_fusion.4), channel_id=1, replica_groups=mesh['dp'=8,'mp'=4] {'dp'}, use_global_device_ids=true, to_apply=%region_39.40 | all-reduce | flops 11520 | bytes 92160 | tf_op jit(solution)/shard_map/psum | solution.py:299
  987.8 20.1 %reduce-scatter.15.cloned.1.call-done = f32[96,384]{1,0:T(8,128)} async-done(((f32[768,384]{1,0:T(8,128)}), f32[96,384]{1,0:T(8,128)}) %reduce-scatter.15.cloned.1.call-update) | async-done | bytes 147472
  1012.4 77.2 %reduce-scatter.13.cloned.1.call-done = f32[96,1152]{1,0:T(8,128)} async-done(((f32[768,1152]{1,0:T(8,128)}), f32[96,1152]{1,0:T(8,128)}) %reduce-scatter.13.cloned.1.call-update) | async-done | bytes 442384
  1102.5 85.7 %reduce-scatter.11.cloned.1.call-done = f32[2,96,768]{2,1,0:T(8,128)} async-done(((f32[2,768,768]{2,1,0:T(8,128)}), f32[2,96,768]{2,1,0:T(8,128)}) %reduce-scatter.11.cloned.1.call-update) | async-done | bytes 589840 | tf_op jit(solution)/shard_map/reduce_scatter | solution.py:291
  1191.2 95.5 %reduce-scatter.9.cloned.1.call-done = f32[2,96,768]{2,1,0:T(8,128)} async-done(((f32[2,768,768]{2,1,0:T(8,128)}), f32[2,96,768]{2,1,0:T(8,128)}) %reduce-scatter.9.cloned.1.call-update) | async-done | bytes 589840 | tf_op jit(solution)/shard_map/reduce_scatter | solution.py:290
  (463 shorter events, 290.9 us)
Async XLA Ops:
  7.2 61.4 %all-gather.4.cloned.1.call-start = ((), (), s32[]{:S(2)}) async-start(), calls=%async_computation.4 | async-start | bytes 2654208 | tf_op jit(solution)/shard_map/all_gather | solution.py:241
  9.5 191.2 %all-reduce.10.cloned.1.call-start = ((), (), s32[]{:S(2)}) async-start(), calls=%async_computation.5 | async-start | bytes 9437184 | tf_op jit(solution)/shard_map/psum | solution.py:62
  10.4 84.0 %copy-start.66 = (f32[3,64]{1,0:T(4,128)}, f32[3,64]{1,0:T(4,128)S(1)}, u32[]{:S(2)}) copy-start(f32[3,64]{1,0:T(4,128)S(1)} %add.348) | copy-start | bytes 2308
  107.2 148.5 %all-gather.6.cloned.1.call-start = ((), (), s32[]{:S(2)}) async-start(), calls=%async_computation.6 | async-start | bytes 2654208 | tf_op jit(solution)/shard_map/all_gather | solution.py:243
  108.1 201.0 %all-gather.8.cloned.1.call-start = ((), (), s32[]{:S(2)}) async-start(), calls=%async_computation.7 | async-start | bytes 2654208 | tf_op jit(solution)/shard_map/all_gather | solution.py:244
  108.9 260.1 %all-reduce.12.cloned.1.call-start = ((), (), s32[]{:S(2)}) async-start(), calls=%async_computation.8 | async-start | bytes 4718592 | tf_op jit(solution)/shard_map/psum | solution.py:70
  109.6 259.4 %copy-start.62 = (f32[768]{0:T(1024)}, f32[768]{0:T(1024)S(1)}, u32[]{:S(2)}) copy-start(f32[768]{0:T(1024)S(1)} %get-tuple-element.163) | copy-start | bytes 9220
  109.7 146.1 %copy-start.91 = (f32[768]{0:T(1024)}, f32[768]{0:T(1024)S(1)}, u32[]{:S(2)}) copy-start(f32[768]{0:T(1024)S(1)} %get-tuple-element.167) | copy-start | bytes 9220
  205.1 163.9 %copy-start.49 = (f32[1536]{0:T(1024)}, f32[1536]{0:T(1024)S(1)}, u32[]{:S(2)}) copy-start(f32[1536]{0:T(1024)S(1)} %broadcast_multiply_fusion.11) | copy-start | bytes 18436
  205.8 163.3 %copy-start.53 = (f32[1536]{0:T(1024)}, f32[1536]{0:T(1024)S(1)}, u32[]{:S(2)}) copy-start(f32[1536]{0:T(1024)S(1)} %add_rsqrt_fusion.3) | copy-start | bytes 18436
  314.7 177.7 %all-reduce.14.cloned.1.call-start = ((), (), s32[]{:S(2)}) async-start(), calls=%async_computation.9 | async-start | bytes 9437184 | tf_op jit(solution)/shard_map/psum | solution.py:62
  398.2 177.9 %all-reduce.16.cloned.1.call-start = ((), (), s32[]{:S(2)}) async-start(), calls=%async_computation.10 | async-start | bytes 4718592 | tf_op jit(solution)/shard_map/psum | solution.py:70
  520.1 133.7 %all-reduce.18.cloned.1.call-start = ((), (), s32[]{:S(2)}) async-start(), calls=%async_computation.11 | async-start | bytes 4718592 | tf_op jit(solution)/shard_map/psum | solution.py:121
  597.9 161.0 %all-reduce.20.cloned.1.call-start = ((), (), s32[]{:S(2)}) async-start(), calls=%async_computation.12 | async-start | bytes 4718592 | tf_op jit(solution)/shard_map/psum | solution.py:166
  703.1 134.0 %all-reduce.22.cloned.1.call-start = ((), (), s32[]{:S(2)}) async-start(), calls=%async_computation.13 | async-start | bytes 4718592 | tf_op jit(solution)/shard_map/psum | solution.py:121
  781.2 200.8 %all-reduce.24.cloned.1.call-start = ((), (), s32[]{:S(2)}) async-start(), calls=%async_computation.14 | async-start | bytes 4718592 | tf_op jit(solution)/shard_map/psum | solution.py:166
  884.3 123.5 %reduce-scatter.15.cloned.1.call-start = ((), (), s32[]{:S(2)}) async-start(), calls=%async_computation.18 | async-start | bytes 1327104
  893.7 196.0 %reduce-scatter.13.cloned.1.call-start = ((), (), s32[]{:S(2)}) async-start(), calls=%async_computation.17 | async-start | bytes 3981312
  914.6 273.6 %reduce-scatter.11.cloned.1.call-start = ((), (), s32[]{:S(2)}) async-start(), calls=%async_computation.16 | async-start | bytes 5308416 | tf_op jit(solution)/shard_map/reduce_scatter | solution.py:291
  927.3 359.4 %reduce-scatter.9.cloned.1.call-start = ((), (), s32[]{:S(2)}) async-start(), calls=%async_computation.15 | async-start | bytes 5308416 | tf_op jit(solution)/shard_map/reduce_scatter | solution.py:290
  1091.2 97.0 %copy-start.36 = (f32[2,96,768]{2,1,0:T(8,128)S(1)}, f32[2,96,768]{2,1,0:T(8,128)}, u32[]{:S(2)}) copy-start(f32[2,96,768]{2,1,0:T(8,128)} %param.32) | copy-start | bytes 1769476
  1094.9 191.8 %copy-start.38 = (f32[2,96,768]{2,1,0:T(8,128)S(1)}, f32[2,96,768]{2,1,0:T(8,128)}, u32[]{:S(2)}) copy-start(f32[2,96,768]{2,1,0:T(8,128)} %param.31) | copy-start | bytes 1769476
  1094.9 191.8 %copy-start.46 = (f32[2,96,768]{2,1,0:T(8,128)S(1)}, f32[2,96,768]{2,1,0:T(8,128)}, u32[]{:S(2)}) copy-start(f32[2,96,768]{2,1,0:T(8,128)} %param.38) | copy-start | bytes 1769476
  1094.9 191.8 %copy-start.47 = (f32[2,96,768]{2,1,0:T(8,128)S(1)}, f32[2,96,768]{2,1,0:T(8,128)}, u32[]{:S(2)}) copy-start(f32[2,96,768]{2,1,0:T(8,128)} %param.45) | copy-start | bytes 1769476
  (112 other events, 1133.2 us)
Sparse Core Ops, SparseCore 0:
  10.8 57.7 all-gather.3
  107.4 93.3 all-reduce.9
  203.5 52.2 all-gather.5
  258.4 50.6 all-gather.7
  314.8 54.1 all-reduce.11
  398.3 94.0 all-reduce.13
  520.2 55.8 all-reduce.15
  598.1 55.7 all-reduce.17
  703.2 55.7 all-reduce.19
  781.3 55.7 all-reduce.21
  884.5 55.7 all-reduce.23
  943.5 64.3 reduce-scatter.14
  1011.5 78.0 reduce-scatter.12
  1093.1 94.9 reduce-scatter.10
  1191.7 94.9 reduce-scatter.8
where the time goes:
time: 1300 us
  waiting for transfers between devices  843 us (65%)
  matrix products  149 us (11%)
  local copies, waits for them, and re-layouts  112 us (9%)
  other arithmetic  102 us (8%)
  blocking collectives  73.7 us (6%)
  between operations  16.4 us (1%)
    psum x2, waiting for transfers between devices, forward_layer(): attended = lax.psum(partial_attn, 'mp') + rows[0]  185 us
    psum x2, waiting for transfers between devices, backward_layer(): lax.psum(partial_up.astype(jnp.bfloat16), 'mp').astype(jnp.float32)  112 us
    psum x2, waiting for transfers between devices, forward_layer(): lax.psum(partial_ffn.astype(jnp.bfloat16), 'mp').astype(jnp.float32)  105 us
    unnamed x17, waiting for transfers between devices  97.5 us
    reduce_scatter x1, waiting for transfers between devices, local(): lax.psum_scatter(stacked_mats[2], 'dp', scatter_dimension=1, tiled=True)  95.5 us
    reduce_scatter x1, waiting for transfers between devices, local(): lax.psum_scatter(stacked_mats[3], 'dp', scatter_dimension=1, tiled=True)  85.7 us
    unnamed x276, local copies, waits for them, and re-layouts  69 us
    psum x2, waiting for transfers between devices, backward_layer(): lax.psum(partial_in.astype(jnp.bfloat16), 'mp').astype(jnp.float32)  55.8 us
  transfers between devices with their start and end apart: 15, of which 14 were waited for; matrix products, arithmetic and copies ran while one was open for 9% of the time, Pallas kernels for 0%

commit v1 on v0

v1 whole, which is shorter than its diff:
```python
import jax
import jax.numpy as jnp
from jax import lax
from jax.sharding import PartitionSpec as P

HEAD_DIM = 64
LAYERS = 2
ADAM_STEP = 10

EPS_NORM = 1e-12
EPS_ADAM = 1e-08
RATE_MATRIX = 0.04
RATE_VECTOR = 0.3
DECAY_MATRIX = 0.01

F32 = jnp.float32
BF16 = jnp.bfloat16
AXES = ("dp", "mp")


class Links:
    def __init__(self, n_dp):
        self.count = n_dp * 4
        self.bits = n_dp.bit_length() - 1
        dp_at = lax.axis_index("dp")
        mp_at = lax.axis_index("mp")
        self.at_x = mp_at // 2
        self.core = mp_at % 2
        self.at_y = dp_at % 2
        self.dp_at = dp_at

    def swap(self, array, mask0, mask1=None):
        mask1 = mask0 if mask1 is None else mask1
        pairs = [(i, i ^ (mask1 if i & 1 else mask0)) for i in range(self.count)]
        return lax.ppermute(array, AXES, pairs)

    def swap_core(self, array):
        return self.swap(array, 1)

    def swap_x(self, array):
        return self.swap(array, 2)

    def gather(self, piece):
        block = piece[None]
        for bit in range(1, self.bits):
            other = self.swap(block, 4 << bit)
            mine = ((self.dp_at >> bit) & 1) == 0
            block = jnp.concatenate([jnp.where(mine, block, other), jnp.where(mine, other, block)])
        near = self.swap(block, 4, 2)
        far = self.swap(jnp.stack([block, near]), 2, 4)
        first = self.core == 0
        own_far = jnp.where(first, near, far[0])
        other_near = jnp.where(first, far[0], near)
        other_far = far[1]
        return self.rows(block, own_far), self.rows(other_near, other_far)

    def rows(self, same, other):
        low = self.at_y == 0
        both = jnp.stack([jnp.where(low, same, other), jnp.where(low, other, same)], axis=1)
        return both.reshape(-1, both.shape[-1])

    def scatter(self, grad_own, grad_other):
        rows = grad_own.shape[0] >> self.bits
        low = self.at_y == 0

        def halves(grad):
            grad = grad.reshape(-1, 2, rows, grad.shape[-1])
            return jnp.where(low, grad[:, 0], grad[:, 1]), jnp.where(low, grad[:, 1], grad[:, 0])

        own_same, own_far = halves(grad_own)
        other_same, other_far = halves(grad_other)
        first = self.core == 0
        came = self.swap(jnp.stack([jnp.where(first, other_same, own_far), other_far]), 2, 4)
        keep = own_same.astype(F32) + came[0].astype(F32)
        give = jnp.where(first, own_far, other_same).astype(F32) + came[1].astype(F32)
        came = self.swap(give.astype(BF16), 4, 2)
        keep = keep + came.astype(F32)
        for bit in reversed(range(1, self.bits)):
            half = keep.shape[0] // 2
            mine = ((self.dp_at >> bit) & 1) == 0
            give = jnp.where(mine, keep[half:], keep[:half]).astype(BF16)
            keep = jnp.where(mine, keep[:half], keep[half:])
            keep = keep + self.swap(give, 4 << bit).astype(F32)
        return keep[0]


def norm_parts(residual, gain_row, shift_row):
    center = residual - jnp.mean(residual, axis=-1, keepdims=True)
    inv_std = lax.rsqrt(jnp.mean(center * center, axis=-1, keepdims=True) + EPS_NORM)
    scaled = center * inv_std
    return (scaled * gain_row + shift_row, scaled, inv_std)


def norm_back(grad_output, scaled, inv_std, gain_row):
    upstream = grad_output * gain_row
    mean_up = jnp.mean(upstream, axis=-1, keepdims=True)
    mean_cross = jnp.mean(upstream * scaled, axis=-1, keepdims=True)
    return inv_std * (upstream - mean_up - scaled * mean_cross)


def dot(a, b, dims):
    return lax.dot_general(a, b, (dims, ((), ())), preferred_element_type=F32)


NN = ((1,), (0,))
NT = ((1,), (1,))
TN = ((0,), (0,))


def both_cores(links, partial):
    low = partial.astype(BF16)
    return low.astype(F32) + links.swap_core(low).astype(F32)


def heads_of(rows_in):
    return rows_in.reshape(rows_in.shape[0], -1, HEAD_DIM)


def attend(queries, keys, values, mask):
    scores = jnp.einsum("qhe,khe->hqk", heads_of(queries), heads_of(keys), preferred_element_type=F32)
    scores = jnp.where(mask[None, None, :], scores, -1000000000.0)
    shifted = jnp.exp(scores - jnp.max(scores, axis=-1, keepdims=True))
    probs = shifted / jnp.sum(shifted, axis=-1, keepdims=True)
    context = jnp.einsum("hqk,khe->qhe", probs.astype(BF16), heads_of(values), preferred_element_type=F32)
    return context.reshape(queries.shape).astype(BF16), probs


def attend_back(grad_context, queries, keys, values, probs):
    low = probs.astype(BF16)
    grad_heads = heads_of(grad_context)
    grad_values = jnp.einsum("hqk,qhe->khe", low, grad_heads, preferred_element_type=F32)
    grad_probs = jnp.einsum("qhe,khe->hqk", grad_heads, heads_of(values), preferred_element_type=F32)
    inner = jnp.sum(probs * grad_probs, axis=-1, keepdims=True)
    grad_scores = (probs * (grad_probs - inner)).astype(BF16)
    grad_queries = jnp.einsum("hqk,khe->qhe", grad_scores, heads_of(keys), preferred_element_type=F32)
    grad_queries = (grad_queries.astype(BF16) * 0.125).reshape(queries.shape)
    grad_keys = jnp.einsum("hqk,qhe->khe", grad_scores, heads_of(queries), preferred_element_type=F32)
    return grad_queries, grad_keys.reshape(keys.shape), grad_values.reshape(values.shape)


def gelu_parts(pre):
    cdf = 0.5 * (1.0 + lax.erf(pre * 0.7071067811865476))
    pdf = jnp.exp(-0.5 * pre * pre) * 0.3989422804014327
    return (pre * cdf).astype(BF16), cdf + pre * pdf


def forward_layer(links, hidden, low_other, weights, head_b, ffn_b, rows, masks, full):
    in_low = hidden.astype(BF16)
    third = head_b[0].shape[-1]
    columns = 3 * third
    parts, near, far = [], [], []
    for g in range(2):
        weight = weights[0][g]
        projected = dot(in_low, weight[:, :columns], NN)
        queries = ((projected[:, :third] + head_b[g][0]) * 0.125).astype(BF16)
        keys = projected[:, third : 2 * third].astype(BF16)
        values = (projected[:, 2 * third :] + head_b[g][1]).astype(BF16)
        near.append((queries, keys, values))
        if low_other is not None:
            other = dot(low_other, weight[:, third:columns], NN)
            far += [other[:, :third].astype(BF16), (other[:, third:] + head_b[g][1]).astype(BF16)]
    if low_other is None:
        sent = jnp.concatenate([near[1][1][full:], near[1][2][full:], near[0][1][full:], near[0][2][full:]], axis=1)
        far = jnp.split(links.swap_x(sent), 4, axis=1)
    partial = 0.0
    for g in range(2):
        queries, keys, values = near[g]
        keys_half = jnp.concatenate([keys[full:], far[2 * g]])
        values_half = jnp.concatenate([values[full:], far[2 * g + 1]])
        context_full, probs_full = attend(queries[:full], keys[:full], values[:full], masks[0])
        context_half, probs_half = attend(queries[full:], keys_half, values_half, masks[1])
        context = jnp.concatenate([context_full, context_half])
        partial = partial + dot(context, weights[0][g][:, columns:], NT)
        parts.append((queries, keys, values, keys_half, values_half, probs_full, probs_half, context))
    attended = both_cores(links, partial) + rows[0]
    normed, scaled_one, inv_one = norm_parts(hidden + attended, rows[2], rows[3])
    normed_low = normed.astype(BF16)
    partial = 0.0
    ffn_parts = []
    wide = ffn_b[0].shape[-1]
    for g in range(2):
        weight = weights[1][g]
        activated, slope = gelu_parts(dot(normed_low, weight[:, :wide], NN) + ffn_b[g])
        partial = partial + dot(activated, weight[:, wide:], NT)
        ffn_parts.append((activated, slope))
    result, scaled_two, inv_two = norm_parts(normed + both_cores(links, partial) + rows[1], rows[4], rows[5])
    return result, (in_low, parts, scaled_one, inv_one, normed_low, ffn_parts, scaled_two, inv_two)


def backward_layer(links, grad_output, record, weights, rows, full):
    in_low, parts, scaled_one, inv_one, normed_low, ffn_parts, scaled_two, inv_two = record
    gain_two = jnp.sum(grad_output * scaled_two, axis=0)
    shift_two = jnp.sum(grad_output, axis=0)
    upper = norm_back(grad_output, scaled_two, inv_two, rows[4])
    upper_low = upper.astype(BF16)
    partial = 0.0
    ffn_grads, ffn_vecs = [], []
    for g in range(2):
        weight = weights[1][g]
        activated, slope = ffn_parts[g]
        wide = activated.shape[1]
        grad_pre = (dot(upper_low, weight[:, wide:], NN) * slope).astype(BF16)
        partial = partial + dot(grad_pre, weight[:, :wide], NT)
        grad_up = dot(normed_low, grad_pre, TN).astype(BF16)
        grad_down = dot(upper_low, activated, TN).astype(BF16)
        ffn_grads.append(jnp.concatenate([grad_up, grad_down], axis=1))
        ffn_vecs.append(jnp.sum(grad_pre.astype(F32), axis=0))
    grad_normed = upper + both_cores(links, partial)
    gain_one = jnp.sum(grad_normed * scaled_one, axis=0)
    shift_one = jnp.sum(grad_normed, axis=0)
    lower = norm_back(grad_normed, scaled_one, inv_one, rows[2])
    lower_low = lower.astype(BF16)
    partial = 0.0
    attn_grads, head_vecs, contexts, halves = [], [], [], []
    for g in range(2):
        queries, keys, values, keys_half, values_half, probs_full, probs_half, context = parts[g]
        grad_context = dot(lower_low, weights[0][g][:, 3 * queries.shape[1] :], NN).astype(BF16)
        contexts.append(grad_context)
        halves.append(attend_back(grad_context[full:], queries[full:], keys_half, values_half, probs_half))
    own = halves[0][0].shape[0]
    sent = jnp.concatenate([halves[1][1][own:], halves[1][2][own:], halves[0][1][own:], halves[0][2][own:]], axis=1)
    came = jnp.split(links.swap_x(sent.astype(BF16)).astype(F32), 4, axis=1)
    for g in range(2):
        weight = weights[0][g]
        queries, keys, values, keys_half, values_half, probs_full, probs_half, context = parts[g]
        third = queries.shape[1]
        dq_half, dk_half, dv_half = halves[g]
        dq_full, dk_full, dv_full = attend_back(
            contexts[g][:full], queries[:full], keys[:full], values[:full], probs_full
        )
        dk = jnp.concatenate([dk_full, dk_half[:own] + came[2 * g]]).astype(BF16)
        dv = jnp.concatenate([dv_full, dv_half[:own] + came[2 * g + 1]]).astype(BF16)
        grad_qkv = jnp.concatenate([jnp.concatenate([dq_full, dq_half]), dk, dv], axis=1)
        partial = partial + dot(grad_qkv, weight[:, : 3 * third], NT)
        grad_in = dot(in_low, grad_qkv, TN).astype(BF16)
        grad_out = dot(lower_low, context, TN).astype(BF16)
        attn_grads.append(jnp.concatenate([grad_in, grad_out], axis=1))
        sums = jnp.sum(grad_qkv.astype(F32), axis=0)
        head_vecs.append(jnp.stack([sums[:third], sums[2 * third :]]))
    grad_hidden = lower + both_cores(links, partial)
    row_grads = jnp.stack(
        [jnp.sum(lower, axis=0), jnp.sum(upper, axis=0), gain_one, shift_one, gain_two, shift_two]
    )
    return grad_hidden, attn_grads, ffn_grads, (head_vecs, ffn_vecs, row_grads)


def adam_step(master, moment, second, gradient, step_rate, decay_rate):
    correction = 1.0 - 0.5**ADAM_STEP
    moment_new = 0.5 * moment + 0.5 * gradient
    second_new = 0.5 * second + 0.5 * gradient * gradient
    update = (
        moment_new / correction / (jnp.sqrt(second_new / correction) + EPS_ADAM)
        + decay_rate * master
    )
    return (master - step_rate * update, moment_new, second_new)


def to_groups(vector, at, count):
    zeros = jnp.zeros(vector.shape[:-1] + (count, vector.shape[-1]), F32)
    zeros = lax.dynamic_update_index_in_dim(zeros, vector, at, axis=vector.ndim - 1)
    return zeros.reshape(vector.shape[:-1] + (-1,))


def local(n_dp, *args):
    (
        inputs,
        cotangent,
        word_lengths,
        word_count,
        attn_in,
        attn_out,
        ffn_up,
        ffn_down,
        head_bias,
        ffn_bias,
        row_params,
    ) = args[:11]
    moments, seconds = args[11:18], args[18:25]
    links = Links(n_dp)
    at_x = links.at_x
    seq_len = inputs.shape[0] // word_count.shape[0]
    half = seq_len // 2
    third, wide = attn_in.shape[3], ffn_up.shape[2]
    slots = jnp.arange(word_lengths.shape[1], dtype=jnp.int32)
    used = jnp.sum(jnp.where(slots[None, :] < word_count[:, None], word_lengths, 0), axis=1)

    def own_rows(array):
        whole = lax.dynamic_slice_in_dim(array, at_x * 2 * seq_len, seq_len)
        return jnp.concatenate([whole, lax.dynamic_slice_in_dim(array, seq_len + at_x * half, half)])

    def all_rows(array):
        low = array.astype(BF16)
        other = links.swap_x(low)
        low, other = low.astype(F32), other.astype(F32)
        first = at_x == 0
        return jnp.concatenate(
            [
                jnp.where(first, low[:seq_len], other[:seq_len]),
                jnp.where(first, low[seq_len:], other[seq_len:]),
                jnp.where(first, other[seq_len:], low[seq_len:]),
                jnp.where(first, other[:seq_len], low[:seq_len]),
            ]
        )

    places = jnp.arange(half, dtype=jnp.int32)
    used_full = jnp.where(at_x == 0, used[0], used[2])
    mask_full = jnp.arange(seq_len, dtype=jnp.int32) < used_full
    mask_half = jnp.concatenate([places + at_x * half, places + (1 - at_x) * half]) < used[1]
    masks = (mask_full, mask_half)
    row_mask = jnp.concatenate([mask_full, mask_half[:half]]).astype(F32)[:, None]

    weights = []
    for layer in range(LAYERS):
        attn = jnp.concatenate([attn_in[layer, 0], attn_in[layer, 1], attn_in[layer, 2], attn_out[layer]], axis=1)
        ffn = jnp.concatenate([ffn_up[layer], ffn_down[layer]], axis=1)
        weights.append((links.gather(attn.astype(BF16)), links.gather(ffn.astype(BF16))))
    bias_far = links.swap_x(jnp.concatenate([head_bias.reshape(-1), ffn_bias.reshape(-1)]))
    head_b = (head_bias, bias_far[: head_bias.size].reshape(head_bias.shape))
    ffn_b = (ffn_bias, bias_far[head_bias.size :].reshape(ffn_bias.shape))

    hidden = own_rows(inputs)
    low_other = lax.dynamic_slice_in_dim(inputs, seq_len + (1 - at_x) * half, half).astype(BF16)
    records = []
    for layer in range(LAYERS):
        hidden, record = forward_layer(
            links,
            hidden,
            low_other if layer == 0 else None,
            weights[layer],
            [b[layer] for b in head_b],
            [b[layer] for b in ffn_b],
            row_params[layer],
            masks,
            seq_len,
        )
        records.append(record)
    encoded = all_rows(hidden)
    grad_hidden = own_rows(cotangent) * row_mask
    matrix_grads, vector_grads = [None] * LAYERS, [None] * LAYERS
    for layer in reversed(range(LAYERS)):
        grad_hidden, attn_grads, ffn_grads, vector_grads[layer] = backward_layer(
            links, grad_hidden, records[layer], weights[layer], row_params[layer], seq_len
        )
        matrix_grads[layer] = (links.scatter(*attn_grads), links.scatter(*ffn_grads))
    input_grad = all_rows(grad_hidden)

    group = at_x * 2 + links.core
    other_group = (1 - at_x) * 2 + links.core
    head_sum = jnp.stack(
        [
            to_groups(v[0][0], group, 4) + to_groups(v[0][1], other_group, 4)
            for v in vector_grads
        ]
    )
    ffn_sum = jnp.stack(
        [
            to_groups(v[1][0], group, 4) + to_groups(v[1][1], other_group, 4)
            for v in vector_grads
        ]
    )
    row_sum = jnp.where(links.core == 0, jnp.stack([v[2] for v in vector_grads]), 0.0)
    head_sum, ffn_sum, row_sum = lax.psum((head_sum, ffn_sum, row_sum), AXES)
    head_grad = lax.dynamic_slice_in_dim(head_sum, group * third, third, axis=2)
    ffn_grad = lax.dynamic_slice_in_dim(ffn_sum, group * wide, wide, axis=1)

    attn = jnp.stack([m[0] for m in matrix_grads])
    ffn = jnp.stack([m[1] for m in matrix_grads])
    gradients = (
        jnp.stack([attn[:, :, k * third : (k + 1) * third] for k in range(3)], axis=1),
        attn[:, :, 3 * third :],
        ffn[:, :, :wide],
        ffn[:, :, wide:],
        head_grad,
        ffn_grad,
        row_sum,
    )
    params = (attn_in, attn_out, ffn_up, ffn_down, head_bias, ffn_bias, row_params)
    stepped = [
        adam_step(
            params[i],
            moments[i],
            seconds[i],
            gradients[i],
            RATE_MATRIX if i < 4 else RATE_VECTOR,
            DECAY_MATRIX if i < 4 else 0.0,
        )
        for i in range(7)
    ]
    news, moms, vars_ = zip(*stepped)
    copies = tuple(news[i].astype(BF16) for i in range(4))
    return (encoded, input_grad) + news + moms + vars_ + copies


def solution(mesh):
    n_dp = mesh.shape["dp"]
    row = P("dp", None)
    state = (
        P(None, None, "dp", "mp"),
        P(None, "dp", "mp"),
        P(None, "dp", "mp"),
        P(None, "dp", "mp"),
        P(None, None, "mp"),
        P(None, "mp"),
        P(),
    )

    def step(*args):
        return local(n_dp, *args)

    return jax.shard_map(
        step,
        mesh=mesh,
        in_specs=(row, row, row, P("dp")) + state * 3,
        out_specs=(row, row) + state * 3 + state[:4],
        check_vma=False,
    )
```

time: 1300 us -> 844 us (0.65)
  waiting for transfers between devices: 843 us -> 301 us
  blocking collectives: 73.7 us -> 0 us
  starting transfers between devices: 0.87 us -> 52.9 us
  other arithmetic: 102 us -> 151 us
  matrix products: 149 us -> 183 us
    psum x8 -> x1, waiting for transfers between devices: 458 us -> 115 us  [local(): head_sum, ffn_sum, row_sum = lax.psum((head_sum, ffn_sum, row_sum), AXES)]
    ppermute x0 -> x46, waiting for transfers between devices: none -> 186 us  [swap(): return lax.ppermute(array, AXES, pairs)]
    reduce_scatter x2 -> x0, waiting for transfers between devices: 181 us -> none  [the longest x1 95.5 us: local(): lax.psum_scatter(stacked_mats[2], 'dp', scatter_dimension=1, tiled=True)]
    all_gather x3 -> x0, waiting for transfers between devices: 106 us -> none  [the longest x1 47.2 us: local(): lax.all_gather(ffn_up.astype(jnp.bfloat16), 'dp', axis=1, tiled=True)]
    unnamed x17 -> x1, waiting for transfers between devices: 97.5 us -> 0.02 us
    ppermute x0 -> x46, starting transfers between devices: none -> 52.9 us  [swap(): return lax.ppermute(array, AXES, pairs)]
    psum x1 -> x0, blocking collectives: 38.2 us -> none  [local(): lax.psum((stacked_vecs[0], stacked_vecs[1], stacked_vecs[2]), 'dp')]
    all_gather x1 -> x0, blocking collectives: 35.5 us -> none  [local(): lax.all_gather(attn_out.astype(jnp.bfloat16), 'dp', axis=1, tiled=True)]
  transfers between devices with their start and end apart: 15 -> 47, of which waited for: 14 -> 19; matrix products, arithmetic and copies ran while one was open for 9% -> 47% of each run, Pallas kernels for 0% -> 0%
where the time goes in v1:
time: 844 us; the launch traced here: 831 us
  waiting for transfers between devices  301 us (36%)
  matrix products  183 us (22%)
  other arithmetic  151 us (18%)
  local copies, waits for them, and re-layouts  124 us (15%)
  starting transfers between devices  52.9 us (6%)
  between operations  19.7 us (2%)
    ppermute x46, waiting for transfers between devices, swap(): return lax.ppermute(array, AXES, pairs)  186 us
    psum x1, waiting for transfers between devices, local(): head_sum, ffn_sum, row_sum = lax.psum((head_sum, ffn_sum, row_sum), AXES)  115 us
    dot_general x50, matrix products, dot(): return lax.dot_general(a, b, (dims, ((), ())), preferred_element_type=F32)  94.9 us
    ppermute x46, starting transfers between devices, swap(): return lax.ppermute(array, AXES, pairs)  52.9 us
    unnamed x637, local copies, waits for them, and re-layouts  49.5 us
    sub x8, matrix products, attend(): shifted = jnp.exp(scores - jnp.max(scores, axis=-1, keepdims=True))  28.6 us
    dot_general x8, matrix products, attend(): jnp.einsum('hqk,khe->qhe', probs.astype(BF16), heads_of(values), preferre...  19.4 us
  transfers between devices with their start and end apart: 47, of which 19 were waited for; matrix products, arithmetic and copies ran while one was open for 47% of the time, Pallas kernels for 0%

profile of v1, /device:TPU:0, one launch (start us, length us, event | category | flops | bytes accessed | tf_op | source)
XLA Modules:
  0.0 831.1 jit_solution(2778515474140437774)
XLA Ops:
  39.4 24.1 %collective-permute-done.1 = bf16[2,96,768]{2,1,0:T(8,128)(2,1)S(1)} collective-permute-done((bf16[2,96,768]{2,1,0:T(8,128)(2,1)S(1)}, bf16[2,96,768]{2,1,0:T(8,128)(2,1)S(1)}, u32[]{:S(2)}, u32[]{:S(2)}) %collective-permute-start.1) | collective-permute-done | bytes 294944 | tf_op jit(solution)/shard_map/ppermute | solution.py:35
  67.2 6.3 collective-permute-done.2
  81.4 13.7 %collective-permute-done.18 = bf16[2,96,1536]{2,1,0:T(8,128)(2,1)} collective-permute-done((bf16[2,96,1536]{2,1,0:T(8,128)(2,1)}, bf16[2,96,1536]{2,1,0:T(8,128)(2,1)}, u32[]{:S(2)}, u32[]{:S(2)}) %collective-permute-start.18) | collective-permute-done | bytes 589856 | tf_op jit(solution)/shard_map/ppermute | solution.py:35
  95.1 12.6 %collective-permute-done.7 = bf16[2,96,1536]{2,1,0:T(8,128)(2,1)} collective-permute-done((bf16[2,96,1536]{2,1,0:T(8,128)(2,1)}, bf16[2,96,1536]{2,1,0:T(8,128)(2,1)}, u32[]{:S(2)}, u32[]{:S(2)}) %collective-permute-start.7) | collective-permute-done | bytes 589856 | tf_op jit(solution)/shard_map/ppermute | solution.py:35
  136.8 4.4 fusion.264
  166.8 12.0 %collective-permute-done.13 = bf16[4,96,768]{2,1,0:T(8,128)(2,1)S(1)} collective-permute-done((bf16[4,96,768]{2,1,0:T(8,128)(2,1)S(1)}, bf16[4,96,768]{2,1,0:T(8,128)(2,1)S(1)}, u32[]{:S(2)}, u32[]{:S(2)}) %collective-permute-start.13) | collective-permute-done | bytes 589856 | tf_op jit(solution)/shard_map/ppermute | solution.py:35
  181.2 26.5 %collective-permute-done.9 = bf16[2,4,96,1536]{3,2,1,0:T(8,128)(2,1)S(1)} collective-permute-done((bf16[2,4,96,1536]{3,2,1,0:T(8,128)(2,1)S(1)}, bf16[2,4,96,1536]{3,2,1,0:T(8,128)(2,1)S(1)}, u32[]{:S(2)}, u32[]{:S(2)}) %collective-permute-start.9) | collective-permute-done | bytes 2359328 | tf_op jit(solution)/shard_map/ppermute | solution.py:35
  233.0 4.4 fusion.273
  237.5 4.4 fusion.271
  249.3 8.4 %collective-permute-done.15 = bf16[256,768]{0,1:T(8,128)(2,1)} collective-permute-done((bf16[256,768]{0,1:T(8,128)(2,1)}, bf16[256,768]{0,1:T(8,128)(2,1)}, u32[]{:S(2)}, u32[]{:S(2)}) %collective-permute-start.15) | collective-permute-done | bytes 393248 | tf_op jit(solution)/shard_map/ppermute | solution.py:35
  343.4 4.3 copy.184
  350.8 4.7 copy.187
  403.1 14.8 %collective-permute-done.22 = bf16[768,768]{0,1:T(8,128)(2,1)} collective-permute-done((bf16[768,768]{0,1:T(8,128)(2,1)}, bf16[768,768]{0,1:T(8,128)(2,1)}, u32[]{:S(2)}, u32[]{:S(2)}) %collective-permute-start.22) | collective-permute-done | bytes 1179680 | tf_op jit(solution)/shard_map/ppermute | solution.py:35
  427.1 6.1 copy.194
  502.3 4.6 copy.181
  513.7 9.1 %collective-permute-done.35 = bf16[4,96,768]{2,1,0:T(8,128)(2,1)S(1)} collective-permute-done((bf16[4,96,768]{2,1,0:T(8,128)(2,1)S(1)}, bf16[4,96,768]{2,1,0:T(8,128)(2,1)S(1)}, u32[]{:S(2)}, u32[]{:S(2)}) %collective-permute-start.35) | collective-permute-done | bytes 589856 | tf_op jit(solution)/shard_map/ppermute | solution.py:35
  526.4 12.2 %collective-permute-done.36 = bf16[2,96,768]{2,1,0:T(8,128)(2,1)S(1)} collective-permute-done((bf16[2,96,768]{2,1,0:T(8,128)(2,1)S(1)}, bf16[2,96,768]{2,1,0:T(8,128)(2,1)S(1)}, u32[]{:S(2)}, u32[]{:S(2)}) %collective-permute-start.36) | collective-permute-done | bytes 294944 | tf_op jit(solution)/shard_map/ppermute | solution.py:35
  541.8 4.1 collective-permute-done.37
  615.0 115.1 %all-reduce.3.cloned.1.call-done = (f32[2,2,768]{2,1,0:T(2,128)}, f32[2,3072]{1,0:T(2,128)}, f32[2,6,768]{2,1,0:T(8,128)}) async-done(((f32[2,2,768]{2,1,0:T(2,128)}, f32[2,3072]{1,0:T(2,128)}, f32[2,6,768]{2,1,0:T(8,128)}), (f32[2,2,768]{2,1,0:T(2,128)}, f32[2,3072]{1,0:T(2,128)}, f32[2,6,768]{2,1,0:T(8,128)})) %all-reduce.3.cloned.1.call-update) | async-done | bytes 73744 | tf_op jit(solution)/shard_map/psum | solution.py:362
  747.6 13.4 %collective-permute-done.31 = bf16[4,96,768]{2,1,0:T(8,128)(2,1)S(1)} collective-permute-done((bf16[4,96,768]{2,1,0:T(8,128)(2,1)S(1)}, bf16[4,96,768]{2,1,0:T(8,128)(2,1)S(1)}, u32[]{:S(2)}, u32[]{:S(2)}) %collective-permute-start.31) | collective-permute-done | bytes 589856 | tf_op jit(solution)/shard_map/ppermute | solution.py:35
  770.6 9.4 %collective-permute-start.33 = (bf16[1,96,768]{2,1,0:T(8,128)(2,1)S(1)}, bf16[1,96,768]{2,1,0:T(8,128)(2,1)S(1)}, u32[]{:S(2)}, u32[]{:S(2)}) collective-permute-start(bf16[1,96,768]{2,1,0:T(8,128)(2,1)S(1)} %select_convert_fusion.7), channel_id=1, source_target_pairs={{0,8},{1,9},{2,10},{3,11},{4,12},{5,13},{6,14},{7,15},{8,0},{9,1},... | collective-permute-start | bytes 442376 | tf_op jit(solution)/shard_map/ppermute | solution.py:35
  780.1 3.6 collective-permute-start.40
  789.6 20.7 %collective-permute-done.40 = bf16[2,96,1536]{2,1,0:T(8,128)(2,1)S(1)} collective-permute-done((bf16[2,96,1536]{2,1,0:T(8,128)(2,1)S(1)}, bf16[2,96,1536]{2,1,0:T(8,128)(2,1)S(1)}, u32[]{:S(2)}, u32[]{:S(2)}) %collective-permute-start.40) | collective-permute-done | bytes 589856 | tf_op jit(solution)/shard_map/ppermute | solution.py:35
  813.9 6.2 copy.195
  (1114 shorter events, 466.2 us)
Async XLA Ops:
  7.2 722.8 %all-reduce.3.cloned.1.call-start = ((), (), s32[]{:S(2)}) async-start(), calls=%async_computation | async-start | bytes 172032 | tf_op jit(solution)/shard_map/psum | solution.py:362
  13.1 52.1 %collective-permute-start.6 = (bf16[1,96,1536]{2,1,0:T(8,128)(2,1)}, bf16[1,96,1536]{2,1,0:T(8,128)(2,1)}, u32[]{:S(2)}, u32[]{:S(2)}) collective-permute-start(bf16[1,96,1536]{2,1,0:T(8,128)(2,1)} %pad_maximum_fusion.41), channel_id=1, source_target_pairs={{0,8},{1,9},{2,10},{3,11},{4,12},{5,13},{6,14},{7,15},{8,0},{9,1},... | collective-permute-start | bytes 884744 | tf_op jit(solution)/shard_map/ppermute | solution.py:35
  18.2 60.0 %collective-permute-start.4 = (f32[2304]{0:T(1024)}, f32[2304]{0:T(1024)}, u32[]{:S(2)}, u32[]{:S(2)}) collective-permute-start(f32[2304]{0:T(1024)} %pad_maximum_fusion.66), channel_id=1, source_target_pairs={{0,2},{1,3},{2,0},{3,1},{4,6},{5,7},{6,4},{7,5},{8,10},{9,11},{10,... | collective-permute-start | bytes 27656 | tf_op jit(solution)/shard_map/ppermute | solution.py:35
  39.2 56.0 %collective-permute-start.18 = (bf16[2,96,1536]{2,1,0:T(8,128)(2,1)}, bf16[2,96,1536]{2,1,0:T(8,128)(2,1)}, u32[]{:S(2)}, u32[]{:S(2)}) collective-permute-start(bf16[2,96,1536]{2,1,0:T(8,128)(2,1)} %pad_maximum_fusion.33), channel_id=1, source_target_pairs={{0,16},{1,17},{2,18},{3,19},{4,20},{5,21},{6,22},{7,23},{8,24},{9,... | collective-permute-start | bytes 1769480 | tf_op jit(solution)/shard_map/ppermute | solution.py:35
  67.2 40.6 %collective-permute-start.7 = (bf16[2,96,1536]{2,1,0:T(8,128)(2,1)}, bf16[2,96,1536]{2,1,0:T(8,128)(2,1)}, u32[]{:S(2)}, u32[]{:S(2)}) collective-permute-start(bf16[2,96,1536]{2,1,0:T(8,128)(2,1)} %pad_maximum_fusion.31), channel_id=1, source_target_pairs={{0,16},{1,17},{2,18},{3,19},{4,20},{5,21},{6,22},{7,23},{8,24},{9,... | collective-permute-start | bytes 1769480 | tf_op jit(solution)/shard_map/ppermute | solution.py:35
  75.5 38.4 %collective-permute-start.3 = (bf16[2,4,96,768]{3,2,1,0:T(8,128)(2,1)}, bf16[2,4,96,768]{3,2,1,0:T(8,128)(2,1)}, u32[]{:S(2)}, u32[]{:S(2)}) collective-permute-start(bf16[2,4,96,768]{3,2,1,0:T(8,128)(2,1)} %pad_maximum_fusion.15), channel_id=1, source_target_pairs={{0,2},{1,5},{2,0},{3,7},{4,6},{5,1},{6,4},{7,3},{8,10},{9,13},{10,... | collective-permute-start | bytes 3538952 | tf_op jit(solution)/shard_map/ppermute | solution.py:35
  81.4 80.0 %collective-permute-start.12 = (bf16[2,96,768]{2,1,0:T(8,128)(2,1)}, bf16[2,96,768]{2,1,0:T(8,128)(2,1)}, u32[]{:S(2)}, u32[]{:S(2)}) collective-permute-start(bf16[2,96,768]{2,1,0:T(8,128)(2,1)} %pad_maximum_fusion.42), channel_id=1, source_target_pairs={{0,16},{1,17},{2,18},{3,19},{4,20},{5,21},{6,22},{7,23},{8,24},{9,... | collective-permute-start | bytes 884744 | tf_op jit(solution)/shard_map/ppermute | solution.py:35
  112.3 45.9 %collective-permute-start.8 = (bf16[4,96,1536]{2,1,0:T(8,128)(2,1)}, bf16[4,96,1536]{2,1,0:T(8,128)(2,1)}, u32[]{:S(2)}, u32[]{:S(2)}) collective-permute-start(bf16[4,96,1536]{2,1,0:T(8,128)(2,1)} %get-tuple-element.217), channel_id=1, source_target_pairs={{0,4},{1,3},{2,6},{3,1},{4,0},{5,7},{6,2},{7,5},{8,12},{9,11},{10,... | collective-permute-start | bytes 3538952 | tf_op jit(solution)/shard_map/ppermute | solution.py:35
  159.8 47.9 %collective-permute-start.9 = (bf16[2,4,96,1536]{3,2,1,0:T(8,128)(2,1)S(1)}, bf16[2,4,96,1536]{3,2,1,0:T(8,128)(2,1)S(1)}, u32[]{:S(2)}, u32[]{:S(2)}) collective-permute-start(bf16[2,4,96,1536]{3,2,1,0:T(8,128)(2,1)S(1)} %pad_maximum_fusion.3), channel_id=1, source_target_pairs={{0,2},{1,5},{2,0},{3,7},{4,6},{5,1},{6,4},{7,3},{8,10},{9,13},{10,... | collective-permute-start | bytes 7077896 | tf_op jit(solution)/shard_map/ppermute | solution.py:35
  165.2 53.0 %collective-permute-start.19 = (bf16[4,96,1536]{2,1,0:T(8,128)(2,1)S(1)}, bf16[4,96,1536]{2,1,0:T(8,128)(2,1)S(1)}, u32[]{:S(2)}, u32[]{:S(2)}) collective-permute-start(bf16[4,96,1536]{2,1,0:T(8,128)(2,1)S(1)} %get-tuple-element.213), channel_id=1, source_target_pairs={{0,4},{1,3},{2,6},{3,1},{4,0},{5,7},{6,2},{7,5},{8,12},{9,11},{10,... | collective-permute-start | bytes 3538952 | tf_op jit(solution)/shard_map/ppermute | solution.py:35
  179.0 42.7 %collective-permute-start.14 = (bf16[2,4,96,768]{3,2,1,0:T(8,128)(2,1)S(1)}, bf16[2,4,96,768]{3,2,1,0:T(8,128)(2,1)S(1)}, u32[]{:S(2)}, u32[]{:S(2)}) collective-permute-start(bf16[2,4,96,768]{3,2,1,0:T(8,128)(2,1)S(1)} %pad_maximum_fusion.19), channel_id=1, source_target_pairs={{0,2},{1,5},{2,0},{3,7},{4,6},{5,1},{6,4},{7,3},{8,10},{9,13},{10,... | collective-permute-start | bytes 3538952 | tf_op jit(solution)/shard_map/ppermute | solution.py:35
  220.1 56.0 %collective-permute-start.20 = (bf16[2,4,96,1536]{3,2,1,0:T(8,128)(2,1)}, bf16[2,4,96,1536]{3,2,1,0:T(8,128)(2,1)}, u32[]{:S(2)}, u32[]{:S(2)}) collective-permute-start(bf16[2,4,96,1536]{3,2,1,0:T(8,128)(2,1)} %pad_maximum_fusion.6), channel_id=1, source_target_pairs={{0,2},{1,5},{2,0},{3,7},{4,6},{5,1},{6,4},{7,3},{8,10},{9,13},{10,... | collective-permute-start | bytes 7077896 | tf_op jit(solution)/shard_map/ppermute | solution.py:35
  359.8 104.2 %collective-permute-start.42 = (bf16[2,4,96,1536]{3,2,1,0:T(8,128)(2,1)}, bf16[2,4,96,1536]{3,2,1,0:T(8,128)(2,1)}, u32[]{:S(2)}, u32[]{:S(2)}) collective-permute-start(bf16[2,4,96,1536]{3,2,1,0:T(8,128)(2,1)} %pad_maximum_fusion.14), channel_id=1, source_target_pairs={{0,2},{1,5},{2,0},{3,7},{4,6},{5,1},{6,4},{7,3},{8,10},{9,13},{10,... | collective-permute-start | bytes 7077896 | tf_op jit(solution)/shard_map/ppermute | solution.py:35
  361.3 56.7 %collective-permute-start.22 = (bf16[768,768]{0,1:T(8,128)(2,1)}, bf16[768,768]{0,1:T(8,128)(2,1)}, u32[]{:S(2)}, u32[]{:S(2)}) collective-permute-start(bf16[768,768]{0,1:T(8,128)(2,1)} %get-tuple-element.181), channel_id=1, source_target_pairs={{0,2},{1,3},{2,0},{3,1},{4,6},{5,7},{6,4},{7,5},{8,10},{9,11},{10,... | collective-permute-start | bytes 3538952 | tf_op jit(solution)/shard_map/ppermute | solution.py:35
  463.4 43.6 %collective-permute-start.34 = (bf16[2,4,96,768]{3,2,1,0:T(8,128)(2,1)}, bf16[2,4,96,768]{3,2,1,0:T(8,128)(2,1)}, u32[]{:S(2)}, u32[]{:S(2)}) collective-permute-start(bf16[2,4,96,768]{3,2,1,0:T(8,128)(2,1)} %pad_maximum_fusion.28), channel_id=1, source_target_pairs={{0,2},{1,5},{2,0},{3,7},{4,6},{5,1},{6,4},{7,3},{8,10},{9,13},{10,... | collective-permute-start | bytes 3538952 | tf_op jit(solution)/shard_map/ppermute | solution.py:35
  467.5 56.8 %collective-permute-start.43 = (bf16[4,96,1536]{2,1,0:T(8,128)(2,1)}, bf16[4,96,1536]{2,1,0:T(8,128)(2,1)}, u32[]{:S(2)}, u32[]{:S(2)}) collective-permute-start(bf16[4,96,1536]{2,1,0:T(8,128)(2,1)} %fusion.44), channel_id=1, source_target_pairs={{0,4},{1,3},{2,6},{3,1},{4,0},{5,7},{6,2},{7,5},{8,12},{9,11},{10,... | collective-permute-start | bytes 3538952 | tf_op jit(solution)/shard_map/ppermute | solution.py:35
  489.0 57.6 %collective-permute-start.26 = (bf16[768,768]{0,1:T(8,128)(2,1)}, bf16[768,768]{0,1:T(8,128)(2,1)}, u32[]{:S(2)}, u32[]{:S(2)}) collective-permute-start(bf16[768,768]{0,1:T(8,128)(2,1)} %add_convert_fusion.2), channel_id=1, source_target_pairs={{0,1},{1,0},{2,3},{3,2},{4,5},{5,4},{6,7},{7,6},{8,9},{9,8},{10,11... | collective-permute-start | bytes 3538952 | tf_op jit(solution)/shard_map/ppermute | solution.py:35
  511.9 223.7 %collective-permute-start.38 = (bf16[2,4,96,1536]{3,2,1,0:T(8,128)(2,1)}, bf16[2,4,96,1536]{3,2,1,0:T(8,128)(2,1)}, u32[]{:S(2)}, u32[]{:S(2)}) collective-permute-start(bf16[2,4,96,1536]{3,2,1,0:T(8,128)(2,1)} %pad_maximum_fusion.11), channel_id=1, source_target_pairs={{0,2},{1,5},{2,0},{3,7},{4,6},{5,1},{6,4},{7,3},{8,10},{9,13},{10,... | collective-permute-start | bytes 7077896 | tf_op jit(solution)/shard_map/ppermute | solution.py:35
  539.8 46.7 %collective-permute-start.44 = (bf16[2,96,1536]{2,1,0:T(8,128)(2,1)}, bf16[2,96,1536]{2,1,0:T(8,128)(2,1)}, u32[]{:S(2)}, u32[]{:S(2)}) collective-permute-start(bf16[2,96,1536]{2,1,0:T(8,128)(2,1)} %select_convert_fusion), channel_id=1, source_target_pairs={{0,16},{1,17},{2,18},{3,19},{4,20},{5,21},{6,22},{7,23},{8,24},{9,... | collective-permute-start | bytes 1769480 | tf_op jit(solution)/shard_map/ppermute | solution.py:35
  588.8 153.3 %collective-permute-start.45 = (bf16[1,96,1536]{2,1,0:T(8,128)(2,1)}, bf16[1,96,1536]{2,1,0:T(8,128)(2,1)}, u32[]{:S(2)}, u32[]{:S(2)}) collective-permute-start(bf16[1,96,1536]{2,1,0:T(8,128)(2,1)} %select_convert_fusion.2), channel_id=1, source_target_pairs={{0,8},{1,9},{2,10},{3,11},{4,12},{5,13},{6,14},{7,15},{8,0},{9,1},... | collective-permute-start | bytes 884744 | tf_op jit(solution)/shard_map/ppermute | solution.py:35
  608.6 131.3 %collective-permute-start.30 = (bf16[2,4,96,768]{3,2,1,0:T(8,128)(2,1)}, bf16[2,4,96,768]{3,2,1,0:T(8,128)(2,1)}, u32[]{:S(2)}, u32[]{:S(2)}) collective-permute-start(bf16[2,4,96,768]{3,2,1,0:T(8,128)(2,1)} %pad_maximum_fusion.25), channel_id=1, source_target_pairs={{0,2},{1,5},{2,0},{3,7},{4,6},{5,1},{6,4},{7,3},{8,10},{9,13},{10,... | collective-permute-start | bytes 3538952 | tf_op jit(solution)/shard_map/ppermute | solution.py:35
  615.0 129.1 %collective-permute-start.28 = (bf16[768,768]{0,1:T(8,128)(2,1)}, bf16[768,768]{0,1:T(8,128)(2,1)}, u32[]{:S(2)}, u32[]{:S(2)}) collective-permute-start(bf16[768,768]{0,1:T(8,128)(2,1)} %add_convert_fusion.1), channel_id=1, source_target_pairs={{0,1},{1,0},{2,3},{3,2},{4,5},{5,4},{6,7},{7,6},{8,9},{9,8},{10,11... | collective-permute-start | bytes 3538952 | tf_op jit(solution)/shard_map/ppermute | solution.py:35
  746.0 42.9 %collective-permute-start.29 = (bf16[768,768]{0,1:T(8,128)(2,1)S(1)}, bf16[768,768]{0,1:T(8,128)(2,1)S(1)}, u32[]{:S(2)}, u32[]{:S(2)}) collective-permute-start(bf16[768,768]{0,1:T(8,128)(2,1)S(1)} %get-tuple-element.148), channel_id=1, source_target_pairs={{0,2},{1,3},{2,0},{3,1},{4,6},{5,7},{6,4},{7,5},{8,10},{9,11},{10,... | collective-permute-start | bytes 3538952 | tf_op jit(solution)/shard_map/ppermute | solution.py:35
  780.1 30.2 %collective-permute-start.40 = (bf16[2,96,1536]{2,1,0:T(8,128)(2,1)S(1)}, bf16[2,96,1536]{2,1,0:T(8,128)(2,1)S(1)}, u32[]{:S(2)}, u32[]{:S(2)}) collective-permute-start(bf16[2,96,1536]{2,1,0:T(8,128)(2,1)S(1)} %select_convert_fusion.1), channel_id=1, source_target_pairs={{0,16},{1,17},{2,18},{3,19},{4,20},{5,21},{6,22},{7,23},{8,24},{9,... | collective-permute-start | bytes 1769480 | tf_op jit(solution)/shard_map/ppermute | solution.py:35
  (342 other events, 2528.3 us)
Sparse Core Ops, SparseCore 0:
  610.1 119.8 all-reduce.2

commit v2 on v1

v2 whole, which is shorter than its diff:
```python
import functools

import jax
import jax.numpy as jnp
from jax import lax
from jax.experimental import pallas as pl
from jax.experimental.pallas import tpu as pltpu
from jax.sharding import PartitionSpec as P

HEAD_DIM = 64
LAYERS = 2
ADAM_STEP = 10

EPS_NORM = 1e-12
EPS_ADAM = 1e-08
RATE_MATRIX = 0.04
RATE_VECTOR = 0.3
DECAY_MATRIX = 0.01

F32 = jnp.float32
BF16 = jnp.bfloat16
AXES = ("dp", "mp")
NN = ((1,), (0,))
NT = ((1,), (1,))
TN = ((0,), (0,))


def dot(a, b, dims):
    return lax.dot_general(a, b, (dims, ((), ())), preferred_element_type=F32)


def tie(*arrays):
    return lax.optimization_barrier(arrays)


class Links:
    def __init__(self, n_dp):
        self.n_dp = n_dp
        self.count = n_dp * 4
        self.bits = n_dp.bit_length() - 1
        dp_at = lax.axis_index("dp")
        mp_at = lax.axis_index("mp")
        self.at_x = mp_at // 2
        self.core = mp_at % 2
        self.at_y = dp_at % 2
        self.dp_at = dp_at
        self.places = jnp.stack([self.core, self.at_y]).astype(jnp.int32)

    def swap(self, array, mask0, mask1=None):
        mask1 = mask0 if mask1 is None else mask1
        pairs = [(i, i ^ (mask1 if i & 1 else mask0)) for i in range(self.count)]
        return lax.ppermute(array, AXES, pairs)

    def swap_core(self, array):
        return self.swap(array, 1)

    def swap_x(self, array):
        return self.swap(array, 2)

    def gather_bit(self, block, bit):
        other = self.swap(block, 4 << bit)
        mine = ((self.dp_at >> bit) & 1) == 0
        return jnp.concatenate([jnp.where(mine, block, other), jnp.where(mine, other, block)])

    def gather_rest(self, block):
        for bit in range(2, self.bits):
            block = self.gather_bit(block, bit)
        return block

    def gather_near(self, block):
        return self.swap(block, 4, 2)

    def gather_far(self, block, near):
        far = self.swap(jnp.stack([block, near]), 2, 4)
        first = self.core == 0
        own_far = jnp.where(first, near, far[0])
        other_near = jnp.where(first, far[0], near)
        return self.rows(block, own_far), self.rows(other_near, far[1])

    def rows(self, same, other):
        low = self.at_y == 0
        both = jnp.stack([jnp.where(low, same, other), jnp.where(low, other, same)], axis=1)
        return both.reshape(-1, both.shape[-1])

    def scatter_first(self, keep, give):
        came = self.swap(give, 2, 4)
        return keep[0].astype(F32) + came[0].astype(F32), (keep[1].astype(F32) + came[1].astype(F32)).astype(BF16)

    def scatter_second(self, keep, give):
        return keep + self.swap(give, 4, 2).astype(F32)

    def scatter_bit(self, keep, bit):
        half = keep.shape[0] // 2
        mine = ((self.dp_at >> bit) & 1) == 0
        give = jnp.where(mine, keep[half:], keep[:half]).astype(BF16)
        keep = jnp.where(mine, keep[:half], keep[half:])
        return keep + self.swap(give, 4 << bit).astype(F32)

    def scatter_rest_from(self, keep, top):
        for bit in reversed(range(1, top + 1)):
            keep = self.scatter_bit(keep, bit)
        return keep[0]

    def scatter_rest(self, keep):
        return self.scatter_rest_from(keep, self.bits - 1)

def norm_parts(residual, gain_row, shift_row):
    center = residual - jnp.mean(residual, axis=-1, keepdims=True)
    inv_std = lax.rsqrt(jnp.mean(center * center, axis=-1, keepdims=True) + EPS_NORM)
    scaled = center * inv_std
    return (scaled * gain_row + shift_row, scaled, inv_std)


def norm_back(grad_output, scaled, inv_std, gain_row):
    upstream = grad_output * gain_row
    mean_up = jnp.mean(upstream, axis=-1, keepdims=True)
    mean_cross = jnp.mean(upstream * scaled, axis=-1, keepdims=True)
    return inv_std * (upstream - mean_up - scaled * mean_cross)


def adam_step(master, moment, second, gradient, step_rate, decay_rate):
    correction = 1.0 - 0.5**ADAM_STEP
    moment_new = 0.5 * moment + 0.5 * gradient
    second_new = 0.5 * second + 0.5 * gradient * gradient
    update = (
        moment_new / correction / (jnp.sqrt(second_new / correction) + EPS_ADAM)
        + decay_rate * master
    )
    return (master - step_rate * update, moment_new, second_new)


def key_bias(limit, count, lanes):
    places = lax.broadcasted_iota(jnp.int32, (count, lanes), 0)
    return jnp.where(places < limit, 0.0, -1000000000.0)


def head_parts(qkv, far, swapped, g, h, full):
    third = qkv[g].shape[1] // 3
    k_at, v_at = third + h * HEAD_DIM, 2 * third + h * HEAD_DIM
    f_at = (g ^ swapped) * 2 * third + h * HEAD_DIM
    keys = qkv[g][:full, k_at : k_at + HEAD_DIM]
    values = qkv[g][:full, v_at : v_at + HEAD_DIM]
    keys_half = jnp.concatenate([qkv[g][full:, k_at : k_at + HEAD_DIM], far[:, f_at : f_at + HEAD_DIM]])
    f_at += third
    values_half = jnp.concatenate([qkv[g][full:, v_at : v_at + HEAD_DIM], far[:, f_at : f_at + HEAD_DIM]])
    return keys, values, keys_half, values_half


def fill_bias(limits, bias, full, half):
    bias[0] = key_bias(limits[0], full, half)
    bias[1, :half] = key_bias(limits[1], half, half)
    bias[1, half:] = key_bias(limits[2], half, half)


def attend_unit(keys, values, queries, bias_rows):
    scores = dot(keys, queries, NT) + bias_rows
    peak = jnp.max(scores, axis=0, keepdims=True)
    shifted = jnp.exp(scores - peak)
    total = jnp.sum(shifted, axis=0, keepdims=True)
    probs = (shifted * (1.0 / total)).astype(BF16)
    return dot(values, probs, TN), peak + jnp.log(total)


def full_kernel(limits, qkv0, qkv1, ctx0, ctx1, lse, bias):
    qkv, ctx = (qkv0, qkv1), (ctx0, ctx1)
    full, half = bias.shape
    third = qkv0.shape[1] // 3
    heads = third // HEAD_DIM
    bias[...] = key_bias(limits[0], full, half)
    for g in range(2):
        outs = [[], []]
        for h in range(heads):
            columns = slice(h * HEAD_DIM, (h + 1) * HEAD_DIM)
            keys = qkv[g][:full, third + h * HEAD_DIM : third + (h + 1) * HEAD_DIM]
            values = qkv[g][:full, 2 * third + h * HEAD_DIM : 2 * third + (h + 1) * HEAD_DIM]
            for part in range(2):
                rows = slice(part * half, (part + 1) * half)
                out, log_total = attend_unit(keys, values, qkv[g][rows, columns], bias[...])
                lse[g * heads + h : g * heads + h + 1, rows] = log_total
                outs[part].append(out)
        for part in range(2):
            rows = slice(part * half, (part + 1) * half)
            ctx[g][rows, :] = jnp.concatenate(outs[part], axis=0).T.astype(BF16)


def half_kernel(swapped, limits, qkv0, qkv1, far, _a, _b, _c, ctx0, ctx1, lse, bias):
    qkv, ctx = (qkv0, qkv1), (ctx0, ctx1)
    half = far.shape[0]
    full = 2 * half
    heads = qkv0.shape[1] // 3 // HEAD_DIM
    bias[:half] = key_bias(limits[1], half, half)
    bias[half:] = key_bias(limits[2], half, half)
    for g in range(2):
        outs = []
        for h in range(heads):
            _, _, keys, values = head_parts(qkv, far, swapped, g, h, full)
            columns = slice(h * HEAD_DIM, (h + 1) * HEAD_DIM)
            out, log_total = attend_unit(keys, values, qkv[g][full:, columns], bias[...])
            lse[g * heads + h : g * heads + h + 1, :] = log_total
            outs.append(out)
        ctx[g][...] = jnp.concatenate(outs, axis=0).T.astype(BF16)


def attend_back_unit(keys, values, queries, grad_rows, log_total, bias_rows):
    probs = jnp.exp(dot(keys, queries, NT) + bias_rows - log_total)
    grad_probs = dot(values, grad_rows, NT)
    inner = jnp.sum(probs * grad_probs, axis=0, keepdims=True)
    grad_scores = (probs * (grad_probs - inner)).astype(BF16)
    grad_values = dot(probs.astype(BF16), grad_rows, NN)
    grad_keys = dot(grad_scores, queries, NN)
    grad_queries = dot(keys, grad_scores, TN)
    return grad_queries, grad_keys, grad_values


def half_back_kernel(swapped, limits, qkv0, qkv1, far, dctx0, dctx1, lse, dq0, dq1, own, sent, bias):
    qkv, dctx, dq = (qkv0, qkv1), (dctx0, dctx1), (dq0, dq1)
    half = far.shape[0]
    full = 2 * half
    third = qkv0.shape[1] // 3
    heads = third // HEAD_DIM
    fill_bias(limits, bias, full, half)
    for g in range(2):
        queries_out, keys_out, values_out = [], [], []
        for h in range(heads):
            _, _, keys, values = head_parts(qkv, far, swapped, g, h, full)
            columns = slice(h * HEAD_DIM, (h + 1) * HEAD_DIM)
            gq, gk, gv = attend_back_unit(
                keys,
                values,
                qkv[g][full:, columns],
                dctx[g][full:, columns],
                lse[g * heads + h : g * heads + h + 1, full:],
                bias[1],
            )
            queries_out.append(gq)
            keys_out.append(gk)
            values_out.append(gv)
        dq[g][...] = jnp.concatenate(queries_out, axis=0).T.astype(BF16) * 0.125
        both = jnp.concatenate(keys_out + values_out, axis=1)
        own[:, 2 * third * g : 2 * third * (g + 1)] = both[:half]
        other = 1 - g
        sent[:, 2 * third * other : 2 * third * (other + 1)] = both[half:].astype(BF16)


def full_back_kernel(limits, qkv0, qkv1, dctx0, dctx1, lse, dqkv0, dqkv1, bias):
    qkv, dctx, dqkv = (qkv0, qkv1), (dctx0, dctx1), (dqkv0, dqkv1)
    full = qkv0.shape[0] * 2 // 3
    half = full // 2
    third = qkv0.shape[1] // 3
    heads = third // HEAD_DIM
    bias[...] = key_bias(limits[0], full, half)
    for g in range(2):
        queries_out, keys_out, values_out = [[], []], [], []
        for h in range(heads):
            columns = slice(h * HEAD_DIM, (h + 1) * HEAD_DIM)
            keys = qkv[g][:full, third + h * HEAD_DIM : third + (h + 1) * HEAD_DIM]
            values = qkv[g][:full, 2 * third + h * HEAD_DIM : 2 * third + (h + 1) * HEAD_DIM]
            sums = None
            for part in range(2):
                rows = slice(part * half, (part + 1) * half)
                gq, gk, gv = attend_back_unit(
                    keys,
                    values,
                    qkv[g][rows, columns],
                    dctx[g][rows, columns],
                    lse[g * heads + h : g * heads + h + 1, rows],
                    bias[...],
                )
                queries_out[part].append(gq)
                sums = (gk, gv) if sums is None else (sums[0] + gk, sums[1] + gv)
            keys_out.append(sums[0].astype(BF16))
            values_out.append(sums[1].astype(BF16))
        for part in range(2):
            rows = slice(part * half, (part + 1) * half)
            dqkv[g][rows, :third] = jnp.concatenate(queries_out[part], axis=0).T.astype(BF16) * 0.125
        dqkv[g][:full, third:] = jnp.concatenate(keys_out + values_out, axis=1)


def half_fill_kernel(dq0, dq1, own, came, _a, _b, dqkv0, dqkv1):
    half = own.shape[0]
    full = 2 * half
    third = dq0.shape[1]
    for g, (dq, dqkv) in enumerate(((dq0, dqkv0), (dq1, dqkv1))):
        columns = slice(2 * third * g, 2 * third * (g + 1))
        both = (own[:, columns] + came[:, columns].astype(F32)).astype(BF16)
        dqkv[...] = jnp.concatenate([dq[...], both], axis=1)


VMEM = pl.BlockSpec(memory_space=pltpu.VMEM)
SMEM = pl.BlockSpec(memory_space=pltpu.SMEM)
ROOM = pltpu.CompilerParams(vmem_limit_bytes=32 * 1024 * 1024)


def call(kernel, outs, ins, scratch=()):
    specs = [SMEM if a.dtype == jnp.int32 else VMEM for a in ins]
    return pl.pallas_call(
        kernel,
        out_shape=[jax.ShapeDtypeStruct(s, d) for s, d in outs],
        in_specs=specs,
        out_specs=[VMEM] * len(outs),
        scratch_shapes=list(scratch),
        compiler_params=ROOM,
    )(*ins)


def attend_full(limits, qkv):
    tokens, third = qkv[0].shape[0], qkv[0].shape[1] // 3
    half = tokens // 3
    ctx0, ctx1, lse = call(
        full_kernel,
        [((tokens, third), BF16)] * 2 + [((2 * third // HEAD_DIM, tokens), F32)],
        (limits, *qkv),
        [pltpu.VMEM((2 * half, half), F32)],
    )
    return (ctx0, ctx1), lse


def attend_half(limits, qkv, far, ctx, lse, swapped):
    half, third = far.shape[0], ctx[0].shape[1]
    rows = pl.BlockSpec((half, third), lambda i: (2, 0))
    ctx0, ctx1, lse = pl.pallas_call(
        functools.partial(half_kernel, swapped),
        grid=(1,),
        out_shape=[jax.ShapeDtypeStruct(a.shape, a.dtype) for a in (*ctx, lse)],
        in_specs=[SMEM] + [VMEM] * 3 + [pl.BlockSpec(memory_space=pl.ANY)] * 3,
        out_specs=[rows, rows, pl.BlockSpec((lse.shape[0], half), lambda i: (0, 2))],
        scratch_shapes=[pltpu.VMEM((2 * half, half), F32)],
        input_output_aliases={4: 0, 5: 1, 6: 2},
        compiler_params=ROOM,
    )(limits, *qkv, far, *ctx, lse)
    return (ctx0, ctx1), lse


def attend_half_back(limits, qkv, far, dctx, lse, swapped):
    half, third = far.shape[0], qkv[0].shape[1] // 3
    dq0, dq1, own, sent = call(
        functools.partial(half_back_kernel, swapped),
        [((half, third), BF16)] * 2 + [((half, 4 * third), F32), ((half, 4 * third), BF16)],
        (limits, *qkv, far, *dctx, lse),
        [pltpu.VMEM((2, 2 * half, half), F32)],
    )
    return (dq0, dq1), own, sent


def attend_full_back(limits, qkv, dctx, lse):
    half = qkv[0].shape[0] // 3
    return call(
        full_back_kernel,
        [(qkv[0].shape, BF16)] * 2,
        (limits, *qkv, *dctx, lse),
        [pltpu.VMEM((2 * half, half), F32)],
    )


def fill_half(dqkv, dq, own, came):
    tokens, columns = dqkv[0].shape
    half = own.shape[0]
    rows = pl.BlockSpec((half, columns), lambda i: (2, 0))
    return pl.pallas_call(
        half_fill_kernel,
        grid=(1,),
        out_shape=[jax.ShapeDtypeStruct(d.shape, d.dtype) for d in dqkv],
        in_specs=[VMEM] * 4 + [pl.BlockSpec(memory_space=pl.ANY)] * 2,
        out_specs=[rows] * 2,
        input_output_aliases={4: 0, 5: 1},
        compiler_params=ROOM,
    )(*dq, own, came, *dqkv)

def wgrad_kernel(count, places, *refs):
    lefts, rights = refs[:count], (refs[count : 2 * count], refs[2 * count : 3 * count])
    keep, give, whole = refs[3 * count :]
    first, at_y = places[0] == 0, places[1]
    blocks, rows = keep.shape[1], keep.shape[2]
    turned = [left[...].T for left in lefts]
    for g in range(2):
        at = 0
        for left, right in zip(turned, rights[g]):
            wide = right.shape[1]
            whole[:, at : at + wide] = dot(left, right[...], NN).astype(BF16)
            at += wide
        for y in range(2):
            same = at_y == y
            if g == 0:
                targets = ((same, keep, 0), (~same & first, keep, 1), (~same & ~first, give, 0))
            else:
                targets = ((same & first, give, 0), (same & ~first, keep, 1), (~same, give, 1))
            for when, ref, slot in targets:

                @pl.when(when)
                def _(ref=ref, slot=slot, y=y):
                    for z in range(blocks):
                        ref[slot, z] = whole[(2 * z + y) * rows : (2 * z + y + 1) * rows, :]


def weight_grads(links, lefts, rights):
    features = lefts[0].shape[1]
    columns = sum(r.shape[1] for r in rights[0])
    blocks = links.n_dp // 2
    rows = features // links.n_dp
    if rows % 16 == 0:
        return call(
            functools.partial(wgrad_kernel, len(lefts)),
            [((2, blocks, rows, columns), BF16)] * 2,
            (links.places, *lefts, *rights[0], *rights[1]),
            [pltpu.VMEM((features, columns), BF16)],
        )
    low, first = links.at_y == 0, links.core == 0
    parts = []
    for group in rights:
        grad = jnp.concatenate([dot(a, b, TN) for a, b in zip(lefts, group)], axis=1).astype(BF16)
        grad = grad.reshape(blocks, 2, rows, columns)
        parts += [jnp.where(low, grad[:, 0], grad[:, 1]), jnp.where(low, grad[:, 1], grad[:, 0])]
    own_same, own_far, other_same, other_far = parts
    keep = jnp.stack([own_same, jnp.where(first, own_far, other_same)])
    return keep, jnp.stack([jnp.where(first, other_same, own_far), other_far])

def both_cores(links, partial):
    low = partial.astype(BF16)
    return low.astype(F32) + links.swap_core(low).astype(F32)


def gelu_parts(pre):
    cdf = 0.5 * (1.0 + lax.erf(pre * 0.7071067811865476))
    pdf = jnp.exp(-0.5 * pre * pre) * 0.3989422804014327
    return (pre * cdf).astype(BF16), cdf + pre * pdf


def project(low, weight, bias, scale):
    return ((dot(low, weight, NN) + bias) * scale).astype(BF16)


def up_part(normed_low, weights, ffn_b):
    wide = ffn_b[0].shape[-1]
    return [gelu_parts(dot(normed_low, weights[g][:, :wide], NN) + ffn_b[g]) for g in range(2)]


def down_part(ffn_parts, weights):
    wide = ffn_parts[0][0].shape[1]
    return sum(dot(ffn_parts[g][0], weights[g][:, wide:], NT) for g in range(2))


def local(n_dp, *args):
    (
        inputs,
        cotangent,
        word_lengths,
        word_count,
        attn_in,
        attn_out,
        ffn_up,
        ffn_down,
        head_bias,
        ffn_bias,
        row_params,
    ) = args[:11]
    moments, seconds = args[11:18], args[18:25]
    links = Links(n_dp)
    at_x, core = links.at_x, links.core
    seq_len = inputs.shape[0] // word_count.shape[0]
    half = seq_len // 2
    third, wide = attn_in.shape[3], ffn_up.shape[2]

    def own_rows(array):
        whole = lax.dynamic_slice_in_dim(array, at_x * 2 * seq_len, seq_len)
        return jnp.concatenate([whole, lax.dynamic_slice_in_dim(array, seq_len + at_x * half, half)])

    def all_rows(array):
        low = array.astype(BF16)
        part = low.shape[0] // 2
        piece = links.swap_x(lax.dynamic_slice_in_dim(low, core * part, part))
        twin = links.swap_core(piece)
        first = core == 0
        other = jnp.concatenate([jnp.where(first, piece, twin), jnp.where(first, twin, piece)])
        low, other = low.astype(F32), other.astype(F32)
        first = at_x == 0
        return jnp.concatenate(
            [
                jnp.where(first, low[:seq_len], other[:seq_len]),
                jnp.where(first, low[seq_len:], other[seq_len:]),
                jnp.where(first, other[seq_len:], low[seq_len:]),
                jnp.where(first, other[:seq_len], low[:seq_len]),
            ]
        )

    attn_w, ffn_w = [], []
    for layer in range(LAYERS):
        attn = [attn_in[layer, 0], attn_in[layer, 1], attn_in[layer, 2], attn_out[layer]]
        attn_w.append(jnp.concatenate(attn, axis=1).astype(BF16)[None])
        ffn_w.append(jnp.concatenate([ffn_up[layer], ffn_down[layer]], axis=1).astype(BF16)[None])
    a0 = links.gather_bit(attn_w[0], 1)
    a0, f0 = tie(a0, ffn_w[0])
    f0 = links.gather_bit(f0, 1)
    a0 = links.gather_rest(a0)
    a0, f0, a1, f1 = tie(a0, f0, attn_w[1], ffn_w[1])
    near = links.gather_near(a0)
    f0 = links.gather_rest(f0)
    a1 = links.gather_bit(a1, 1)
    a0 = links.gather_far(a0, near)

    bias_far = links.swap_x(jnp.concatenate([head_bias.reshape(-1), ffn_bias.reshape(-1)]))
    head_b = (head_bias, bias_far[: head_bias.size].reshape(head_bias.shape))
    ffn_b = (ffn_bias, bias_far[head_bias.size :].reshape(ffn_bias.shape))
    zeros = jnp.zeros((third,), F32)
    qkv_b = [[jnp.concatenate([b[layer, 0], zeros, b[layer, 1]]) for b in head_b] for layer in range(LAYERS)]
    scale = jnp.concatenate([jnp.full((third,), 0.125, F32), jnp.ones((2 * third,), F32)])

    slots = jnp.arange(word_lengths.shape[1], dtype=jnp.int32)
    used = jnp.sum(jnp.where(slots[None, :] < word_count[:, None], word_lengths, 0), axis=1)
    used_full = jnp.where(at_x == 0, used[0], used[2])
    limits = jnp.stack([used_full, used[1] - at_x * half, used[1] - (1 - at_x) * half]).astype(jnp.int32)
    places = jnp.arange(seq_len, dtype=jnp.int32)
    row_mask = jnp.concatenate([places < limits[0], places[:half] < limits[1]]).astype(F32)[:, None]

    hidden = own_rows(inputs)
    low_other = lax.dynamic_slice_in_dim(inputs, seq_len + (1 - at_x) * half, half).astype(BF16)
    in_low = [hidden.astype(BF16), None]
    qkv, far, ctx, lse = [None] * 2, [None] * 2, [None] * 2, [None] * 2
    weight_a, weight_f = [a0, None], [None, None]

    def qkv_of(layer):
        return [
            project(in_low[layer], weight_a[layer][g][:, : 3 * third], qkv_b[layer][g], scale) for g in range(2)
        ]

    def out_part(layer):
        return sum(dot(ctx[layer][g], weight_a[layer][g][:, 3 * third :], NT) for g in range(2))

    norms = [None] * 2
    ffn_parts = [None] * 2

    qkv[0] = qkv_of(0)
    far[0] = jnp.concatenate(
        [
            (dot(low_other, a0[g][:, third : 3 * third], NN) + qkv_b[0][g][third:]).astype(BF16)
            for g in range(2)
        ],
        axis=1,
    )
    ctx[0], lse[0] = attend_full(limits, qkv[0])
    ctx[0], lse[0] = attend_half(limits, qkv[0], far[0], ctx[0], lse[0], 0)
    c0, c1, f0, a1 = tie(*ctx[0], f0, a1)
    ctx[0] = (c0, c1)
    near = links.gather_near(f0)
    a1 = links.gather_rest(a1)
    f1 = links.gather_bit(f1, 1)
    attended = both_cores(links, out_part(0)) + row_params[0, 0]
    normed, scaled_one, inv_one = norm_parts(hidden + attended, row_params[0, 2], row_params[0, 3])
    normed, near, a1, f1 = tie(normed, near, a1, f1)
    f0 = links.gather_far(f0, near)
    near = links.gather_near(a1)
    f1 = links.gather_rest(f1)
    weight_f[0] = f0
    normed_low = normed.astype(BF16)
    ffn_parts[0] = up_part(normed_low, f0, [b[0] for b in ffn_b])
    act, near, f1 = tie(ffn_parts[0][0][0], near, f1)
    ffn_parts[0][0] = (act, ffn_parts[0][0][1])
    a1 = links.gather_far(a1, near)
    weight_a[1] = a1
    near = links.gather_near(f1)
    fed = both_cores(links, down_part(ffn_parts[0], f0)) + row_params[0, 1]
    hidden, scaled_two, inv_two = norm_parts(normed + fed, row_params[0, 4], row_params[0, 5])
    norms[0] = (normed_low, scaled_one, inv_one, scaled_two, inv_two)

    in_low[1] = hidden.astype(BF16)
    qkv[1] = qkv_of(1)
    q0, q1, near = tie(*qkv[1], near)
    qkv[1] = [q0, q1]
    f1 = links.gather_far(f1, near)
    weight_f[1] = f1
    far[1] = links.swap_x(jnp.concatenate([q0[seq_len:, third:], q1[seq_len:, third:]], axis=1))
    ctx[1], lse[1] = attend_full(limits, qkv[1])
    ctx[1], lse[1] = attend_half(limits, qkv[1], far[1], ctx[1], lse[1], 1)
    attended = both_cores(links, out_part(1)) + row_params[1, 0]
    normed, scaled_one, inv_one = norm_parts(hidden + attended, row_params[1, 2], row_params[1, 3])
    normed_low = normed.astype(BF16)
    ffn_parts[1] = up_part(normed_low, f1, [b[1] for b in ffn_b])
    fed = both_cores(links, down_part(ffn_parts[1], f1)) + row_params[1, 1]
    hidden, scaled_two, inv_two = norm_parts(normed + fed, row_params[1, 4], row_params[1, 5])
    norms[1] = (normed_low, scaled_one, inv_one, scaled_two, inv_two)
    encoded = all_rows(hidden)

    def ffn_back(layer, grad_output):
        normed_low, _, _, scaled_two, inv_two = norms[layer]
        upper = norm_back(grad_output, scaled_two, inv_two, row_params[layer, 4])
        upper_low = upper.astype(BF16)
        grad_pre = [
            (dot(upper_low, weight_f[layer][g][:, wide:], NN) * ffn_parts[layer][g][1]).astype(BF16) for g in range(2)
        ]
        partial = sum(dot(grad_pre[g], weight_f[layer][g][:, :wide], NT) for g in range(2))
        grad_normed = upper + both_cores(links, partial)
        pieces = weight_grads(
            links,
            (normed_low, upper_low),
            [(grad_pre[g], ffn_parts[layer][g][0]) for g in range(2)],
        )
        vectors = (
            jnp.sum(upper, axis=0),
            jnp.sum(grad_output * scaled_two, axis=0),
            jnp.sum(grad_output, axis=0),
            [jnp.sum(p.astype(F32), axis=0) for p in grad_pre],
        )
        return grad_normed, pieces, vectors

    def attn_back(layer, grad_normed, hook):
        _, scaled_one, inv_one, _, _ = norms[layer]
        lower = norm_back(grad_normed, scaled_one, inv_one, row_params[layer, 2])
        lower_low = lower.astype(BF16)
        weight = weight_a[layer]
        dctx = [dot(lower_low, weight[g][:, 3 * third :], NN).astype(BF16) for g in range(2)]
        swapped = layer
        dq, own, sent = attend_half_back(limits, qkv[layer], far[layer], dctx, lse[layer], swapped)
        came = links.swap_x(sent)
        dqkv = attend_full_back(limits, qkv[layer], dctx, lse[layer])
        dqkv = fill_half(dqkv, dq, own, came)
        dqkv = hook(dqkv)
        partial = sum(dot(dqkv[g], weight[g][:, : 3 * third], NT) for g in range(2))
        grad_hidden = lower + both_cores(links, partial)
        pieces = weight_grads(links, (in_low[layer], lower_low), [(dqkv[g], ctx[layer][g]) for g in range(2)])
        sums = [jnp.sum(d.astype(F32), axis=0) for d in dqkv]
        vectors = (
            jnp.sum(lower, axis=0),
            jnp.sum(grad_normed * scaled_one, axis=0),
            jnp.sum(grad_normed, axis=0),
            [jnp.concatenate([s[:third], s[2 * third :]]) for s in sums],
        )
        return grad_hidden, pieces, vectors

    grad_hidden = own_rows(cotangent) * row_mask
    vectors = [None, None]
    grad_normed, pieces, fvec = ffn_back(1, grad_hidden)
    state = {}

    def hook1(dqkv):
        f_keep, f_give = links.scatter_first(*pieces)
        d0, d1, f_keep, f_give = tie(*dqkv, f_keep, f_give)
        state["f1"] = links.scatter_second(f_keep, f_give)
        return [d0, d1]

    grad_hidden, a_pieces, avec = attn_back(1, grad_normed, hook1)
    vectors[1] = (fvec, avec)
    grad_hidden, f1s = tie(grad_hidden, state["f1"])
    a_keep, a_give = links.scatter_first(*a_pieces)
    grad_normed, pieces, fvec = ffn_back(0, grad_hidden)
    f1s = links.scatter_bit(f1s, links.bits - 1)
    grad_normed, a_keep, a_give, f1s = tie(grad_normed, a_keep, a_give, f1s)
    a1s = links.scatter_second(a_keep, a_give)
    f1s = links.scatter_rest_from(f1s, links.bits - 2)

    def hook0(dqkv):
        f_keep, f_give = links.scatter_first(*pieces)
        d0, d1, f_keep, f_give, a, f = tie(*dqkv, f_keep, f_give, a1s, f1s)
        state["f0"] = links.scatter_second(f_keep, f_give)
        state["a1"], state["f1"] = a, f
        return [d0, d1]

    grad_hidden, a_pieces, avec = attn_back(0, grad_normed, hook0)
    vectors[0] = (fvec, avec)
    a1s = links.scatter_rest(state["a1"])
    f1s = state["f1"]
    a_keep, a_give = links.scatter_first(*a_pieces)
    f0s = links.scatter_rest(state["f0"])
    a0s = links.scatter_rest(links.scatter_second(a_keep, a_give))
    input_grad = all_rows(grad_hidden)

    own = jnp.concatenate([v for layer in vectors for v in (layer[1][3][0], layer[0][3][0])])
    other = jnp.concatenate([v for layer in vectors for v in (layer[1][3][1], layer[0][3][1])])
    rows = jnp.concatenate(
        [
            r
            for fv, av in vectors
            for r in (av[0], fv[0], av[1], av[2], fv[1], fv[2])
        ]
    )
    came = links.swap_x(jnp.concatenate([other, rows]).reshape(-1, 128)).reshape(-1)
    sums = (jnp.concatenate([own, rows]) + came).reshape(-1, 128)
    for bit in range(links.bits):
        sums = sums + links.swap(sums, 4 << bit)
    sums = sums.reshape(-1)
    size = own.shape[0] // LAYERS
    head_grad = jnp.stack([sums[i * size : i * size + 2 * third].reshape(2, third) for i in range(LAYERS)])
    ffn_grad = jnp.stack([sums[i * size + 2 * third : (i + 1) * size] for i in range(LAYERS)])
    row_grad = sums[LAYERS * size :].reshape(row_params.shape)

    attn = jnp.stack([a0s, a1s])
    ffn = jnp.stack([f0s, f1s])
    gradients = (
        jnp.stack([attn[:, :, k * third : (k + 1) * third] for k in range(3)], axis=1),
        attn[:, :, 3 * third :],
        ffn[:, :, :wide],
        ffn[:, :, wide:],
        head_grad,
        ffn_grad,
        row_grad,
    )
    params = (attn_in, attn_out, ffn_up, ffn_down, head_bias, ffn_bias, row_params)
    stepped = [
        adam_step(
            params[i],
            moments[i],
            seconds[i],
            gradients[i],
            RATE_MATRIX if i < 4 else RATE_VECTOR,
            DECAY_MATRIX if i < 4 else 0.0,
        )
        for i in range(7)
    ]
    news, moms, vars_ = zip(*stepped)
    copies = tuple(news[i].astype(BF16) for i in range(4))
    return (encoded, input_grad) + news + moms + vars_ + copies


def solution(mesh):
    n_dp = mesh.shape["dp"]
    row = P("dp", None)
    state = (
        P(None, None, "dp", "mp"),
        P(None, "dp", "mp"),
        P(None, "dp", "mp"),
        P(None, "dp", "mp"),
        P(None, None, "mp"),
        P(None, "mp"),
        P(),
    )

    def step(*args):
        return local(n_dp, *args)

    return jax.shard_map(
        step,
        mesh=mesh,
        in_specs=(row, row, row, P("dp")) + state * 3,
        out_specs=(row, row) + state * 3 + state[:4],
        check_vma=False,
    )
```

time: 844 us -> 516 us (0.61)
  matrix products: 183 us -> 49.9 us
  other arithmetic: 151 us -> 56.7 us
  local copies, waits for them, and re-layouts: 124 us -> 29.7 us
  Pallas kernels: 0 us -> 60.3 us
  waiting for transfers between devices: 301 us -> 259 us
  between operations: 19.7 us -> 6 us
  starting transfers between devices: 52.9 us -> 44.3 us
    psum x1 -> x0, waiting for transfers between devices: 115 us -> none  [local(): head_sum, ffn_sum, row_sum = lax.psum((head_sum, ffn_sum, row_sum), AXES)]
    ppermute x46 -> x52, waiting for transfers between devices: 186 us -> 259 us  [swap(): return lax.ppermute(array, AXES, pairs)]
    pallas_call x0 -> x14, Pallas kernels: none -> 60.3 us  [the longest x10 52.3 us: call(): pl.pallas_call(kernel, out_shape=[jax.ShapeDtypeStruct(s, d) for s, d in...]
    dot_general x40 -> x0, matrix products: 59.1 us -> none  [the longest x8 19.4 us: attend(): jnp.einsum('hqk,khe->qhe', probs.astype(BF16), heads_of(values), preferre...]
    dot_general x50 -> x34, matrix products: 94.9 us -> 49.9 us  [dot(): return lax.dot_general(a, b, (dims, ((), ())), preferred_element_type=F32)]
    unnamed x637 -> x227, local copies, waits for them, and re-layouts: 49.5 us -> 19.8 us
    sub x8 -> x0, matrix products: 28.6 us -> none  [attend(): shifted = jnp.exp(scores - jnp.max(scores, axis=-1, keepdims=True))]
    concatenate x27 -> x14, other arithmetic: 29.1 us -> 3.08 us  [the longest x2 1.53 us: local(): attn_w.append(jnp.concatenate(attn, axis=1).astype(BF16)[None])]
  transfers between devices with their start and end apart: 47 -> 52, of which waited for: 19 -> 29; matrix products, arithmetic and copies ran while one was open for 47% -> 17% of each run, Pallas kernels for 0% -> 11%
where the time goes in v2:
time: 516 us; the launch traced here: 506 us
  waiting for transfers between devices  259 us (50%)
  Pallas kernels  60.3 us (12%)
  other arithmetic  56.7 us (11%)
  matrix products  49.9 us (10%)
  starting transfers between devices  44.3 us (9%)
  local copies, waits for them, and re-layouts  29.7 us (6%)
  between operations  6 us (1%)
    ppermute x52, waiting for transfers between devices, swap(): return lax.ppermute(array, AXES, pairs)  259 us
    pallas_call x10, Pallas kernels, call(): pl.pallas_call(kernel, out_shape=[jax.ShapeDtypeStruct(s, d) for s, d in...  52.3 us
    dot_general x34, matrix products, dot(): return lax.dot_general(a, b, (dims, ((), ())), preferred_element_type=F32)  49.9 us
    ppermute x52, starting transfers between devices, swap(): return lax.ppermute(array, AXES, pairs)  44.3 us
    unnamed x227, local copies, waits for them, and re-layouts  19.8 us
  transfers between devices with their start and end apart: 52, of which 29 were waited for; matrix products, arithmetic and copies ran while one was open for 17% of the time, Pallas kernels for 11%

profile of v2, /device:TPU:0, one launch (start us, length us, event | category | flops | bytes accessed | tf_op | source)
XLA Modules:
  0.0 506.0 jit_solution(15864656968777415872)
XLA Ops:
  22.2 12.1 %collective-permute-done.1 = bf16[2,96,768]{2,1,0:T(8,128)(2,1)S(1)} collective-permute-done((bf16[2,96,768]{2,1,0:T(8,128)(2,1)S(1)}, bf16[2,96,768]{2,1,0:T(8,128)(2,1)S(1)}, u32[]{:S(2)}, u32[]{:S(2)}) %collective-permute-start.1) | collective-permute-done | bytes 294944 | tf_op jit(solution)/shard_map/ppermute | solution.py:52
  47.4 19.8 %collective-permute-done.6 = bf16[2,96,1536]{2,1,0:T(8,128)(2,1)S(1)} collective-permute-done((bf16[2,96,1536]{2,1,0:T(8,128)(2,1)S(1)}, bf16[2,96,1536]{2,1,0:T(8,128)(2,1)S(1)}, u32[]{:S(2)}, u32[]{:S(2)}) %collective-permute-start.6) | collective-permute-done | bytes 589856 | tf_op jit(solution)/shard_map/ppermute | solution.py:52
  74.0 6.6 %shard_map.448 = (bf16[768,192]{1,0:T(8,128)(2,1)S(1)}, bf16[768,192]{1,0:T(8,128)(2,1)S(1)}, f32[6,768]{1,0:T(8,128)S(1)}) custom-call(s32[3]{0:T(128)S(1)} %pad_add_fusion.limits, bf16[768,576]{1,0:T(8,128)(2,1)S(1)} %multiply_convert_fusion.7.qkv0, bf16[768,576]{1,0:T(8,128)(2,1)S(1)} %multiply_convert_fusion.6.qkv1), custom_call_target="tpu_custom_call" | custom-call | tf_op jit(solution)/shard_map/pallas_call | solution.py:296
  89.1 12.6 %collective-permute-done.10 = bf16[2,96,768]{2,1,0:T(8,128)(2,1)S(1)} collective-permute-done((bf16[2,96,768]{2,1,0:T(8,128)(2,1)S(1)}, bf16[2,96,768]{2,1,0:T(8,128)(2,1)S(1)}, u32[]{:S(2)}, u32[]{:S(2)}) %collective-permute-start.10) | collective-permute-done | bytes 294944 | tf_op jit(solution)/shard_map/ppermute | solution.py:52
  110.0 24.2 %collective-permute-done.14 = bf16[2,96,1536]{2,1,0:T(8,128)(2,1)S(1)} collective-permute-done((bf16[2,96,1536]{2,1,0:T(8,128)(2,1)S(1)}, bf16[2,96,1536]{2,1,0:T(8,128)(2,1)S(1)}, u32[]{:S(2)}, u32[]{:S(2)}) %collective-permute-start.14) | collective-permute-done | bytes 589856 | tf_op jit(solution)/shard_map/ppermute | solution.py:52
  134.4 4.9 collective-permute-done.12
  152.2 24.6 %collective-permute-done.16 = bf16[2,4,96,768]{3,2,1,0:T(8,128)(2,1)S(1)} collective-permute-done((bf16[2,4,96,768]{3,2,1,0:T(8,128)(2,1)S(1)}, bf16[2,4,96,768]{3,2,1,0:T(8,128)(2,1)S(1)}, u32[]{:S(2)}, u32[]{:S(2)}) %collective-permute-start.16) | collective-permute-done | bytes 1179680 | tf_op jit(solution)/shard_map/ppermute | solution.py:52
  182.5 6.6 %shard_map.450 = (bf16[768,192]{1,0:T(8,128)(2,1)S(1)}, bf16[768,192]{1,0:T(8,128)(2,1)S(1)}, f32[6,768]{1,0:T(8,128)S(1)}) custom-call(s32[3]{0:T(128)S(1)} %pad_add_fusion.limits, bf16[768,576]{1,0:T(8,128)(2,1)S(1)} %multiply_convert_fusion.5.qkv0, bf16[768,576]{1,0:T(8,128)(2,1)S(1)} %multiply_convert_fusion.4.qkv1), custom_call_target="tpu_custom_call" | custom-call | tf_op jit(solution)/shard_map/pallas_call | solution.py:296
  201.4 24.4 %collective-permute-done.20 = bf16[2,4,96,1536]{3,2,1,0:T(8,128)(2,1)S(1)} collective-permute-done((bf16[2,4,96,1536]{3,2,1,0:T(8,128)(2,1)S(1)}, bf16[2,4,96,1536]{3,2,1,0:T(8,128)(2,1)S(1)}, u32[]{:S(2)}, u32[]{:S(2)}) %collective-permute-start.20) | collective-permute-done | bytes 2359328 | tf_op jit(solution)/shard_map/ppermute | solution.py:52
  259.3 4.9 shard_map.455
  272.5 6.9 %shard_map.453 = (bf16[768,576]{1,0:T(8,128)(2,1)S(1)}, bf16[768,576]{1,0:T(8,128)(2,1)S(1)}) custom-call(s32[3]{0:T(128)S(1)} %pad_add_fusion.limits, bf16[768,576]{1,0:T(8,128)(2,1)S(1)} %multiply_convert_fusion.5.qkv0, bf16[768,576]{1,0:T(8,128)(2,1)S(1)} %multiply_convert_fusion.4.qkv1, bf16[768,192]{1,0:T(8,128)(2,1)S(1)} %convolution_convert_fusion.3.dctx0, ...), custom_call_target="tpu_custom_call" | custom-call | tf_op jit(solution)/shard_map/pallas_call | solution.py:296
  285.0 16.5 %collective-permute-done.25.came = bf16[256,768]{1,0:T(8,128)(2,1)S(1)} collective-permute-done((bf16[256,768]{1,0:T(8,128)(2,1)S(1)}, bf16[256,768]{1,0:T(8,128)(2,1)S(1)}, u32[]{:S(2)}, u32[]{:S(2)}) %collective-permute-start.25) | collective-permute-done | bytes 393248 | tf_op jit(solution)/shard_map/ppermute | solution.py:52
  314.1 14.4 %collective-permute-done.28 = bf16[4,96,1536]{2,1,0:T(8,128)(2,1)S(1)} collective-permute-done((bf16[4,96,1536]{2,1,0:T(8,128)(2,1)S(1)}, bf16[4,96,1536]{2,1,0:T(8,128)(2,1)S(1)}, u32[]{:S(2)}, u32[]{:S(2)}) %collective-permute-start.28) | collective-permute-done | bytes 1179680 | tf_op jit(solution)/shard_map/ppermute | solution.py:52
  343.4 4.9 shard_map.460
  348.6 7.6 %collective-permute-done.31 = bf16[2,96,1536]{2,1,0:T(8,128)(2,1)S(1)} collective-permute-done((bf16[2,96,1536]{2,1,0:T(8,128)(2,1)S(1)}, bf16[2,96,1536]{2,1,0:T(8,128)(2,1)S(1)}, u32[]{:S(2)}, u32[]{:S(2)}) %collective-permute-start.31) | collective-permute-done | bytes 589856 | tf_op jit(solution)/shard_map/ppermute | solution.py:52
  369.9 6.9 %shard_map.458 = (bf16[768,576]{1,0:T(8,128)(2,1)S(1)}, bf16[768,576]{1,0:T(8,128)(2,1)S(1)}) custom-call(s32[3]{0:T(128)S(1)} %pad_add_fusion.limits, bf16[768,576]{1,0:T(8,128)(2,1)S(1)} %copy-done.1, bf16[768,576]{1,0:T(8,128)(2,1)S(1)} %multiply_convert_fusion.6.qkv1, bf16[768,192]{1,0:T(8,128)(2,1)S(1)} %convolution_convert_fusion.1.dctx0, ...), custom_call_target="tpu_custom_call" | custom-call | tf_op jit(solution)/shard_map/pallas_call | solution.py:296
  378.1 14.1 %collective-permute-done.32.came = bf16[256,768]{1,0:T(8,128)(2,1)S(1)} collective-permute-done((bf16[256,768]{1,0:T(8,128)(2,1)S(1)}, bf16[256,768]{1,0:T(8,128)(2,1)S(1)}, u32[]{:S(2)}, u32[]{:S(2)}) %collective-permute-start.32) | collective-permute-done | bytes 393248 | tf_op jit(solution)/shard_map/ppermute | solution.py:52
  409.2 4.6 shard_map.461
  419.9 5.0 collective-permute-done.43
  427.0 4.5 collective-permute-done.44
  431.6 13.4 %collective-permute-done.39 = bf16[2,4,96,768]{3,2,1,0:T(8,128)(2,1)S(1)} collective-permute-done((bf16[2,4,96,768]{3,2,1,0:T(8,128)(2,1)}, bf16[2,4,96,768]{3,2,1,0:T(8,128)(2,1)S(1)}, u32[]{:S(2)}, u32[]{:S(2)}) %collective-permute-start.39) | collective-permute-done | bytes 1179680 | tf_op jit(solution)/shard_map/ppermute | solution.py:52
  455.8 26.2 %collective-permute-done.46 = bf16[2,96,1536]{2,1,0:T(8,128)(2,1)S(1)} collective-permute-done((bf16[2,96,1536]{2,1,0:T(8,128)(2,1)S(1)}, bf16[2,96,1536]{2,1,0:T(8,128)(2,1)S(1)}, u32[]{:S(2)}, u32[]{:S(2)}) %collective-permute-start.46) | collective-permute-done | bytes 589856 | tf_op jit(solution)/shard_map/ppermute | solution.py:52
  482.6 5.8 %collective-permute-done.41 = bf16[2,96,768]{2,1,0:T(8,128)(2,1)S(1)} collective-permute-done((bf16[2,96,768]{2,1,0:T(8,128)(2,1)S(1)}, bf16[2,96,768]{2,1,0:T(8,128)(2,1)S(1)}, u32[]{:S(2)}, u32[]{:S(2)}) %collective-permute-start.41) | collective-permute-done | bytes 294944 | tf_op jit(solution)/shard_map/ppermute | solution.py:52
  488.6 6.1 %collective-permute-done.47 = bf16[1,96,1536]{2,1,0:T(8,128)(2,1)S(1)} collective-permute-done((bf16[1,96,1536]{2,1,0:T(8,128)(2,1)S(1)}, bf16[1,96,1536]{2,1,0:T(8,128)(2,1)S(1)}, u32[]{:S(2)}, u32[]{:S(2)}) %collective-permute-start.47) | collective-permute-done | bytes 294944 | tf_op jit(solution)/shard_map/ppermute | solution.py:52
  (542 shorter events, 222.4 us)
Async XLA Ops:
  2.9 38.1 %collective-permute-start.5 = (f32[2304]{0:T(1024)}, f32[2304]{0:T(1024)S(1)}, u32[]{:S(2)}, u32[]{:S(2)}) collective-permute-start(f32[2304]{0:T(1024)} %pad_maximum_fusion.34), channel_id=1, source_target_pairs={{0,2},{1,3},{2,0},{3,1},{4,6},{5,7},{6,4},{7,5},{8,10},{9,11},{10,... | collective-permute-start | bytes 27656 | tf_op jit(solution)/shard_map/ppermute | solution.py:52
  41.2 25.9 %collective-permute-start.6 = (bf16[2,96,1536]{2,1,0:T(8,128)(2,1)S(1)}, bf16[2,96,1536]{2,1,0:T(8,128)(2,1)S(1)}, u32[]{:S(2)}, u32[]{:S(2)}) collective-permute-start(bf16[2,96,1536]{2,1,0:T(8,128)(2,1)S(1)} %pad_maximum_fusion.19), channel_id=1, source_target_pairs={{0,16},{1,17},{2,18},{3,19},{4,20},{5,21},{6,22},{7,23},{8,24},{9,... | collective-permute-start | bytes 1769480 | tf_op jit(solution)/shard_map/ppermute | solution.py:52
  46.0 21.3 %collective-permute-start.4 = (bf16[2,4,96,768]{3,2,1,0:T(8,128)(2,1)S(1)}, bf16[2,4,96,768]{3,2,1,0:T(8,128)(2,1)S(1)}, u32[]{:S(2)}, u32[]{:S(2)}) collective-permute-start(bf16[2,4,96,768]{3,2,1,0:T(8,128)(2,1)S(1)} %pad_maximum_fusion.9), channel_id=1, source_target_pairs={{0,2},{1,5},{2,0},{3,7},{4,6},{5,1},{6,4},{7,3},{8,10},{9,13},{10,... | collective-permute-start | bytes 3538952 | tf_op jit(solution)/shard_map/ppermute | solution.py:52
  46.8 39.4 %collective-permute-start.11 = (bf16[1,96,1536]{2,1,0:T(8,128)(2,1)}, bf16[1,96,1536]{2,1,0:T(8,128)(2,1)S(1)}, u32[]{:S(2)}, u32[]{:S(2)}) collective-permute-start(bf16[1,96,1536]{2,1,0:T(8,128)(2,1)} %get-tuple-element.113), channel_id=1, source_target_pairs={{0,8},{1,9},{2,10},{3,11},{4,12},{5,13},{6,14},{7,15},{8,0},{9,1},... | collective-permute-start | bytes 884744 | tf_op jit(solution)/shard_map/ppermute | solution.py:52
  104.1 35.2 %collective-permute-start.12 = (bf16[2,4,96,1536]{3,2,1,0:T(8,128)(2,1)S(1)}, bf16[2,4,96,1536]{3,2,1,0:T(8,128)(2,1)S(1)}, u32[]{:S(2)}, u32[]{:S(2)}) collective-permute-start(bf16[2,4,96,1536]{3,2,1,0:T(8,128)(2,1)S(1)} %pad_maximum_fusion.3), channel_id=1, source_target_pairs={{0,2},{1,5},{2,0},{3,7},{4,6},{5,1},{6,4},{7,3},{8,10},{9,13},{10,... | collective-permute-start | bytes 7077896 | tf_op jit(solution)/shard_map/ppermute | solution.py:52
  105.6 28.6 %collective-permute-start.14 = (bf16[2,96,1536]{2,1,0:T(8,128)(2,1)S(1)}, bf16[2,96,1536]{2,1,0:T(8,128)(2,1)S(1)}, u32[]{:S(2)}, u32[]{:S(2)}) collective-permute-start(bf16[2,96,1536]{2,1,0:T(8,128)(2,1)S(1)} %pad_maximum_fusion.21), channel_id=1, source_target_pairs={{0,16},{1,17},{2,18},{3,19},{4,20},{5,21},{6,22},{7,23},{8,24},{9,... | collective-permute-start | bytes 1769480 | tf_op jit(solution)/shard_map/ppermute | solution.py:52
  108.3 38.9 %collective-permute-start.13 = (bf16[4,96,768]{2,1,0:T(8,128)(2,1)S(1)}, bf16[4,96,768]{2,1,0:T(8,128)(2,1)S(1)}, u32[]{:S(2)}, u32[]{:S(2)}) collective-permute-start(bf16[4,96,768]{2,1,0:T(8,128)(2,1)S(1)} %pad_maximum_fusion.20), channel_id=1, source_target_pairs={{0,4},{1,3},{2,6},{3,1},{4,0},{5,7},{6,2},{7,5},{8,12},{9,11},{10,... | collective-permute-start | bytes 1769480 | tf_op jit(solution)/shard_map/ppermute | solution.py:52
  148.5 28.2 %collective-permute-start.16 = (bf16[2,4,96,768]{3,2,1,0:T(8,128)(2,1)S(1)}, bf16[2,4,96,768]{3,2,1,0:T(8,128)(2,1)S(1)}, u32[]{:S(2)}, u32[]{:S(2)}) collective-permute-start(bf16[2,4,96,768]{3,2,1,0:T(8,128)(2,1)S(1)} %pad_maximum_fusion.14), channel_id=1, source_target_pairs={{0,2},{1,5},{2,0},{3,7},{4,6},{5,1},{6,4},{7,3},{8,10},{9,13},{10,... | collective-permute-start | bytes 3538952 | tf_op jit(solution)/shard_map/ppermute | solution.py:52
  150.1 30.5 %collective-permute-start.17 = (bf16[4,96,1536]{2,1,0:T(8,128)(2,1)S(1)}, bf16[4,96,1536]{2,1,0:T(8,128)(2,1)S(1)}, u32[]{:S(2)}, u32[]{:S(2)}) collective-permute-start(bf16[4,96,1536]{2,1,0:T(8,128)(2,1)S(1)} %pad_maximum_fusion.13), channel_id=1, source_target_pairs={{0,4},{1,3},{2,6},{3,1},{4,0},{5,7},{6,2},{7,5},{8,12},{9,11},{10,... | collective-permute-start | bytes 3538952 | tf_op jit(solution)/shard_map/ppermute | solution.py:52
  196.8 28.9 %collective-permute-start.20 = (bf16[2,4,96,1536]{3,2,1,0:T(8,128)(2,1)S(1)}, bf16[2,4,96,1536]{3,2,1,0:T(8,128)(2,1)S(1)}, u32[]{:S(2)}, u32[]{:S(2)}) collective-permute-start(bf16[2,4,96,1536]{3,2,1,0:T(8,128)(2,1)S(1)} %pad_maximum_fusion.6), channel_id=1, source_target_pairs={{0,2},{1,5},{2,0},{3,7},{4,6},{5,1},{6,4},{7,3},{8,10},{9,13},{10,... | collective-permute-start | bytes 7077896 | tf_op jit(solution)/shard_map/ppermute | solution.py:52
  264.1 37.5 %collective-permute-start.26 = (bf16[2,4,96,1536]{3,2,1,0:T(8,128)(2,1)S(1)}, bf16[2,4,96,1536]{3,2,1,0:T(8,128)(2,1)S(1)}, u32[]{:S(2)}, u32[]{:S(2)}) collective-permute-start(bf16[2,4,96,1536]{3,2,1,0:T(8,128)(2,1)S(1)} %get-tuple-element.139), channel_id=1, source_target_pairs={{0,2},{1,5},{2,0},{3,7},{4,6},{5,1},{6,4},{7,3},{8,10},{9,13},{10,... | collective-permute-start | bytes 7077896 | tf_op jit(solution)/shard_map/ppermute | solution.py:52
  265.4 19.2 %collective-permute-start.23 = (bf16[384,768]{1,0:T(8,128)(2,1)S(1)}, bf16[384,768]{1,0:T(8,128)(2,1)S(1)}, u32[]{:S(2)}, u32[]{:S(2)}) collective-permute-start(bf16[384,768]{1,0:T(8,128)(2,1)S(1)} %collective-permute-done.22), channel_id=1, source_target_pairs={{0,1},{1,0},{2,3},{3,2},{4,5},{5,4},{6,7},{7,6},{8,9},{9,8},{10,11... | collective-permute-start | bytes 1769480 | tf_op jit(solution)/shard_map/ppermute | solution.py:52
  305.3 23.2 %collective-permute-start.28 = (bf16[4,96,1536]{2,1,0:T(8,128)(2,1)S(1)}, bf16[4,96,1536]{2,1,0:T(8,128)(2,1)S(1)}, u32[]{:S(2)}, u32[]{:S(2)}) collective-permute-start(bf16[4,96,1536]{2,1,0:T(8,128)(2,1)S(1)} %get-tuple-element.143), channel_id=1, source_target_pairs={{0,4},{1,3},{2,6},{3,1},{4,0},{5,7},{6,2},{7,5},{8,12},{9,11},{10,... | collective-permute-start | bytes 3538952 | tf_op jit(solution)/shard_map/ppermute | solution.py:52
  313.2 35.1 %collective-permute-start.30 = (bf16[2,4,96,768]{3,2,1,0:T(8,128)(2,1)S(1)}, bf16[2,4,96,768]{3,2,1,0:T(8,128)(2,1)S(1)}, u32[]{:S(2)}, u32[]{:S(2)}) collective-permute-start(bf16[2,4,96,768]{3,2,1,0:T(8,128)(2,1)S(1)} %get-tuple-element.146), channel_id=1, source_target_pairs={{0,2},{1,5},{2,0},{3,7},{4,6},{5,1},{6,4},{7,3},{8,10},{9,13},{10,... | collective-permute-start | bytes 3538952 | tf_op jit(solution)/shard_map/ppermute | solution.py:52
  330.1 26.1 %collective-permute-start.31 = (bf16[2,96,1536]{2,1,0:T(8,128)(2,1)S(1)}, bf16[2,96,1536]{2,1,0:T(8,128)(2,1)S(1)}, u32[]{:S(2)}, u32[]{:S(2)}) collective-permute-start(bf16[2,96,1536]{2,1,0:T(8,128)(2,1)S(1)} %select_convert_fusion.1), channel_id=1, source_target_pairs={{0,16},{1,17},{2,18},{3,19},{4,20},{5,21},{6,22},{7,23},{8,24},{9,... | collective-permute-start | bytes 1769480 | tf_op jit(solution)/shard_map/ppermute | solution.py:52
  348.3 44.3 %collective-permute-start.33 = (bf16[2,4,96,1536]{3,2,1,0:T(8,128)(2,1)S(1)}, bf16[2,4,96,1536]{3,2,1,0:T(8,128)(2,1)S(1)}, u32[]{:S(2)}, u32[]{:S(2)}) collective-permute-start(bf16[2,4,96,1536]{3,2,1,0:T(8,128)(2,1)S(1)} %get-tuple-element.159), channel_id=1, source_target_pairs={{0,2},{1,5},{2,0},{3,7},{4,6},{5,1},{6,4},{7,3},{8,10},{9,13},{10,... | collective-permute-start | bytes 7077896 | tf_op jit(solution)/shard_map/ppermute | solution.py:52
  359.4 33.0 %collective-permute-start.34 = (bf16[4,96,768]{2,1,0:T(8,128)(2,1)S(1)}, bf16[4,96,768]{2,1,0:T(8,128)(2,1)S(1)}, u32[]{:S(2)}, u32[]{:S(2)}) collective-permute-start(bf16[4,96,768]{2,1,0:T(8,128)(2,1)S(1)} %get-tuple-element.161), channel_id=1, source_target_pairs={{0,4},{1,3},{2,6},{3,1},{4,0},{5,7},{6,2},{7,5},{8,12},{9,11},{10,... | collective-permute-start | bytes 1769480 | tf_op jit(solution)/shard_map/ppermute | solution.py:52
  416.4 32.2 %collective-permute-start.36 = (bf16[768,768]{1,0:T(8,128)(2,1)}, bf16[768,768]{1,0:T(8,128)(2,1)}, u32[]{:S(2)}, u32[]{:S(2)}) collective-permute-start(bf16[768,768]{1,0:T(8,128)(2,1)} %add_convert_fusion.1), channel_id=1, source_target_pairs={{0,1},{1,0},{2,3},{3,2},{4,5},{5,4},{6,7},{7,6},{8,9},{9,8},{10,11... | collective-permute-start | bytes 3538952 | tf_op jit(solution)/shard_map/ppermute | solution.py:52
  416.4 29.4 %collective-permute-start.45 = (bf16[4,96,1536]{2,1,0:T(8,128)(2,1)}, bf16[4,96,1536]{2,1,0:T(8,128)(2,1)}, u32[]{:S(2)}, u32[]{:S(2)}) collective-permute-start(bf16[4,96,1536]{2,1,0:T(8,128)(2,1)} %get-tuple-element.169), channel_id=1, source_target_pairs={{0,4},{1,3},{2,6},{3,1},{4,0},{5,7},{6,2},{7,5},{8,12},{9,11},{10,... | collective-permute-start | bytes 3538952 | tf_op jit(solution)/shard_map/ppermute | solution.py:52
  417.0 28.0 %collective-permute-start.39 = (bf16[2,4,96,768]{3,2,1,0:T(8,128)(2,1)}, bf16[2,4,96,768]{3,2,1,0:T(8,128)(2,1)S(1)}, u32[]{:S(2)}, u32[]{:S(2)}) collective-permute-start(bf16[2,4,96,768]{3,2,1,0:T(8,128)(2,1)} %get-tuple-element.166), channel_id=1, source_target_pairs={{0,2},{1,5},{2,0},{3,7},{4,6},{5,1},{6,4},{7,3},{8,10},{9,13},{10,... | collective-permute-start | bytes 3538952 | tf_op jit(solution)/shard_map/ppermute | solution.py:52
  447.7 34.3 %collective-permute-start.46 = (bf16[2,96,1536]{2,1,0:T(8,128)(2,1)S(1)}, bf16[2,96,1536]{2,1,0:T(8,128)(2,1)S(1)}, u32[]{:S(2)}, u32[]{:S(2)}) collective-permute-start(bf16[2,96,1536]{2,1,0:T(8,128)(2,1)S(1)} %select_convert_fusion), channel_id=1, source_target_pairs={{0,16},{1,17},{2,18},{3,19},{4,20},{5,21},{6,22},{7,23},{8,24},{9,... | collective-permute-start | bytes 1769480 | tf_op jit(solution)/shard_map/ppermute | solution.py:52
  450.7 31.8 %collective-permute-start.37 = (bf16[384,768]{1,0:T(8,128)(2,1)S(1)}, bf16[384,768]{1,0:T(8,128)(2,1)S(1)}, u32[]{:S(2)}, u32[]{:S(2)}) collective-permute-start(bf16[384,768]{1,0:T(8,128)(2,1)S(1)} %constant_dynamic-slice_fusion), channel_id=1, source_target_pairs={{0,2},{1,3},{2,0},{3,1},{4,6},{5,7},{6,4},{7,5},{8,10},{9,11},{10,... | collective-permute-start | bytes 1769480 | tf_op jit(solution)/shard_map/ppermute | solution.py:52
  455.3 33.0 %collective-permute-start.41 = (bf16[2,96,768]{2,1,0:T(8,128)(2,1)S(1)}, bf16[2,96,768]{2,1,0:T(8,128)(2,1)S(1)}, u32[]{:S(2)}, u32[]{:S(2)}) collective-permute-start(bf16[2,96,768]{2,1,0:T(8,128)(2,1)S(1)} %select_convert_fusion.4), channel_id=1, source_target_pairs={{0,16},{1,17},{2,18},{3,19},{4,20},{5,21},{6,22},{7,23},{8,24},{9,... | collective-permute-start | bytes 884744 | tf_op jit(solution)/shard_map/ppermute | solution.py:52
  482.5 20.2 %collective-permute-start.38 = (bf16[384,768]{1,0:T(8,128)(2,1)S(1)}, bf16[384,768]{1,0:T(8,128)(2,1)S(1)}, u32[]{:S(2)}, u32[]{:S(2)}) collective-permute-start(bf16[384,768]{1,0:T(8,128)(2,1)S(1)} %collective-permute-done.37), channel_id=1, source_target_pairs={{0,1},{1,0},{2,3},{3,2},{4,5},{5,4},{6,7},{7,6},{8,9},{9,8},{10,11... | collective-permute-start | bytes 1769480 | tf_op jit(solution)/shard_map/ppermute | solution.py:52
  (136 other events, 1088.0 us)

commit v3 on v2

--- a/solution.py
+++ b/solution.py
@@ -34,88 +34,96 @@
 
 
 class Links:
-    def __init__(self, n_dp):
+    def __init__(self, n_dp, rows):
         self.n_dp = n_dp
         self.count = n_dp * 4
-        self.bits = n_dp.bit_length() - 1
+        self.z_masks = [1 << bit for bit in reversed(range(n_dp.bit_length() - 2))]
+        self.order = [0]
+        for mask in self.z_masks:
+            self.order += [place ^ mask for place in self.order]
+        self.aligned = rows % 16 == 0
         dp_at = lax.axis_index("dp")
         mp_at = lax.axis_index("mp")
         self.at_x = mp_at // 2
         self.core = mp_at % 2
         self.at_y = dp_at % 2
-        self.dp_at = dp_at
-        self.places = jnp.stack([self.core, self.at_y]).astype(jnp.int32)
+        self.at_z = dp_at // 2
+        self.places = jnp.stack([self.core, self.at_y, self.at_z]).astype(jnp.int32)
 
     def swap(self, array, mask0, mask1=None):
         mask1 = mask0 if mask1 is None else mask1
         pairs = [(i, i ^ (mask1 if i & 1 else mask0)) for i in range(self.count)]
         return lax.ppermute(array, AXES, pairs)
 
+    def swap_as(self, name, swap, *args):
+        with jax.named_scope(name):
+            return swap(*args)
+
     def swap_core(self, array):
         return self.swap(array, 1)
 
     def swap_x(self, array):
         return self.swap(array, 2)
 
-    def gather_bit(self, block, bit):
-        other = self.swap(block, 4 << bit)
-        mine = ((self.dp_at >> bit) & 1) == 0
-        return jnp.concatenate([jnp.where(mine, block, other), jnp.where(mine, other, block)])
-
-    def gather_rest(self, block):
-        for bit in range(2, self.bits):
-            block = self.gather_bit(block, bit)
-        return block
-
-    def gather_near(self, block):
-        return self.swap(block, 4, 2)
-
-    def gather_far(self, block, near):
-        far = self.swap(jnp.stack([block, near]), 2, 4)
-        first = self.core == 0
-        own_far = jnp.where(first, near, far[0])
-        other_near = jnp.where(first, far[0], near)
-        return self.rows(block, own_far), self.rows(other_near, far[1])
-
-    def rows(self, same, other):
-        low = self.at_y == 0
-        both = jnp.stack([jnp.where(low, same, other), jnp.where(low, other, same)], axis=1)
-        return both.reshape(-1, both.shape[-1])
-
-    def scatter_first(self, keep, give):
-        came = self.swap(give, 2, 4)
-        return keep[0].astype(F32) + came[0].astype(F32), (keep[1].astype(F32) + came[1].astype(F32)).astype(BF16)
-
-    def scatter_second(self, keep, give):
-        return keep + self.swap(give, 4, 2).astype(F32)
-
-    def scatter_bit(self, keep, bit):
-        half = keep.shape[0] // 2
-        mine = ((self.dp_at >> bit) & 1) == 0
-        give = jnp.where(mine, keep[half:], keep[:half]).astype(BF16)
-        keep = jnp.where(mine, keep[:half], keep[half:])
-        return keep + self.swap(give, 4 << bit).astype(F32)
-
-    def scatter_rest_from(self, keep, top):
-        for bit in reversed(range(1, top + 1)):
-            keep = self.scatter_bit(keep, bit)
-        return keep[0]
-
-    def scatter_rest(self, keep):
-        return self.scatter_rest_from(keep, self.bits - 1)
-
-def norm_parts(residual, gain_row, shift_row):
-    center = residual - jnp.mean(residual, axis=-1, keepdims=True)
-    inv_std = lax.rsqrt(jnp.mean(center * center, axis=-1, keepdims=True) + EPS_NORM)
-    scaled = center * inv_std
-    return (scaled * gain_row + shift_row, scaled, inv_std)
-
-
-def norm_back(grad_output, scaled, inv_std, gain_row):
-    upstream = grad_output * gain_row
-    mean_up = jnp.mean(upstream, axis=-1, keepdims=True)
-    mean_cross = jnp.mean(upstream * scaled, axis=-1, keepdims=True)
-    return inv_std * (upstream - mean_up - scaled * mean_cross)
+    def swap_z(self, array, mask):
+        return self.swap(array, 8 * mask)
+
+    def swap_near(self, array):
+        return self.swap(array, 4, 2)
+
+    def swap_far(self, array):
+        return self.swap(array, 2, 4)
+
+    def last_z(self, block, masks):
+        for mask in masks[:-1]:
+            block = jnp.concatenate([block, self.swap_z(block, mask)])
+        return block, self.swap_z(block, masks[-1])
+
+    def scatter_z(self, parts, masks):
+        for mask in masks[:-1]:
+            half = parts.shape[0] // 2
+            parts = parts[:half] + self.swap_z(parts[half:].astype(BF16), mask).astype(F32)
+        half = parts.shape[0] // 2
+        return parts[:half], self.swap_z(parts[half:].astype(BF16), masks[-1])
+
+    def assemble(self, two, far):
+        if self.aligned:
+            shape = (far.shape[1], 2) + far.shape[2:]
+            kernel = functools.partial(assemble_kernel, self.order)
+            both = call(kernel, [(shape, far.dtype)] * 2, (self.places, two, far), name="assemble")
+        else:
+            order = jnp.array(inverse(self.order))[jnp.arange(far.shape[1]) ^ self.at_z]
+            two, far = jnp.take(two, order, axis=1), jnp.take(far, order, axis=1)
+            first, low = self.core == 0, self.at_y == 0
+            own_far = jnp.where(first, two[1], far[0])
+            other_same = jnp.where(first, far[0], two[1])
+            both = [
+                jnp.stack([jnp.where(low, same, other), jnp.where(low, other, same)], axis=1)
+                for same, other in ((two[0], own_far), (other_same, far[1]))
+            ]
+        return [w.reshape(-1, w.shape[-1]) for w in both]
+
+
+def inverse(order):
+    return [order.index(place) for place in range(len(order))]
+
+
+def assemble_kernel(order, places, two, far, own, other):
+    first, at_y, at_z = places[0] == 0, places[1], places[2]
+    for m, distance in enumerate(order):
+        j = distance ^ at_z
+        own[j, at_y] = two[0, m]
+        other[j, 1 - at_y] = far[1, m]
+
+        @pl.when(first)
+        def _(j=j, m=m):
+            own[j, 1 - at_y] = two[1, m]
+            other[j, at_y] = far[0, m]
+
+        @pl.when(~first)
+        def _(j=j, m=m):
+            own[j, 1 - at_y] = far[0, m]
+            other[j, at_y] = two[1, m]
 
 
 def adam_step(master, moment, second, gradient, step_rate, decay_rate):
@@ -289,9 +297,10 @@
 VMEM = pl.BlockSpec(memory_space=pltpu.VMEM)
 SMEM = pl.BlockSpec(memory_space=pltpu.SMEM)
 ROOM = pltpu.CompilerParams(vmem_limit_bytes=32 * 1024 * 1024)
-
-
-def call(kernel, outs, ins, scratch=()):
+CHEAP = pl.CostEstimate(flops=1, bytes_accessed=1, transcendentals=0)
+
+
+def call(kernel, outs, ins, scratch=(), name=None):
     specs = [SMEM if a.dtype == jnp.int32 else VMEM for a in ins]
     return pl.pallas_call(
         kernel,
@@ -300,6 +309,8 @@
         out_specs=[VMEM] * len(outs),
         scratch_shapes=list(scratch),
         compiler_params=ROOM,
+        cost_estimate=CHEAP,
+        name=name,
     )(*ins)
 
 
@@ -311,6 +322,7 @@
         [((tokens, third), BF16)] * 2 + [((2 * third // HEAD_DIM, tokens), F32)],
         (limits, *qkv),
         [pltpu.VMEM((2 * half, half), F32)],
+        name="attend_full",
     )
     return (ctx0, ctx1), lse
 
@@ -327,6 +339,8 @@
         scratch_shapes=[pltpu.VMEM((2 * half, half), F32)],
         input_output_aliases={4: 0, 5: 1, 6: 2},
         compiler_params=ROOM,
+        cost_estimate=CHEAP,
+        name="attend_half",
     )(limits, *qkv, far, *ctx, lse)
     return (ctx0, ctx1), lse
 
@@ -338,6 +352,7 @@
         [((half, third), BF16)] * 2 + [((half, 4 * third), F32), ((half, 4 * third), BF16)],
         (limits, *qkv, far, *dctx, lse),
         [pltpu.VMEM((2, 2 * half, half), F32)],
+        name="attend_half_back",
     )
     return (dq0, dq1), own, sent
 
@@ -349,6 +364,7 @@
         [(qkv[0].shape, BF16)] * 2,
         (limits, *qkv, *dctx, lse),
         [pltpu.VMEM((2 * half, half), F32)],
+        name="attend_full_back",
     )
 
 
@@ -364,12 +380,14 @@
         out_specs=[rows] * 2,
         input_output_aliases={4: 0, 5: 1},
         compiler_params=ROOM,
+        cost_estimate=CHEAP,
+        name="fill_half",
     )(*dq, own, came, *dqkv)
 
-def wgrad_kernel(count, places, *refs):
+def wgrad_kernel(count, order, places, *refs):
     lefts, rights = refs[:count], (refs[count : 2 * count], refs[2 * count : 3 * count])
     keep, give, whole = refs[3 * count :]
-    first, at_y = places[0] == 0, places[1]
+    first, at_y, at_z = places[0] == 0, places[1], places[2]
     blocks, rows = keep.shape[1], keep.shape[2]
     turned = [left[...].T for left in lefts]
     for g in range(2):
@@ -388,8 +406,8 @@
 
                 @pl.when(when)
                 def _(ref=ref, slot=slot, y=y):
-                    for z in range(blocks):
-                        ref[slot, z] = whole[(2 * z + y) * rows : (2 * z + y + 1) * rows, :]
+                    for m, distance in enumerate(order):
+                        ref[slot, m] = whole[pl.ds((2 * (distance ^ at_z) + y) * rows, rows), :]
 
 
 def weight_grads(links, lefts, rights):
@@ -397,46 +415,230 @@
     columns = sum(r.shape[1] for r in rights[0])
     blocks = links.n_dp // 2
     rows = features // links.n_dp
-    if rows % 16 == 0:
+    if links.aligned:
         return call(
-            functools.partial(wgrad_kernel, len(lefts)),
+            functools.partial(wgrad_kernel, len(lefts), links.order),
             [((2, blocks, rows, columns), BF16)] * 2,
             (links.places, *lefts, *rights[0], *rights[1]),
             [pltpu.VMEM((features, columns), BF16)],
+            name="weight_grads",
         )
     low, first = links.at_y == 0, links.core == 0
     parts = []
     for group in rights:
         grad = jnp.concatenate([dot(a, b, TN) for a, b in zip(lefts, group)], axis=1).astype(BF16)
-        grad = grad.reshape(blocks, 2, rows, columns)
+        grad = jnp.take(grad.reshape(blocks, 2, rows, columns), jnp.array(links.order) ^ links.at_z, axis=0)
         parts += [jnp.where(low, grad[:, 0], grad[:, 1]), jnp.where(low, grad[:, 1], grad[:, 0])]
     own_same, own_far, other_same, other_far = parts
     keep = jnp.stack([own_same, jnp.where(first, own_far, other_same)])
     return keep, jnp.stack([jnp.where(first, other_same, own_far), other_far])
 
-def both_cores(links, partial):
-    low = partial.astype(BF16)
-    return low.astype(F32) + links.swap_core(low).astype(F32)
-
-
-def gelu_parts(pre):
-    cdf = 0.5 * (1.0 + lax.erf(pre * 0.7071067811865476))
-    pdf = jnp.exp(-0.5 * pre * pre) * 0.3989422804014327
-    return (pre * cdf).astype(BF16), cdf + pre * pdf
-
-
-def project(low, weight, bias, scale):
-    return ((dot(low, weight, NN) + bias) * scale).astype(BF16)
-
-
-def up_part(normed_low, weights, ffn_b):
-    wide = ffn_b[0].shape[-1]
-    return [gelu_parts(dot(normed_low, weights[g][:, :wide], NN) + ffn_b[g]) for g in range(2)]
-
-
-def down_part(ffn_parts, weights):
-    wide = ffn_parts[0][0].shape[1]
-    return sum(dot(ffn_parts[g][0], weights[g][:, wide:], NT) for g in range(2))
+def both_cores(links, parts):
+    return (*parts, *[links.swap_as("core", links.swap_core, part) for part in parts])
+
+
+def thirds(shape):
+    return [((shape[0] // 3, shape[1]), BF16)] * 3
+
+
+def core_sum(parts, at, rows):
+    return parts[at][rows, :].astype(F32) + parts[at + 3][rows, :].astype(F32)
+
+
+def norm_kernel(step, *refs):
+    parts, (residual, rows, out, low, scaled, inverse) = refs[:6], refs[6:]
+    wide = out.shape[1]
+    third = parts[0].shape[0]
+    for part in range(3):
+
+        @pl.loop(0, third // step)
+        def _(i, part=part):
+            inner = pl.ds(i * step, step)
+            at = pl.ds(part * third + i * step, step)
+            total = residual[at, :] + (core_sum(parts, part, inner) + rows[0:1, :])
+            center = total - jnp.sum(total, axis=-1, keepdims=True) * (1.0 / wide)
+            inv_std = lax.rsqrt(jnp.sum(center * center, axis=-1, keepdims=True) * (1.0 / wide) + EPS_NORM)
+            normal = center * inv_std
+            result = normal * rows[1:2, :] + rows[2:3, :]
+            out[at, :] = result
+            low[at, :] = result.astype(BF16)
+            scaled[at, :] = normal
+            inverse[at, :] = inv_std
+
+
+def add_norm(parts, residual, rows):
+    shape = residual.shape
+    return call(
+        functools.partial(norm_kernel, 64),
+        [(shape, F32), (shape, BF16), (shape, F32), ((shape[0], 1), F32)],
+        (*parts, residual, rows),
+        name="add_norm",
+    )
+
+
+def norm_back_kernel(step, *refs):
+    base, *parts, scaled, inverse, gain, out, low, sums = refs
+    wide = out.shape[1]
+    third = out.shape[0] // 3
+    sums[...] = jnp.zeros_like(sums)
+    for part in range(3):
+
+        @pl.loop(0, third // step)
+        def _(i, part=part):
+            at = pl.ds(part * third + i * step, step)
+            grad = base[at, :]
+            if parts:
+                grad = grad + core_sum(parts, part, pl.ds(i * step, step))
+            normal = scaled[at, :]
+            upstream = grad * gain[...]
+            mean_up = jnp.sum(upstream, axis=-1, keepdims=True) * (1.0 / wide)
+            mean_cross = jnp.sum(upstream * normal, axis=-1, keepdims=True) * (1.0 / wide)
+            result = inverse[at, :] * (upstream - mean_up - normal * mean_cross)
+            out[at, :] = result
+            low[at, :] = result.astype(BF16)
+            for k, term in enumerate((result, grad * normal, grad)):
+                sums[8 * k : 8 * (k + 1), :] += jnp.sum(term.reshape(-1, 8, wide), axis=0)
+
+
+def norm_back(parts, scaled, inverse, gain):
+    shape = scaled.shape
+    return call(
+        functools.partial(norm_back_kernel, 64),
+        [(shape, F32), (shape, BF16), ((24, shape[1]), F32)],
+        (*parts, scaled, inverse, gain),
+        name="norm_back",
+    )
+
+
+def final_sum_kernel(base, *refs):
+    parts, out = refs[:6], refs[6]
+    third = parts[0].shape[0]
+    for part in range(3):
+        at = slice(part * third, (part + 1) * third)
+        out[at, :] = (base[at, :] + core_sum(parts, part, slice(None))).astype(BF16)
+
+
+def chunks(count, step=256):
+    return [slice(at, at + step) for at in range(0, count, step)]
+
+
+def qkv_kernel(low, w0, w1, bias, *refs):
+    *other, out0, out1, extra = refs
+    columns = out0.shape[1]
+    third = columns // 3
+    half = extra.shape[0]
+    scale = jnp.where(lax.broadcasted_iota(jnp.int32, (1, columns), 1) < third, 0.125, 1.0)
+    for g, (weight, out) in enumerate(((w0, out0), (w1, out1))):
+        at = slice(2 * third * g, 2 * third * (g + 1))
+        for rows in chunks(low.shape[0]):
+            out[rows, :] = ((dot(low[rows, :], weight[:, :columns], NN) + bias[g : g + 1, :]) * scale).astype(BF16)
+        if other:
+            more = dot(other[0][...], weight[:, :columns], NN) + bias[g : g + 1, :]
+            extra[:, at] = more[:, third:].astype(BF16)
+        else:
+            extra[:, at] = out[2 * half :, third:]
+
+
+def project(low, weights, bias, other=None):
+    tokens, columns = low.shape[0], bias.shape[1]
+    half = tokens // 3
+    ins = (low, *weights, bias) + (() if other is None else (other,))
+    q0, q1, extra = call(
+        qkv_kernel,
+        [((tokens, columns), BF16)] * 2 + [((half, 4 * columns // 3), BF16)],
+        ins,
+        name="queries_keys_values",
+    )
+    return [q0, q1], extra
+
+
+def out_kernel(ctx0, ctx1, w0, w1, *outs):
+    third = ctx0.shape[1]
+    at = w0.shape[1] - third
+    tails = (w0[:, at:], w1[:, at:])
+    for rows, out in zip(chunks(ctx0.shape[0], outs[0].shape[0]), outs):
+        out[...] = (dot(ctx0[rows, :], tails[0], NT) + dot(ctx1[rows, :], tails[1], NT)).astype(BF16)
+
+
+def ffn_kernel(low, w0, w1, bias, act0, act1, slope0, slope1, *outs):
+    wide = bias.shape[1]
+    groups = ((w0, act0, slope0), (w1, act1, slope1))
+    for at, rows in enumerate(chunks(low.shape[0], 128)):
+        total = None
+        for g, (weight, act, slope) in enumerate(groups):
+            pre = dot(low[rows, :], weight[:, :wide], NN) + bias[g : g + 1, :]
+            cdf = 0.5 * (1.0 + lax.erf(pre * 0.7071067811865476))
+            slope[rows, :] = cdf + pre * (jnp.exp(-0.5 * pre * pre) * 0.3989422804014327)
+            active = (pre * cdf).astype(BF16)
+            act[rows, :] = active
+            part = dot(active, weight[:, wide:], NT)
+            total = part if total is None else total + part
+        inner = slice(at % 2 * 128, (at % 2 + 1) * 128)
+        outs[at // 2][inner, :] = total.astype(BF16)
+
+
+def feed_forward(low, weights, bias):
+    shape = (low.shape[0], bias.shape[1])
+    act0, act1, slope0, slope1, *partial = call(
+        ffn_kernel,
+        [(shape, BF16)] * 2 + [(shape, F32)] * 2 + thirds(low.shape),
+        (low, *weights, bias),
+        name="feed_forward",
+    )
+    return [(act0, slope0), (act1, slope1)], partial
+
+
+def add_rows(array):
+    return jnp.sum(array.astype(F32).reshape(-1, 8, array.shape[1]), axis=0)
+
+
+def ffn_back_kernel(low, w0, w1, slope0, slope1, pre0, pre1, sums):
+    wide = slope0.shape[1]
+    for g, (weight, slope, pre) in enumerate(((w0, slope0, pre0), (w1, slope1, pre1))):
+        total = None
+        for rows in chunks(low.shape[0]):
+            grad = (dot(low[rows, :], weight[:, wide:], NN) * slope[rows, :]).astype(BF16)
+            pre[rows, :] = grad
+            part = add_rows(grad)
+            total = part if total is None else total + part
+        sums[8 * g : 8 * (g + 1), :] = total
+
+
+def ffn_back_first(low, weights, slopes):
+    shape = slopes[0].shape
+    pre0, pre1, sums = call(
+        ffn_back_kernel,
+        [(shape, BF16)] * 2 + [((16, shape[1]), F32)],
+        (low, *weights, *slopes),
+        name="pre_grad",
+    )
+    return [pre0, pre1], sums
+
+
+def back_out_kernel(d0, d1, w0, w1, *outs):
+    wide = d0.shape[1]
+    for rows, out in zip(chunks(d0.shape[0], outs[0].shape[0]), outs):
+        out[...] = (dot(d0[rows, :], w0[:, :wide], NT) + dot(d1[rows, :], w1[:, :wide], NT)).astype(BF16)
+
+
+def qkv_back_kernel(d0, d1, w0, w1, *refs):
+    *outs, sums = refs
+    back_out_kernel(d0, d1, w0, w1, *outs)
+    for g, d in enumerate((d0, d1)):
+        total = None
+        for rows in chunks(d.shape[0]):
+            part = add_rows(d[rows, :])
+            total = part if total is None else total + part
+        sums[8 * g : 8 * (g + 1), :] = total
+
+
+def context_grad_kernel(low, w0, w1, out0, out1):
+    third = out0.shape[1]
+    at = w0.shape[1] - third
+    for weight, out in ((w0, out0), (w1, out1)):
+        tail = weight[:, at:]
+        for rows in chunks(low.shape[0]):
+            out[rows, :] = dot(low[rows, :], tail, NN).astype(BF16)
 
 
 def local(n_dp, *args):
@@ -454,7 +656,7 @@
         row_params,
     ) = args[:11]
     moments, seconds = args[11:18], args[18:25]
-    links = Links(n_dp)
+    links = Links(n_dp, attn_out.shape[1])
     at_x, core = links.at_x, links.core
     seq_len = inputs.shape[0] // word_count.shape[0]
     half = seq_len // 2
@@ -464,11 +666,14 @@
         whole = lax.dynamic_slice_in_dim(array, at_x * 2 * seq_len, seq_len)
         return jnp.concatenate([whole, lax.dynamic_slice_in_dim(array, seq_len + at_x * half, half)])
 
-    def all_rows(array):
-        low = array.astype(BF16)
+    def rows_first(low):
         part = low.shape[0] // 2
-        piece = links.swap_x(lax.dynamic_slice_in_dim(low, core * part, part))
-        twin = links.swap_core(piece)
+        return links.swap_as("rows_x", links.swap_x, lax.dynamic_slice_in_dim(low, core * part, part))
+
+    def rows_second(piece):
+        return links.swap_as("rows_core", links.swap_core, piece)
+
+    def all_rows(low, piece, twin):
         first = core == 0
         other = jnp.concatenate([jnp.where(first, piece, twin), jnp.where(first, twin, piece)])
         low, other = low.astype(F32), other.astype(F32)
@@ -482,27 +687,42 @@
             ]
         )
 
-    attn_w, ffn_w = [], []
-    for layer in range(LAYERS):
+    def packed_attn(layer):
         attn = [attn_in[layer, 0], attn_in[layer, 1], attn_in[layer, 2], attn_out[layer]]
-        attn_w.append(jnp.concatenate(attn, axis=1).astype(BF16)[None])
-        ffn_w.append(jnp.concatenate([ffn_up[layer], ffn_down[layer]], axis=1).astype(BF16)[None])
-    a0 = links.gather_bit(attn_w[0], 1)
-    a0, f0 = tie(a0, ffn_w[0])
-    f0 = links.gather_bit(f0, 1)
-    a0 = links.gather_rest(a0)
-    a0, f0, a1, f1 = tie(a0, f0, attn_w[1], ffn_w[1])
-    near = links.gather_near(a0)
-    f0 = links.gather_rest(f0)
-    a1 = links.gather_bit(a1, 1)
-    a0 = links.gather_far(a0, near)
-
-    bias_far = links.swap_x(jnp.concatenate([head_bias.reshape(-1), ffn_bias.reshape(-1)]))
+        return jnp.concatenate([a.astype(BF16) for a in attn], axis=1)[None]
+
+    def packed_ffn(layer):
+        return jnp.concatenate([ffn_up[layer].astype(BF16), ffn_down[layer].astype(BF16)], axis=1)[None]
+
+    z_one, z_rest = links.z_masks[:1], links.z_masks[1:]
+    join = jnp.concatenate
+
+    a0 = packed_attn(0)
+    a0_in = links.swap_as("attn0_z2", links.swap_z, a0, links.z_masks[0])
+    a0_in, f0, later = tie(a0_in, packed_ffn(0), join([packed_attn(1), packed_ffn(1)], axis=2))
+    a0 = join([a0, a0_in])
+    a0, a0_in = links.swap_as("attn0_z1", links.last_z, a0, z_rest)
+    f0_in = links.swap_as("ffn0_z2", links.swap_z, f0, links.z_masks[0])
+    a0_in, f0_in, later = tie(a0_in, f0_in, later)
+    a0, f0 = join([a0, a0_in]), join([f0, f0_in])
+    near = links.swap_as("attn0_near", links.swap_near, a0)
+    f0, f0_in = links.swap_as("ffn0_z1", links.last_z, f0, z_rest)
+    later_in = links.swap_as("layer1_z2", links.swap_z, later, links.z_masks[0])
+    biases = jnp.concatenate([head_bias.reshape(-1), ffn_bias.reshape(-1)])
+    near, biases = tie(near, biases)
+    two = jnp.stack([a0, near])
+    far_part = links.swap_as("attn0_far", links.swap_far, two)
+    bias_far = links.swap_as("biases", links.swap_x, biases)
+    far_part, bias_far, later_in = tie(far_part, bias_far, later_in)
+    later = join([later, later_in])
+    a0 = links.assemble(two, far_part)
     head_b = (head_bias, bias_far[: head_bias.size].reshape(head_bias.shape))
     ffn_b = (ffn_bias, bias_far[head_bias.size :].reshape(ffn_bias.shape))
     zeros = jnp.zeros((third,), F32)
-    qkv_b = [[jnp.concatenate([b[layer, 0], zeros, b[layer, 1]]) for b in head_b] for layer in range(LAYERS)]
-    scale = jnp.concatenate([jnp.full((third,), 0.125, F32), jnp.ones((2 * third,), F32)])
+    qkv_b = [
+        jnp.stack([jnp.concatenate([b[layer, 0], zeros, b[layer, 1]]) for b in head_b]) for layer in range(LAYERS)
+    ]
+    ffn_b = [jnp.stack([b[layer] for b in ffn_b]) for layer in range(LAYERS)]
 
     slots = jnp.arange(word_lengths.shape[1], dtype=jnp.int32)
     used = jnp.sum(jnp.where(slots[None, :] < word_count[:, None], word_lengths, 0), axis=1)
@@ -517,165 +737,202 @@
     qkv, far, ctx, lse = [None] * 2, [None] * 2, [None] * 2, [None] * 2
     weight_a, weight_f = [a0, None], [None, None]
 
-    def qkv_of(layer):
-        return [
-            project(in_low[layer], weight_a[layer][g][:, : 3 * third], qkv_b[layer][g], scale) for g in range(2)
-        ]
-
     def out_part(layer):
-        return sum(dot(ctx[layer][g], weight_a[layer][g][:, 3 * third :], NT) for g in range(2))
+        return call(out_kernel, thirds(hidden.shape), (*ctx[layer], *weight_a[layer]), name="attention_out")
 
     norms = [None] * 2
     ffn_parts = [None] * 2
 
-    qkv[0] = qkv_of(0)
-    far[0] = jnp.concatenate(
-        [
-            (dot(low_other, a0[g][:, third : 3 * third], NN) + qkv_b[0][g][third:]).astype(BF16)
-            for g in range(2)
-        ],
-        axis=1,
-    )
+    row_parts = [
+        [jnp.stack([row_params[i, k] for k in ks]) for ks in ((0, 2, 3), (1, 4, 5))] for i in range(LAYERS)
+    ]
+    row_parts = [
+        [jnp.stack([row_params[i, k] for k in ks]) for ks in ((0, 2, 3), (1, 4, 5))] for i in range(LAYERS)
+    ]
+    qkv[0], far[0] = project(in_low[0], a0, qkv_b[0], low_other)
+    q0, q1, far[0], f0_in, later = tie(*qkv[0], far[0], f0_in, later)
+    f0 = join([f0, f0_in])
+    near = links.swap_as("ffn0_near", links.swap_near, f0)
+    later, later_in = links.swap_as("layer1_z1", links.last_z, later, z_rest)
+    qkv[0] = [q0, q1]
     ctx[0], lse[0] = attend_full(limits, qkv[0])
     ctx[0], lse[0] = attend_half(limits, qkv[0], far[0], ctx[0], lse[0], 0)
-    c0, c1, f0, a1 = tie(*ctx[0], f0, a1)
+    c0, c1, near = tie(*ctx[0], near)
     ctx[0] = (c0, c1)
-    near = links.gather_near(f0)
-    a1 = links.gather_rest(a1)
-    f1 = links.gather_bit(f1, 1)
-    attended = both_cores(links, out_part(0)) + row_params[0, 0]
-    normed, scaled_one, inv_one = norm_parts(hidden + attended, row_params[0, 2], row_params[0, 3])
-    normed, near, a1, f1 = tie(normed, near, a1, f1)
-    f0 = links.gather_far(f0, near)
-    near = links.gather_near(a1)
-    f1 = links.gather_rest(f1)
+    f0two = jnp.stack([f0, near])
+    f0far = links.swap_as("ffn0_far", links.swap_far, f0two)
+    normed, normed_low, scaled_one, inv_one = add_norm(both_cores(links, out_part(0)), hidden, row_parts[0][0])
+    normed_low, later_in = tie(normed_low, later_in)
+    later = join([later, later_in])
+    a1, f1 = later[:, :, : 4 * third], later[:, :, 4 * third :]
+    near = links.swap_as("attn1_near", links.swap_near, a1)
+    normed_low, f0far = tie(normed_low, f0far)
+    f0 = links.assemble(f0two, f0far)
     weight_f[0] = f0
-    normed_low = normed.astype(BF16)
-    ffn_parts[0] = up_part(normed_low, f0, [b[0] for b in ffn_b])
-    act, near, f1 = tie(ffn_parts[0][0][0], near, f1)
-    ffn_parts[0][0] = (act, ffn_parts[0][0][1])
-    a1 = links.gather_far(a1, near)
+    ffn_parts[0], partial = feed_forward(normed_low, f0, ffn_b[0])
+    *partial, near, f1 = tie(*partial, near, f1)
+    a1two = jnp.stack([a1, near])
+    a1far = links.swap_as("attn1_far", links.swap_far, a1two)
+    near = links.swap_as("ffn1_near", links.swap_near, f1)
+    fed = both_cores(links, partial)
+    hidden, low, scaled_two, inv_two = add_norm(fed, normed, row_parts[0][1])
+    norms[0] = (normed_low, scaled_one, inv_one, scaled_two, inv_two)
+
+    low, a1far = tie(low, a1far)
+    a1 = links.assemble(a1two, a1far)
     weight_a[1] = a1
-    near = links.gather_near(f1)
-    fed = both_cores(links, down_part(ffn_parts[0], f0)) + row_params[0, 1]
-    hidden, scaled_two, inv_two = norm_parts(normed + fed, row_params[0, 4], row_params[0, 5])
-    norms[0] = (normed_low, scaled_one, inv_one, scaled_two, inv_two)
-
-    in_low[1] = hidden.astype(BF16)
-    qkv[1] = qkv_of(1)
-    q0, q1, near = tie(*qkv[1], near)
-    qkv[1] = [q0, q1]
-    f1 = links.gather_far(f1, near)
+    in_low[1] = low
+    qkv[1], sent = project(low, a1, qkv_b[1])
+    far[1] = links.swap_as("keys_values", links.swap_x, sent)
+    ctx[1], lse[1] = attend_full(limits, qkv[1])
+    c0, c1, near, far[1] = tie(*ctx[1], near, far[1])
+    f1two = jnp.stack([f1, near])
+    f1far = links.swap_as("ffn1_far", links.swap_far, f1two)
+    ctx[1], lse[1] = attend_half(limits, qkv[1], far[1], (c0, c1), lse[1], 1)
+    fed = both_cores(links, out_part(1))
+    normed, normed_low, scaled_one, inv_one = add_norm(fed, hidden, row_parts[1][0])
+    normed_low, f1far = tie(normed_low, f1far)
+    f1 = links.assemble(f1two, f1far)
     weight_f[1] = f1
-    far[1] = links.swap_x(jnp.concatenate([q0[seq_len:, third:], q1[seq_len:, third:]], axis=1))
-    ctx[1], lse[1] = attend_full(limits, qkv[1])
-    ctx[1], lse[1] = attend_half(limits, qkv[1], far[1], ctx[1], lse[1], 1)
-    attended = both_cores(links, out_part(1)) + row_params[1, 0]
-    normed, scaled_one, inv_one = norm_parts(hidden + attended, row_params[1, 2], row_params[1, 3])
-    normed_low = normed.astype(BF16)
-    ffn_parts[1] = up_part(normed_low, f1, [b[1] for b in ffn_b])
-    fed = both_cores(links, down_part(ffn_parts[1], f1)) + row_params[1, 1]
-    hidden, scaled_two, inv_two = norm_parts(normed + fed, row_params[1, 4], row_params[1, 5])
+    ffn_parts[1], partial = feed_forward(normed_low, f1, ffn_b[1])
+    fed = both_cores(links, partial)
+    hidden, low, scaled_two, inv_two = add_norm(fed, normed, row_parts[1][1])
     norms[1] = (normed_low, scaled_one, inv_one, scaled_two, inv_two)
-    encoded = all_rows(hidden)
-
-    def ffn_back(layer, grad_output):
+    state = {}
+
+    def ffn_back(layer, grad_parts, middle):
         normed_low, _, _, scaled_two, inv_two = norms[layer]
-        upper = norm_back(grad_output, scaled_two, inv_two, row_params[layer, 4])
-        upper_low = upper.astype(BF16)
-        grad_pre = [
-            (dot(upper_low, weight_f[layer][g][:, wide:], NN) * ffn_parts[layer][g][1]).astype(BF16) for g in range(2)
-        ]
-        partial = sum(dot(grad_pre[g], weight_f[layer][g][:, :wide], NT) for g in range(2))
-        grad_normed = upper + both_cores(links, partial)
-        pieces = weight_grads(
+        upper, upper_low, row_sums = norm_back(grad_parts, scaled_two, inv_two, row_params[layer, 4:5])
+        slopes = [part[1] for part in ffn_parts[layer]]
+        grad_pre, pre_sums = ffn_back_first(upper_low, weight_f[layer], slopes)
+        grad_pre = middle(grad_pre)
+        keep, give = weight_grads(
             links,
             (normed_low, upper_low),
             [(grad_pre[g], ffn_parts[layer][g][0]) for g in range(2)],
         )
-        vectors = (
-            jnp.sum(upper, axis=0),
-            jnp.sum(grad_output * scaled_two, axis=0),
-            jnp.sum(grad_output, axis=0),
-            [jnp.sum(p.astype(F32), axis=0) for p in grad_pre],
+        g0, g1, give = tie(*grad_pre, give)
+        grad_pre = [g0, g1]
+        came = links.swap_as("ffn%d_grad_far" % layer, links.swap_far, give)
+        partial = call(back_out_kernel, thirds(upper.shape), (*grad_pre, *weight_f[layer]), name="up_back")
+        vectors = (row_sums, pre_sums)
+        return upper, partial, (keep, came), vectors
+
+    def attn_back(layer, grad_parts, during):
+        _, scaled_one, inv_one, _, _ = norms[layer]
+        lower, lower_low, row_sums = norm_back(grad_parts, scaled_one, inv_one, row_params[layer, 2:3])
+        weight = weight_a[layer]
+        shape = (lower.shape[0], third)
+        dctx = call(context_grad_kernel, [(shape, BF16)] * 2, (lower_low, *weight), name="context_grad")
+        dq, own, sent = attend_half_back(limits, qkv[layer], far[layer], dctx, lse[layer], layer)
+        d0, d1, sent = tie(*dctx, sent)
+        came = links.swap_as("keys_values_grad", links.swap_x, sent)
+        dqkv = attend_full_back(limits, qkv[layer], (d0, d1), lse[layer])
+        dqkv, came = during(dqkv, came)
+        dqkv = fill_half(dqkv, dq, own, came)
+        keep, give = weight_grads(links, (in_low[layer], lower_low), [(dqkv[g], ctx[layer][g]) for g in range(2)])
+        d0, d1, give = tie(*dqkv, give)
+        dqkv = [d0, d1]
+        came = links.swap_as("attn%d_grad_far" % layer, links.swap_far, give)
+        *partial, sums = call(
+            qkv_back_kernel,
+            thirds(lower.shape) + [((16, 3 * third), F32)],
+            (*dqkv, *weight),
+            name="qkv_back",
         )
-        return grad_normed, pieces, vectors
-
-    def attn_back(layer, grad_normed, hook):
-        _, scaled_one, inv_one, _, _ = norms[layer]
-        lower = norm_back(grad_normed, scaled_one, inv_one, row_params[layer, 2])
-        lower_low = lower.astype(BF16)
-        weight = weight_a[layer]
-        dctx = [dot(lower_low, weight[g][:, 3 * third :], NN).astype(BF16) for g in range(2)]
-        swapped = layer
-        dq, own, sent = attend_half_back(limits, qkv[layer], far[layer], dctx, lse[layer], swapped)
-        came = links.swap_x(sent)
-        dqkv = attend_full_back(limits, qkv[layer], dctx, lse[layer])
-        dqkv = fill_half(dqkv, dq, own, came)
-        dqkv = hook(dqkv)
-        partial = sum(dot(dqkv[g], weight[g][:, : 3 * third], NT) for g in range(2))
-        grad_hidden = lower + both_cores(links, partial)
-        pieces = weight_grads(links, (in_low[layer], lower_low), [(dqkv[g], ctx[layer][g]) for g in range(2)])
-        sums = [jnp.sum(d.astype(F32), axis=0) for d in dqkv]
-        vectors = (
-            jnp.sum(lower, axis=0),
-            jnp.sum(grad_normed * scaled_one, axis=0),
-            jnp.sum(grad_normed, axis=0),
-            [jnp.concatenate([s[:third], s[2 * third :]]) for s in sums],
-        )
-        return grad_hidden, pieces, vectors
-
-    grad_hidden = own_rows(cotangent) * row_mask
+        vectors = (row_sums, sums)
+        return lower, partial, (keep, came), vectors
+
+    def first_sum(keep, came):
+        return keep.astype(F32) + came.astype(F32)
+
+    def near_swap(name, parts):
+        return parts[0], links.swap_as(name, links.swap_near, parts[1].astype(BF16))
+
+    def add(keep, came):
+        return keep + came.astype(F32)
+
+    z_top, z_last = links.z_masks[:0:-1], z_one
     vectors = [None, None]
-    grad_normed, pieces, fvec = ffn_back(1, grad_hidden)
-    state = {}
-
-    def hook1(dqkv):
-        f_keep, f_give = links.scatter_first(*pieces)
-        d0, d1, f_keep, f_give = tie(*dqkv, f_keep, f_give)
-        state["f1"] = links.scatter_second(f_keep, f_give)
-        return [d0, d1]
-
-    grad_hidden, a_pieces, avec = attn_back(1, grad_normed, hook1)
+    grad_top = own_rows(cotangent) * row_mask
+    upper, partial, (f1k, f1c), fvec = ffn_back(1, (grad_top,), lambda g: g)
+    fed = both_cores(links, partial)
+
+    def during1(dqkv, kv):
+        d0, d1, kv, came = tie(*dqkv, kv, f1c)
+        state["f1"] = near_swap("ffn1_grad_near", first_sum(f1k, came))
+        return [d0, d1], kv
+
+    lower, partial, (a1k, a1c), avec = attn_back(1, (upper, *fed), during1)
     vectors[1] = (fvec, avec)
-    grad_hidden, f1s = tie(grad_hidden, state["f1"])
-    a_keep, a_give = links.scatter_first(*a_pieces)
-    grad_normed, pieces, fvec = ffn_back(0, grad_hidden)
-    f1s = links.scatter_bit(f1s, links.bits - 1)
-    grad_normed, a_keep, a_give, f1s = tie(grad_normed, a_keep, a_give, f1s)
-    a1s = links.scatter_second(a_keep, a_give)
-    f1s = links.scatter_rest_from(f1s, links.bits - 2)
-
-    def hook0(dqkv):
-        f_keep, f_give = links.scatter_first(*pieces)
-        d0, d1, f_keep, f_give, a, f = tie(*dqkv, f_keep, f_give, a1s, f1s)
-        state["f0"] = links.scatter_second(f_keep, f_give)
-        state["a1"], state["f1"] = a, f
-        return [d0, d1]
-
-    grad_hidden, a_pieces, avec = attn_back(0, grad_normed, hook0)
+    fed = both_cores(links, partial)
+
+    def middle0(grad_pre):
+        g0, g1, came = tie(*grad_pre, state["f1"][1])
+        state["f1"] = links.swap_as("ffn1_grad_z1", links.scatter_z, add(state["f1"][0], came), z_top)
+        return [g0, g1]
+
+    upper, partial, (f0k, f0c), fvec = ffn_back(0, (lower, *fed), middle0)
+    fed = both_cores(links, partial)
+
+    def during0(dqkv, kv):
+        d0, d1, came = tie(*dqkv, a1c)
+        state["a1"] = near_swap("attn1_grad_near", first_sum(a1k, came))
+        d0, d1, f1_in, kv, came = tie(d0, d1, state["f1"][1], kv, f0c)
+        state["f1"] = links.swap_as("ffn1_grad_z2", links.scatter_z, add(state["f1"][0], f1_in), z_last)
+        state["f0"] = near_swap("ffn0_grad_near", first_sum(f0k, came))
+        return [d0, d1], kv
+
+    lower, partial, (a0k, a0c), avec = attn_back(0, (upper, *fed), during0)
     vectors[0] = (fvec, avec)
-    a1s = links.scatter_rest(state["a1"])
-    f1s = state["f1"]
-    a_keep, a_give = links.scatter_first(*a_pieces)
-    f0s = links.scatter_rest(state["f0"])
-    a0s = links.scatter_rest(links.scatter_second(a_keep, a_give))
-    input_grad = all_rows(grad_hidden)
-
-    own = jnp.concatenate([v for layer in vectors for v in (layer[1][3][0], layer[0][3][0])])
-    other = jnp.concatenate([v for layer in vectors for v in (layer[1][3][1], layer[0][3][1])])
-    rows = jnp.concatenate(
-        [
-            r
-            for fv, av in vectors
-            for r in (av[0], fv[0], av[1], av[2], fv[1], fv[2])
-        ]
-    )
-    came = links.swap_x(jnp.concatenate([other, rows]).reshape(-1, 128)).reshape(-1)
-    sums = (jnp.concatenate([own, rows]) + came).reshape(-1, 128)
-    for bit in range(links.bits):
-        sums = sums + links.swap(sums, 4 << bit)
-    sums = sums.reshape(-1)
+    *partial, came = tie(*partial, state["a1"][1])
+    a1s = links.swap_as("attn1_grad_z1", links.scatter_z, add(state["a1"][0], came), z_top)
+    fed = both_cores(links, partial)
+    grad_hidden = call(final_sum_kernel, [(lower.shape, BF16)], (lower, *fed), name="input_grad")[0]
+
+    own, other = [], []
+    for f, a in vectors:
+        for g, into in enumerate((own, other)):
+            heads = jnp.sum(a[1][8 * g : 8 * (g + 1)], axis=0)
+            into += [heads[:third], heads[2 * third :], jnp.sum(f[1][8 * g : 8 * (g + 1)], axis=0)]
+    own, other = jnp.concatenate(own), jnp.concatenate(other)
+    rows = []
+    for f, a in vectors:
+        upper_sums = jnp.sum(f[0].reshape(3, 8, -1), axis=1)
+        lower_sums = jnp.sum(a[0].reshape(3, 8, -1), axis=1)
+        rows += [lower_sums[0], upper_sums[0], lower_sums[1], lower_sums[2], upper_sums[1], upper_sums[2]]
+    rows = jnp.concatenate(rows)
+    vector, given = (jnp.concatenate([part, rows]).reshape(-1, 128) for part in (own, other))
+
+    grad_hidden, given, f1_in, f0_in = tie(grad_hidden, given, state["f1"][1], state["f0"][1])
+    f1s = add(state["f1"][0], f1_in)[0]
+    f0s = links.swap_as("ffn0_grad_z1", links.scatter_z, add(state["f0"][0], f0_in), z_top)
+    v_in = links.swap_as("vectors_x", links.swap_x, given)
+    came, v_in, grad_hidden, low = tie(a0c, v_in, grad_hidden, low)
+    a0s = near_swap("attn0_grad_near", first_sum(a0k, came))
+    vector = vector + v_in
+    v_in = links.swap_as("vectors_y", links.swap, vector, 4)
+    piece = rows_first(jnp.stack([grad_hidden, low], axis=1))
+    came, v_in, a1_in = tie(a0s[1], v_in, a1s[1])
+    a0s = links.swap_as("attn0_grad_z1", links.scatter_z, add(a0s[0], came), z_top)
+    a1s = links.swap_as("attn1_grad_z2", links.scatter_z, add(a1s[0], a1_in), z_last)
+    vector = vector + v_in
+    v_in = links.swap_as("vectors_z", links.swap_z, vector, links.z_masks[0])
+    piece, v_in, f0_in = tie(piece, v_in, f0s[1])
+    twin = rows_second(piece)
+    vector = vector + v_in
+    f0s = links.swap_as("ffn0_grad_z2", links.scatter_z, add(f0s[0], f0_in), z_last)
+    for mask in links.z_masks[1:]:
+        vector = vector + links.swap_as("vectors_z", links.swap_z, vector, mask)
+    twin, came, a1_in = tie(twin, a0s[1], a1s[1])
+    a0s = links.swap_as("attn0_grad_z2", links.scatter_z, add(a0s[0], came), z_last)
+    a1s = add(a1s[0], a1_in)[0]
+    input_grad = all_rows(grad_hidden, piece[:, 0], twin[:, 0])
+    encoded = all_rows(low, piece[:, 1], twin[:, 1])
+    f0s = add(*f0s)[0]
+    a0s = add(*a0s)[0]
+
+    sums = vector.reshape(-1)
     size = own.shape[0] // LAYERS
     head_grad = jnp.stack([sums[i * size : i * size + 2 * third].reshape(2, third) for i in range(LAYERS)])
     ffn_grad = jnp.stack([sums[i * size + 2 * third : (i + 1) * size] for i in range(LAYERS)])

time: 516 us -> 468 us (0.907); the launches traced: 506 us -> 464 us
  waiting for transfers between devices: 259 us -> 153 us
  Pallas kernels: 60.3 us -> 123 us
  local copies, waits for them, and re-layouts: 29.7 us -> 80.3 us
  matrix products: 49.9 us -> 0 us
  starting transfers between devices: 44.3 us -> 58.7 us
  other arithmetic: 56.7 us -> 42.7 us
    ppermute x52 -> x64, waiting for transfers between devices: 259 us -> 153 us  [swap(): return lax.ppermute(array, AXES, pairs)]
    pallas_call x10 -> x37, Pallas kernels: 52.3 us -> 115 us  [call(): pl.pallas_call(kernel, out_shape=[jax.ShapeDtypeStruct(s, d) for s, d in...]
    dot_general x34 -> x0, matrix products: 49.9 us -> none  [dot(): return lax.dot_general(a, b, (dims, ((), ())), preferred_element_type=F32)]
    unnamed x227 -> x320, local copies, waits for them, and re-layouts: 19.8 us -> 51.2 us
    reduce_sum x20 -> x8, other arithmetic: 18.6 us -> 2.91 us  [the longest x2 1.22 us: local(): jnp.sum(f[1][8 * g:8 * (g + 1)], axis=0)]
    ppermute x52 -> x64, starting transfers between devices: 44.3 us -> 58.7 us  [swap(): return lax.ppermute(array, AXES, pairs)]
    slice x12 -> x21, local copies, waits for them, and re-layouts: 1.05 us -> 10.1 us  [the longest x8 3.86 us: scatter_z(): return (parts[:half], self.swap_z(parts[half:].astype(BF16), masks[-1]))]
    add x18 -> x20, other arithmetic: 5.51 us -> 13.4 us  [the longest x12 8.96 us: add(): return keep + came.astype(F32)]
  transfers between devices with their start and end apart: 52 -> 64, of which waited for: 29 -> 31; matrix products, arithmetic and copies ran while one was open for 17% -> 15% of each run, Pallas kernels for 11% -> 22%
where the time goes in v3:
time: 468 us; the launch traced here: 464 us
  waiting for transfers between devices  153 us (33%)
  Pallas kernels  123 us (26%)
  local copies, waits for them, and re-layouts  80.3 us (17%)
  starting transfers between devices  58.7 us (13%)
  other arithmetic  42.7 us (9%)
  between operations  5.68 us (1%)
    ppermute x64, waiting for transfers between devices, swap(): return lax.ppermute(array, AXES, pairs)  153 us
    pallas_call x37, Pallas kernels, call(): pl.pallas_call(kernel, out_shape=[jax.ShapeDtypeStruct(s, d) for s, d in...  115 us
    ppermute x64, starting transfers between devices, swap(): return lax.ppermute(array, AXES, pairs)  58.7 us
    unnamed x320, local copies, waits for them, and re-layouts  51.2 us
  transfers between devices with their start and end apart: 64, of which 31 were waited for; matrix products, arithmetic and copies ran while one was open for 15% of the time, Pallas kernels for 22%

profile of v3, /device:TPU:0, one launch (start us, length us, event | category | flops | bytes accessed | tf_op | source)
XLA Modules:
  0.0 463.9 jit_solution(4940531482299646291)
XLA Ops:
  3.0 4.1 collective-permute-start
  8.2 5.8 %collective-permute-done = bf16[1,96,768]{2,1,0:T(8,128)(2,1)S(1)} collective-permute-done((bf16[1,96,768]{2,1,0:T(8,128)(2,1)S(1)}, bf16[1,96,768]{2,1,0:T(8,128)(2,1)S(1)}, u32[]{:S(2)}, u32[]{:S(2)}) %collective-permute-start) | collective-permute-done | bytes 147488 | tf_op jit(solution)/shard_map/attn0_z2/ppermute | solution.py:56
  18.5 10.0 %collective-permute-done.1 = bf16[2,96,768]{2,1,0:T(8,128)(2,1)S(1)} collective-permute-done((bf16[2,96,768]{2,1,0:T(8,128)(2,1)S(1)}, bf16[2,96,768]{2,1,0:T(8,128)(2,1)S(1)}, u32[]{:S(2)}, u32[]{:S(2)}) %collective-permute-start.1) | collective-permute-done | bytes 294944 | tf_op jit(solution)/shard_map/attn0_z1/ppermute | solution.py:56
  51.3 11.6 %collective-permute-done.6 = bf16[1,96,2304]{2,1,0:T(8,128)(2,1)S(1)} collective-permute-done((bf16[1,96,2304]{2,1,0:T(8,128)(2,1)S(1)}, bf16[1,96,2304]{2,1,0:T(8,128)(2,1)S(1)}, u32[]{:S(2)}, u32[]{:S(2)}) %collective-permute-start.6) | collective-permute-done | bytes 442400 | tf_op jit(solution)/shard_map/layer1_z2/ppermute | solution.py:56
  75.4 6.6 %attend_full.2 = (bf16[768,192]{1,0:T(8,128)(2,1)S(1)}, bf16[768,192]{1,0:T(8,128)(2,1)S(1)}, f32[6,768]{1,0:T(8,128)S(1)}) custom-call(s32[3]{0:T(128)S(1)} %get-tuple-element.629.limits, bf16[768,576]{1,0:T(8,128)(2,1)S(1)} %get-tuple-element.254.qkv0, bf16[768,576]{1,0:T(8,128)(2,1)S(1)} %get-tuple-element.255.qkv1), custom_call_target="tpu_custom_call" | custom-call | flops 1 | bytes 1 | tf_op jit(solution)/shard_map/attend_full/pallas_call | solution.py:305
  85.9 6.4 %collective-permute-done.8 = bf16[4,96,1536]{2,1,0:T(8,128)(2,1)S(1)} collective-permute-done((bf16[4,96,1536]{2,1,0:T(8,128)(2,1)S(1)}, bf16[4,96,1536]{2,1,0:T(8,128)(2,1)S(1)}, u32[]{:S(2)}, u32[]{:S(2)}) %collective-permute-start.8) | collective-permute-done | bytes 1179680 | tf_op jit(solution)/shard_map/ffn0_near/ppermute | solution.py:56
  101.4 9.7 %collective-permute-done.12 = bf16[2,96,2304]{2,1,0:T(8,128)(2,1)S(1)} collective-permute-done((bf16[2,96,2304]{2,1,0:T(8,128)(2,1)S(1)}, bf16[2,96,2304]{2,1,0:T(8,128)(2,1)S(1)}, u32[]{:S(2)}, u32[]{:S(2)}) %collective-permute-start.12) | collective-permute-done | bytes 884768 | tf_op jit(solution)/shard_map/layer1_z1/ppermute | solution.py:56
  113.1 14.7 %collective-permute-done.13.far = bf16[2,4,96,1536]{3,2,1,0:T(8,128)(2,1)S(1)} collective-permute-done((bf16[2,4,96,1536]{3,2,1,0:T(8,128)(2,1)S(1)}, bf16[2,4,96,1536]{3,2,1,0:T(8,128)(2,1)S(1)}, u32[]{:S(2)}, u32[]{:S(2)}) %collective-permute-start.13) | collective-permute-done | bytes 2359328 | tf_op jit(solution)/shard_map/ffn0_far/ppermute | solution.py:56
  128.9 6.5 %feed_forward.2 = (bf16[768,768]{1,0:T(8,128)(2,1)S(1)}, bf16[768,768]{1,0:T(8,128)(2,1)S(1)}, f32[768,768]{1,0:T(8,128)S(1)}, f32[768,768]{1,0:T(8,128)S(1)}, b...) custom-call(bf16[768,768]{1,0:T(8,128)(2,1)S(1)} %get-tuple-element.272.low.refs_0_, ...), custom_call_target="tpu_custom_call" | custom-call | flops 1 | bytes 1 | tf_op jit(solution)/shard_map/feed_forward/pallas_call | solution.py:305
  145.1 15.2 %collective-permute-done.18.far = bf16[2,4,96,768]{3,2,1,0:T(8,128)(2,1)S(1)} collective-permute-done((bf16[2,4,96,768]{3,2,1,0:T(8,128)(2,1)S(1)}, bf16[2,4,96,768]{3,2,1,0:T(8,128)(2,1)S(1)}, u32[]{:S(2)}, u32[]{:S(2)}) %collective-permute-start.18) | collective-permute-done | bytes 1179680 | tf_op jit(solution)/shard_map/attn1_far/ppermute | solution.py:56
  164.9 6.6 %attend_full.3 = (bf16[768,192]{1,0:T(8,128)(2,1)S(1)}, bf16[768,192]{1,0:T(8,128)(2,1)S(1)}, f32[6,768]{1,0:T(8,128)S(1)}) custom-call(s32[3]{0:T(128)S(1)} %get-tuple-element.629.limits, bf16[768,576]{1,0:T(8,128)(2,1)S(1)} %get-tuple-element.290.qkv0, bf16[768,576]{1,0:T(8,128)(2,1)S(1)} %get-tuple-element.291.qkv1), custom_call_target="tpu_custom_call" | custom-call | flops 1 | bytes 1 | tf_op jit(solution)/shard_map/attend_full/pallas_call | solution.py:305
  184.9 15.9 %collective-permute-done.24.far = bf16[2,4,96,1536]{3,2,1,0:T(8,128)(2,1)S(1)} collective-permute-done((bf16[2,4,96,1536]{3,2,1,0:T(8,128)(2,1)S(1)}, bf16[2,4,96,1536]{3,2,1,0:T(8,128)(2,1)S(1)}, u32[]{:S(2)}, u32[]{:S(2)}) %collective-permute-start.24) | collective-permute-done | bytes 2359328 | tf_op jit(solution)/shard_map/ffn1_far/ppermute | solution.py:56
  201.8 6.4 %feed_forward.3 = (bf16[768,768]{1,0:T(8,128)(2,1)S(1)}, bf16[768,768]{1,0:T(8,128)(2,1)S(1)}, f32[768,768]{1,0:T(8,128)S(1)}, f32[768,768]{1,0:T(8,128)S(1)}, b...) custom-call(bf16[768,768]{1,0:T(8,128)(2,1)S(1)} %get-tuple-element.308.low.refs_0_, ...), custom_call_target="tpu_custom_call" | custom-call | flops 1 | bytes 1 | tf_op jit(solution)/shard_map/feed_forward/pallas_call | solution.py:305
  214.8 4.0 add_norm.7
  226.7 4.9 %weight_grads.4 = (bf16[2,4,96,1536]{3,2,1,0:T(8,128)(2,1)S(1)}, bf16[2,4,96,1536]{3,2,1,0:T(8,128)(2,1)S(1)}) custom-call(s32[3]{0:T(128)S(1)} %get-tuple-element.630.places, bf16[768,768]{1,0:T(8,128)(2,1)S(1)} %get-tuple-element.308.low.refs_0_, bf16[768,768]{1,0:T(8,128)(2,1)S(1)} %get-tuple-element.319.low.refs_1_, ...), custom_call_target="tpu_custom_call" | custom-call | flops 1 | bytes 1 | tf_op jit(solution)/shard_map/weight_grads/pallas_call | solution.py:305
  248.3 6.9 %attend_full_back.2 = (bf16[768,576]{1,0:T(8,128)(2,1)S(1)}, bf16[768,576]{1,0:T(8,128)(2,1)S(1)}) custom-call(s32[3]{0:T(128)S(1)} %get-tuple-element.629.limits, bf16[768,576]{1,0:T(8,128)(2,1)S(1)} %get-tuple-element.290.qkv0, bf16[768,576]{1,0:T(8,128)(2,1)S(1)} %get-tuple-element.291.qkv1, bf16[768,192]{1,0:T(8,128)(2,1)S(1)} %get-tuple-element.343.dctx0, ...), custom_call_target="tpu_custom_call" | custom-call | flops 1 | bytes 1 | tf_op jit(solution)/shard_map/attend_full_back/pallas_call | solution.py:305
  255.2 16.9 %collective-permute-done.31.came = bf16[256,768]{1,0:T(8,128)(2,1)S(1)} collective-permute-done((bf16[256,768]{1,0:T(8,128)(2,1)S(1)}, bf16[256,768]{1,0:T(8,128)(2,1)S(1)}, u32[]{:S(2)}, u32[]{:S(2)}) %collective-permute-start.31) | collective-permute-done | bytes 393248 | tf_op jit(solution)/shard_map/keys_values_grad/ppermute | solution.py:56
  289.3 4.2 weight_grads.5
  304.6 5.1 %weight_grads.6 = (bf16[2,4,96,1536]{3,2,1,0:T(8,128)(2,1)S(1)}, bf16[2,4,96,1536]{3,2,1,0:T(8,128)(2,1)S(1)}) custom-call(s32[3]{0:T(128)S(1)} %get-tuple-element.630.places, bf16[768,768]{1,0:T(8,128)(2,1)S(1)} %copy-done.27, bf16[768,768]{1,0:T(8,128)(2,1)S(1)} %get-tuple-element.363.low.refs_1_, bf16[768,768]{1,0:T(8,128)(2,1)S(1)} %get-tuple-element.375.refs_2_.d0, ...), custom_call_target="tpu_custom_call" | custom-call | flops 1 | bytes 1 | tf_op jit(solution)/shard_map/weight_grads/pallas_call | solution.py:305
  328.0 6.9 %attend_full_back.3 = (bf16[768,576]{1,0:T(8,128)(2,1)S(1)}, bf16[768,576]{1,0:T(8,128)(2,1)S(1)}) custom-call(s32[3]{0:T(128)S(1)} %get-tuple-element.629.limits, bf16[768,576]{1,0:T(8,128)(2,1)S(1)} %copy-done.9, bf16[768,576]{1,0:T(8,128)(2,1)S(1)} %copy-done.11, bf16[768,192]{1,0:T(8,128)(2,1)S(1)} %get-tuple-element.390.dctx0, ...), custom_call_target="tpu_custom_call" | custom-call | flops 1 | bytes 1 | tf_op jit(solution)/shard_map/attend_full_back/pallas_call | solution.py:305
  338.5 11.6 %collective-permute-done.42.came = bf16[256,768]{1,0:T(8,128)(2,1)S(1)} collective-permute-done((bf16[256,768]{1,0:T(8,128)(2,1)S(1)}, bf16[256,768]{1,0:T(8,128)(2,1)S(1)}, u32[]{:S(2)}, u32[]{:S(2)}) %collective-permute-start.42) | collective-permute-done | bytes 393248 | tf_op jit(solution)/shard_map/keys_values_grad/ppermute | solution.py:56
  356.6 4.9 %weight_grads.7 = (bf16[2,4,96,768]{3,2,1,0:T(8,128)(2,1)S(1)}, bf16[2,4,96,768]{3,2,1,0:T(8,128)(2,1)}) custom-call(s32[3]{0:T(128)S(1)} %get-tuple-element.630.places, bf16[768,768]{1,0:T(8,128)(2,1)S(1)} %copy-done.13, bf16[768,768]{1,0:T(8,128)(2,1)S(1)} %get-tuple-element.382.low.refs_1_, bf16[768,576]{1,0:T(8,128)(2,1)S(1)} %get-tuple-element.408.refs_2_.d0, ...), custom_call_target="tpu_custom_call" | custom-call | flops 1 | bytes 1 | tf_op jit(solution)/shard_map/weight_grads/pallas_call | solution.py:305
  373.5 6.4 %collective-permute-start.55 = (bf16[2,96,768]{2,1,0:T(8,128)(2,1)}, bf16[2,96,768]{2,1,0:T(8,128)(2,1)S(1)}, u32[]{:S(2)}, u32[]{:S(2)}) collective-permute-start(bf16[2,96,768]{2,1,0:T(8,128)(2,1)} %slice.756), channel_id=1, source_target_pairs={{0,8},{1,9},{2,10},{3,11},{4,12},{5,13},{6,14},{7,15},{8,0},{9,1},... | collective-permute-start | bytes 884744 | tf_op jit(solution)/shard_map/attn1_grad_z1/ppermute | solution.py:56
  407.1 12.8 %collective-permute-done.52 = bf16[384,2,768]{2,0,1:T(8,128)(2,1)} collective-permute-done((bf16[384,2,768]{2,0,1:T(8,128)(2,1)S(1)}, bf16[384,2,768]{2,0,1:T(8,128)(2,1)}, u32[]{:S(2)}, u32[]{:S(2)}) %collective-permute-start.52) | collective-permute-done | bytes 1179680 | tf_op jit(solution)/shard_map/rows_x/ppermute | solution.py:56
  (605 shorter events, 253.8 us)
Async XLA Ops:
  44.1 18.7 %collective-permute-start.4 = (bf16[2,4,96,768]{3,2,1,0:T(8,128)(2,1)S(1)}, bf16[2,4,96,768]{3,2,1,0:T(8,128)(2,1)S(1)}, u32[]{:S(2)}, u32[]{:S(2)}) collective-permute-start(bf16[2,4,96,768]{3,2,1,0:T(8,128)(2,1)S(1)} %pad_maximum_fusion.5.two), channel_id=1, source_target_pairs={{0,2},{1,5},{2,0},{3,7},{4,6},{5,1},{6,4},{7,3},{8,10},{9,13},{10,... | collective-permute-start | bytes 3538952 | tf_op jit(solution)/shard_map/attn0_far/ppermute | solution.py:56
  49.5 22.2 %collective-permute-start.7 = (bf16[2,96,1536]{2,1,0:T(8,128)(2,1)}, bf16[2,96,1536]{2,1,0:T(8,128)(2,1)}, u32[]{:S(2)}, u32[]{:S(2)}) collective-permute-start(bf16[2,96,1536]{2,1,0:T(8,128)(2,1)} %pad_maximum_fusion.10), channel_id=1, source_target_pairs={{0,8},{1,9},{2,10},{3,11},{4,12},{5,13},{6,14},{7,15},{8,0},{9,1},... | collective-permute-start | bytes 1769480 | tf_op jit(solution)/shard_map/ffn0_z1/ppermute | solution.py:56
  92.5 35.2 %collective-permute-start.13 = (bf16[2,4,96,1536]{3,2,1,0:T(8,128)(2,1)S(1)}, bf16[2,4,96,1536]{3,2,1,0:T(8,128)(2,1)S(1)}, u32[]{:S(2)}, u32[]{:S(2)}) collective-permute-start(bf16[2,4,96,1536]{3,2,1,0:T(8,128)(2,1)S(1)} %pad_maximum_fusion.3.two), channel_id=1, source_target_pairs={{0,2},{1,5},{2,0},{3,7},{4,6},{5,1},{6,4},{7,3},{8,10},{9,13},{10,... | collective-permute-start | bytes 7077896 | tf_op jit(solution)/shard_map/ffn0_far/ppermute | solution.py:56
  93.6 17.5 %collective-permute-start.12 = (bf16[2,96,2304]{2,1,0:T(8,128)(2,1)S(1)}, bf16[2,96,2304]{2,1,0:T(8,128)(2,1)S(1)}, u32[]{:S(2)}, u32[]{:S(2)}) collective-permute-start(bf16[2,96,2304]{2,1,0:T(8,128)(2,1)S(1)} %pad_maximum_fusion.7), channel_id=1, source_target_pairs={{0,8},{1,9},{2,10},{3,11},{4,12},{5,13},{6,14},{7,15},{8,0},{9,1},... | collective-permute-start | bytes 2654216 | tf_op jit(solution)/shard_map/layer1_z1/ppermute | solution.py:56
  111.2 26.6 %collective-permute-start.14 = (bf16[4,96,768]{2,1,0:T(8,128)(2,1)S(1)}, bf16[4,96,768]{2,1,0:T(8,128)(2,1)S(1)}, u32[]{:S(2)}, u32[]{:S(2)}) collective-permute-start(bf16[4,96,768]{2,1,0:T(8,128)(2,1)S(1)} %get-tuple-element.561), channel_id=1, source_target_pairs={{0,4},{1,3},{2,6},{3,1},{4,0},{5,7},{6,2},{7,5},{8,12},{9,11},{10,... | collective-permute-start | bytes 1769480 | tf_op jit(solution)/shard_map/attn1_near/ppermute | solution.py:56
  138.0 22.4 %collective-permute-start.18 = (bf16[2,4,96,768]{3,2,1,0:T(8,128)(2,1)S(1)}, bf16[2,4,96,768]{3,2,1,0:T(8,128)(2,1)S(1)}, u32[]{:S(2)}, u32[]{:S(2)}) collective-permute-start(bf16[2,4,96,768]{3,2,1,0:T(8,128)(2,1)S(1)} %pad_maximum_fusion.6.two), channel_id=1, source_target_pairs={{0,2},{1,5},{2,0},{3,7},{4,6},{5,1},{6,4},{7,3},{8,10},{9,13},{10,... | collective-permute-start | bytes 3538952 | tf_op jit(solution)/shard_map/attn1_far/ppermute | solution.py:56
  139.0 32.5 %collective-permute-start.19 = (bf16[4,96,1536]{2,1,0:T(8,128)(2,1)S(1)}, bf16[4,96,1536]{2,1,0:T(8,128)(2,1)S(1)}, u32[]{:S(2)}, u32[]{:S(2)}) collective-permute-start(bf16[4,96,1536]{2,1,0:T(8,128)(2,1)S(1)} %slice.548), channel_id=1, source_target_pairs={{0,4},{1,3},{2,6},{3,1},{4,0},{5,7},{6,2},{7,5},{8,12},{9,11},{10,... | collective-permute-start | bytes 3538952 | tf_op jit(solution)/shard_map/ffn1_near/ppermute | solution.py:56
  171.8 28.9 %collective-permute-start.24 = (bf16[2,4,96,1536]{3,2,1,0:T(8,128)(2,1)S(1)}, bf16[2,4,96,1536]{3,2,1,0:T(8,128)(2,1)S(1)}, u32[]{:S(2)}, u32[]{:S(2)}) collective-permute-start(bf16[2,4,96,1536]{3,2,1,0:T(8,128)(2,1)S(1)} %pad_maximum_fusion.4.two), channel_id=1, source_target_pairs={{0,2},{1,5},{2,0},{3,7},{4,6},{5,1},{6,4},{7,3},{8,10},{9,13},{10,... | collective-permute-start | bytes 7077896 | tf_op jit(solution)/shard_map/ffn1_far/ppermute | solution.py:56
  231.6 40.6 %collective-permute-start.32 = (bf16[2,4,96,1536]{3,2,1,0:T(8,128)(2,1)S(1)}, bf16[2,4,96,1536]{3,2,1,0:T(8,128)(2,1)S(1)}, u32[]{:S(2)}, u32[]{:S(2)}) collective-permute-start(bf16[2,4,96,1536]{3,2,1,0:T(8,128)(2,1)S(1)} %get-tuple-element.348), channel_id=1, source_target_pairs={{0,2},{1,5},{2,0},{3,7},{4,6},{5,1},{6,4},{7,3},{8,10},{9,13},{10,... | collective-permute-start | bytes 7077896 | tf_op jit(solution)/shard_map/ffn1_grad_far/ppermute | solution.py:56
  247.3 24.9 %collective-permute-start.31 = (bf16[256,768]{1,0:T(8,128)(2,1)S(1)}, bf16[256,768]{1,0:T(8,128)(2,1)S(1)}, u32[]{:S(2)}, u32[]{:S(2)}) collective-permute-start(bf16[256,768]{1,0:T(8,128)(2,1)S(1)} %get-tuple-element.347), channel_id=1, source_target_pairs={{0,2},{1,3},{2,0},{3,1},{4,6},{5,7},{6,4},{7,5},{8,10},{9,11},{10,... | collective-permute-start | bytes 1179656 | tf_op jit(solution)/shard_map/keys_values_grad/ppermute | solution.py:56
  275.5 29.0 %collective-permute-start.36 = (bf16[4,96,1536]{2,1,0:T(8,128)(2,1)}, bf16[4,96,1536]{2,1,0:T(8,128)(2,1)}, u32[]{:S(2)}, u32[]{:S(2)}) collective-permute-start(bf16[4,96,1536]{2,1,0:T(8,128)(2,1)} %fusion.3), channel_id=1, source_target_pairs={{0,4},{1,3},{2,6},{3,1},{4,0},{5,7},{6,2},{7,5},{8,12},{9,11},{10,... | collective-permute-start | bytes 3538952 | tf_op jit(solution)/shard_map/ffn1_grad_near/ppermute | solution.py:56
  298.3 36.7 %collective-permute-start.40 = (bf16[2,4,96,768]{3,2,1,0:T(8,128)(2,1)S(1)}, bf16[2,4,96,768]{3,2,1,0:T(8,128)(2,1)}, u32[]{:S(2)}, u32[]{:S(2)}) collective-permute-start(bf16[2,4,96,768]{3,2,1,0:T(8,128)(2,1)S(1)} %get-tuple-element.394), channel_id=1, source_target_pairs={{0,2},{1,5},{2,0},{3,7},{4,6},{5,1},{6,4},{7,3},{8,10},{9,13},{10,... | collective-permute-start | bytes 3538952 | tf_op jit(solution)/shard_map/attn1_grad_far/ppermute | solution.py:56
  309.7 40.4 %collective-permute-start.43 = (bf16[2,4,96,1536]{3,2,1,0:T(8,128)(2,1)S(1)}, bf16[2,4,96,1536]{3,2,1,0:T(8,128)(2,1)S(1)}, u32[]{:S(2)}, u32[]{:S(2)}) collective-permute-start(bf16[2,4,96,1536]{3,2,1,0:T(8,128)(2,1)S(1)} %get-tuple-element.399), channel_id=1, source_target_pairs={{0,2},{1,5},{2,0},{3,7},{4,6},{5,1},{6,4},{7,3},{8,10},{9,13},{10,... | collective-permute-start | bytes 7077896 | tf_op jit(solution)/shard_map/ffn0_grad_far/ppermute | solution.py:56
  317.7 20.8 %collective-permute-start.41 = (bf16[2,96,1536]{2,1,0:T(8,128)(2,1)S(1)}, bf16[2,96,1536]{2,1,0:T(8,128)(2,1)S(1)}, u32[]{:S(2)}, u32[]{:S(2)}) collective-permute-start(bf16[2,96,1536]{2,1,0:T(8,128)(2,1)S(1)} %slice.753), channel_id=1, source_target_pairs={{0,8},{1,9},{2,10},{3,11},{4,12},{5,13},{6,14},{7,15},{8,0},{9,1},... | collective-permute-start | bytes 1769480 | tf_op jit(solution)/shard_map/ffn1_grad_z1/ppermute | solution.py:56
  337.7 27.7 %collective-permute-start.45 = (bf16[4,96,768]{2,1,0:T(8,128)(2,1)S(1)}, bf16[4,96,768]{2,1,0:T(8,128)(2,1)S(1)}, u32[]{:S(2)}, u32[]{:S(2)}) collective-permute-start(bf16[4,96,768]{2,1,0:T(8,128)(2,1)S(1)} %fusion.11), channel_id=1, source_target_pairs={{0,4},{1,3},{2,6},{3,1},{4,0},{5,7},{6,2},{7,5},{8,12},{9,11},{10,... | collective-permute-start | bytes 1769480 | tf_op jit(solution)/shard_map/attn1_grad_near/ppermute | solution.py:56
  352.1 30.6 %collective-permute-start.50 = (bf16[4,96,1536]{2,1,0:T(8,128)(2,1)}, bf16[4,96,1536]{2,1,0:T(8,128)(2,1)}, u32[]{:S(2)}, u32[]{:S(2)}) collective-permute-start(bf16[4,96,1536]{2,1,0:T(8,128)(2,1)} %fusion.4), channel_id=1, source_target_pairs={{0,4},{1,3},{2,6},{3,1},{4,0},{5,7},{6,2},{7,5},{8,12},{9,11},{10,... | collective-permute-start | bytes 3538952 | tf_op jit(solution)/shard_map/ffn0_grad_near/ppermute | solution.py:56
  355.2 27.5 %collective-permute-start.49 = (bf16[1,96,1536]{2,1,0:T(8,128)(2,1)}, bf16[1,96,1536]{2,1,0:T(8,128)(2,1)}, u32[]{:S(2)}, u32[]{:S(2)}) collective-permute-start(bf16[1,96,1536]{2,1,0:T(8,128)(2,1)} %slice.757), channel_id=1, source_target_pairs={{0,16},{1,17},{2,18},{3,19},{4,20},{5,21},{6,22},{7,23},{8,24},{9,... | collective-permute-start | bytes 884744 | tf_op jit(solution)/shard_map/ffn1_grad_z2/ppermute | solution.py:56
  366.0 19.6 %collective-permute-start.44 = (bf16[2,4,96,768]{3,2,1,0:T(8,128)(2,1)}, bf16[2,4,96,768]{3,2,1,0:T(8,128)(2,1)}, u32[]{:S(2)}, u32[]{:S(2)}) collective-permute-start(bf16[2,4,96,768]{3,2,1,0:T(8,128)(2,1)} %get-tuple-element.406), channel_id=1, source_target_pairs={{0,2},{1,5},{2,0},{3,7},{4,6},{5,1},{6,4},{7,3},{8,10},{9,13},{10,... | collective-permute-start | bytes 3538952 | tf_op jit(solution)/shard_map/attn0_grad_far/ppermute | solution.py:56
  373.5 22.0 %collective-permute-start.55 = (bf16[2,96,768]{2,1,0:T(8,128)(2,1)}, bf16[2,96,768]{2,1,0:T(8,128)(2,1)S(1)}, u32[]{:S(2)}, u32[]{:S(2)}) collective-permute-start(bf16[2,96,768]{2,1,0:T(8,128)(2,1)} %slice.756), channel_id=1, source_target_pairs={{0,8},{1,9},{2,10},{3,11},{4,12},{5,13},{6,14},{7,15},{8,0},{9,1},... | collective-permute-start | bytes 884744 | tf_op jit(solution)/shard_map/attn1_grad_z1/ppermute | solution.py:56
  385.5 21.7 %collective-permute-start.57 = (bf16[2,96,1536]{2,1,0:T(8,128)(2,1)S(1)}, bf16[2,96,1536]{2,1,0:T(8,128)(2,1)S(1)}, u32[]{:S(2)}, u32[]{:S(2)}) collective-permute-start(bf16[2,96,1536]{2,1,0:T(8,128)(2,1)S(1)} %slice.752), channel_id=1, source_target_pairs={{0,8},{1,9},{2,10},{3,11},{4,12},{5,13},{6,14},{7,15},{8,0},{9,1},... | collective-permute-start | bytes 1769480 | tf_op jit(solution)/shard_map/ffn0_grad_z1/ppermute | solution.py:56
  390.8 29.1 %collective-permute-start.52 = (bf16[384,2,768]{2,0,1:T(8,128)(2,1)S(1)}, bf16[384,2,768]{2,0,1:T(8,128)(2,1)}, u32[]{:S(2)}, u32[]{:S(2)}) collective-permute-start(bf16[384,2,768]{2,0,1:T(8,128)(2,1)S(1)} %fusion.2), channel_id=1, source_target_pairs={{0,2},{1,3},{2,0},{3,1},{4,6},{5,7},{6,4},{7,5},{8,10},{9,11},{10,... | collective-permute-start | bytes 3538952 | tf_op jit(solution)/shard_map/rows_x/ppermute | solution.py:56
  401.6 45.3 %collective-permute-start.60 = (bf16[1,96,768]{2,1,0:T(8,128)(2,1)}, bf16[1,96,768]{2,1,0:T(8,128)(2,1)}, u32[]{:S(2)}, u32[]{:S(2)}) collective-permute-start(bf16[1,96,768]{2,1,0:T(8,128)(2,1)} %slice.759), channel_id=1, source_target_pairs={{0,16},{1,17},{2,18},{3,19},{4,20},{5,21},{6,22},{7,23},{8,24},{9,... | collective-permute-start | bytes 442376 | tf_op jit(solution)/shard_map/attn1_grad_z2/ppermute | solution.py:56
  404.2 42.7 %collective-permute-start.59 = (bf16[2,96,768]{2,1,0:T(8,128)(2,1)}, bf16[2,96,768]{2,1,0:T(8,128)(2,1)}, u32[]{:S(2)}, u32[]{:S(2)}) collective-permute-start(bf16[2,96,768]{2,1,0:T(8,128)(2,1)} %slice.755), channel_id=1, source_target_pairs={{0,8},{1,9},{2,10},{3,11},{4,12},{5,13},{6,14},{7,15},{8,0},{9,1},... | collective-permute-start | bytes 884744 | tf_op jit(solution)/shard_map/attn0_grad_z1/ppermute | solution.py:56
  426.2 20.7 %collective-permute-start.58 = (bf16[384,2,768]{2,0,1:T(8,128)(2,1)}, bf16[384,2,768]{2,0,1:T(8,128)(2,1)}, u32[]{:S(2)}, u32[]{:S(2)}) collective-permute-start(bf16[384,2,768]{2,0,1:T(8,128)(2,1)} %collective-permute-done.52), channel_id=1, source_target_pairs={{0,1},{1,0},{2,3},{3,2},{4,5},{5,4},{6,7},{7,6},{8,9},{9,8},{10,11... | collective-permute-start | bytes 3538952 | tf_op jit(solution)/shard_map/rows_core/ppermute | solution.py:56
  (193 other events, 1280.4 us)

commit v4 on v3

--- a/solution.py
+++ b/solution.py
@@ -48,7 +48,7 @@
         self.core = mp_at % 2
         self.at_y = dp_at % 2
         self.at_z = dp_at // 2
-        self.places = jnp.stack([self.core, self.at_y, self.at_z]).astype(jnp.int32)
+        self.places = jnp.stack([self.core, self.at_y, self.at_z, self.at_x]).astype(jnp.int32)
 
     def swap(self, array, mask0, mask1=None):
         mask1 = mask0 if mask1 is None else mask1
@@ -86,20 +86,21 @@
         half = parts.shape[0] // 2
         return parts[:half], self.swap_z(parts[half:].astype(BF16), masks[-1])
 
-    def assemble(self, two, far):
+    def assemble(self, block, near, far_block, far_near):
+        parts = (block, near, far_block, far_near)
         if self.aligned:
-            shape = (far.shape[1], 2) + far.shape[2:]
+            shape = (block.shape[0], 2) + block.shape[1:]
             kernel = functools.partial(assemble_kernel, self.order)
-            both = call(kernel, [(shape, far.dtype)] * 2, (self.places, two, far), name="assemble")
+            both = call(kernel, [(shape, block.dtype)] * 2, (self.places, *parts), name="assemble")
         else:
-            order = jnp.array(inverse(self.order))[jnp.arange(far.shape[1]) ^ self.at_z]
-            two, far = jnp.take(two, order, axis=1), jnp.take(far, order, axis=1)
+            order = jnp.array(inverse(self.order))[jnp.arange(block.shape[0]) ^ self.at_z]
+            block, near, far_block, far_near = (jnp.take(part, order, axis=0) for part in parts)
             first, low = self.core == 0, self.at_y == 0
-            own_far = jnp.where(first, two[1], far[0])
-            other_same = jnp.where(first, far[0], two[1])
+            own_far = jnp.where(first, near, far_block)
+            other_same = jnp.where(first, far_block, near)
             both = [
                 jnp.stack([jnp.where(low, same, other), jnp.where(low, other, same)], axis=1)
-                for same, other in ((two[0], own_far), (other_same, far[1]))
+                for same, other in ((block, own_far), (other_same, far_near))
             ]
         return [w.reshape(-1, w.shape[-1]) for w in both]
 
@@ -108,22 +109,22 @@
     return [order.index(place) for place in range(len(order))]
 
 
-def assemble_kernel(order, places, two, far, own, other):
+def assemble_kernel(order, places, block, near, far_block, far_near, own, other):
     first, at_y, at_z = places[0] == 0, places[1], places[2]
     for m, distance in enumerate(order):
         j = distance ^ at_z
-        own[j, at_y] = two[0, m]
-        other[j, 1 - at_y] = far[1, m]
+        own[j, at_y] = block[m]
+        other[j, 1 - at_y] = far_near[m]
 
         @pl.when(first)
         def _(j=j, m=m):
-            own[j, 1 - at_y] = two[1, m]
-            other[j, at_y] = far[0, m]
+            own[j, 1 - at_y] = near[m]
+            other[j, at_y] = far_block[m]
 
         @pl.when(~first)
         def _(j=j, m=m):
-            own[j, 1 - at_y] = far[0, m]
-            other[j, at_y] = two[1, m]
+            own[j, 1 - at_y] = far_block[m]
+            other[j, at_y] = near[m]
 
 
 def adam_step(master, moment, second, gradient, step_rate, decay_rate):
@@ -152,12 +153,6 @@
     f_at += third
     values_half = jnp.concatenate([qkv[g][full:, v_at : v_at + HEAD_DIM], far[:, f_at : f_at + HEAD_DIM]])
     return keys, values, keys_half, values_half
-
-
-def fill_bias(limits, bias, full, half):
-    bias[0] = key_bias(limits[0], full, half)
-    bias[1, :half] = key_bias(limits[1], half, half)
-    bias[1, half:] = key_bias(limits[2], half, half)
 
 
 def attend_unit(keys, values, queries, bias_rows):
@@ -191,7 +186,7 @@
             ctx[g][rows, :] = jnp.concatenate(outs[part], axis=0).T.astype(BF16)
 
 
-def half_kernel(swapped, limits, qkv0, qkv1, far, _a, _b, _c, ctx0, ctx1, lse, bias):
+def half_kernel(swapped, limits, qkv0, qkv1, far, ctx0, ctx1, lse, bias):
     qkv, ctx = (qkv0, qkv1), (ctx0, ctx1)
     half = far.shape[0]
     full = 2 * half
@@ -226,7 +221,8 @@
     full = 2 * half
     third = qkv0.shape[1] // 3
     heads = third // HEAD_DIM
-    fill_bias(limits, bias, full, half)
+    bias[:half] = key_bias(limits[1], half, half)
+    bias[half:] = key_bias(limits[2], half, half)
     for g in range(2):
         queries_out, keys_out, values_out = [], [], []
         for h in range(heads):
@@ -237,8 +233,8 @@
                 values,
                 qkv[g][full:, columns],
                 dctx[g][full:, columns],
-                lse[g * heads + h : g * heads + h + 1, full:],
-                bias[1],
+                lse[g * heads + h : g * heads + h + 1, :],
+                bias[...],
             )
             queries_out.append(gq)
             keys_out.append(gk)
@@ -252,8 +248,7 @@
 
 def full_back_kernel(limits, qkv0, qkv1, dctx0, dctx1, lse, dqkv0, dqkv1, bias):
     qkv, dctx, dqkv = (qkv0, qkv1), (dctx0, dctx1), (dqkv0, dqkv1)
-    full = qkv0.shape[0] * 2 // 3
-    half = full // 2
+    full, half = bias.shape
     third = qkv0.shape[1] // 3
     heads = third // HEAD_DIM
     bias[...] = key_bias(limits[0], full, half)
@@ -281,12 +276,10 @@
         for part in range(2):
             rows = slice(part * half, (part + 1) * half)
             dqkv[g][rows, :third] = jnp.concatenate(queries_out[part], axis=0).T.astype(BF16) * 0.125
-        dqkv[g][:full, third:] = jnp.concatenate(keys_out + values_out, axis=1)
-
-
-def half_fill_kernel(dq0, dq1, own, came, _a, _b, dqkv0, dqkv1):
-    half = own.shape[0]
-    full = 2 * half
+        dqkv[g][:, third:] = jnp.concatenate(keys_out + values_out, axis=1)
+
+
+def half_fill_kernel(dq0, dq1, own, came, dqkv0, dqkv1):
     third = dq0.shape[1]
     for g, (dq, dqkv) in enumerate(((dq0, dqkv0), (dq1, dqkv1))):
         columns = slice(2 * third * g, 2 * third * (g + 1))
@@ -296,7 +289,7 @@
 
 VMEM = pl.BlockSpec(memory_space=pltpu.VMEM)
 SMEM = pl.BlockSpec(memory_space=pltpu.SMEM)
-ROOM = pltpu.CompilerParams(vmem_limit_bytes=32 * 1024 * 1024)
+ROOM = pltpu.CompilerParams(vmem_limit_bytes=16 * 1024 * 1024)
 CHEAP = pl.CostEstimate(flops=1, bytes_accessed=1, transcendentals=0)
 
 
@@ -319,30 +312,24 @@
     half = tokens // 3
     ctx0, ctx1, lse = call(
         full_kernel,
-        [((tokens, third), BF16)] * 2 + [((2 * third // HEAD_DIM, tokens), F32)],
+        [((2 * half, third), BF16)] * 2 + [((2 * third // HEAD_DIM, 2 * half), F32)],
         (limits, *qkv),
         [pltpu.VMEM((2 * half, half), F32)],
         name="attend_full",
     )
-    return (ctx0, ctx1), lse
-
-
-def attend_half(limits, qkv, far, ctx, lse, swapped):
-    half, third = far.shape[0], ctx[0].shape[1]
-    rows = pl.BlockSpec((half, third), lambda i: (2, 0))
-    ctx0, ctx1, lse = pl.pallas_call(
+    return [ctx0, ctx1], lse
+
+
+def attend_half(limits, qkv, far, swapped):
+    half, third = far.shape[0], qkv[0].shape[1] // 3
+    ctx0, ctx1, lse = call(
         functools.partial(half_kernel, swapped),
-        grid=(1,),
-        out_shape=[jax.ShapeDtypeStruct(a.shape, a.dtype) for a in (*ctx, lse)],
-        in_specs=[SMEM] + [VMEM] * 3 + [pl.BlockSpec(memory_space=pl.ANY)] * 3,
-        out_specs=[rows, rows, pl.BlockSpec((lse.shape[0], half), lambda i: (0, 2))],
-        scratch_shapes=[pltpu.VMEM((2 * half, half), F32)],
-        input_output_aliases={4: 0, 5: 1, 6: 2},
-        compiler_params=ROOM,
-        cost_estimate=CHEAP,
+        [((half, third), BF16)] * 2 + [((2 * third // HEAD_DIM, half), F32)],
+        (limits, *qkv, far),
+        [pltpu.VMEM((2 * half, half), F32)],
         name="attend_half",
-    )(limits, *qkv, far, *ctx, lse)
-    return (ctx0, ctx1), lse
+    )
+    return [ctx0, ctx1], lse
 
 
 def attend_half_back(limits, qkv, far, dctx, lse, swapped):
@@ -351,7 +338,7 @@
         functools.partial(half_back_kernel, swapped),
         [((half, third), BF16)] * 2 + [((half, 4 * third), F32), ((half, 4 * third), BF16)],
         (limits, *qkv, far, *dctx, lse),
-        [pltpu.VMEM((2, 2 * half, half), F32)],
+        [pltpu.VMEM((2 * half, half), F32)],
         name="attend_half_back",
     )
     return (dq0, dq1), own, sent
@@ -361,77 +348,70 @@
     half = qkv[0].shape[0] // 3
     return call(
         full_back_kernel,
-        [(qkv[0].shape, BF16)] * 2,
+        [((2 * half, qkv[0].shape[1]), BF16)] * 2,
         (limits, *qkv, *dctx, lse),
         [pltpu.VMEM((2 * half, half), F32)],
         name="attend_full_back",
     )
 
 
-def fill_half(dqkv, dq, own, came):
-    tokens, columns = dqkv[0].shape
-    half = own.shape[0]
-    rows = pl.BlockSpec((half, columns), lambda i: (2, 0))
-    return pl.pallas_call(
-        half_fill_kernel,
-        grid=(1,),
-        out_shape=[jax.ShapeDtypeStruct(d.shape, d.dtype) for d in dqkv],
-        in_specs=[VMEM] * 4 + [pl.BlockSpec(memory_space=pl.ANY)] * 2,
-        out_specs=[rows] * 2,
-        input_output_aliases={4: 0, 5: 1},
-        compiler_params=ROOM,
-        cost_estimate=CHEAP,
-        name="fill_half",
-    )(*dq, own, came, *dqkv)
-
-def wgrad_kernel(count, order, places, *refs):
-    lefts, rights = refs[:count], (refs[count : 2 * count], refs[2 * count : 3 * count])
-    keep, give, whole = refs[3 * count :]
+def fill_half(dq, own, came):
+    shape = (own.shape[0], 3 * dq[0].shape[1])
+    return call(half_fill_kernel, [(shape, BF16)] * 2, (*dq, own, came), name="fill_half")
+
+
+def wgrad_kernel(count, pieces, order, places, *refs):
+    step = count * pieces
+    lefts, rights = refs[:count], (refs[count : count + step], refs[count + step : count + 2 * step])
+    keep0, keep1, give0, give1, whole = refs[count + 2 * step :]
     first, at_y, at_z = places[0] == 0, places[1], places[2]
-    blocks, rows = keep.shape[1], keep.shape[2]
+    rows = keep0.shape[1]
     turned = [left[...].T for left in lefts]
     for g in range(2):
         at = 0
-        for left, right in zip(turned, rights[g]):
+        for k, left in enumerate(turned):
+            right = [ref[...] for ref in rights[g][k * pieces : (k + 1) * pieces]]
+            right = right[0] if pieces == 1 else jnp.concatenate(right)
             wide = right.shape[1]
-            whole[:, at : at + wide] = dot(left, right[...], NN).astype(BF16)
+            whole[:, at : at + wide] = dot(left, right, NN).astype(BF16)
             at += wide
         for y in range(2):
             same = at_y == y
             if g == 0:
-                targets = ((same, keep, 0), (~same & first, keep, 1), (~same & ~first, give, 0))
+                targets = ((same, keep0), (~same & first, keep1), (~same & ~first, give0))
             else:
-                targets = ((same & first, give, 0), (same & ~first, keep, 1), (~same, give, 1))
-            for when, ref, slot in targets:
+                targets = ((same & first, give0), (same & ~first, keep1), (~same, give1))
+            for when, ref in targets:
 
                 @pl.when(when)
-                def _(ref=ref, slot=slot, y=y):
+                def _(ref=ref, y=y):
                     for m, distance in enumerate(order):
-                        ref[slot, m] = whole[pl.ds((2 * (distance ^ at_z) + y) * rows, rows), :]
+                        from_row = pl.ds(pl.multiple_of((2 * (distance ^ at_z) + y) * rows, 16), rows)
+                        ref[m] = whole[from_row, :]
 
 
 def weight_grads(links, lefts, rights):
     features = lefts[0].shape[1]
-    columns = sum(r.shape[1] for r in rights[0])
+    columns = sum(r[0].shape[1] for r in rights[0])
     blocks = links.n_dp // 2
     rows = features // links.n_dp
     if links.aligned:
         return call(
-            functools.partial(wgrad_kernel, len(lefts), links.order),
-            [((2, blocks, rows, columns), BF16)] * 2,
-            (links.places, *lefts, *rights[0], *rights[1]),
+            functools.partial(wgrad_kernel, len(lefts), len(rights[0][0]), links.order),
+            [((blocks, rows, columns), BF16)] * 4,
+            (links.places, *lefts, *[piece for group in rights for right in group for piece in right]),
             [pltpu.VMEM((features, columns), BF16)],
             name="weight_grads",
         )
     low, first = links.at_y == 0, links.core == 0
     parts = []
     for group in rights:
-        grad = jnp.concatenate([dot(a, b, TN) for a, b in zip(lefts, group)], axis=1).astype(BF16)
+        grad = jnp.concatenate([dot(a, jnp.concatenate(b), TN) for a, b in zip(lefts, group)], axis=1).astype(BF16)
         grad = jnp.take(grad.reshape(blocks, 2, rows, columns), jnp.array(links.order) ^ links.at_z, axis=0)
         parts += [jnp.where(low, grad[:, 0], grad[:, 1]), jnp.where(low, grad[:, 1], grad[:, 0])]
     own_same, own_far, other_same, other_far = parts
-    keep = jnp.stack([own_same, jnp.where(first, own_far, other_same)])
-    return keep, jnp.stack([jnp.where(first, other_same, own_far), other_far])
+    return own_same, jnp.where(first, own_far, other_same), jnp.where(first, other_same, own_far), other_far
+
 
 def both_cores(links, parts):
     return (*parts, *[links.swap_as("core", links.swap_core, part) for part in parts])
@@ -552,12 +532,18 @@
     return [q0, q1], extra
 
 
-def out_kernel(ctx0, ctx1, w0, w1, *outs):
-    third = ctx0.shape[1]
+def row_thirds(full0, full1, half0, half1):
+    half = half0.shape[0]
+    rows = [slice(0, half), slice(half, 2 * half), slice(0, half)]
+    return [((full0, full1) if k < 2 else (half0, half1), rows[k]) for k in range(3)]
+
+
+def out_kernel(full0, full1, half0, half1, w0, w1, *outs):
+    third = full0.shape[1]
     at = w0.shape[1] - third
     tails = (w0[:, at:], w1[:, at:])
-    for rows, out in zip(chunks(ctx0.shape[0], outs[0].shape[0]), outs):
-        out[...] = (dot(ctx0[rows, :], tails[0], NT) + dot(ctx1[rows, :], tails[1], NT)).astype(BF16)
+    for (pair, rows), out in zip(row_thirds(full0, full1, half0, half1), outs):
+        out[...] = (dot(pair[0][rows, :], tails[0], NT) + dot(pair[1][rows, :], tails[1], NT)).astype(BF16)
 
 
 def ffn_kernel(low, w0, w1, bias, act0, act1, slope0, slope1, *outs):
@@ -621,15 +607,18 @@
         out[...] = (dot(d0[rows, :], w0[:, :wide], NT) + dot(d1[rows, :], w1[:, :wide], NT)).astype(BF16)
 
 
-def qkv_back_kernel(d0, d1, w0, w1, *refs):
+def qkv_back_kernel(full0, full1, half0, half1, w0, w1, *refs):
     *outs, sums = refs
-    back_out_kernel(d0, d1, w0, w1, *outs)
-    for g, d in enumerate((d0, d1)):
-        total = None
-        for rows in chunks(d.shape[0]):
-            part = add_rows(d[rows, :])
-            total = part if total is None else total + part
-        sums[8 * g : 8 * (g + 1), :] = total
+    wide = full0.shape[1]
+    totals = [None, None]
+    for (pair, rows), out in zip(row_thirds(full0, full1, half0, half1), outs):
+        parts = [ref[rows, :] for ref in pair]
+        out[...] = (dot(parts[0], w0[:, :wide], NT) + dot(parts[1], w1[:, :wide], NT)).astype(BF16)
+        for g in range(2):
+            part = add_rows(parts[g])
+            totals[g] = part if totals[g] is None else totals[g] + part
+    for g in range(2):
+        sums[8 * g : 8 * (g + 1), :] = totals[g]
 
 
 def context_grad_kernel(low, w0, w1, out0, out1):
@@ -639,6 +628,112 @@
         tail = weight[:, at:]
         for rows in chunks(low.shape[0]):
             out[rows, :] = dot(low[rows, :], tail, NN).astype(BF16)
+
+
+def adam_kernel(splits, count, *refs):
+    keep, came, *refs = refs
+    ins, outs = refs[: 3 * len(splits)], refs[3 * len(splits) + count :]
+    for i, ranges in enumerate(splits):
+        master, moment, second = ins[3 * i : 3 * i + 3]
+        results = outs[4 * i : 4 * i + 4]
+        for k, (low, high) in enumerate(ranges):
+            at = (0, k) if len(ranges) > 1 else (0,)
+            grad = keep[0, :, low:high] + came[0, :, low:high].astype(F32)
+            new = adam_step(master[at], moment[at], second[at], grad, RATE_MATRIX, DECAY_MATRIX)
+            for ref, value in zip(results, (*new, new[0].astype(BF16))):
+                ref[at] = value
+
+
+def adam_layer(layer, splits, keep, came, states, before):
+    def block(array):
+        rest = array.shape[1:]
+        return pl.BlockSpec((1,) + rest, lambda i, n=len(rest): (layer,) + (0,) * n)
+
+    flat = [a for state in states for a in state]
+    outs, specs = [], []
+    for state in states:
+        outs += [jax.ShapeDtypeStruct(state[0].shape, d) for d in (F32, F32, F32, BF16)]
+        specs += [block(state[0])] * 4
+    before = [] if before is None else before
+    results = pl.pallas_call(
+        functools.partial(adam_kernel, splits, len(before)),
+        grid=(1,),
+        out_shape=outs,
+        in_specs=[VMEM] * 2 + [block(a) for a in flat] + [pl.BlockSpec(memory_space=pl.ANY)] * len(before),
+        out_specs=specs,
+        input_output_aliases={2 + len(flat) + i: i for i in range(len(before))},
+        compiler_params=ROOM,
+        cost_estimate=CHEAP,
+        name="adam",
+    )(keep, came, *flat, *before)
+    return list(results)
+
+
+def pack_kernel(*refs):
+    *parts, own, other = refs
+    own[...] = jnp.zeros_like(own)
+    other[...] = jnp.zeros_like(other)
+    for layer in range(LAYERS):
+        upper, pre, lower, heads = parts[4 * layer : 4 * layer + 4]
+        third = heads.shape[1] // 3
+
+        def total(ref, k):
+            return jnp.sum(ref[8 * k : 8 * (k + 1), :], axis=0, keepdims=True)
+
+        rows = [(lower, 0), (upper, 0), (lower, 1), (lower, 2), (upper, 1), (upper, 2)]
+        for k, row in enumerate(rows):
+            value = total(*row)
+            own[6 * layer + k : 6 * layer + k + 1, :] = value
+            other[6 * layer + k : 6 * layer + k + 1, :] = value
+        for g, ref in enumerate((own, other)):
+            at = 6 * LAYERS + layer
+            ref[at : at + 1, :] = total(pre, g)
+            head = total(heads, g)
+            at += LAYERS
+            ref[at : at + 1, : 2 * third] = jnp.concatenate([head[:, :third], head[:, 2 * third :]], axis=1)
+
+
+def vector_adam_kernel(grads, *refs):
+    ins, outs = refs[:9], refs[9:]
+    third = ins[0].shape[2]
+
+    def update(i, at, grad):
+        new = adam_step(ins[3 * i][at], ins[3 * i + 1][at], ins[3 * i + 2][at], grad, RATE_VECTOR, 0.0)
+        for k, value in enumerate(new):
+            outs[3 * i + k][at] = value
+
+    for layer in range(LAYERS):
+        at = 7 * LAYERS + layer
+        for k in range(2):
+            grad = grads[at : at + 1, k * third : (k + 1) * third]
+            update(0, (layer, slice(k, k + 1)), grad)
+        update(1, (slice(layer, layer + 1),), grads[at - LAYERS : at - LAYERS + 1, :])
+        update(2, (layer,), grads[6 * layer : 6 * layer + 6, :])
+
+
+def rows_kernel(places, low, piece, twin, out):
+    first, at_x = places[0] == 0, places[3]
+    half = low.shape[0] // 3
+    part = piece.shape[0]
+
+    def put(start, rows):
+        out[pl.ds(pl.multiple_of(start, 8), rows.shape[0]), :] = rows.astype(F32)
+
+    def put_other(upper, lower):
+        put((1 - at_x) * 4 * half, upper[...])
+        put((1 - at_x) * 4 * half + part, lower[: 2 * half - part, :])
+        put(2 * half + (1 - at_x) * half, lower[2 * half - part :, :])
+
+    put(at_x * 4 * half, low[: 2 * half, :])
+    put(2 * half + at_x * half, low[2 * half :, :])
+
+    @pl.when(first)
+    def _():
+        put_other(piece, twin)
+
+    @pl.when(~first)
+    def _():
+        put_other(twin, piece)
 
 
 def local(n_dp, *args):
@@ -674,18 +769,7 @@
         return links.swap_as("rows_core", links.swap_core, piece)
 
     def all_rows(low, piece, twin):
-        first = core == 0
-        other = jnp.concatenate([jnp.where(first, piece, twin), jnp.where(first, twin, piece)])
-        low, other = low.astype(F32), other.astype(F32)
-        first = at_x == 0
-        return jnp.concatenate(
-            [
-                jnp.where(first, low[:seq_len], other[:seq_len]),
-                jnp.where(first, low[seq_len:], other[seq_len:]),
-                jnp.where(first, other[seq_len:], low[seq_len:]),
-                jnp.where(first, other[:seq_len], low[:seq_len]),
-            ]
-        )
+        return call(rows_kernel, [(inputs.shape, F32)], (links.places, low, piece, twin), name="all_rows")[0]
 
     def packed_attn(layer):
         attn = [attn_in[layer, 0], attn_in[layer, 1], attn_in[layer, 2], attn_out[layer]]
@@ -703,19 +787,21 @@
     a0 = join([a0, a0_in])
     a0, a0_in = links.swap_as("attn0_z1", links.last_z, a0, z_rest)
     f0_in = links.swap_as("ffn0_z2", links.swap_z, f0, links.z_masks[0])
-    a0_in, f0_in, later = tie(a0_in, f0_in, later)
+    biases = jnp.concatenate([head_bias.reshape(-1), ffn_bias.reshape(-1)])
+    a0_in, f0_in, later, biases = tie(a0_in, f0_in, later, biases)
     a0, f0 = join([a0, a0_in]), join([f0, f0_in])
+    bias_far = links.swap_as("biases", links.swap_x, biases)
     near = links.swap_as("attn0_near", links.swap_near, a0)
+    a0far = links.swap_as("attn0_far", links.swap_far, a0)
     f0, f0_in = links.swap_as("ffn0_z1", links.last_z, f0, z_rest)
     later_in = links.swap_as("layer1_z2", links.swap_z, later, links.z_masks[0])
-    biases = jnp.concatenate([head_bias.reshape(-1), ffn_bias.reshape(-1)])
-    near, biases = tie(near, biases)
-    two = jnp.stack([a0, near])
-    far_part = links.swap_as("attn0_far", links.swap_far, two)
-    bias_far = links.swap_as("biases", links.swap_x, biases)
-    far_part, bias_far, later_in = tie(far_part, bias_far, later_in)
-    later = join([later, later_in])
-    a0 = links.assemble(two, far_part)
+    near, bias_far = tie(near, bias_far)
+    a0last = links.swap_as("attn0_far_near", links.swap_far, near)
+    a0far, a0last, f0_in = tie(a0far, a0last, f0_in)
+    f0 = join([f0, f0_in])
+    f0near = links.swap_as("ffn0_near", links.swap_near, f0)
+    f0far = links.swap_as("ffn0_far", links.swap_far, f0)
+    a0 = links.assemble(a0, near, a0far, a0last)
     head_b = (head_bias, bias_far[: head_bias.size].reshape(head_bias.shape))
     ffn_b = (ffn_bias, bias_far[head_bias.size :].reshape(ffn_bias.shape))
     zeros = jnp.zeros((third,), F32)
@@ -738,7 +824,9 @@
     weight_a, weight_f = [a0, None], [None, None]
 
     def out_part(layer):
-        return call(out_kernel, thirds(hidden.shape), (*ctx[layer], *weight_a[layer]), name="attention_out")
+        return call(
+            out_kernel, thirds(hidden.shape), (*ctx[layer][0], *ctx[layer][1], *weight_a[layer]), name="attention_out"
+        )
 
     norms = [None] * 2
     ffn_parts = [None] * 2
@@ -750,49 +838,46 @@
         [jnp.stack([row_params[i, k] for k in ks]) for ks in ((0, 2, 3), (1, 4, 5))] for i in range(LAYERS)
     ]
     qkv[0], far[0] = project(in_low[0], a0, qkv_b[0], low_other)
-    q0, q1, far[0], f0_in, later = tie(*qkv[0], far[0], f0_in, later)
-    f0 = join([f0, f0_in])
-    near = links.swap_as("ffn0_near", links.swap_near, f0)
+    whole, whole_lse = attend_full(limits, qkv[0])
+    *whole, f0near, later_in = tie(*whole, f0near, later_in)
+    f0last = links.swap_as("ffn0_far_near", links.swap_far, f0near)
+    later = join([later, later_in])
     later, later_in = links.swap_as("layer1_z1", links.last_z, later, z_rest)
-    qkv[0] = [q0, q1]
-    ctx[0], lse[0] = attend_full(limits, qkv[0])
-    ctx[0], lse[0] = attend_half(limits, qkv[0], far[0], ctx[0], lse[0], 0)
-    c0, c1, near = tie(*ctx[0], near)
-    ctx[0] = (c0, c1)
-    f0two = jnp.stack([f0, near])
-    f0far = links.swap_as("ffn0_far", links.swap_far, f0two)
+    split, split_lse = attend_half(limits, qkv[0], far[0], 0)
+    *split, f0far = tie(*split, f0far)
+    ctx[0], lse[0] = (whole, split), (whole_lse, split_lse)
     normed, normed_low, scaled_one, inv_one = add_norm(both_cores(links, out_part(0)), hidden, row_parts[0][0])
-    normed_low, later_in = tie(normed_low, later_in)
+    normed_low, later_in, f0last = tie(normed_low, later_in, f0last)
     later = join([later, later_in])
     a1, f1 = later[:, :, : 4 * third], later[:, :, 4 * third :]
-    near = links.swap_as("attn1_near", links.swap_near, a1)
-    normed_low, f0far = tie(normed_low, f0far)
-    f0 = links.assemble(f0two, f0far)
+    a1near = links.swap_as("attn1_near", links.swap_near, a1)
+    a1far = links.swap_as("attn1_far", links.swap_far, a1)
+    f0 = links.assemble(f0, f0near, f0far, f0last)
     weight_f[0] = f0
     ffn_parts[0], partial = feed_forward(normed_low, f0, ffn_b[0])
-    *partial, near, f1 = tie(*partial, near, f1)
-    a1two = jnp.stack([a1, near])
-    a1far = links.swap_as("attn1_far", links.swap_far, a1two)
-    near = links.swap_as("ffn1_near", links.swap_near, f1)
     fed = both_cores(links, partial)
     hidden, low, scaled_two, inv_two = add_norm(fed, normed, row_parts[0][1])
     norms[0] = (normed_low, scaled_one, inv_one, scaled_two, inv_two)
 
-    low, a1far = tie(low, a1far)
-    a1 = links.assemble(a1two, a1far)
+    low, a1near, a1far = tie(low, a1near, a1far)
+    a1last = links.swap_as("attn1_far_near", links.swap_far, a1near)
+    low, a1last, f1 = tie(low, a1last, f1)
+    f1near = links.swap_as("ffn1_near", links.swap_near, f1)
+    f1far = links.swap_as("ffn1_far", links.swap_far, f1)
+    a1 = links.assemble(a1, a1near, a1far, a1last)
     weight_a[1] = a1
     in_low[1] = low
     qkv[1], sent = project(low, a1, qkv_b[1])
     far[1] = links.swap_as("keys_values", links.swap_x, sent)
-    ctx[1], lse[1] = attend_full(limits, qkv[1])
-    c0, c1, near, far[1] = tie(*ctx[1], near, far[1])
-    f1two = jnp.stack([f1, near])
-    f1far = links.swap_as("ffn1_far", links.swap_far, f1two)
-    ctx[1], lse[1] = attend_half(limits, qkv[1], far[1], (c0, c1), lse[1], 1)
+    whole, whole_lse = attend_full(limits, qkv[1])
+    *whole, far[1], f1near, f1far = tie(*whole, far[1], f1near, f1far)
+    f1last = links.swap_as("ffn1_far_near", links.swap_far, f1near)
+    split, split_lse = attend_half(limits, qkv[1], far[1], 1)
+    ctx[1], lse[1] = (whole, split), (whole_lse, split_lse)
     fed = both_cores(links, out_part(1))
     normed, normed_low, scaled_one, inv_one = add_norm(fed, hidden, row_parts[1][0])
-    normed_low, f1far = tie(normed_low, f1far)
-    f1 = links.assemble(f1two, f1far)
+    normed_low, f1last = tie(normed_low, f1last)
+    f1 = links.assemble(f1, f1near, f1far, f1last)
     weight_f[1] = f1
     ffn_parts[1], partial = feed_forward(normed_low, f1, ffn_b[1])
     fed = both_cores(links, partial)
@@ -806,17 +891,16 @@
         slopes = [part[1] for part in ffn_parts[layer]]
         grad_pre, pre_sums = ffn_back_first(upper_low, weight_f[layer], slopes)
         grad_pre = middle(grad_pre)
-        keep, give = weight_grads(
+        partial = call(back_out_kernel, thirds(upper.shape), (*grad_pre, *weight_f[layer]), name="up_back")
+        fed = both_cores(links, partial)
+        g0, g1, *_ = tie(*grad_pre, *partial)
+        grad_pre = [g0, g1]
+        grads = weight_grads(
             links,
             (normed_low, upper_low),
-            [(grad_pre[g], ffn_parts[layer][g][0]) for g in range(2)],
+            [((grad_pre[g],), (ffn_parts[layer][g][0],)) for g in range(2)],
         )
-        g0, g1, give = tie(*grad_pre, give)
-        grad_pre = [g0, g1]
-        came = links.swap_as("ffn%d_grad_far" % layer, links.swap_far, give)
-        partial = call(back_out_kernel, thirds(upper.shape), (*grad_pre, *weight_f[layer]), name="up_back")
-        vectors = (row_sums, pre_sums)
-        return upper, partial, (keep, came), vectors
+        return upper, fed, grads, (row_sums, pre_sums)
 
     def attn_back(layer, grad_parts, during):
         _, scaled_one, inv_one, _, _ = norms[layer]
@@ -824,146 +908,131 @@
         weight = weight_a[layer]
         shape = (lower.shape[0], third)
         dctx = call(context_grad_kernel, [(shape, BF16)] * 2, (lower_low, *weight), name="context_grad")
-        dq, own, sent = attend_half_back(limits, qkv[layer], far[layer], dctx, lse[layer], layer)
+        dq, own, sent = attend_half_back(limits, qkv[layer], far[layer], dctx, lse[layer][1], layer)
         d0, d1, sent = tie(*dctx, sent)
         came = links.swap_as("keys_values_grad", links.swap_x, sent)
-        dqkv = attend_full_back(limits, qkv[layer], (d0, d1), lse[layer])
+        dqkv = attend_full_back(limits, qkv[layer], (d0, d1), lse[layer][0])
         dqkv, came = during(dqkv, came)
-        dqkv = fill_half(dqkv, dq, own, came)
-        keep, give = weight_grads(links, (in_low[layer], lower_low), [(dqkv[g], ctx[layer][g]) for g in range(2)])
-        d0, d1, give = tie(*dqkv, give)
-        dqkv = [d0, d1]
-        came = links.swap_as("attn%d_grad_far" % layer, links.swap_far, give)
+        dqkv = (dqkv, fill_half(dq, own, came))
         *partial, sums = call(
             qkv_back_kernel,
             thirds(lower.shape) + [((16, 3 * third), F32)],
-            (*dqkv, *weight),
+            (*dqkv[0], *dqkv[1], *weight),
             name="qkv_back",
         )
-        vectors = (row_sums, sums)
-        return lower, partial, (keep, came), vectors
-
-    def first_sum(keep, came):
-        return keep.astype(F32) + came.astype(F32)
-
-    def near_swap(name, parts):
-        return parts[0], links.swap_as(name, links.swap_near, parts[1].astype(BF16))
-
-    def add(keep, came):
-        return keep + came.astype(F32)
+        fed = both_cores(links, partial)
+        d0, d1, *_ = tie(*dqkv[0], *partial)
+        dqkv = ([d0, d1], dqkv[1])
+        rights = [((dqkv[0][g], dqkv[1][g]), (ctx[layer][0][g], ctx[layer][1][g])) for g in range(2)]
+        grads = weight_grads(links, (in_low[layer], lower_low), rights)
+        return lower, fed, grads, (row_sums, sums)
+
+    def add(keep, *came):
+        total = keep.astype(F32)
+        for part in came:
+            total = total + part.astype(F32)
+        return total
+
+    def swap_far(name, give):
+        return links.swap_as(name + "_far", links.swap_far, give)
+
+    def swap_near(name, keep, came):
+        return links.swap_as(name + "_near", links.swap_near, add(keep, came).astype(BF16))
+
+    def scatter_z(name, parts, masks):
+        return links.swap_as(name, links.scatter_z, parts, masks)
 
     z_top, z_last = links.z_masks[:0:-1], z_one
+    state = {}
     vectors = [None, None]
+
     grad_top = own_rows(cotangent) * row_mask
-    upper, partial, (f1k, f1c), fvec = ffn_back(1, (grad_top,), lambda g: g)
-    fed = both_cores(links, partial)
+    encoded_low = low
+    piece = rows_first(low)
+    upper, fed, (f1k0, f1k1, f1g0, f1g1), fvec = ffn_back(1, (grad_top,), lambda g: g)
+    *fed, f1g0, f1g1, piece = tie(*fed, f1g0, f1g1, piece)
+    f1c1 = swap_far("ffn1_grad_1", f1g1)
+    f1c0 = swap_far("ffn1_grad_0", f1g0)
+    twin = rows_second(piece)
 
     def during1(dqkv, kv):
-        d0, d1, kv, came = tie(*dqkv, kv, f1c)
-        state["f1"] = near_swap("ffn1_grad_near", first_sum(f1k, came))
+        d0, d1, kv, came = tie(*dqkv, kv, f1c1)
+        state["f1"] = swap_near("ffn1_grad", f1k1, came)
         return [d0, d1], kv
 
-    lower, partial, (a1k, a1c), avec = attn_back(1, (upper, *fed), during1)
+    lower, fed, (a1k0, a1k1, a1g0, a1g1), avec = attn_back(1, (upper, *fed), during1)
     vectors[1] = (fvec, avec)
-    fed = both_cores(links, partial)
-
-    def middle0(grad_pre):
-        g0, g1, came = tie(*grad_pre, state["f1"][1])
-        state["f1"] = links.swap_as("ffn1_grad_z1", links.scatter_z, add(state["f1"][0], came), z_top)
-        return [g0, g1]
-
-    upper, partial, (f0k, f0c), fvec = ffn_back(0, (lower, *fed), middle0)
-    fed = both_cores(links, partial)
+    *fed, a1g0, a1g1 = tie(*fed, a1g0, a1g1)
+    a1c1 = swap_far("attn1_grad_1", a1g1)
+    a1c0 = swap_far("attn1_grad_0", a1g0)
+
+    upper, fed, (f0k0, f0k1, f0g0, f0g1), fvec = ffn_back(0, (lower, *fed), lambda g: g)
+    *fed, f0g0, f0g1, a1c1, f1c0, f1near, twin = tie(*fed, f0g0, f0g1, a1c1, f1c0, state["f1"], twin)
+    state["a1"] = swap_near("attn1_grad", a1k1, a1c1)
+    state["f1"] = scatter_z("ffn1_grad_z1", add(f1k0, f1c0, f1near), z_top)
+    encoded = all_rows(encoded_low, piece, twin)
+    f0c1 = swap_far("ffn0_grad_1", f0g1)
+    f0c0 = swap_far("ffn0_grad_0", f0g0)
 
     def during0(dqkv, kv):
-        d0, d1, came = tie(*dqkv, a1c)
-        state["a1"] = near_swap("attn1_grad_near", first_sum(a1k, came))
-        d0, d1, f1_in, kv, came = tie(d0, d1, state["f1"][1], kv, f0c)
-        state["f1"] = links.swap_as("ffn1_grad_z2", links.scatter_z, add(state["f1"][0], f1_in), z_last)
-        state["f0"] = near_swap("ffn0_grad_near", first_sum(f0k, came))
+        d0, d1, kv, f1_in, came, far, near = tie(*dqkv, kv, state["f1"][1], f0c1, a1c0, state["a1"])
+        state["f0"] = swap_near("ffn0_grad", f0k1, came)
+        state["a1"] = scatter_z("attn1_grad_z1", add(a1k0, far, near), z_top)
+        state["f1"] = scatter_z("ffn1_grad_z2", add(state["f1"][0], f1_in), z_last)
         return [d0, d1], kv
 
-    lower, partial, (a0k, a0c), avec = attn_back(0, (upper, *fed), during0)
+    lower, fed, (a0k0, a0k1, a0g0, a0g1), avec = attn_back(0, (upper, *fed), during0)
     vectors[0] = (fvec, avec)
-    *partial, came = tie(*partial, state["a1"][1])
-    a1s = links.swap_as("attn1_grad_z1", links.scatter_z, add(state["a1"][0], came), z_top)
-    fed = both_cores(links, partial)
+    *fed, a0g0, a0g1, a1_in = tie(*fed, a0g0, a0g1, state["a1"][1])
+    a1s = scatter_z("attn1_grad_z2", add(state["a1"][0], a1_in), z_last)
+    a0c1 = swap_far("attn0_grad_1", a0g1)
+    a0c0 = swap_far("attn0_grad_0", a0g0)
     grad_hidden = call(final_sum_kernel, [(lower.shape, BF16)], (lower, *fed), name="input_grad")[0]
-
-    own, other = [], []
-    for f, a in vectors:
-        for g, into in enumerate((own, other)):
-            heads = jnp.sum(a[1][8 * g : 8 * (g + 1)], axis=0)
-            into += [heads[:third], heads[2 * third :], jnp.sum(f[1][8 * g : 8 * (g + 1)], axis=0)]
-    own, other = jnp.concatenate(own), jnp.concatenate(other)
-    rows = []
-    for f, a in vectors:
-        upper_sums = jnp.sum(f[0].reshape(3, 8, -1), axis=1)
-        lower_sums = jnp.sum(a[0].reshape(3, 8, -1), axis=1)
-        rows += [lower_sums[0], upper_sums[0], lower_sums[1], lower_sums[2], upper_sums[1], upper_sums[2]]
-    rows = jnp.concatenate(rows)
-    vector, given = (jnp.concatenate([part, rows]).reshape(-1, 128) for part in (own, other))
-
-    grad_hidden, given, f1_in, f0_in = tie(grad_hidden, given, state["f1"][1], state["f0"][1])
-    f1s = add(state["f1"][0], f1_in)[0]
-    f0s = links.swap_as("ffn0_grad_z1", links.scatter_z, add(state["f0"][0], f0_in), z_top)
+    sums = [part for f, a in vectors for part in (*f, *a)]
+    vector, given = call(pack_kernel, [((8 * LAYERS, inputs.shape[1]), F32)] * 2, sums, name="vector_grads")
+
+    attn_splits = ([(k * third, (k + 1) * third) for k in range(3)], [(3 * third, 4 * third)])
+    ffn_splits = ([(0, wide)], [(wide, 2 * wide)])
+    params = (attn_in, attn_out, ffn_up, ffn_down, head_bias, ffn_bias, row_params)
+    states = [(params[i], moments[i], seconds[i]) for i in range(7)]
+
+    attn_splits = ([(k * third, (k + 1) * third) for k in range(3)], [(3 * third, 4 * third)])
+    ffn_splits = ([(0, wide)], [(wide, 2 * wide)])
+    params = (attn_in, attn_out, ffn_up, ffn_down, head_bias, ffn_bias, row_params)
+    states = [(params[i], moments[i], seconds[i]) for i in range(7)]
+
+    grad_hidden, given, f0c0, f0near, f1_in = tie(grad_hidden, given, f0c0, state["f0"], state["f1"][1])
+    f0s = scatter_z("ffn0_grad_z1", add(f0k0, f0c0, f0near), z_top)
     v_in = links.swap_as("vectors_x", links.swap_x, given)
-    came, v_in, grad_hidden, low = tie(a0c, v_in, grad_hidden, low)
-    a0s = near_swap("attn0_grad_near", first_sum(a0k, came))
+    came, a0c0, v_in, a1_in = tie(a0c1, a0c0, v_in, a1s[1])
+    a0near = swap_near("attn0_grad", a0k1, came)
     vector = vector + v_in
+    grad_hidden, vector, f1s, a1s0 = tie(grad_hidden, vector, state["f1"][0], a1s[0])
+    piece = rows_first(grad_hidden)
+    ffn_new = adam_layer(1, ffn_splits, f1s, f1_in, states[2:4], None)
+    attn_new = adam_layer(1, attn_splits, a1s0, a1_in, states[:2], None)
+    a0near, vector, ffn_new[0], attn_new[0] = tie(a0near, vector, ffn_new[0], attn_new[0])
+    a0s = scatter_z("attn0_grad_z1", add(a0k0, a0c0, a0near), z_top)
     v_in = links.swap_as("vectors_y", links.swap, vector, 4)
-    piece = rows_first(jnp.stack([grad_hidden, low], axis=1))
-    came, v_in, a1_in = tie(a0s[1], v_in, a1s[1])
-    a0s = links.swap_as("attn0_grad_z1", links.scatter_z, add(a0s[0], came), z_top)
-    a1s = links.swap_as("attn1_grad_z2", links.scatter_z, add(a1s[0], a1_in), z_last)
+    f0_in, v_in, encoded = tie(f0s[1], v_in, encoded)
+    f0s = scatter_z("ffn0_grad_z2", add(f0s[0], f0_in), z_last)
     vector = vector + v_in
     v_in = links.swap_as("vectors_z", links.swap_z, vector, links.z_masks[0])
-    piece, v_in, f0_in = tie(piece, v_in, f0s[1])
+    came, piece, v_in = tie(a0s[1], piece, v_in)
+    a0s = scatter_z("attn0_grad_z2", add(a0s[0], came), z_last)
     twin = rows_second(piece)
     vector = vector + v_in
-    f0s = links.swap_as("ffn0_grad_z2", links.scatter_z, add(f0s[0], f0_in), z_last)
     for mask in links.z_masks[1:]:
         vector = vector + links.swap_as("vectors_z", links.swap_z, vector, mask)
-    twin, came, a1_in = tie(twin, a0s[1], a1s[1])
-    a0s = links.swap_as("attn0_grad_z2", links.scatter_z, add(a0s[0], came), z_last)
-    a1s = add(a1s[0], a1_in)[0]
-    input_grad = all_rows(grad_hidden, piece[:, 0], twin[:, 0])
-    encoded = all_rows(low, piece[:, 1], twin[:, 1])
-    f0s = add(*f0s)[0]
-    a0s = add(*a0s)[0]
-
-    sums = vector.reshape(-1)
-    size = own.shape[0] // LAYERS
-    head_grad = jnp.stack([sums[i * size : i * size + 2 * third].reshape(2, third) for i in range(LAYERS)])
-    ffn_grad = jnp.stack([sums[i * size + 2 * third : (i + 1) * size] for i in range(LAYERS)])
-    row_grad = sums[LAYERS * size :].reshape(row_params.shape)
-
-    attn = jnp.stack([a0s, a1s])
-    ffn = jnp.stack([f0s, f1s])
-    gradients = (
-        jnp.stack([attn[:, :, k * third : (k + 1) * third] for k in range(3)], axis=1),
-        attn[:, :, 3 * third :],
-        ffn[:, :, :wide],
-        ffn[:, :, wide:],
-        head_grad,
-        ffn_grad,
-        row_grad,
-    )
-    params = (attn_in, attn_out, ffn_up, ffn_down, head_bias, ffn_bias, row_params)
-    stepped = [
-        adam_step(
-            params[i],
-            moments[i],
-            seconds[i],
-            gradients[i],
-            RATE_MATRIX if i < 4 else RATE_VECTOR,
-            DECAY_MATRIX if i < 4 else 0.0,
-        )
-        for i in range(7)
-    ]
-    news, moms, vars_ = zip(*stepped)
-    copies = tuple(news[i].astype(BF16) for i in range(4))
-    return (encoded, input_grad) + news + moms + vars_ + copies
+    ffn_new = adam_layer(0, ffn_splits, f0s[0], f0s[1], states[2:4], ffn_new)
+    input_grad = all_rows(grad_hidden, piece, twin)
+    flat = [a for state in states[4:] for a in state]
+    vector_new = call(vector_adam_kernel, [(a.shape, F32) for a in flat], (vector, *flat), name="vector_adam")
+    a0_in, input_grad = tie(a0s[1], input_grad)
+    attn_new = adam_layer(0, attn_splits, a0s[0], a0_in, states[:2], attn_new)
+
+    new = [attn_new[:4], attn_new[4:], ffn_new[:4], ffn_new[4:]] + [vector_new[3 * i : 3 * i + 3] for i in range(3)]
+    return (encoded, input_grad) + tuple(new[i][k] for k in range(3) for i in range(7)) + tuple(n[3] for n in new[:4])
 
 
 def solution(mesh):

time: 468 us -> 411 us (0.88)
  local copies, waits for them, and re-layouts: 80.3 us -> 42.6 us
  other arithmetic: 42.7 us -> 8.98 us
  Pallas kernels: 123 us -> 135 us
    unnamed x320 -> x256, local copies, waits for them, and re-layouts: 51.2 us -> 33.4 us
    pallas_call x37 -> x45, Pallas kernels: 115 us -> 129 us  [call(): pl.pallas_call(kernel, out_shape=[jax.ShapeDtypeStruct(s, d) for s, d in...]
    add x16 -> x8, other arithmetic: 13.4 us -> 1.63 us  [add(): total = total + part.astype(F32)]
    slice x10 -> x0, local copies, waits for them, and re-layouts: 6.72 us -> none  [the longest x4 3.03 us: local(): heads[2 * third:]]
    convert_element_type x7 -> x4, other arithmetic: 7.54 us -> 1.19 us  [swap_near(): add(keep, came).astype(BF16)]
    concatenate x2 -> x0, other arithmetic: 4.98 us -> none  [all_rows(): jnp.concatenate([jnp.where(first, low[:seq_len], other[:seq_len]), jnp.wh...]
    ppermute x64 -> x74, waiting for transfers between devices: 153 us -> 157 us  [swap(): return lax.ppermute(array, AXES, pairs)]
    ppermute x64 -> x74, starting transfers between devices: 58.7 us -> 57.8 us  [swap(): return lax.ppermute(array, AXES, pairs)]
  transfers between devices with their start and end apart: 64 -> 74, of which waited for: 31 -> 38; matrix products, arithmetic and copies ran while one was open for 15% -> 5% of each run, Pallas kernels for 22% -> 30%
where the time goes in v4:
time: 411 us; the launch traced here: 407 us
  waiting for transfers between devices  157 us (38%)
  Pallas kernels  135 us (33%)
  starting transfers between devices  57.8 us (14%)
  local copies, waits for them, and re-layouts  42.6 us (10%)
  other arithmetic  8.98 us (2%)
  between operations  5.61 us (1%)
    ppermute x74, waiting for transfers between devices, swap(): return lax.ppermute(array, AXES, pairs)  157 us
    pallas_call x45, Pallas kernels, call(): pl.pallas_call(kernel, out_shape=[jax.ShapeDtypeStruct(s, d) for s, d in...  129 us
    ppermute x74, starting transfers between devices, swap(): return lax.ppermute(array, AXES, pairs)  57.8 us
    unnamed x256, local copies, waits for them, and re-layouts  33.4 us
  transfers between devices with their start and end apart: 74, of which 38 were waited for; matrix products, arithmetic and copies ran while one was open for 5% of the time, Pallas kernels for 30%

profile of v4, /device:TPU:0, one launch (start us, length us, event | category | flops | bytes accessed | tf_op | source)
XLA Modules:
  0.0 407.3 jit_solution(8095100762856501217)
XLA Ops:
  2.1 4.1 %collective-permute-start = (bf16[1,96,768]{2,1,0:T(8,128)(2,1)S(1)}, bf16[1,96,768]{2,1,0:T(8,128)(2,1)S(1)}, u32[]{:S(2)}, u32[]{:S(2)}) collective-permute-start(bf16[1,96,768]{2,1,0:T(8,128)(2,1)S(1)} %maximum_bitcast_fusion.2), channel_id=1, source_target_pairs={{0,16},{1,17},{2,18},{3,19},{4,20},{5,21},{6,22},{7,23},{8,24},{9,... | collective-permute-start | bytes 442376 | tf_op jit(solution)/shard_map/attn0_z2/ppermute | solution.py:56
  7.5 5.7 %collective-permute-done = bf16[1,96,768]{2,1,0:T(8,128)(2,1)S(1)} collective-permute-done((bf16[1,96,768]{2,1,0:T(8,128)(2,1)S(1)}, bf16[1,96,768]{2,1,0:T(8,128)(2,1)S(1)}, u32[]{:S(2)}, u32[]{:S(2)}) %collective-permute-start) | collective-permute-done | bytes 147488 | tf_op jit(solution)/shard_map/attn0_z2/ppermute | solution.py:56
  22.7 4.8 %collective-permute-done.1 = bf16[2,96,768]{2,1,0:T(8,128)(2,1)S(1)} collective-permute-done((bf16[2,96,768]{2,1,0:T(8,128)(2,1)S(1)}, bf16[2,96,768]{2,1,0:T(8,128)(2,1)S(1)}, u32[]{:S(2)}, u32[]{:S(2)}) %collective-permute-start.1) | collective-permute-done | bytes 294944 | tf_op jit(solution)/shard_map/attn0_z1/ppermute | solution.py:56
  37.6 7.5 %collective-permute-done.4 = f32[2304]{0:T(1024)S(1)} collective-permute-done((f32[2304]{0:T(1024)S(1)}, f32[2304]{0:T(1024)S(1)}, u32[]{:S(2)}, u32[]{:S(2)}) %collective-permute-start.4) | collective-permute-done | bytes 9248 | tf_op jit(solution)/shard_map/biases/ppermute | solution.py:56
  51.2 6.3 %collective-permute-done.6.far_near = bf16[4,96,768]{2,1,0:T(8,128)(2,1)S(1)} collective-permute-done((bf16[4,96,768]{2,1,0:T(8,128)(2,1)S(1)}, bf16[4,96,768]{2,1,0:T(8,128)(2,1)S(1)}, u32[]{:S(2)}, u32[]{:S(2)}) %collective-permute-start.6) | collective-permute-done | bytes 589856 | tf_op jit(solution)/shard_map/attn0_far_near/ppermute | solution.py:56
  71.6 6.6 %attend_full.2 = (bf16[512,192]{1,0:T(8,128)(2,1)S(1)}, bf16[512,192]{1,0:T(8,128)(2,1)S(1)}, f32[6,512]{1,0:T(8,128)S(1)}) custom-call(s32[3]{0:T(128)S(1)} %pad_add_fusion.1.limits, bf16[768,576]{1,0:T(8,128)(2,1)S(1)} %get-tuple-element.334.qkv0, bf16[768,576]{1,0:T(8,128)(2,1)S(1)} %get-tuple-element.335.qkv1), custom_call_target="tpu_custom_call" | custom-call | flops 1 | bytes 1 | tf_op jit(solution)/shard_map/attend_full/pallas_call | solution.py:298
  78.3 10.1 %collective-permute-done.8.near = bf16[4,96,1536]{2,1,0:T(8,128)(2,1)} collective-permute-done((bf16[4,96,1536]{2,1,0:T(8,128)(2,1)}, bf16[4,96,1536]{2,1,0:T(8,128)(2,1)}, u32[]{:S(2)}, u32[]{:S(2)}) %collective-permute-start.8) | collective-permute-done | bytes 1179680 | tf_op jit(solution)/shard_map/ffn0_near/ppermute | solution.py:56
  111.2 6.4 %feed_forward.2 = (bf16[768,768]{1,0:T(8,128)(2,1)S(1)}, bf16[768,768]{1,0:T(8,128)(2,1)S(1)}, f32[768,768]{1,0:T(8,128)S(1)}, f32[768,768]{1,0:T(8,128)S(1)}, b...) custom-call(bf16[768,768]{1,0:T(8,128)(2,1)S(1)} %get-tuple-element.353.low.refs_0_, ...), custom_call_target="tpu_custom_call" | custom-call | flops 1 | bytes 1 | tf_op jit(solution)/shard_map/feed_forward/pallas_call | solution.py:298
  131.7 9.2 %collective-permute-done.21.far_near = bf16[4,96,768]{2,1,0:T(8,128)(2,1)S(1)} collective-permute-done((bf16[4,96,768]{2,1,0:T(8,128)(2,1)S(1)}, bf16[4,96,768]{2,1,0:T(8,128)(2,1)S(1)}, u32[]{:S(2)}, u32[]{:S(2)}) %collective-permute-start.21) | collective-permute-done | bytes 589856 | tf_op jit(solution)/shard_map/attn1_far_near/ppermute | solution.py:56
  147.0 6.6 %attend_full.3 = (bf16[512,192]{1,0:T(8,128)(2,1)S(1)}, bf16[512,192]{1,0:T(8,128)(2,1)S(1)}, f32[6,512]{1,0:T(8,128)S(1)}) custom-call(s32[3]{0:T(128)S(1)} %pad_add_fusion.1.limits, bf16[768,576]{1,0:T(8,128)(2,1)S(1)} %get-tuple-element.371.qkv0, bf16[768,576]{1,0:T(8,128)(2,1)S(1)} %get-tuple-element.372.qkv1), custom_call_target="tpu_custom_call" | custom-call | flops 1 | bytes 1 | tf_op jit(solution)/shard_map/attend_full/pallas_call | solution.py:298
  156.6 19.9 %collective-permute-done.22.far = bf16[256,768]{1,0:T(8,128)(2,1)S(1)} collective-permute-done((bf16[256,768]{1,0:T(8,128)(2,1)S(1)}, bf16[256,768]{1,0:T(8,128)(2,1)S(1)}, u32[]{:S(2)}, u32[]{:S(2)}) %collective-permute-start.22) | collective-permute-done | bytes 393248 | tf_op jit(solution)/shard_map/keys_values/ppermute | solution.py:56
  198.1 6.5 %feed_forward.3 = (bf16[768,768]{1,0:T(8,128)(2,1)S(1)}, bf16[768,768]{1,0:T(8,128)(2,1)S(1)}, f32[768,768]{1,0:T(8,128)S(1)}, f32[768,768]{1,0:T(8,128)S(1)}, b...) custom-call(bf16[768,768]{1,0:T(8,128)(2,1)S(1)} %get-tuple-element.388.low.refs_0_, ...), custom_call_target="tpu_custom_call" | custom-call | flops 1 | bytes 1 | tf_op jit(solution)/shard_map/feed_forward/pallas_call | solution.py:298
  207.5 4.1 add_norm.7
  220.2 4.9 %weight_grads.4 = (bf16[4,96,1536]{2,1,0:T(8,128)(2,1)S(1)}, bf16[4,96,1536]{2,1,0:T(8,128)(2,1)S(1)}, bf16[4,96,1536]{2,1,0:T(8,128)(2,1)S(1)}, bf16[4,96,1536]{2,1,0:T(8,128)(2,1)S(1)}) custom-call(s32[4]{0:T(128)S(1)} %pad_add_fusion.places, bf16[768,768]{1,0:T(8,128)(2,1)S(1)} %get-tuple-element.388.low.refs_0_, ...), custom_call_target="tpu_custom_call" | custom-call | flops 1 | bytes 1 | tf_op jit(solution)/shard_map/weight_grads/pallas_call | solution.py:298
  238.8 7.0 %attend_full_back.2 = (bf16[512,576]{1,0:T(8,128)(2,1)S(1)}, bf16[512,576]{1,0:T(8,128)(2,1)S(1)}) custom-call(s32[3]{0:T(128)S(1)} %pad_add_fusion.1.limits, bf16[768,576]{1,0:T(8,128)(2,1)S(1)} %copy-done.14, bf16[768,576]{1,0:T(8,128)(2,1)S(1)} %copy-done.17, bf16[768,192]{1,0:T(8,128)(2,1)S(1)} %get-tuple-element.429.dctx0, ...), custom_call_target="tpu_custom_call" | custom-call | flops 1 | bytes 1 | tf_op jit(solution)/shard_map/attend_full_back/pallas_call | solution.py:298
  245.7 6.0 %collective-permute-done.36.came = bf16[256,768]{1,0:T(8,128)(2,1)S(1)} collective-permute-done((bf16[256,768]{1,0:T(8,128)(2,1)S(1)}, bf16[256,768]{1,0:T(8,128)(2,1)S(1)}, u32[]{:S(2)}, u32[]{:S(2)}) %collective-permute-start.36) | collective-permute-done | bytes 393248 | tf_op jit(solution)/shard_map/keys_values_grad/ppermute | solution.py:56
  271.1 4.9 %weight_grads.6 = (bf16[4,96,1536]{2,1,0:T(8,128)(2,1)S(1)}, bf16[4,96,1536]{2,1,0:T(8,128)(2,1)S(1)}, bf16[4,96,1536]{2,1,0:T(8,128)(2,1)S(1)}, bf16[4,96,1536]{2,1,0:T(8,128)(2,1)S(1)}) custom-call(s32[4]{0:T(128)S(1)} %pad_add_fusion.places, bf16[768,768]{1,0:T(8,128)(2,1)S(1)} %copy-done.28, bf16[768,768]{1,0:T(8,128)(2,1)S(1)} %get-tuple-element.459.low.refs_1_, ...), custom_call_target="tpu_custom_call" | custom-call | flops 1 | bytes 1 | tf_op jit(solution)/shard_map/weight_grads/pallas_call | solution.py:298
  277.6 5.7 %collective-permute-done.44 = bf16[4,96,768]{2,1,0:T(8,128)(2,1)S(1)} collective-permute-done((bf16[4,96,768]{2,1,0:T(8,128)(2,1)S(1)}, bf16[4,96,768]{2,1,0:T(8,128)(2,1)S(1)}, u32[]{:S(2)}, u32[]{:S(2)}) %collective-permute-start.44) | collective-permute-done | bytes 589856 | tf_op jit(solution)/shard_map/attn1_grad_1_far/ppermute | solution.py:56
  295.8 6.9 %attend_full_back.3 = (bf16[512,576]{1,0:T(8,128)(2,1)S(1)}, bf16[512,576]{1,0:T(8,128)(2,1)S(1)}) custom-call(s32[3]{0:T(128)S(1)} %pad_add_fusion.1.limits, bf16[768,576]{1,0:T(8,128)(2,1)S(1)} %copy-done.9, bf16[768,576]{1,0:T(8,128)(2,1)S(1)} %copy-done.11, bf16[768,192]{1,0:T(8,128)(2,1)S(1)} %get-tuple-element.494.dctx0, ...), custom_call_target="tpu_custom_call" | custom-call | flops 1 | bytes 1 | tf_op jit(solution)/shard_map/attend_full_back/pallas_call | solution.py:298
  304.3 12.7 %collective-permute-done.48.came = bf16[256,768]{1,0:T(8,128)(2,1)S(1)} collective-permute-done((bf16[256,768]{1,0:T(8,128)(2,1)S(1)}, bf16[256,768]{1,0:T(8,128)(2,1)S(1)}, u32[]{:S(2)}, u32[]{:S(2)}) %collective-permute-start.48) | collective-permute-done | bytes 393248 | tf_op jit(solution)/shard_map/keys_values_grad/ppermute | solution.py:56
  335.0 14.0 %collective-permute-done.59.refs_1_ = bf16[1,96,1536]{2,1,0:T(8,128)(2,1)S(1)} collective-permute-done((bf16[1,96,1536]{2,1,0:T(8,128)(2,1)S(1)}, bf16[1,96,1536]{2,1,0:T(8,128)(2,1)S(1)}, u32[]{:S(2)}, u32[]{:S(2)}) %collective-permute-start.59) | collective-permute-done | bytes 294944 | tf_op jit(solution)/shard_map/ffn1_grad_z2/ppermute | solution.py:56
  374.8 4.8 %collective-permute-done.69 = f32[16,768]{1,0:T(8,128)S(1)} collective-permute-done((f32[16,768]{1,0:T(8,128)S(1)}, f32[16,768]{1,0:T(8,128)S(1)}, u32[]{:S(2)}, u32[]{:S(2)}) %collective-permute-start.69) | collective-permute-done | bytes 49184 | tf_op jit(solution)/shard_map/vectors_z/ppermute | solution.py:56
  383.3 9.1 %collective-permute-done.73 = f32[16,768]{1,0:T(8,128)S(1)} collective-permute-done((f32[16,768]{1,0:T(8,128)S(1)}, f32[16,768]{1,0:T(8,128)S(1)}, u32[]{:S(2)}, u32[]{:S(2)}) %collective-permute-start.73) | collective-permute-done | bytes 49184 | tf_op jit(solution)/shard_map/vectors_z/ppermute | solution.py:56
  393.1 6.2 %collective-permute-done.72.refs_1_ = bf16[1,96,1536]{2,1,0:T(8,128)(2,1)S(1)} collective-permute-done((bf16[1,96,1536]{2,1,0:T(8,128)(2,1)S(1)}, bf16[1,96,1536]{2,1,0:T(8,128)(2,1)S(1)}, u32[]{:S(2)}, u32[]{:S(2)}) %collective-permute-start.72) | collective-permute-done | bytes 294944 | tf_op jit(solution)/shard_map/ffn0_grad_z2/ppermute | solution.py:56
  (521 shorter events, 221.8 us)
Async XLA Ops:
  59.2 29.2 %collective-permute-start.8 = (bf16[4,96,1536]{2,1,0:T(8,128)(2,1)}, bf16[4,96,1536]{2,1,0:T(8,128)(2,1)}, u32[]{:S(2)}, u32[]{:S(2)}) collective-permute-start(bf16[4,96,1536]{2,1,0:T(8,128)(2,1)} %constant_dynamic-update-slice_fusion.block), channel_id=1, source_target_pairs={{0,4},{1,3},{2,6},{3,1},{4,0},{5,7},{6,2},{7,5},{8,12},{9,11},{10,... | collective-permute-start | bytes 3538952 | tf_op jit(solution)/shard_map/ffn0_near/ppermute | solution.py:56
  61.5 33.8 %collective-permute-start.10 = (bf16[4,96,1536]{2,1,0:T(8,128)(2,1)}, bf16[4,96,1536]{2,1,0:T(8,128)(2,1)}, u32[]{:S(2)}, u32[]{:S(2)}) collective-permute-start(bf16[4,96,1536]{2,1,0:T(8,128)(2,1)} %constant_dynamic-update-slice_fusion.block), channel_id=1, source_target_pairs={{0,2},{1,5},{2,0},{3,7},{4,6},{5,1},{6,4},{7,3},{8,10},{9,13},{10,... | collective-permute-start | bytes 3538952 | tf_op jit(solution)/shard_map/ffn0_far/ppermute | solution.py:56
  104.9 26.0 %collective-permute-start.19 = (bf16[4,96,768]{2,1,0:T(8,128)(2,1)S(1)}, bf16[4,96,768]{2,1,0:T(8,128)(2,1)S(1)}, u32[]{:S(2)}, u32[]{:S(2)}) collective-permute-start(bf16[4,96,768]{2,1,0:T(8,128)(2,1)S(1)} %slice.294.block), channel_id=1, source_target_pairs={{0,4},{1,3},{2,6},{3,1},{4,0},{5,7},{6,2},{7,5},{8,12},{9,11},{10,... | collective-permute-start | bytes 1769480 | tf_op jit(solution)/shard_map/attn1_near/ppermute | solution.py:56
  106.5 24.5 %collective-permute-start.20 = (bf16[4,96,768]{2,1,0:T(8,128)(2,1)S(1)}, bf16[4,96,768]{2,1,0:T(8,128)(2,1)S(1)}, u32[]{:S(2)}, u32[]{:S(2)}) collective-permute-start(bf16[4,96,768]{2,1,0:T(8,128)(2,1)S(1)} %slice.294.block), channel_id=1, source_target_pairs={{0,2},{1,5},{2,0},{3,7},{4,6},{5,1},{6,4},{7,3},{8,10},{9,13},{10,... | collective-permute-start | bytes 1769480 | tf_op jit(solution)/shard_map/attn1_far/ppermute | solution.py:56
  140.9 36.3 %collective-permute-start.23 = (bf16[4,96,1536]{2,1,0:T(8,128)(2,1)S(1)}, bf16[4,96,1536]{2,1,0:T(8,128)(2,1)}, u32[]{:S(2)}, u32[]{:S(2)}) collective-permute-start(bf16[4,96,1536]{2,1,0:T(8,128)(2,1)S(1)} %slice.295.block), channel_id=1, source_target_pairs={{0,4},{1,3},{2,6},{3,1},{4,0},{5,7},{6,2},{7,5},{8,12},{9,11},{10,... | collective-permute-start | bytes 3538952 | tf_op jit(solution)/shard_map/ffn1_near/ppermute | solution.py:56
  141.4 35.8 %collective-permute-start.24 = (bf16[4,96,1536]{2,1,0:T(8,128)(2,1)S(1)}, bf16[4,96,1536]{2,1,0:T(8,128)(2,1)S(1)}, u32[]{:S(2)}, u32[]{:S(2)}) collective-permute-start(bf16[4,96,1536]{2,1,0:T(8,128)(2,1)S(1)} %slice.295.block), channel_id=1, source_target_pairs={{0,2},{1,5},{2,0},{3,7},{4,6},{5,1},{6,4},{7,3},{8,10},{9,13},{10,... | collective-permute-start | bytes 3538952 | tf_op jit(solution)/shard_map/ffn1_far/ppermute | solution.py:56
  145.4 31.1 %collective-permute-start.22 = (bf16[256,768]{1,0:T(8,128)(2,1)S(1)}, bf16[256,768]{1,0:T(8,128)(2,1)S(1)}, u32[]{:S(2)}, u32[]{:S(2)}) collective-permute-start(bf16[256,768]{1,0:T(8,128)(2,1)S(1)} %get-tuple-element.375), channel_id=1, source_target_pairs={{0,2},{1,3},{2,0},{3,1},{4,6},{5,7},{6,4},{7,5},{8,10},{9,11},{10,... | collective-permute-start | bytes 1179656 | tf_op jit(solution)/shard_map/keys_values/ppermute | solution.py:56
  227.1 24.6 %collective-permute-start.37 = (bf16[4,96,1536]{2,1,0:T(8,128)(2,1)S(1)}, bf16[4,96,1536]{2,1,0:T(8,128)(2,1)S(1)}, u32[]{:S(2)}, u32[]{:S(2)}) collective-permute-start(bf16[4,96,1536]{2,1,0:T(8,128)(2,1)S(1)} %get-tuple-element.435), channel_id=1, source_target_pairs={{0,2},{1,5},{2,0},{3,7},{4,6},{5,1},{6,4},{7,3},{8,10},{9,13},{10,... | collective-permute-start | bytes 3538952 | tf_op jit(solution)/shard_map/ffn1_grad_1_far/ppermute | solution.py:56
  237.3 33.8 %collective-permute-start.45 = (bf16[4,96,1536]{2,1,0:T(8,128)(2,1)S(1)}, bf16[4,96,1536]{2,1,0:T(8,128)(2,1)S(1)}, u32[]{:S(2)}, u32[]{:S(2)}) collective-permute-start(bf16[4,96,1536]{2,1,0:T(8,128)(2,1)S(1)} %get-tuple-element.476), channel_id=1, source_target_pairs={{0,2},{1,5},{2,0},{3,7},{4,6},{5,1},{6,4},{7,3},{8,10},{9,13},{10,... | collective-permute-start | bytes 3538952 | tf_op jit(solution)/shard_map/ffn1_grad_0_far/ppermute | solution.py:56
  254.5 28.9 %collective-permute-start.46 = (bf16[4,96,1536]{2,1,0:T(8,128)(2,1)S(1)}, bf16[4,96,1536]{2,1,0:T(8,128)(2,1)S(1)}, u32[]{:S(2)}, u32[]{:S(2)}) collective-permute-start(bf16[4,96,1536]{2,1,0:T(8,128)(2,1)S(1)} %add_convert_fusion.1), channel_id=1, source_target_pairs={{0,4},{1,3},{2,6},{3,1},{4,0},{5,7},{6,2},{7,5},{8,12},{9,11},{10,... | collective-permute-start | bytes 3538952 | tf_op jit(solution)/shard_map/ffn1_grad_near/ppermute | solution.py:56
  260.7 22.6 %collective-permute-start.44 = (bf16[4,96,768]{2,1,0:T(8,128)(2,1)S(1)}, bf16[4,96,768]{2,1,0:T(8,128)(2,1)S(1)}, u32[]{:S(2)}, u32[]{:S(2)}) collective-permute-start(bf16[4,96,768]{2,1,0:T(8,128)(2,1)S(1)} %get-tuple-element.475), channel_id=1, source_target_pairs={{0,2},{1,5},{2,0},{3,7},{4,6},{5,1},{6,4},{7,3},{8,10},{9,13},{10,... | collective-permute-start | bytes 1769480 | tf_op jit(solution)/shard_map/attn1_grad_1_far/ppermute | solution.py:56
  276.0 26.7 %collective-permute-start.51 = (bf16[4,96,768]{2,1,0:T(8,128)(2,1)S(1)}, bf16[4,96,768]{2,1,0:T(8,128)(2,1)S(1)}, u32[]{:S(2)}, u32[]{:S(2)}) collective-permute-start(bf16[4,96,768]{2,1,0:T(8,128)(2,1)S(1)} %get-tuple-element.504), channel_id=1, source_target_pairs={{0,2},{1,5},{2,0},{3,7},{4,6},{5,1},{6,4},{7,3},{8,10},{9,13},{10,... | collective-permute-start | bytes 1769480 | tf_op jit(solution)/shard_map/attn1_grad_0_far/ppermute | solution.py:56
  283.5 33.5 %collective-permute-start.52 = (bf16[4,96,768]{2,1,0:T(8,128)(2,1)S(1)}, bf16[4,96,768]{2,1,0:T(8,128)(2,1)S(1)}, u32[]{:S(2)}, u32[]{:S(2)}) collective-permute-start(bf16[4,96,768]{2,1,0:T(8,128)(2,1)S(1)} %add_convert_fusion.3), channel_id=1, source_target_pairs={{0,4},{1,3},{2,6},{3,1},{4,0},{5,7},{6,2},{7,5},{8,12},{9,11},{10,... | collective-permute-start | bytes 1769480 | tf_op jit(solution)/shard_map/attn1_grad_near/ppermute | solution.py:56
  284.1 33.0 %collective-permute-start.50 = (bf16[4,96,1536]{2,1,0:T(8,128)(2,1)S(1)}, bf16[4,96,1536]{2,1,0:T(8,128)(2,1)S(1)}, u32[]{:S(2)}, u32[]{:S(2)}) collective-permute-start(bf16[4,96,1536]{2,1,0:T(8,128)(2,1)S(1)} %get-tuple-element.503), channel_id=1, source_target_pairs={{0,2},{1,5},{2,0},{3,7},{4,6},{5,1},{6,4},{7,3},{8,10},{9,13},{10,... | collective-permute-start | bytes 3538952 | tf_op jit(solution)/shard_map/ffn0_grad_1_far/ppermute | solution.py:56
  286.1 30.9 %collective-permute-start.49 = (bf16[2,96,1536]{2,1,0:T(8,128)(2,1)S(1)}, bf16[2,96,1536]{2,1,0:T(8,128)(2,1)S(1)}, u32[]{:S(2)}, u32[]{:S(2)}) collective-permute-start(bf16[2,96,1536]{2,1,0:T(8,128)(2,1)S(1)} %slice.352), channel_id=1, source_target_pairs={{0,8},{1,9},{2,10},{3,11},{4,12},{5,13},{6,14},{7,15},{8,0},{9,1},... | collective-permute-start | bytes 1769480 | tf_op jit(solution)/shard_map/ffn1_grad_z1/ppermute | solution.py:56
  295.2 21.8 %collective-permute-start.48 = (bf16[256,768]{1,0:T(8,128)(2,1)S(1)}, bf16[256,768]{1,0:T(8,128)(2,1)S(1)}, u32[]{:S(2)}, u32[]{:S(2)}) collective-permute-start(bf16[256,768]{1,0:T(8,128)(2,1)S(1)} %get-tuple-element.499), channel_id=1, source_target_pairs={{0,2},{1,3},{2,0},{3,1},{4,6},{5,7},{6,4},{7,5},{8,10},{9,11},{10,... | collective-permute-start | bytes 1179656 | tf_op jit(solution)/shard_map/keys_values_grad/ppermute | solution.py:56
  302.7 31.6 %collective-permute-start.57 = (bf16[4,96,1536]{2,1,0:T(8,128)(2,1)S(1)}, bf16[4,96,1536]{2,1,0:T(8,128)(2,1)S(1)}, u32[]{:S(2)}, u32[]{:S(2)}) collective-permute-start(bf16[4,96,1536]{2,1,0:T(8,128)(2,1)S(1)} %get-tuple-element.540), channel_id=1, source_target_pairs={{0,2},{1,5},{2,0},{3,7},{4,6},{5,1},{6,4},{7,3},{8,10},{9,13},{10,... | collective-permute-start | bytes 3538952 | tf_op jit(solution)/shard_map/ffn0_grad_0_far/ppermute | solution.py:56
  324.1 26.9 %collective-permute-start.58 = (bf16[4,96,1536]{2,1,0:T(8,128)(2,1)S(1)}, bf16[4,96,1536]{2,1,0:T(8,128)(2,1)S(1)}, u32[]{:S(2)}, u32[]{:S(2)}) collective-permute-start(bf16[4,96,1536]{2,1,0:T(8,128)(2,1)S(1)} %add_convert_fusion), channel_id=1, source_target_pairs={{0,4},{1,3},{2,6},{3,1},{4,0},{5,7},{6,2},{7,5},{8,12},{9,11},{10,... | collective-permute-start | bytes 3538952 | tf_op jit(solution)/shard_map/ffn0_grad_near/ppermute | solution.py:56
  328.3 24.8 %collective-permute-start.61 = (bf16[4,96,768]{2,1,0:T(8,128)(2,1)S(1)}, bf16[4,96,768]{2,1,0:T(8,128)(2,1)S(1)}, u32[]{:S(2)}, u32[]{:S(2)}) collective-permute-start(bf16[4,96,768]{2,1,0:T(8,128)(2,1)S(1)} %get-tuple-element.547), channel_id=1, source_target_pairs={{0,2},{1,5},{2,0},{3,7},{4,6},{5,1},{6,4},{7,3},{8,10},{9,13},{10,... | collective-permute-start | bytes 1769480 | tf_op jit(solution)/shard_map/attn0_grad_1_far/ppermute | solution.py:56
  329.9 25.5 %collective-permute-start.62 = (bf16[4,96,768]{2,1,0:T(8,128)(2,1)S(1)}, bf16[4,96,768]{2,1,0:T(8,128)(2,1)S(1)}, u32[]{:S(2)}, u32[]{:S(2)}) collective-permute-start(bf16[4,96,768]{2,1,0:T(8,128)(2,1)S(1)} %get-tuple-element.548), channel_id=1, source_target_pairs={{0,2},{1,5},{2,0},{3,7},{4,6},{5,1},{6,4},{7,3},{8,10},{9,13},{10,... | collective-permute-start | bytes 1769480 | tf_op jit(solution)/shard_map/attn0_grad_0_far/ppermute | solution.py:56
  334.4 18.8 %collective-permute-start.64 = (bf16[1,96,768]{2,1,0:T(8,128)(2,1)S(1)}, bf16[1,96,768]{2,1,0:T(8,128)(2,1)S(1)}, u32[]{:S(2)}, u32[]{:S(2)}) collective-permute-start(bf16[1,96,768]{2,1,0:T(8,128)(2,1)S(1)} %slice.358), channel_id=1, source_target_pairs={{0,16},{1,17},{2,18},{3,19},{4,20},{5,21},{6,22},{7,23},{8,24},{9,... | collective-permute-start | bytes 442376 | tf_op jit(solution)/shard_map/attn1_grad_z2/ppermute | solution.py:56
  379.6 23.0 %collective-permute-start.71 = (bf16[384,768]{1,0:T(8,128)(2,1)S(1)}, bf16[384,768]{1,0:T(8,128)(2,1)S(1)}, u32[]{:S(2)}, u32[]{:S(2)}) collective-permute-start(bf16[384,768]{1,0:T(8,128)(2,1)S(1)} %collective-permute-done.68.piece), channel_id=1, source_target_pairs={{0,1},{1,0},{2,3},{3,2},{4,5},{5,4},{6,7},{7,6},{8,9},{9,8},{10,11... | collective-permute-start | bytes 1769480 | tf_op jit(solution)/shard_map/rows_core/ppermute | solution.py:56
  379.8 19.4 %collective-permute-start.72 = (bf16[1,96,1536]{2,1,0:T(8,128)(2,1)S(1)}, bf16[1,96,1536]{2,1,0:T(8,128)(2,1)S(1)}, u32[]{:S(2)}, u32[]{:S(2)}) collective-permute-start(bf16[1,96,1536]{2,1,0:T(8,128)(2,1)S(1)} %slice.353), channel_id=1, source_target_pairs={{0,16},{1,17},{2,18},{3,19},{4,20},{5,21},{6,22},{7,23},{8,24},{9,... | collective-permute-start | bytes 884744 | tf_op jit(solution)/shard_map/ffn0_grad_z2/ppermute | solution.py:56
  381.3 24.4 %collective-permute-start.70 = (bf16[1,96,768]{2,1,0:T(8,128)(2,1)S(1)}, bf16[1,96,768]{2,1,0:T(8,128)(2,1)S(1)}, u32[]{:S(2)}, u32[]{:S(2)}) collective-permute-start(bf16[1,96,768]{2,1,0:T(8,128)(2,1)S(1)} %slice.357), channel_id=1, source_target_pairs={{0,16},{1,17},{2,18},{3,19},{4,20},{5,21},{6,22},{7,23},{8,24},{9,... | collective-permute-start | bytes 442376 | tf_op jit(solution)/shard_map/attn0_grad_z2/ppermute | solution.py:56
  (173 other events, 1100.1 us)

commit v5 on v4

--- a/solution.py
+++ b/solution.py
@@ -23,6 +23,7 @@
 NN = ((1,), (0,))
 NT = ((1,), (1,))
 TN = ((0,), (0,))
+PARTS = 3
 
 
 def dot(a, b, dims):
@@ -76,24 +77,26 @@
 
     def last_z(self, block, masks):
         for mask in masks[:-1]:
-            block = jnp.concatenate([block, self.swap_z(block, mask)])
+            block = jnp.concatenate([block, self.swap_z(block, mask)], axis=-3)
         return block, self.swap_z(block, masks[-1])
 
     def scatter_z(self, parts, masks):
         for mask in masks[:-1]:
-            half = parts.shape[0] // 2
-            parts = parts[:half] + self.swap_z(parts[half:].astype(BF16), mask).astype(F32)
-        half = parts.shape[0] // 2
-        return parts[:half], self.swap_z(parts[half:].astype(BF16), masks[-1])
-
-    def assemble(self, block, near, far_block, far_near):
-        parts = (block, near, far_block, far_near)
+            half = parts.shape[-3] // 2
+            parts = parts[..., :half, :, :] + self.swap_z(parts[..., half:, :, :].astype(BF16), mask).astype(F32)
+        half = parts.shape[-3] // 2
+        return parts[..., :half, :, :], self.swap_z(parts[..., half:, :, :].astype(BF16), masks[-1])
+
+    def assemble(self, *parts):
         if self.aligned:
-            shape = (block.shape[0], 2) + block.shape[1:]
+            shape = parts[0].shape[-3:]
             kernel = functools.partial(assemble_kernel, self.order)
-            both = call(kernel, [(shape, block.dtype)] * 2, (self.places, *parts), name="assemble")
+            outs = [((shape[0], 2) + shape[1:], parts[0].dtype)] * 2
+            both = call(kernel, outs, (self.places, *parts), name="assemble")
         else:
-            order = jnp.array(inverse(self.order))[jnp.arange(block.shape[0]) ^ self.at_z]
+            if len(parts) == 2:
+                parts = [part[k] for part in parts for k in range(2)]
+            order = jnp.array(inverse(self.order))[jnp.arange(parts[0].shape[0]) ^ self.at_z]
             block, near, far_block, far_near = (jnp.take(part, order, axis=0) for part in parts)
             first, low = self.core == 0, self.at_y == 0
             own_far = jnp.where(first, near, far_block)
@@ -109,7 +112,11 @@
     return [order.index(place) for place in range(len(order))]
 
 
-def assemble_kernel(order, places, block, near, far_block, far_near, own, other):
+def assemble_kernel(order, places, *refs):
+    *parts, own, other = refs
+    if len(parts) == 2:
+        parts = [part.at[k] for part in parts for k in range(2)]
+    block, near, far_block, far_near = parts
     first, at_y, at_z = places[0] == 0, places[1], places[2]
     for m, distance in enumerate(order):
         j = distance ^ at_z
@@ -288,14 +295,15 @@
 
 
 VMEM = pl.BlockSpec(memory_space=pltpu.VMEM)
+ANY = pl.BlockSpec(memory_space=pl.ANY)
 SMEM = pl.BlockSpec(memory_space=pltpu.SMEM)
-ROOM = pltpu.CompilerParams(vmem_limit_bytes=16 * 1024 * 1024)
+ROOM = pltpu.CompilerParams(vmem_limit_bytes=8 * 1024 * 1024)
 CHEAP = pl.CostEstimate(flops=1, bytes_accessed=1, transcendentals=0)
 
 
-def call(kernel, outs, ins, scratch=(), name=None):
-    specs = [SMEM if a.dtype == jnp.int32 else VMEM for a in ins]
-    return pl.pallas_call(
+def call(kernel, outs, ins, scratch=(), name=None, place=VMEM):
+    specs = [SMEM if a.dtype == jnp.int32 else place for a in ins]
+    results = pl.pallas_call(
         kernel,
         out_shape=[jax.ShapeDtypeStruct(s, d) for s, d in outs],
         in_specs=specs,
@@ -305,6 +313,7 @@
         cost_estimate=CHEAP,
         name=name,
     )(*ins)
+    return list(results)
 
 
 def attend_full(limits, qkv):
@@ -417,19 +426,29 @@
     return (*parts, *[links.swap_as("core", links.swap_core, part) for part in parts])
 
 
-def thirds(shape):
-    return [((shape[0] // 3, shape[1]), BF16)] * 3
+def in_parts(shape):
+    return [((shape[0] // PARTS, shape[1]), BF16)] * PARTS
 
 
 def core_sum(parts, at, rows):
-    return parts[at][rows, :].astype(F32) + parts[at + 3][rows, :].astype(F32)
+    return parts[at][rows, :].astype(F32) + parts[at + PARTS][rows, :].astype(F32)
+
+
+def put_parts(outs, at, value):
+    step = outs[0].shape[0]
+    done = 0
+    while done < value.shape[0]:
+        part, inner = divmod(at + done, step)
+        count = min(step - inner, value.shape[0] - done)
+        outs[part][inner : inner + count, :] = value[done : done + count, :].astype(BF16)
+        done += count
 
 
 def norm_kernel(step, *refs):
-    parts, (residual, rows, out, low, scaled, inverse) = refs[:6], refs[6:]
+    parts, (residual, rows, out, low, scaled, inverse) = refs[: 2 * PARTS], refs[2 * PARTS :]
     wide = out.shape[1]
     third = parts[0].shape[0]
-    for part in range(3):
+    for part in range(PARTS):
 
         @pl.loop(0, third // step)
         def _(i, part=part):
@@ -459,9 +478,9 @@
 def norm_back_kernel(step, *refs):
     base, *parts, scaled, inverse, gain, out, low, sums = refs
     wide = out.shape[1]
-    third = out.shape[0] // 3
+    third = out.shape[0] // PARTS
     sums[...] = jnp.zeros_like(sums)
-    for part in range(3):
+    for part in range(PARTS):
 
         @pl.loop(0, third // step)
         def _(i, part=part):
@@ -491,9 +510,9 @@
 
 
 def final_sum_kernel(base, *refs):
-    parts, out = refs[:6], refs[6]
+    parts, out = refs[: 2 * PARTS], refs[2 * PARTS]
     third = parts[0].shape[0]
-    for part in range(3):
+    for part in range(PARTS):
         at = slice(part * third, (part + 1) * third)
         out[at, :] = (base[at, :] + core_sum(parts, part, slice(None))).astype(BF16)
 
@@ -542,14 +561,14 @@
     third = full0.shape[1]
     at = w0.shape[1] - third
     tails = (w0[:, at:], w1[:, at:])
-    for (pair, rows), out in zip(row_thirds(full0, full1, half0, half1), outs):
-        out[...] = (dot(pair[0][rows, :], tails[0], NT) + dot(pair[1][rows, :], tails[1], NT)).astype(BF16)
+    for k, (pair, rows) in enumerate(row_thirds(full0, full1, half0, half1)):
+        put_parts(outs, k * half0.shape[0], dot(pair[0][rows, :], tails[0], NT) + dot(pair[1][rows, :], tails[1], NT))
 
 
 def ffn_kernel(low, w0, w1, bias, act0, act1, slope0, slope1, *outs):
     wide = bias.shape[1]
     groups = ((w0, act0, slope0), (w1, act1, slope1))
-    for at, rows in enumerate(chunks(low.shape[0], 128)):
+    for rows in chunks(low.shape[0], 128):
         total = None
         for g, (weight, act, slope) in enumerate(groups):
             pre = dot(low[rows, :], weight[:, :wide], NN) + bias[g : g + 1, :]
@@ -559,15 +578,14 @@
             act[rows, :] = active
             part = dot(active, weight[:, wide:], NT)
             total = part if total is None else total + part
-        inner = slice(at % 2 * 128, (at % 2 + 1) * 128)
-        outs[at // 2][inner, :] = total.astype(BF16)
+        put_parts(outs, rows.start, total)
 
 
 def feed_forward(low, weights, bias):
     shape = (low.shape[0], bias.shape[1])
     act0, act1, slope0, slope1, *partial = call(
         ffn_kernel,
-        [(shape, BF16)] * 2 + [(shape, F32)] * 2 + thirds(low.shape),
+        [(shape, BF16)] * 2 + [(shape, F32)] * 2 + in_parts(low.shape),
         (low, *weights, bias),
         name="feed_forward",
     )
@@ -603,17 +621,17 @@
 
 def back_out_kernel(d0, d1, w0, w1, *outs):
     wide = d0.shape[1]
-    for rows, out in zip(chunks(d0.shape[0], outs[0].shape[0]), outs):
-        out[...] = (dot(d0[rows, :], w0[:, :wide], NT) + dot(d1[rows, :], w1[:, :wide], NT)).astype(BF16)
+    for rows in chunks(d0.shape[0]):
+        put_parts(outs, rows.start, dot(d0[rows, :], w0[:, :wide], NT) + dot(d1[rows, :], w1[:, :wide], NT))
 
 
 def qkv_back_kernel(full0, full1, half0, half1, w0, w1, *refs):
     *outs, sums = refs
     wide = full0.shape[1]
     totals = [None, None]
-    for (pair, rows), out in zip(row_thirds(full0, full1, half0, half1), outs):
+    for k, (pair, rows) in enumerate(row_thirds(full0, full1, half0, half1)):
         parts = [ref[rows, :] for ref in pair]
-        out[...] = (dot(parts[0], w0[:, :wide], NT) + dot(parts[1], w1[:, :wide], NT)).astype(BF16)
+        put_parts(outs, k * half0.shape[0], dot(parts[0], w0[:, :wide], NT) + dot(parts[1], w1[:, :wide], NT))
         for g in range(2):
             part = add_rows(parts[g])
             totals[g] = part if totals[g] is None else totals[g] + part
@@ -783,24 +801,31 @@
 
     a0 = packed_attn(0)
     a0_in = links.swap_as("attn0_z2", links.swap_z, a0, links.z_masks[0])
-    a0_in, f0, later = tie(a0_in, packed_ffn(0), join([packed_attn(1), packed_ffn(1)], axis=2))
+    later = join([packed_attn(1), packed_ffn(1)], axis=2)
+    biases = jnp.concatenate([head_bias.reshape(-1), ffn_bias.reshape(-1)])
+    a0_in, f0, later, biases = tie(a0_in, packed_ffn(0), later, biases)
     a0 = join([a0, a0_in])
     a0, a0_in = links.swap_as("attn0_z1", links.last_z, a0, z_rest)
     f0_in = links.swap_as("ffn0_z2", links.swap_z, f0, links.z_masks[0])
-    biases = jnp.concatenate([head_bias.reshape(-1), ffn_bias.reshape(-1)])
-    a0_in, f0_in, later, biases = tie(a0_in, f0_in, later, biases)
+    later_near = links.swap_as("layer1_near", links.swap_near, later)
+    bias_far = links.swap_as("biases", links.swap_x, biases)
+    a0_in, f0_in, later_near, bias_far = tie(a0_in, f0_in, later_near, bias_far)
     a0, f0 = join([a0, a0_in]), join([f0, f0_in])
-    bias_far = links.swap_as("biases", links.swap_x, biases)
     near = links.swap_as("attn0_near", links.swap_near, a0)
     a0far = links.swap_as("attn0_far", links.swap_far, a0)
     f0, f0_in = links.swap_as("ffn0_z1", links.last_z, f0, z_rest)
-    later_in = links.swap_as("layer1_z2", links.swap_z, later, links.z_masks[0])
-    near, bias_far = tie(near, bias_far)
+    later = jnp.stack([later, later_near])
+    a1, f1 = later[..., : 4 * third], later[..., 4 * third :]
+    a1_in = links.swap_as("attn1_z2", links.swap_z, a1, links.z_masks[0])
+    near, f1 = tie(near, f1)
     a0last = links.swap_as("attn0_far_near", links.swap_far, near)
-    a0far, a0last, f0_in = tie(a0far, a0last, f0_in)
+    a0far, a0last, f0_in, a1_in, f1 = tie(a0far, a0last, f0_in, a1_in, f1)
     f0 = join([f0, f0_in])
     f0near = links.swap_as("ffn0_near", links.swap_near, f0)
     f0far = links.swap_as("ffn0_far", links.swap_far, f0)
+    a1 = join([a1, a1_in], axis=1)
+    a1, a1_in = links.swap_as("attn1_z1", links.last_z, a1, z_rest)
+    f1_in = links.swap_as("ffn1_z2", links.swap_z, f1, links.z_masks[0])
     a0 = links.assemble(a0, near, a0far, a0last)
     head_b = (head_bias, bias_far[: head_bias.size].reshape(head_bias.shape))
     ffn_b = (ffn_bias, bias_far[head_bias.size :].reshape(ffn_bias.shape))
@@ -825,7 +850,7 @@
 
     def out_part(layer):
         return call(
-            out_kernel, thirds(hidden.shape), (*ctx[layer][0], *ctx[layer][1], *weight_a[layer]), name="attention_out"
+            out_kernel, in_parts(hidden.shape), (*ctx[layer][0], *ctx[layer][1], *weight_a[layer]), name="attention_out"
         )
 
     norms = [None] * 2
@@ -839,45 +864,41 @@
     ]
     qkv[0], far[0] = project(in_low[0], a0, qkv_b[0], low_other)
     whole, whole_lse = attend_full(limits, qkv[0])
-    *whole, f0near, later_in = tie(*whole, f0near, later_in)
+    *whole, f0near, a1_in, f1_in = tie(*whole, f0near, a1_in, f1_in)
     f0last = links.swap_as("ffn0_far_near", links.swap_far, f0near)
-    later = join([later, later_in])
-    later, later_in = links.swap_as("layer1_z1", links.last_z, later, z_rest)
+    a1 = join([a1, a1_in], axis=1)
+    f1 = join([f1, f1_in], axis=1)
+    f1, f1_in = links.swap_as("ffn1_z1", links.last_z, f1, z_rest)
     split, split_lse = attend_half(limits, qkv[0], far[0], 0)
     *split, f0far = tie(*split, f0far)
     ctx[0], lse[0] = (whole, split), (whole_lse, split_lse)
     normed, normed_low, scaled_one, inv_one = add_norm(both_cores(links, out_part(0)), hidden, row_parts[0][0])
-    normed_low, later_in, f0last = tie(normed_low, later_in, f0last)
-    later = join([later, later_in])
-    a1, f1 = later[:, :, : 4 * third], later[:, :, 4 * third :]
-    a1near = links.swap_as("attn1_near", links.swap_near, a1)
+    normed_low, f0last, a1 = tie(normed_low, f0last, a1)
     a1far = links.swap_as("attn1_far", links.swap_far, a1)
     f0 = links.assemble(f0, f0near, f0far, f0last)
     weight_f[0] = f0
     ffn_parts[0], partial = feed_forward(normed_low, f0, ffn_b[0])
+    *partial, a1far, f1_in = tie(*partial, a1far, f1_in)
+    f1_own, f1_near = join([f1[0], f1_in[0]]), join([f1[1], f1_in[1]])
+    f1far = links.swap_as("ffn1_far", links.swap_far, f1_own)
     fed = both_cores(links, partial)
     hidden, low, scaled_two, inv_two = add_norm(fed, normed, row_parts[0][1])
     norms[0] = (normed_low, scaled_one, inv_one, scaled_two, inv_two)
 
-    low, a1near, a1far = tie(low, a1near, a1far)
-    a1last = links.swap_as("attn1_far_near", links.swap_far, a1near)
-    low, a1last, f1 = tie(low, a1last, f1)
-    f1near = links.swap_as("ffn1_near", links.swap_near, f1)
-    f1far = links.swap_as("ffn1_far", links.swap_far, f1)
-    a1 = links.assemble(a1, a1near, a1far, a1last)
+    a1 = links.assemble(a1, a1far)
     weight_a[1] = a1
     in_low[1] = low
     qkv[1], sent = project(low, a1, qkv_b[1])
     far[1] = links.swap_as("keys_values", links.swap_x, sent)
     whole, whole_lse = attend_full(limits, qkv[1])
-    *whole, far[1], f1near, f1far = tie(*whole, far[1], f1near, f1far)
-    f1last = links.swap_as("ffn1_far_near", links.swap_far, f1near)
+    *whole, far[1], f1_near, f1far = tie(*whole, far[1], f1_near, f1far)
+    f1last = links.swap_as("ffn1_far_near", links.swap_far, f1_near)
     split, split_lse = attend_half(limits, qkv[1], far[1], 1)
     ctx[1], lse[1] = (whole, split), (whole_lse, split_lse)
     fed = both_cores(links, out_part(1))
     normed, normed_low, scaled_one, inv_one = add_norm(fed, hidden, row_parts[1][0])
     normed_low, f1last = tie(normed_low, f1last)
-    f1 = links.assemble(f1, f1near, f1far, f1last)
+    f1 = links.assemble(f1_own, f1_near, f1far, f1last)
     weight_f[1] = f1
     ffn_parts[1], partial = feed_forward(normed_low, f1, ffn_b[1])
     fed = both_cores(links, partial)
@@ -891,7 +912,7 @@
         slopes = [part[1] for part in ffn_parts[layer]]
         grad_pre, pre_sums = ffn_back_first(upper_low, weight_f[layer], slopes)
         grad_pre = middle(grad_pre)
-        partial = call(back_out_kernel, thirds(upper.shape), (*grad_pre, *weight_f[layer]), name="up_back")
+        partial = call(back_out_kernel, in_parts(upper.shape), (*grad_pre, *weight_f[layer]), name="up_back")
         fed = both_cores(links, partial)
         g0, g1, *_ = tie(*grad_pre, *partial)
         grad_pre = [g0, g1]
@@ -902,21 +923,22 @@
         )
         return upper, fed, grads, (row_sums, pre_sums)
 
-    def attn_back(layer, grad_parts, during):
+    def attn_back(layer, grad_parts, first, early, during):
         _, scaled_one, inv_one, _, _ = norms[layer]
         lower, lower_low, row_sums = norm_back(grad_parts, scaled_one, inv_one, row_params[layer, 2:3])
+        lower_low = first(lower_low)
         weight = weight_a[layer]
         shape = (lower.shape[0], third)
         dctx = call(context_grad_kernel, [(shape, BF16)] * 2, (lower_low, *weight), name="context_grad")
         dq, own, sent = attend_half_back(limits, qkv[layer], far[layer], dctx, lse[layer][1], layer)
-        d0, d1, sent = tie(*dctx, sent)
+        d0, d1, sent = early(*dctx, sent)
         came = links.swap_as("keys_values_grad", links.swap_x, sent)
         dqkv = attend_full_back(limits, qkv[layer], (d0, d1), lse[layer][0])
         dqkv, came = during(dqkv, came)
         dqkv = (dqkv, fill_half(dq, own, came))
         *partial, sums = call(
             qkv_back_kernel,
-            thirds(lower.shape) + [((16, 3 * third), F32)],
+            in_parts(lower.shape) + [((16, 3 * third), F32)],
             (*dqkv[0], *dqkv[1], *weight),
             name="qkv_back",
         )
@@ -952,45 +974,50 @@
     upper, fed, (f1k0, f1k1, f1g0, f1g1), fvec = ffn_back(1, (grad_top,), lambda g: g)
     *fed, f1g0, f1g1, piece = tie(*fed, f1g0, f1g1, piece)
     f1c1 = swap_far("ffn1_grad_1", f1g1)
-    f1c0 = swap_far("ffn1_grad_0", f1g0)
     twin = rows_second(piece)
 
     def during1(dqkv, kv):
-        d0, d1, kv, came = tie(*dqkv, kv, f1c1)
-        state["f1"] = swap_near("ffn1_grad", f1k1, came)
+        d0, d1, kv, state["f1_far_1"], given = tie(*dqkv, kv, f1c1, f1g0)
+        state["f1_far_0"] = swap_far("ffn1_grad_0", given)
         return [d0, d1], kv
 
-    lower, fed, (a1k0, a1k1, a1g0, a1g1), avec = attn_back(1, (upper, *fed), during1)
+    lower, fed, (a1k0, a1k1, a1g0, a1g1), avec = attn_back(1, (upper, *fed), lambda low: low, tie, during1)
     vectors[1] = (fvec, avec)
     *fed, a1g0, a1g1 = tie(*fed, a1g0, a1g1)
-    a1c1 = swap_far("attn1_grad_1", a1g1)
-    a1c0 = swap_far("attn1_grad_0", a1g0)
-
-    upper, fed, (f0k0, f0k1, f0g0, f0g1), fvec = ffn_back(0, (lower, *fed), lambda g: g)
-    *fed, f0g0, f0g1, a1c1, f1c0, f1near, twin = tie(*fed, f0g0, f0g1, a1c1, f1c0, state["f1"], twin)
-    state["a1"] = swap_near("attn1_grad", a1k1, a1c1)
-    state["f1"] = scatter_z("ffn1_grad_z1", add(f1k0, f1c0, f1near), z_top)
-    encoded = all_rows(encoded_low, piece, twin)
+    a1c = swap_far("attn1_grad", jnp.stack([a1g0, a1g1]))
+
+    def middle0(grad_pre):
+        g0, g1, came = tie(*grad_pre, state["f1_far_0"])
+        state["f1"] = scatter_z("ffn1_grad_z1", jnp.stack([add(f1k0, came), add(f1k1, state["f1_far_1"])]), z_top)
+        return [g0, g1]
+
+    upper, fed, (f0k0, f0k1, f0g0, f0g1), fvec = ffn_back(0, (lower, *fed), middle0)
+    *fed, f0g0, f0g1, a1c = tie(*fed, f0g0, f0g1, a1c)
+    state["a1_near"] = swap_near("attn1_grad", a1k1, a1c[1])
     f0c1 = swap_far("ffn0_grad_1", f0g1)
     f0c0 = swap_far("ffn0_grad_0", f0g0)
 
+
+    def first0(lower_low):
+        lower_low, state["twin"] = tie(lower_low, twin)
+        return lower_low
+
     def during0(dqkv, kv):
-        d0, d1, kv, f1_in, came, far, near = tie(*dqkv, kv, state["f1"][1], f0c1, a1c0, state["a1"])
+        d0, d1, kv, came, f1_in, near = tie(*dqkv, kv, f0c1, state["f1"][1], state["a1_near"])
         state["f0"] = swap_near("ffn0_grad", f0k1, came)
-        state["a1"] = scatter_z("attn1_grad_z1", add(a1k0, far, near), z_top)
+        state["a1"] = scatter_z("attn1_grad_z1", add(a1k0, a1c[0], near), z_top)
         state["f1"] = scatter_z("ffn1_grad_z2", add(state["f1"][0], f1_in), z_last)
         return [d0, d1], kv
 
-    lower, fed, (a0k0, a0k1, a0g0, a0g1), avec = attn_back(0, (upper, *fed), during0)
+    lower, fed, (a0k0, a0k1, a0g0, a0g1), avec = attn_back(0, (upper, *fed), first0, tie, during0)
     vectors[0] = (fvec, avec)
-    *fed, a0g0, a0g1, a1_in = tie(*fed, a0g0, a0g1, state["a1"][1])
-    a1s = scatter_z("attn1_grad_z2", add(state["a1"][0], a1_in), z_last)
+    sums = [part for f, a in vectors for part in (*f, *a)]
+    vector, given = call(pack_kernel, [((8 * LAYERS, inputs.shape[1]), F32)] * 2, sums, name="vector_grads")
+    *fed, a0g0, a0g1, given = tie(*fed, a0g0, a0g1, given)
     a0c1 = swap_far("attn0_grad_1", a0g1)
     a0c0 = swap_far("attn0_grad_0", a0g0)
+    v_in = links.swap_as("vectors_x", links.swap_x, given)
     grad_hidden = call(final_sum_kernel, [(lower.shape, BF16)], (lower, *fed), name="input_grad")[0]
-    sums = [part for f, a in vectors for part in (*f, *a)]
-    vector, given = call(pack_kernel, [((8 * LAYERS, inputs.shape[1]), F32)] * 2, sums, name="vector_grads")
-
     attn_splits = ([(k * third, (k + 1) * third) for k in range(3)], [(3 * third, 4 * third)])
     ffn_splits = ([(0, wide)], [(wide, 2 * wide)])
     params = (attn_in, attn_out, ffn_up, ffn_down, head_bias, ffn_bias, row_params)
@@ -1001,34 +1028,43 @@
     params = (attn_in, attn_out, ffn_up, ffn_down, head_bias, ffn_bias, row_params)
     states = [(params[i], moments[i], seconds[i]) for i in range(7)]
 
-    grad_hidden, given, f0c0, f0near, f1_in = tie(grad_hidden, given, f0c0, state["f0"], state["f1"][1])
+    order = links.places
+    grad_hidden, v_in, f0c0, f0near, a1_in, order = tie(
+        grad_hidden, v_in, f0c0, state["f0"], state["a1"][1], order
+    )
     f0s = scatter_z("ffn0_grad_z1", add(f0k0, f0c0, f0near), z_top)
-    v_in = links.swap_as("vectors_x", links.swap_x, given)
-    came, a0c0, v_in, a1_in = tie(a0c1, a0c0, v_in, a1s[1])
+    a1s = scatter_z("attn1_grad_z2", add(state["a1"][0], a1_in), z_last)
+    vector = vector + v_in
+    v_in = links.swap_as("vectors_y", links.swap, vector, 4)
+    encoded = all_rows(encoded_low, piece, state["twin"])
+    came, a0c0, v_in, f1_in, encoded, order = tie(a0c1, a0c0, v_in, state["f1"][1], encoded, order)
     a0near = swap_near("attn0_grad", a0k1, came)
-    vector = vector + v_in
-    grad_hidden, vector, f1s, a1s0 = tie(grad_hidden, vector, state["f1"][0], a1s[0])
-    piece = rows_first(grad_hidden)
-    ffn_new = adam_layer(1, ffn_splits, f1s, f1_in, states[2:4], None)
-    attn_new = adam_layer(1, attn_splits, a1s0, a1_in, states[:2], None)
-    a0near, vector, ffn_new[0], attn_new[0] = tie(a0near, vector, ffn_new[0], attn_new[0])
-    a0s = scatter_z("attn0_grad_z1", add(a0k0, a0c0, a0near), z_top)
-    v_in = links.swap_as("vectors_y", links.swap, vector, 4)
-    f0_in, v_in, encoded = tie(f0s[1], v_in, encoded)
-    f0s = scatter_z("ffn0_grad_z2", add(f0s[0], f0_in), z_last)
+    f1s = add(state["f1"][0], f1_in)
+    f1near = links.swap_as("ffn1_grad_near", links.swap_near, f1s[1].astype(BF16))
     vector = vector + v_in
     v_in = links.swap_as("vectors_z", links.swap_z, vector, links.z_masks[0])
-    came, piece, v_in = tie(a0s[1], piece, v_in)
-    a0s = scatter_z("attn0_grad_z2", add(a0s[0], came), z_last)
-    twin = rows_second(piece)
+    a0near, v_in, f1near, a1_in, order = tie(a0near, v_in, f1near, a1s[1], order)
+    a1s = (a1s[0], a1_in)
+    a0s = scatter_z("attn0_grad_z1", add(a0k0, a0c0, a0near), z_top)
     vector = vector + v_in
     for mask in links.z_masks[1:]:
         vector = vector + links.swap_as("vectors_z", links.swap_z, vector, mask)
-    ffn_new = adam_layer(0, ffn_splits, f0s[0], f0s[1], states[2:4], ffn_new)
-    input_grad = all_rows(grad_hidden, piece, twin)
+    f0_in, grad_hidden, order = tie(f0s[1], grad_hidden, order)
+    f0s = scatter_z("ffn0_grad_z2", add(f0s[0], f0_in), z_last)
+    piece = rows_first(grad_hidden)
+    ffn_new = adam_layer(1, ffn_splits, f1s[0], f1near, states[2:4], None)
+    attn_new = adam_layer(1, attn_splits, *a1s, states[:2], None)
+    came, f0_in, vector, ffn_new[0], attn_new[0], order = tie(
+        a0s[1], f0s[1], vector, ffn_new[0], attn_new[0], order
+    )
+    a0s = scatter_z("attn0_grad_z2", add(a0s[0], came), z_last)
+    piece, order = tie(piece, order)
+    twin = rows_second(piece)
     flat = [a for state in states[4:] for a in state]
     vector_new = call(vector_adam_kernel, [(a.shape, F32) for a in flat], (vector, *flat), name="vector_adam")
-    a0_in, input_grad = tie(a0s[1], input_grad)
+    ffn_new = adam_layer(0, ffn_splits, f0s[0], f0_in, states[2:4], ffn_new)
+    input_grad = all_rows(grad_hidden, piece, twin)
+    a0_in, input_grad, order = tie(a0s[1], input_grad, order)
     attn_new = adam_layer(0, attn_splits, a0s[0], a0_in, states[:2], attn_new)
 
     new = [attn_new[:4], attn_new[4:], ffn_new[:4], ffn_new[4:]] + [vector_new[3 * i : 3 * i + 3] for i in range(3)]

time: 411 us -> 395 us (0.961)
  waiting for transfers between devices: 157 us -> 122 us
  starting transfers between devices: 57.8 us -> 67.1 us
  local copies, waits for them, and re-layouts: 42.6 us -> 48.5 us
  other arithmetic: 8.98 us -> 13.2 us
    ppermute x74 -> x73, waiting for transfers between devices: 157 us -> 122 us  [swap(): return lax.ppermute(array, AXES, pairs)]
    ppermute x74 -> x73, starting transfers between devices: 57.8 us -> 67.1 us  [swap(): return lax.ppermute(array, AXES, pairs)]
    unnamed x256 -> x265, local copies, waits for them, and re-layouts: 33.4 us -> 35.5 us
  transfers between devices with their start and end apart: 74 -> 73, of which waited for: 38 -> 27; matrix products, arithmetic and copies ran while one was open for 5% -> 7% of each run, Pallas kernels for 30% -> 31%
where the time goes in v5:
time: 395 us; the launch traced here: 391 us
  Pallas kernels  135 us (34%)
  waiting for transfers between devices  122 us (31%)
  starting transfers between devices  67.1 us (17%)
  local copies, waits for them, and re-layouts  48.5 us (12%)
  other arithmetic  13.2 us (3%)
  between operations  5.78 us (1%)
    pallas_call x45, Pallas kernels, call(): pl.pallas_call(kernel, out_shape=[jax.ShapeDtypeStruct(s, d) for s, d in...  129 us
    ppermute x73, waiting for transfers between devices, swap(): return lax.ppermute(array, AXES, pairs)  122 us
    ppermute x73, starting transfers between devices, swap(): return lax.ppermute(array, AXES, pairs)  67.1 us
    unnamed x265, local copies, waits for them, and re-layouts  35.5 us
  transfers between devices with their start and end apart: 73, of which 27 were waited for; matrix products, arithmetic and copies ran while one was open for 7% of the time, Pallas kernels for 31%

profile of v5, /device:TPU:0, one launch (start us, length us, event | category | flops | bytes accessed | tf_op | source)
XLA Modules:
  0.0 391.1 jit_solution(8256847031056764092)
XLA Ops:
  2.1 4.1 %collective-permute-start = (bf16[1,96,768]{2,1,0:T(8,128)(2,1)S(1)}, bf16[1,96,768]{2,1,0:T(8,128)(2,1)S(1)}, u32[]{:S(2)}, u32[]{:S(2)}) collective-permute-start(bf16[1,96,768]{2,1,0:T(8,128)(2,1)S(1)} %maximum_bitcast_fusion.2), channel_id=1, source_target_pairs={{0,16},{1,17},{2,18},{3,19},{4,20},{5,21},{6,22},{7,23},{8,24},{9,... | collective-permute-start | bytes 442376 | tf_op jit(solution)/shard_map/attn0_z2/ppermute | solution.py:57
  9.4 3.8 collective-permute-done
  38.8 10.8 %collective-permute-done.5.refs_1_ = bf16[4,96,768]{2,1,0:T(8,128)(2,1)S(1)} collective-permute-done((bf16[4,96,768]{2,1,0:T(8,128)(2,1)S(1)}, bf16[4,96,768]{2,1,0:T(8,128)(2,1)S(1)}, u32[]{:S(2)}, u32[]{:S(2)}) %collective-permute-start.5) | collective-permute-done | bytes 589856 | tf_op jit(solution)/shard_map/attn0_near/ppermute | solution.py:57
  54.8 7.4 %collective-permute-done.9 = bf16[2,1,96,768]{3,2,1,0:T(8,128)(2,1)S(1)} collective-permute-done((bf16[2,1,96,768]{3,2,1,0:T(8,128)(2,1)S(1)}, bf16[2,1,96,768]{3,2,1,0:T(8,128)(2,1)S(1)}, u32[]{:S(2)}, u32[]{:S(2)}) %collective-permute-start.9) | collective-permute-done | bytes 294944 | tf_op jit(solution)/shard_map/attn1_z2/ppermute | solution.py:57
  78.9 6.6 %attend_full.2 = (bf16[512,192]{1,0:T(8,128)(2,1)S(1)}, bf16[512,192]{1,0:T(8,128)(2,1)S(1)}, f32[6,512]{1,0:T(8,128)S(1)}) custom-call(s32[3]{0:T(128)S(1)} %pad_add_fusion.limits, bf16[768,576]{1,0:T(8,128)(2,1)S(1)} %get-tuple-element.339.qkv0, bf16[768,576]{1,0:T(8,128)(2,1)S(1)} %get-tuple-element.340.qkv1), custom_call_target="tpu_custom_call" | custom-call | flops 1 | bytes 1 | tf_op jit(solution)/shard_map/attend_full/pallas_call | solution.py:306
  86.2 5.7 %collective-permute-done.11 = bf16[2,2,96,768]{3,2,1,0:T(8,128)(2,1)} collective-permute-done((bf16[2,2,96,768]{3,2,1,0:T(8,128)(2,1)}, bf16[2,2,96,768]{3,2,1,0:T(8,128)(2,1)}, u32[]{:S(2)}, u32[]{:S(2)}) %collective-permute-start.11) | collective-permute-done | bytes 589856 | tf_op jit(solution)/shard_map/attn1_z1/ppermute | solution.py:57
  98.2 3.7 attend_half.2
  116.9 6.4 %feed_forward.2 = (bf16[768,768]{1,0:T(8,128)(2,1)S(1)}, bf16[768,768]{1,0:T(8,128)(2,1)S(1)}, f32[768,768]{1,0:T(8,128)S(1)}, f32[768,768]{1,0:T(8,128)S(1)}, b...) custom-call(bf16[768,768]{1,0:T(8,128)(2,1)S(1)} %get-tuple-element.359.low.refs_0_, ...), custom_call_target="tpu_custom_call" | custom-call | flops 1 | bytes 1 | tf_op jit(solution)/shard_map/feed_forward/pallas_call | solution.py:306
  126.8 7.3 %collective-permute-done.19 = bf16[2,2,96,1536]{3,2,1,0:T(8,128)(2,1)S(1)} collective-permute-done((bf16[2,2,96,1536]{3,2,1,0:T(8,128)(2,1)S(1)}, bf16[2,2,96,1536]{3,2,1,0:T(8,128)(2,1)S(1)}, u32[]{:S(2)}, u32[]{:S(2)}) %collective-permute-start.19) | collective-permute-done | bytes 1179680 | tf_op jit(solution)/shard_map/ffn1_z1/ppermute | solution.py:57
  147.6 6.6 %attend_full.3 = (bf16[512,192]{1,0:T(8,128)(2,1)S(1)}, bf16[512,192]{1,0:T(8,128)(2,1)S(1)}, f32[6,512]{1,0:T(8,128)S(1)}) custom-call(s32[3]{0:T(128)S(1)} %pad_add_fusion.limits, bf16[768,576]{1,0:T(8,128)(2,1)S(1)} %get-tuple-element.377.qkv0, bf16[768,576]{1,0:T(8,128)(2,1)S(1)} %get-tuple-element.378.qkv1), custom_call_target="tpu_custom_call" | custom-call | flops 1 | bytes 1 | tf_op jit(solution)/shard_map/attend_full/pallas_call | solution.py:306
  180.4 6.5 %feed_forward.3 = (bf16[768,768]{1,0:T(8,128)(2,1)S(1)}, bf16[768,768]{1,0:T(8,128)(2,1)S(1)}, f32[768,768]{1,0:T(8,128)S(1)}, f32[768,768]{1,0:T(8,128)S(1)}, b...) custom-call(bf16[768,768]{1,0:T(8,128)(2,1)S(1)} %get-tuple-element.394.low.refs_0_, ...), custom_call_target="tpu_custom_call" | custom-call | flops 1 | bytes 1 | tf_op jit(solution)/shard_map/feed_forward/pallas_call | solution.py:306
  189.9 4.0 %add_norm.7 = (f32[768,768]{1,0:T(8,128)}, bf16[768,768]{1,0:T(8,128)(2,1)S(1)}, f32[768,768]{1,0:T(8,128)S(1)}, f32[768,1]{1,0:T(8,128)S(1)}) custom-call(bf16[256,768]{1,0:T(8,128)(2,1)S(1)} %get-tuple-element.399.refs_0_, bf16[256,768]{1,0:T(8,128)(2,1)S(1)} %get-tuple-element.400.refs_1_, bf16[256,768]{1,0:T(8,128)(2,1)S(1)} %get-tuple-element.401.refs_2_, ...), custom_call_target="tpu_custom_call" | custom-call | flops 1 | bytes 1 | tf_op jit(solution)/shard_map/add_norm/pallas_call | solution.py:306
  202.7 4.9 %weight_grads.4 = (bf16[4,96,1536]{2,1,0:T(8,128)(2,1)S(1)}, bf16[4,96,1536]{2,1,0:T(8,128)(2,1)S(1)}, bf16[4,96,1536]{2,1,0:T(8,128)(2,1)S(1)}, bf16[4,96,1536]{2,1,0:T(8,128)(2,1)S(1)}) custom-call(s32[4]{0:T(128)S(1)} %pad_add_fusion.1.places, bf16[768,768]{1,0:T(8,128)(2,1)S(1)} %get-tuple-element.394.low.refs_0_, ...), custom_call_target="tpu_custom_call" | custom-call | flops 1 | bytes 1 | tf_op jit(solution)/shard_map/weight_grads/pallas_call | solution.py:306
  219.5 6.9 %attend_full_back.2 = (bf16[512,576]{1,0:T(8,128)(2,1)S(1)}, bf16[512,576]{1,0:T(8,128)(2,1)S(1)}) custom-call(s32[3]{0:T(128)S(1)} %pad_add_fusion.limits, bf16[768,576]{1,0:T(8,128)(2,1)S(1)} %copy-done.14, bf16[768,576]{1,0:T(8,128)(2,1)S(1)} %copy-done.17, bf16[768,192]{1,0:T(8,128)(2,1)S(1)} %get-tuple-element.435.dctx0, ...), custom_call_target="tpu_custom_call" | custom-call | flops 1 | bytes 1 | tf_op jit(solution)/shard_map/attend_full_back/pallas_call | solution.py:306
  226.5 7.5 %collective-permute-done.36.came = bf16[256,768]{1,0:T(8,128)(2,1)S(1)} collective-permute-done((bf16[256,768]{1,0:T(8,128)(2,1)S(1)}, bf16[256,768]{1,0:T(8,128)(2,1)S(1)}, u32[]{:S(2)}, u32[]{:S(2)}) %collective-permute-start.36) | collective-permute-done | bytes 393248 | tf_op jit(solution)/shard_map/keys_values_grad/ppermute | solution.py:57
  238.7 3.9 weight_grads.5
  256.3 4.9 %weight_grads.6 = (bf16[4,96,1536]{2,1,0:T(8,128)(2,1)S(1)}, bf16[4,96,1536]{2,1,0:T(8,128)(2,1)S(1)}, bf16[4,96,1536]{2,1,0:T(8,128)(2,1)S(1)}, bf16[4,96,1536]{2,1,0:T(8,128)(2,1)S(1)}) custom-call(s32[4]{0:T(128)S(1)} %pad_add_fusion.1.places, bf16[768,768]{1,0:T(8,128)(2,1)S(1)} %copy-done.28, bf16[768,768]{1,0:T(8,128)(2,1)S(1)} %get-tuple-element.467.low.refs_1_, ...), custom_call_target="tpu_custom_call" | custom-call | flops 1 | bytes 1 | tf_op jit(solution)/shard_map/weight_grads/pallas_call | solution.py:306
  276.4 6.9 %attend_full_back.3 = (bf16[512,576]{1,0:T(8,128)(2,1)S(1)}, bf16[512,576]{1,0:T(8,128)(2,1)S(1)}) custom-call(s32[3]{0:T(128)S(1)} %pad_add_fusion.limits, bf16[768,576]{1,0:T(8,128)(2,1)S(1)} %copy-done.9, bf16[768,576]{1,0:T(8,128)(2,1)S(1)} %copy-done.11, bf16[768,192]{1,0:T(8,128)(2,1)S(1)} %get-tuple-element.501.dctx0, ...), custom_call_target="tpu_custom_call" | custom-call | flops 1 | bytes 1 | tf_op jit(solution)/shard_map/attend_full_back/pallas_call | solution.py:306
  283.4 12.8 %collective-permute-done.47.came = bf16[256,768]{1,0:T(8,128)(2,1)S(1)} collective-permute-done((bf16[256,768]{1,0:T(8,128)(2,1)S(1)}, bf16[256,768]{1,0:T(8,128)(2,1)S(1)}, u32[]{:S(2)}, u32[]{:S(2)}) %collective-permute-start.47) | collective-permute-done | bytes 393248 | tf_op jit(solution)/shard_map/keys_values_grad/ppermute | solution.py:57
  314.9 4.8 %collective-permute-done.57 = bf16[4,96,1536]{2,1,0:T(8,128)(2,1)S(1)} collective-permute-done((bf16[4,96,1536]{2,1,0:T(8,128)(2,1)S(1)}, bf16[4,96,1536]{2,1,0:T(8,128)(2,1)S(1)}, u32[]{:S(2)}, u32[]{:S(2)}) %collective-permute-start.57) | collective-permute-done | bytes 1179680 | tf_op jit(solution)/shard_map/ffn0_grad_0_far/ppermute | solution.py:57
  321.4 4.5 %collective-permute-start.55 = (bf16[4,96,768]{2,1,0:T(8,128)(2,1)S(1)}, bf16[4,96,768]{2,1,0:T(8,128)(2,1)S(1)}, u32[]{:S(2)}, u32[]{:S(2)}) collective-permute-start(bf16[4,96,768]{2,1,0:T(8,128)(2,1)S(1)} %get-tuple-element.539), channel_id=1, source_target_pairs={{0,2},{1,5},{2,0},{3,7},{4,6},{5,1},{6,4},{7,3},{8,10},{9,13},{10,... | collective-permute-start | bytes 1769480 | tf_op jit(solution)/shard_map/attn0_grad_0_far/ppermute | solution.py:57
  327.1 17.8 %collective-permute-done.61 = bf16[2,1,96,1536]{3,2,1,0:T(8,128)(2,1)S(1)} collective-permute-done((bf16[2,1,96,1536]{3,2,1,0:T(8,128)(2,1)S(1)}, bf16[2,1,96,1536]{3,2,1,0:T(8,128)(2,1)S(1)}, u32[]{:S(2)}, u32[]{:S(2)}) %collective-permute-start.61) | collective-permute-done | bytes 589856 | tf_op jit(solution)/shard_map/ffn1_grad_z2/ppermute | solution.py:57
  350.2 10.4 %collective-permute-done.67 = bf16[2,96,1536]{2,1,0:T(8,128)(2,1)S(1)} collective-permute-done((bf16[2,96,1536]{2,1,0:T(8,128)(2,1)S(1)}, bf16[2,96,1536]{2,1,0:T(8,128)(2,1)S(1)}, u32[]{:S(2)}, u32[]{:S(2)}) %collective-permute-start.67) | collective-permute-done | bytes 589856 | tf_op jit(solution)/shard_map/ffn0_grad_z1/ppermute | solution.py:57
  364.8 10.4 %collective-permute-done.71.piece = bf16[384,768]{1,0:T(8,128)(2,1)S(1)} collective-permute-done((bf16[384,768]{1,0:T(8,128)(2,1)S(1)}, bf16[384,768]{1,0:T(8,128)(2,1)S(1)}, u32[]{:S(2)}, u32[]{:S(2)}) %collective-permute-start.71) | collective-permute-done | bytes 589856 | tf_op jit(solution)/shard_map/rows_x/ppermute | solution.py:57
  (536 shorter events, 216.5 us)
Async XLA Ops:
  13.2 19.4 %collective-permute-start.3 = (bf16[1,96,2304]{2,1,0:T(8,128)(2,1)S(1)}, bf16[1,96,2304]{2,1,0:T(8,128)(2,1)S(1)}, u32[]{:S(2)}, u32[]{:S(2)}) collective-permute-start(bf16[1,96,2304]{2,1,0:T(8,128)(2,1)S(1)} %pad_maximum_fusion.9), channel_id=1, source_target_pairs={{0,4},{1,3},{2,6},{3,1},{4,0},{5,7},{6,2},{7,5},{8,12},{9,11},{10,... | collective-permute-start | bytes 1327112 | tf_op jit(solution)/shard_map/layer1_near/ppermute | solution.py:57
  36.1 26.2 %collective-permute-start.6 = (bf16[4,96,768]{2,1,0:T(8,128)(2,1)S(1)}, bf16[4,96,768]{2,1,0:T(8,128)(2,1)S(1)}, u32[]{:S(2)}, u32[]{:S(2)}) collective-permute-start(bf16[4,96,768]{2,1,0:T(8,128)(2,1)S(1)} %pad_maximum_fusion.6.refs_0_), channel_id=1, source_target_pairs={{0,2},{1,5},{2,0},{3,7},{4,6},{5,1},{6,4},{7,3},{8,10},{9,13},{10,... | collective-permute-start | bytes 1769480 | tf_op jit(solution)/shard_map/attn0_far/ppermute | solution.py:57
  37.6 24.7 %collective-permute-start.8 = (bf16[2,96,1536]{2,1,0:T(8,128)(2,1)}, bf16[2,96,1536]{2,1,0:T(8,128)(2,1)}, u32[]{:S(2)}, u32[]{:S(2)}) collective-permute-start(bf16[2,96,1536]{2,1,0:T(8,128)(2,1)} %pad_maximum_fusion.7), channel_id=1, source_target_pairs={{0,8},{1,9},{2,10},{3,11},{4,12},{5,13},{6,14},{7,15},{8,0},{9,1},... | collective-permute-start | bytes 1769480 | tf_op jit(solution)/shard_map/ffn0_z1/ppermute | solution.py:57
  64.6 30.6 %collective-permute-start.10 = (bf16[4,96,1536]{2,1,0:T(8,128)(2,1)}, bf16[4,96,1536]{2,1,0:T(8,128)(2,1)}, u32[]{:S(2)}, u32[]{:S(2)}) collective-permute-start(bf16[4,96,1536]{2,1,0:T(8,128)(2,1)} %constant_dynamic-update-slice_fusion.refs_0_), channel_id=1, source_target_pairs={{0,4},{1,3},{2,6},{3,1},{4,0},{5,7},{6,2},{7,5},{8,12},{9,11},{10,... | collective-permute-start | bytes 3538952 | tf_op jit(solution)/shard_map/ffn0_near/ppermute | solution.py:57
  65.4 36.5 %collective-permute-start.13 = (bf16[4,96,1536]{2,1,0:T(8,128)(2,1)}, bf16[4,96,1536]{2,1,0:T(8,128)(2,1)}, u32[]{:S(2)}, u32[]{:S(2)}) collective-permute-start(bf16[4,96,1536]{2,1,0:T(8,128)(2,1)} %constant_dynamic-update-slice_fusion.refs_0_), channel_id=1, source_target_pairs={{0,2},{1,5},{2,0},{3,7},{4,6},{5,1},{6,4},{7,3},{8,10},{9,13},{10,... | collective-permute-start | bytes 3538952 | tf_op jit(solution)/shard_map/ffn0_far/ppermute | solution.py:57
  68.0 23.9 %collective-permute-start.11 = (bf16[2,2,96,768]{3,2,1,0:T(8,128)(2,1)}, bf16[2,2,96,768]{3,2,1,0:T(8,128)(2,1)}, u32[]{:S(2)}, u32[]{:S(2)}) collective-permute-start(bf16[2,2,96,768]{3,2,1,0:T(8,128)(2,1)} %pad_maximum_fusion.8), channel_id=1, source_target_pairs={{0,8},{1,9},{2,10},{3,11},{4,12},{5,13},{6,14},{7,15},{8,0},{9,1},... | collective-permute-start | bytes 1769480 | tf_op jit(solution)/shard_map/attn1_z1/ppermute | solution.py:57
  68.0 27.2 %collective-permute-start.12 = (bf16[2,1,96,1536]{3,2,1,0:T(8,128)(2,1)}, bf16[2,1,96,1536]{3,2,1,0:T(8,128)(2,1)}, u32[]{:S(2)}, u32[]{:S(2)}) collective-permute-start(bf16[2,1,96,1536]{3,2,1,0:T(8,128)(2,1)} %fusion.5), channel_id=1, source_target_pairs={{0,16},{1,17},{2,18},{3,19},{4,20},{5,21},{6,22},{7,23},{8,24},{9,... | collective-permute-start | bytes 1769480 | tf_op jit(solution)/shard_map/ffn1_z2/ppermute | solution.py:57
  105.8 28.3 %collective-permute-start.19 = (bf16[2,2,96,1536]{3,2,1,0:T(8,128)(2,1)S(1)}, bf16[2,2,96,1536]{3,2,1,0:T(8,128)(2,1)S(1)}, u32[]{:S(2)}, u32[]{:S(2)}) collective-permute-start(bf16[2,2,96,1536]{3,2,1,0:T(8,128)(2,1)S(1)} %constant_dynamic-update-slice_fusion.3), channel_id=1, source_target_pairs={{0,8},{1,9},{2,10},{3,11},{4,12},{5,13},{6,14},{7,15},{8,0},{9,1},... | collective-permute-start | bytes 3538952 | tf_op jit(solution)/shard_map/ffn1_z1/ppermute | solution.py:57
  112.3 21.8 %collective-permute-start.18 = (bf16[2,4,96,768]{3,2,1,0:T(8,128)(2,1)S(1)}, bf16[2,4,96,768]{3,2,1,0:T(8,128)(2,1)S(1)}, u32[]{:S(2)}, u32[]{:S(2)}) collective-permute-start(bf16[2,4,96,768]{3,2,1,0:T(8,128)(2,1)S(1)} %pad_maximum_fusion.2.refs_0_), channel_id=1, source_target_pairs={{0,2},{1,5},{2,0},{3,7},{4,6},{5,1},{6,4},{7,3},{8,10},{9,13},{10,... | collective-permute-start | bytes 3538952 | tf_op jit(solution)/shard_map/attn1_far/ppermute | solution.py:57
  134.4 25.4 %collective-permute-start.24 = (bf16[4,96,1536]{2,1,0:T(8,128)(2,1)S(1)}, bf16[4,96,1536]{2,1,0:T(8,128)(2,1)S(1)}, u32[]{:S(2)}, u32[]{:S(2)}) collective-permute-start(bf16[4,96,1536]{2,1,0:T(8,128)(2,1)S(1)} %pad_maximum_fusion.4.refs_0_), channel_id=1, source_target_pairs={{0,2},{1,5},{2,0},{3,7},{4,6},{5,1},{6,4},{7,3},{8,10},{9,13},{10,... | collective-permute-start | bytes 3538952 | tf_op jit(solution)/shard_map/ffn1_far/ppermute | solution.py:57
  209.4 24.6 %collective-permute-start.37 = (bf16[4,96,1536]{2,1,0:T(8,128)(2,1)S(1)}, bf16[4,96,1536]{2,1,0:T(8,128)(2,1)S(1)}, u32[]{:S(2)}, u32[]{:S(2)}) collective-permute-start(bf16[4,96,1536]{2,1,0:T(8,128)(2,1)S(1)} %get-tuple-element.441), channel_id=1, source_target_pairs={{0,2},{1,5},{2,0},{3,7},{4,6},{5,1},{6,4},{7,3},{8,10},{9,13},{10,... | collective-permute-start | bytes 3538952 | tf_op jit(solution)/shard_map/ffn1_grad_1_far/ppermute | solution.py:57
  242.7 20.1 %collective-permute-start.45 = (bf16[2,4,96,768]{3,2,1,0:T(8,128)(2,1)S(1)}, bf16[2,4,96,768]{3,2,1,0:T(8,128)(2,1)S(1)}, u32[]{:S(2)}, u32[]{:S(2)}) collective-permute-start(bf16[2,4,96,768]{3,2,1,0:T(8,128)(2,1)S(1)} %pad_maximum_fusion.5), channel_id=1, source_target_pairs={{0,2},{1,5},{2,0},{3,7},{4,6},{5,1},{6,4},{7,3},{8,10},{9,13},{10,... | collective-permute-start | bytes 3538952 | tf_op jit(solution)/shard_map/attn1_grad_far/ppermute | solution.py:57
  254.5 41.6 %collective-permute-start.49 = (bf16[2,2,96,1536]{3,2,1,0:T(8,128)(2,1)S(1)}, bf16[2,2,96,1536]{3,2,1,0:T(8,128)(2,1)S(1)}, u32[]{:S(2)}, u32[]{:S(2)}) collective-permute-start(bf16[2,2,96,1536]{3,2,1,0:T(8,128)(2,1)S(1)} %fusion.1), channel_id=1, source_target_pairs={{0,8},{1,9},{2,10},{3,11},{4,12},{5,13},{6,14},{7,15},{8,0},{9,1},... | collective-permute-start | bytes 3538952 | tf_op jit(solution)/shard_map/ffn1_grad_z1/ppermute | solution.py:57
  262.9 33.3 %collective-permute-start.48 = (bf16[4,96,1536]{2,1,0:T(8,128)(2,1)S(1)}, bf16[4,96,1536]{2,1,0:T(8,128)(2,1)S(1)}, u32[]{:S(2)}, u32[]{:S(2)}) collective-permute-start(bf16[4,96,1536]{2,1,0:T(8,128)(2,1)S(1)} %get-tuple-element.507), channel_id=1, source_target_pairs={{0,2},{1,5},{2,0},{3,7},{4,6},{5,1},{6,4},{7,3},{8,10},{9,13},{10,... | collective-permute-start | bytes 3538952 | tf_op jit(solution)/shard_map/ffn0_grad_1_far/ppermute | solution.py:57
  264.8 31.4 %collective-permute-start.50 = (bf16[4,96,768]{2,1,0:T(8,128)(2,1)S(1)}, bf16[4,96,768]{2,1,0:T(8,128)(2,1)S(1)}, u32[]{:S(2)}, u32[]{:S(2)}) collective-permute-start(bf16[4,96,768]{2,1,0:T(8,128)(2,1)S(1)} %fusion.4), channel_id=1, source_target_pairs={{0,4},{1,3},{2,6},{3,1},{4,0},{5,7},{6,2},{7,5},{8,12},{9,11},{10,... | collective-permute-start | bytes 1769480 | tf_op jit(solution)/shard_map/attn1_grad_near/ppermute | solution.py:57
  274.4 21.8 %collective-permute-start.47 = (bf16[256,768]{1,0:T(8,128)(2,1)S(1)}, bf16[256,768]{1,0:T(8,128)(2,1)S(1)}, u32[]{:S(2)}, u32[]{:S(2)}) collective-permute-start(bf16[256,768]{1,0:T(8,128)(2,1)S(1)} %get-tuple-element.506), channel_id=1, source_target_pairs={{0,2},{1,3},{2,0},{3,1},{4,6},{5,7},{6,4},{7,5},{8,10},{9,11},{10,... | collective-permute-start | bytes 1179656 | tf_op jit(solution)/shard_map/keys_values_grad/ppermute | solution.py:57
  274.7 45.0 %collective-permute-start.57 = (bf16[4,96,1536]{2,1,0:T(8,128)(2,1)S(1)}, bf16[4,96,1536]{2,1,0:T(8,128)(2,1)S(1)}, u32[]{:S(2)}, u32[]{:S(2)}) collective-permute-start(bf16[4,96,1536]{2,1,0:T(8,128)(2,1)S(1)} %get-tuple-element.549), channel_id=1, source_target_pairs={{0,2},{1,5},{2,0},{3,7},{4,6},{5,1},{6,4},{7,3},{8,10},{9,13},{10,... | collective-permute-start | bytes 3538952 | tf_op jit(solution)/shard_map/ffn0_grad_0_far/ppermute | solution.py:57
  296.5 29.4 %collective-permute-start.58 = (bf16[4,96,1536]{2,1,0:T(8,128)(2,1)S(1)}, bf16[4,96,1536]{2,1,0:T(8,128)(2,1)S(1)}, u32[]{:S(2)}, u32[]{:S(2)}) collective-permute-start(bf16[4,96,1536]{2,1,0:T(8,128)(2,1)S(1)} %add_convert_fusion), channel_id=1, source_target_pairs={{0,4},{1,3},{2,6},{3,1},{4,0},{5,7},{6,2},{7,5},{8,12},{9,11},{10,... | collective-permute-start | bytes 3538952 | tf_op jit(solution)/shard_map/ffn0_grad_near/ppermute | solution.py:57
  311.9 33.0 %collective-permute-start.61 = (bf16[2,1,96,1536]{3,2,1,0:T(8,128)(2,1)S(1)}, bf16[2,1,96,1536]{3,2,1,0:T(8,128)(2,1)S(1)}, u32[]{:S(2)}, u32[]{:S(2)}) collective-permute-start(bf16[2,1,96,1536]{3,2,1,0:T(8,128)(2,1)S(1)} %slice.412), channel_id=1, source_target_pairs={{0,16},{1,17},{2,18},{3,19},{4,20},{5,21},{6,22},{7,23},{8,24},{9,... | collective-permute-start | bytes 1769480 | tf_op jit(solution)/shard_map/ffn1_grad_z2/ppermute | solution.py:57
  319.7 25.2 %collective-permute-start.54 = (bf16[4,96,768]{2,1,0:T(8,128)(2,1)S(1)}, bf16[4,96,768]{2,1,0:T(8,128)(2,1)S(1)}, u32[]{:S(2)}, u32[]{:S(2)}) collective-permute-start(bf16[4,96,768]{2,1,0:T(8,128)(2,1)S(1)} %get-tuple-element.538), channel_id=1, source_target_pairs={{0,2},{1,5},{2,0},{3,7},{4,6},{5,1},{6,4},{7,3},{8,10},{9,13},{10,... | collective-permute-start | bytes 1769480 | tf_op jit(solution)/shard_map/attn0_grad_1_far/ppermute | solution.py:57
  321.4 23.4 %collective-permute-start.55 = (bf16[4,96,768]{2,1,0:T(8,128)(2,1)S(1)}, bf16[4,96,768]{2,1,0:T(8,128)(2,1)S(1)}, u32[]{:S(2)}, u32[]{:S(2)}) collective-permute-start(bf16[4,96,768]{2,1,0:T(8,128)(2,1)S(1)} %get-tuple-element.539), channel_id=1, source_target_pairs={{0,2},{1,5},{2,0},{3,7},{4,6},{5,1},{6,4},{7,3},{8,10},{9,13},{10,... | collective-permute-start | bytes 1769480 | tf_op jit(solution)/shard_map/attn0_grad_0_far/ppermute | solution.py:57
  326.0 35.8 %collective-permute-start.65 = (bf16[1,96,768]{2,1,0:T(8,128)(2,1)S(1)}, bf16[1,96,768]{2,1,0:T(8,128)(2,1)S(1)}, u32[]{:S(2)}, u32[]{:S(2)}) collective-permute-start(bf16[1,96,768]{2,1,0:T(8,128)(2,1)S(1)} %slice.417), channel_id=1, source_target_pairs={{0,16},{1,17},{2,18},{3,19},{4,20},{5,21},{6,22},{7,23},{8,24},{9,... | collective-permute-start | bytes 442376 | tf_op jit(solution)/shard_map/attn1_grad_z2/ppermute | solution.py:57
  326.1 18.8 %collective-permute-start.60 = (f32[16,768]{1,0:T(8,128)S(1)}, f32[16,768]{1,0:T(8,128)S(1)}, u32[]{:S(2)}, u32[]{:S(2)}) collective-permute-start(f32[16,768]{1,0:T(8,128)S(1)} %add.109), channel_id=1, source_target_pairs={{0,4},{1,5},{2,6},{3,7},{4,0},{5,1},{6,2},{7,3},{8,12},{9,13},{10,... | collective-permute-start | bytes 147464 | tf_op jit(solution)/shard_map/vectors_y/ppermute | solution.py:57
  361.3 17.6 %collective-permute-start.68 = (bf16[1,96,1536]{2,1,0:T(8,128)(2,1)S(1)}, bf16[1,96,1536]{2,1,0:T(8,128)(2,1)S(1)}, u32[]{:S(2)}, u32[]{:S(2)}) collective-permute-start(bf16[1,96,1536]{2,1,0:T(8,128)(2,1)S(1)} %slice.413), channel_id=1, source_target_pairs={{0,16},{1,17},{2,18},{3,19},{4,20},{5,21},{6,22},{7,23},{8,24},{9,... | collective-permute-start | bytes 884744 | tf_op jit(solution)/shard_map/ffn0_grad_z2/ppermute | solution.py:57
  (177 other events, 1126.0 us)

commit v6 on v5

--- a/solution.py
+++ b/solution.py
@@ -868,6 +868,7 @@
     f0last = links.swap_as("ffn0_far_near", links.swap_far, f0near)
     a1 = join([a1, a1_in], axis=1)
     f1 = join([f1, f1_in], axis=1)
+    far[0], f1 = tie(far[0], f1)
     f1, f1_in = links.swap_as("ffn1_z1", links.last_z, f1, z_rest)
     split, split_lse = attend_half(limits, qkv[0], far[0], 0)
     *split, f0far = tie(*split, f0far)
@@ -1037,27 +1038,27 @@
     vector = vector + v_in
     v_in = links.swap_as("vectors_y", links.swap, vector, 4)
     encoded = all_rows(encoded_low, piece, state["twin"])
-    came, a0c0, v_in, f1_in, encoded, order = tie(a0c1, a0c0, v_in, state["f1"][1], encoded, order)
+    came, a0c0, f0_in, f1_in, encoded, order = tie(a0c1, a0c0, f0s[1], state["f1"][1], encoded, order)
     a0near = swap_near("attn0_grad", a0k1, came)
+    f0s = scatter_z("ffn0_grad_z2", add(f0s[0], f0_in), z_last)
     f1s = add(state["f1"][0], f1_in)
     f1near = links.swap_as("ffn1_grad_near", links.swap_near, f1s[1].astype(BF16))
-    vector = vector + v_in
-    v_in = links.swap_as("vectors_z", links.swap_z, vector, links.z_masks[0])
     a0near, v_in, f1near, a1_in, order = tie(a0near, v_in, f1near, a1s[1], order)
     a1s = (a1s[0], a1_in)
     a0s = scatter_z("attn0_grad_z1", add(a0k0, a0c0, a0near), z_top)
     vector = vector + v_in
-    for mask in links.z_masks[1:]:
-        vector = vector + links.swap_as("vectors_z", links.swap_z, vector, mask)
-    f0_in, grad_hidden, order = tie(f0s[1], grad_hidden, order)
-    f0s = scatter_z("ffn0_grad_z2", add(f0s[0], f0_in), z_last)
+    v_in = links.swap_as("vectors_z", links.swap_z, vector, links.z_masks[0])
+    grad_hidden, order = tie(grad_hidden, order)
     piece = rows_first(grad_hidden)
     ffn_new = adam_layer(1, ffn_splits, f1s[0], f1near, states[2:4], None)
     attn_new = adam_layer(1, attn_splits, *a1s, states[:2], None)
-    came, f0_in, vector, ffn_new[0], attn_new[0], order = tie(
-        a0s[1], f0s[1], vector, ffn_new[0], attn_new[0], order
+    came, f0_in, v_in, ffn_new[0], attn_new[0], order = tie(
+        a0s[1], f0s[1], v_in, ffn_new[0], attn_new[0], order
     )
     a0s = scatter_z("attn0_grad_z2", add(a0s[0], came), z_last)
+    vector = vector + v_in
+    for mask in links.z_masks[1:]:
+        vector = vector + links.swap_as("vectors_z", links.swap_z, vector, mask)
     piece, order = tie(piece, order)
     twin = rows_second(piece)
     flat = [a for state in states[4:] for a in state]

time: 395 us -> 388 us (0.982)
  starting transfers between devices: 67.1 us -> 62.5 us
    ppermute x73, starting transfers between devices: 67.1 us -> 62.5 us  [swap(): return lax.ppermute(array, AXES, pairs)]
    unnamed x265 -> x264, local copies, waits for them, and re-layouts: 35.5 us -> 34.5 us
  transfers between devices with their start and end apart: 73 -> 73, of which waited for: 27 -> 30; matrix products, arithmetic and copies ran while one was open for 7% -> 7% of each run, Pallas kernels for 31% -> 31%
where the time goes in v6:
time: 388 us; the launch traced here: 384 us
  Pallas kernels  135 us (35%)
  waiting for transfers between devices  120 us (31%)
  starting transfers between devices  62.5 us (16%)
  local copies, waits for them, and re-layouts  46.3 us (12%)
  other arithmetic  14.5 us (4%)
  between operations  5.86 us (2%)
    pallas_call x45, Pallas kernels, call(): pl.pallas_call(kernel, out_shape=[jax.ShapeDtypeStruct(s, d) for s, d in...  129 us
    ppermute x73, waiting for transfers between devices, swap(): return lax.ppermute(array, AXES, pairs)  120 us
    ppermute x73, starting transfers between devices, swap(): return lax.ppermute(array, AXES, pairs)  62.5 us
    unnamed x264, local copies, waits for them, and re-layouts  34.5 us
  transfers between devices with their start and end apart: 73, of which 30 were waited for; matrix products, arithmetic and copies ran while one was open for 7% of the time, Pallas kernels for 31%

profile of v6, /device:TPU:0, one launch (start us, length us, event | category | flops | bytes accessed | tf_op | source)
XLA Modules:
  0.0 383.7 jit_solution(2040423687359239213)
XLA Ops:
  2.1 4.1 %collective-permute-start = (bf16[1,96,768]{2,1,0:T(8,128)(2,1)S(1)}, bf16[1,96,768]{2,1,0:T(8,128)(2,1)S(1)}, u32[]{:S(2)}, u32[]{:S(2)}) collective-permute-start(bf16[1,96,768]{2,1,0:T(8,128)(2,1)S(1)} %maximum_bitcast_fusion.2), channel_id=1, source_target_pairs={{0,16},{1,17},{2,18},{3,19},{4,20},{5,21},{6,22},{7,23},{8,24},{9,... | collective-permute-start | bytes 442376 | tf_op jit(solution)/shard_map/attn0_z2/ppermute | solution.py:57
  38.8 10.8 %collective-permute-done.5.refs_1_ = bf16[4,96,768]{2,1,0:T(8,128)(2,1)S(1)} collective-permute-done((bf16[4,96,768]{2,1,0:T(8,128)(2,1)S(1)}, bf16[4,96,768]{2,1,0:T(8,128)(2,1)S(1)}, u32[]{:S(2)}, u32[]{:S(2)}) %collective-permute-start.5) | collective-permute-done | bytes 589856 | tf_op jit(solution)/shard_map/attn0_near/ppermute | solution.py:57
  54.8 7.4 %collective-permute-done.9 = bf16[2,1,96,768]{3,2,1,0:T(8,128)(2,1)S(1)} collective-permute-done((bf16[2,1,96,768]{3,2,1,0:T(8,128)(2,1)S(1)}, bf16[2,1,96,768]{3,2,1,0:T(8,128)(2,1)S(1)}, u32[]{:S(2)}, u32[]{:S(2)}) %collective-permute-start.9) | collective-permute-done | bytes 294944 | tf_op jit(solution)/shard_map/attn1_z2/ppermute | solution.py:57
  78.9 6.6 %attend_full.2 = (bf16[512,192]{1,0:T(8,128)(2,1)S(1)}, bf16[512,192]{1,0:T(8,128)(2,1)S(1)}, f32[6,512]{1,0:T(8,128)S(1)}) custom-call(s32[3]{0:T(128)S(1)} %pad_add_fusion.limits, bf16[768,576]{1,0:T(8,128)(2,1)S(1)} %get-tuple-element.339.qkv0, bf16[768,576]{1,0:T(8,128)(2,1)S(1)} %get-tuple-element.340.qkv1), custom_call_target="tpu_custom_call" | custom-call | flops 1 | bytes 1 | tf_op jit(solution)/shard_map/attend_full/pallas_call | solution.py:306
  86.2 5.5 %collective-permute-done.11 = bf16[2,2,96,768]{3,2,1,0:T(8,128)(2,1)} collective-permute-done((bf16[2,2,96,768]{3,2,1,0:T(8,128)(2,1)}, bf16[2,2,96,768]{3,2,1,0:T(8,128)(2,1)}, u32[]{:S(2)}, u32[]{:S(2)}) %collective-permute-start.11) | collective-permute-done | bytes 589856 | tf_op jit(solution)/shard_map/attn1_z1/ppermute | solution.py:57
  116.4 6.4 %feed_forward.2 = (bf16[768,768]{1,0:T(8,128)(2,1)S(1)}, bf16[768,768]{1,0:T(8,128)(2,1)S(1)}, f32[768,768]{1,0:T(8,128)S(1)}, f32[768,768]{1,0:T(8,128)S(1)}, b...) custom-call(bf16[768,768]{1,0:T(8,128)(2,1)S(1)} %get-tuple-element.361.low.refs_0_, ...), custom_call_target="tpu_custom_call" | custom-call | flops 1 | bytes 1 | tf_op jit(solution)/shard_map/feed_forward/pallas_call | solution.py:306
  126.3 6.5 %collective-permute-done.19 = bf16[2,2,96,1536]{3,2,1,0:T(8,128)(2,1)S(1)} collective-permute-done((bf16[2,2,96,1536]{3,2,1,0:T(8,128)(2,1)S(1)}, bf16[2,2,96,1536]{3,2,1,0:T(8,128)(2,1)S(1)}, u32[]{:S(2)}, u32[]{:S(2)}) %collective-permute-start.19) | collective-permute-done | bytes 1179680 | tf_op jit(solution)/shard_map/ffn1_z1/ppermute | solution.py:57
  146.3 6.6 %attend_full.3 = (bf16[512,192]{1,0:T(8,128)(2,1)S(1)}, bf16[512,192]{1,0:T(8,128)(2,1)S(1)}, f32[6,512]{1,0:T(8,128)S(1)}) custom-call(s32[3]{0:T(128)S(1)} %pad_add_fusion.limits, bf16[768,576]{1,0:T(8,128)(2,1)S(1)} %get-tuple-element.379.qkv0, bf16[768,576]{1,0:T(8,128)(2,1)S(1)} %get-tuple-element.380.qkv1), custom_call_target="tpu_custom_call" | custom-call | flops 1 | bytes 1 | tf_op jit(solution)/shard_map/attend_full/pallas_call | solution.py:306
  179.2 6.5 %feed_forward.3 = (bf16[768,768]{1,0:T(8,128)(2,1)S(1)}, bf16[768,768]{1,0:T(8,128)(2,1)S(1)}, f32[768,768]{1,0:T(8,128)S(1)}, f32[768,768]{1,0:T(8,128)S(1)}, b...) custom-call(bf16[768,768]{1,0:T(8,128)(2,1)S(1)} %get-tuple-element.396.low.refs_0_, ...), custom_call_target="tpu_custom_call" | custom-call | flops 1 | bytes 1 | tf_op jit(solution)/shard_map/feed_forward/pallas_call | solution.py:306
  188.6 4.0 %add_norm.7 = (f32[768,768]{1,0:T(8,128)}, bf16[768,768]{1,0:T(8,128)(2,1)S(1)}, f32[768,768]{1,0:T(8,128)S(1)}, f32[768,1]{1,0:T(8,128)S(1)}) custom-call(bf16[256,768]{1,0:T(8,128)(2,1)S(1)} %get-tuple-element.401.refs_0_, bf16[256,768]{1,0:T(8,128)(2,1)S(1)} %get-tuple-element.402.refs_1_, bf16[256,768]{1,0:T(8,128)(2,1)S(1)} %get-tuple-element.403.refs_2_, ...), custom_call_target="tpu_custom_call" | custom-call | flops 1 | bytes 1 | tf_op jit(solution)/shard_map/add_norm/pallas_call | solution.py:306
  201.4 4.9 %weight_grads.4 = (bf16[4,96,1536]{2,1,0:T(8,128)(2,1)S(1)}, bf16[4,96,1536]{2,1,0:T(8,128)(2,1)S(1)}, bf16[4,96,1536]{2,1,0:T(8,128)(2,1)S(1)}, bf16[4,96,1536]{2,1,0:T(8,128)(2,1)S(1)}) custom-call(s32[4]{0:T(128)S(1)} %pad_add_fusion.1.places, bf16[768,768]{1,0:T(8,128)(2,1)S(1)} %get-tuple-element.396.low.refs_0_, ...), custom_call_target="tpu_custom_call" | custom-call | flops 1 | bytes 1 | tf_op jit(solution)/shard_map/weight_grads/pallas_call | solution.py:306
  218.2 6.9 %attend_full_back.2 = (bf16[512,576]{1,0:T(8,128)(2,1)S(1)}, bf16[512,576]{1,0:T(8,128)(2,1)S(1)}) custom-call(s32[3]{0:T(128)S(1)} %pad_add_fusion.limits, bf16[768,576]{1,0:T(8,128)(2,1)S(1)} %copy-done.14, bf16[768,576]{1,0:T(8,128)(2,1)S(1)} %copy-done.17, bf16[768,192]{1,0:T(8,128)(2,1)S(1)} %get-tuple-element.437.dctx0, ...), custom_call_target="tpu_custom_call" | custom-call | flops 1 | bytes 1 | tf_op jit(solution)/shard_map/attend_full_back/pallas_call | solution.py:306
  225.2 7.5 %collective-permute-done.36.came = bf16[256,768]{1,0:T(8,128)(2,1)S(1)} collective-permute-done((bf16[256,768]{1,0:T(8,128)(2,1)S(1)}, bf16[256,768]{1,0:T(8,128)(2,1)S(1)}, u32[]{:S(2)}, u32[]{:S(2)}) %collective-permute-start.36) | collective-permute-done | bytes 393248 | tf_op jit(solution)/shard_map/keys_values_grad/ppermute | solution.py:57
  237.4 3.9 %weight_grads.5 = (bf16[4,96,768]{2,1,0:T(8,128)(2,1)S(1)}, bf16[4,96,768]{2,1,0:T(8,128)(2,1)S(1)}, bf16[4,96,768]{2,1,0:T(8,128)(2,1)S(1)}, bf16[4,96,768]{2,1,0:T(8,128)(2,1)S(1)}) custom-call(s32[4]{0:T(128)S(1)} %pad_add_fusion.1.places, bf16[768,768]{1,0:T(8,128)(2,1)S(1)} %copy-done.30, bf16[768,768]{1,0:T(8,128)(2,1)S(1)} %get-tuple-element.432.low.refs_1_, ...), custom_call_target="tpu_custom_call" | custom-call | flops 1 | bytes 1 | tf_op jit(solution)/shard_map/weight_grads/pallas_call | solution.py:306
  253.9 4.9 %weight_grads.6 = (bf16[4,96,1536]{2,1,0:T(8,128)(2,1)S(1)}, bf16[4,96,1536]{2,1,0:T(8,128)(2,1)S(1)}, bf16[4,96,1536]{2,1,0:T(8,128)(2,1)S(1)}, bf16[4,96,1536]{2,1,0:T(8,128)(2,1)S(1)}) custom-call(s32[4]{0:T(128)S(1)} %pad_add_fusion.1.places, bf16[768,768]{1,0:T(8,128)(2,1)S(1)} %copy-done.28, bf16[768,768]{1,0:T(8,128)(2,1)S(1)} %get-tuple-element.469.low.refs_1_, ...), custom_call_target="tpu_custom_call" | custom-call | flops 1 | bytes 1 | tf_op jit(solution)/shard_map/weight_grads/pallas_call | solution.py:306
  273.6 6.9 %attend_full_back.3 = (bf16[512,576]{1,0:T(8,128)(2,1)S(1)}, bf16[512,576]{1,0:T(8,128)(2,1)S(1)}) custom-call(s32[3]{0:T(128)S(1)} %pad_add_fusion.limits, bf16[768,576]{1,0:T(8,128)(2,1)S(1)} %copy-done.9, bf16[768,576]{1,0:T(8,128)(2,1)S(1)} %copy-done.11, bf16[768,192]{1,0:T(8,128)(2,1)S(1)} %get-tuple-element.503.dctx0, ...), custom_call_target="tpu_custom_call" | custom-call | flops 1 | bytes 1 | tf_op jit(solution)/shard_map/attend_full_back/pallas_call | solution.py:306
  280.5 14.4 %collective-permute-done.47.came = bf16[256,768]{1,0:T(8,128)(2,1)S(1)} collective-permute-done((bf16[256,768]{1,0:T(8,128)(2,1)S(1)}, bf16[256,768]{1,0:T(8,128)(2,1)S(1)}, u32[]{:S(2)}, u32[]{:S(2)}) %collective-permute-start.47) | collective-permute-done | bytes 393248 | tf_op jit(solution)/shard_map/keys_values_grad/ppermute | solution.py:57
  298.3 4.0 %weight_grads.7 = (bf16[4,96,768]{2,1,0:T(8,128)(2,1)S(1)}, bf16[4,96,768]{2,1,0:T(8,128)(2,1)S(1)}, bf16[4,96,768]{2,1,0:T(8,128)(2,1)S(1)}, bf16[4,96,768]{2,1,0:T(8,128)(2,1)S(1)}) custom-call(s32[4]{0:T(128)S(1)} %pad_add_fusion.1.places, bf16[768,768]{1,0:T(8,128)(2,1)S(1)} %copy-done.19, bf16[768,768]{1,0:T(8,128)(2,1)S(1)} %get-tuple-element.498.low.refs_1_, ...), custom_call_target="tpu_custom_call" | custom-call | flops 1 | bytes 1 | tf_op jit(solution)/shard_map/weight_grads/pallas_call | solution.py:306
  308.9 9.5 %collective-permute-done.57 = bf16[4,96,1536]{2,1,0:T(8,128)(2,1)S(1)} collective-permute-done((bf16[4,96,1536]{2,1,0:T(8,128)(2,1)S(1)}, bf16[4,96,1536]{2,1,0:T(8,128)(2,1)S(1)}, u32[]{:S(2)}, u32[]{:S(2)}) %collective-permute-start.57) | collective-permute-done | bytes 1179680 | tf_op jit(solution)/shard_map/ffn0_grad_0_far/ppermute | solution.py:57
  327.2 8.7 %collective-permute-done.61 = bf16[2,1,96,1536]{3,2,1,0:T(8,128)(2,1)S(1)} collective-permute-done((bf16[2,1,96,1536]{3,2,1,0:T(8,128)(2,1)S(1)}, bf16[2,1,96,1536]{3,2,1,0:T(8,128)(2,1)S(1)}, u32[]{:S(2)}, u32[]{:S(2)}) %collective-permute-start.61) | collective-permute-done | bytes 589856 | tf_op jit(solution)/shard_map/ffn1_grad_z2/ppermute | solution.py:57
  337.9 7.8 %collective-permute-done.60 = bf16[2,96,1536]{2,1,0:T(8,128)(2,1)S(1)} collective-permute-done((bf16[2,96,1536]{2,1,0:T(8,128)(2,1)S(1)}, bf16[2,96,1536]{2,1,0:T(8,128)(2,1)S(1)}, u32[]{:S(2)}, u32[]{:S(2)}) %collective-permute-start.60) | collective-permute-done | bytes 589856 | tf_op jit(solution)/shard_map/ffn0_grad_z1/ppermute | solution.py:57
  348.3 5.8 %collective-permute-done.70.piece = bf16[384,768]{1,0:T(8,128)(2,1)S(1)} collective-permute-done((bf16[384,768]{1,0:T(8,128)(2,1)S(1)}, bf16[384,768]{1,0:T(8,128)(2,1)S(1)}, u32[]{:S(2)}, u32[]{:S(2)}) %collective-permute-start.70) | collective-permute-done | bytes 589856 | tf_op jit(solution)/shard_map/rows_x/ppermute | solution.py:57
  354.1 4.9 %collective-permute-done.64.refs_1_ = bf16[1,96,1536]{2,1,0:T(8,128)(2,1)S(1)} collective-permute-done((bf16[1,96,1536]{2,1,0:T(8,128)(2,1)S(1)}, bf16[1,96,1536]{2,1,0:T(8,128)(2,1)S(1)}, u32[]{:S(2)}, u32[]{:S(2)}) %collective-permute-start.64) | collective-permute-done | bytes 294944 | tf_op jit(solution)/shard_map/ffn1_grad_near/ppermute | solution.py:57
  367.0 5.2 %collective-permute-done.66 = bf16[2,96,768]{2,1,0:T(8,128)(2,1)S(1)} collective-permute-done((bf16[2,96,768]{2,1,0:T(8,128)(2,1)S(1)}, bf16[2,96,768]{2,1,0:T(8,128)(2,1)S(1)}, u32[]{:S(2)}, u32[]{:S(2)}) %collective-permute-start.66) | collective-permute-done | bytes 294944 | tf_op jit(solution)/shard_map/attn0_grad_z1/ppermute | solution.py:57
  (535 shorter events, 218.0 us)
Async XLA Ops:
  13.2 19.4 %collective-permute-start.3 = (bf16[1,96,2304]{2,1,0:T(8,128)(2,1)S(1)}, bf16[1,96,2304]{2,1,0:T(8,128)(2,1)S(1)}, u32[]{:S(2)}, u32[]{:S(2)}) collective-permute-start(bf16[1,96,2304]{2,1,0:T(8,128)(2,1)S(1)} %pad_maximum_fusion.10), channel_id=1, source_target_pairs={{0,4},{1,3},{2,6},{3,1},{4,0},{5,7},{6,2},{7,5},{8,12},{9,11},{10,... | collective-permute-start | bytes 1327112 | tf_op jit(solution)/shard_map/layer1_near/ppermute | solution.py:57
  36.1 26.2 %collective-permute-start.6 = (bf16[4,96,768]{2,1,0:T(8,128)(2,1)S(1)}, bf16[4,96,768]{2,1,0:T(8,128)(2,1)S(1)}, u32[]{:S(2)}, u32[]{:S(2)}) collective-permute-start(bf16[4,96,768]{2,1,0:T(8,128)(2,1)S(1)} %pad_maximum_fusion.7.refs_0_), channel_id=1, source_target_pairs={{0,2},{1,5},{2,0},{3,7},{4,6},{5,1},{6,4},{7,3},{8,10},{9,13},{10,... | collective-permute-start | bytes 1769480 | tf_op jit(solution)/shard_map/attn0_far/ppermute | solution.py:57
  37.6 24.7 %collective-permute-start.8 = (bf16[2,96,1536]{2,1,0:T(8,128)(2,1)}, bf16[2,96,1536]{2,1,0:T(8,128)(2,1)}, u32[]{:S(2)}, u32[]{:S(2)}) collective-permute-start(bf16[2,96,1536]{2,1,0:T(8,128)(2,1)} %pad_maximum_fusion.8), channel_id=1, source_target_pairs={{0,8},{1,9},{2,10},{3,11},{4,12},{5,13},{6,14},{7,15},{8,0},{9,1},... | collective-permute-start | bytes 1769480 | tf_op jit(solution)/shard_map/ffn0_z1/ppermute | solution.py:57
  64.6 30.5 %collective-permute-start.10 = (bf16[4,96,1536]{2,1,0:T(8,128)(2,1)}, bf16[4,96,1536]{2,1,0:T(8,128)(2,1)}, u32[]{:S(2)}, u32[]{:S(2)}) collective-permute-start(bf16[4,96,1536]{2,1,0:T(8,128)(2,1)} %constant_dynamic-update-slice_fusion.refs_0_), channel_id=1, source_target_pairs={{0,4},{1,3},{2,6},{3,1},{4,0},{5,7},{6,2},{7,5},{8,12},{9,11},{10,... | collective-permute-start | bytes 3538952 | tf_op jit(solution)/shard_map/ffn0_near/ppermute | solution.py:57
  66.3 25.3 %collective-permute-start.11 = (bf16[2,2,96,768]{3,2,1,0:T(8,128)(2,1)}, bf16[2,2,96,768]{3,2,1,0:T(8,128)(2,1)}, u32[]{:S(2)}, u32[]{:S(2)}) collective-permute-start(bf16[2,2,96,768]{3,2,1,0:T(8,128)(2,1)} %pad_maximum_fusion.9), channel_id=1, source_target_pairs={{0,8},{1,9},{2,10},{3,11},{4,12},{5,13},{6,14},{7,15},{8,0},{9,1},... | collective-permute-start | bytes 1769480 | tf_op jit(solution)/shard_map/attn1_z1/ppermute | solution.py:57
  66.9 28.2 %collective-permute-start.12 = (bf16[2,1,96,1536]{3,2,1,0:T(8,128)(2,1)}, bf16[2,1,96,1536]{3,2,1,0:T(8,128)(2,1)}, u32[]{:S(2)}, u32[]{:S(2)}) collective-permute-start(bf16[2,1,96,1536]{3,2,1,0:T(8,128)(2,1)} %fusion.5), channel_id=1, source_target_pairs={{0,16},{1,17},{2,18},{3,19},{4,20},{5,21},{6,22},{7,23},{8,24},{9,... | collective-permute-start | bytes 1769480 | tf_op jit(solution)/shard_map/ffn1_z2/ppermute | solution.py:57
  71.0 31.6 %collective-permute-start.13 = (bf16[4,96,1536]{2,1,0:T(8,128)(2,1)}, bf16[4,96,1536]{2,1,0:T(8,128)(2,1)S(1)}, u32[]{:S(2)}, u32[]{:S(2)}) collective-permute-start(bf16[4,96,1536]{2,1,0:T(8,128)(2,1)} %constant_dynamic-update-slice_fusion.refs_0_), channel_id=1, source_target_pairs={{0,2},{1,5},{2,0},{3,7},{4,6},{5,1},{6,4},{7,3},{8,10},{9,13},{10,... | collective-permute-start | bytes 3538952 | tf_op jit(solution)/shard_map/ffn0_far/ppermute | solution.py:57
  104.5 28.4 %collective-permute-start.19 = (bf16[2,2,96,1536]{3,2,1,0:T(8,128)(2,1)S(1)}, bf16[2,2,96,1536]{3,2,1,0:T(8,128)(2,1)S(1)}, u32[]{:S(2)}, u32[]{:S(2)}) collective-permute-start(bf16[2,2,96,1536]{3,2,1,0:T(8,128)(2,1)S(1)} %pad_maximum_fusion.2), channel_id=1, source_target_pairs={{0,8},{1,9},{2,10},{3,11},{4,12},{5,13},{6,14},{7,15},{8,0},{9,1},... | collective-permute-start | bytes 3538952 | tf_op jit(solution)/shard_map/ffn1_z1/ppermute | solution.py:57
  111.5 21.4 %collective-permute-start.18 = (bf16[2,4,96,768]{3,2,1,0:T(8,128)(2,1)S(1)}, bf16[2,4,96,768]{3,2,1,0:T(8,128)(2,1)S(1)}, u32[]{:S(2)}, u32[]{:S(2)}) collective-permute-start(bf16[2,4,96,768]{3,2,1,0:T(8,128)(2,1)S(1)} %pad_maximum_fusion.3.refs_0_), channel_id=1, source_target_pairs={{0,2},{1,5},{2,0},{3,7},{4,6},{5,1},{6,4},{7,3},{8,10},{9,13},{10,... | collective-permute-start | bytes 3538952 | tf_op jit(solution)/shard_map/attn1_far/ppermute | solution.py:57
  133.1 25.4 %collective-permute-start.24 = (bf16[4,96,1536]{2,1,0:T(8,128)(2,1)S(1)}, bf16[4,96,1536]{2,1,0:T(8,128)(2,1)S(1)}, u32[]{:S(2)}, u32[]{:S(2)}) collective-permute-start(bf16[4,96,1536]{2,1,0:T(8,128)(2,1)S(1)} %pad_maximum_fusion.5.refs_0_), channel_id=1, source_target_pairs={{0,2},{1,5},{2,0},{3,7},{4,6},{5,1},{6,4},{7,3},{8,10},{9,13},{10,... | collective-permute-start | bytes 3538952 | tf_op jit(solution)/shard_map/ffn1_far/ppermute | solution.py:57
  208.1 24.6 %collective-permute-start.37 = (bf16[4,96,1536]{2,1,0:T(8,128)(2,1)S(1)}, bf16[4,96,1536]{2,1,0:T(8,128)(2,1)S(1)}, u32[]{:S(2)}, u32[]{:S(2)}) collective-permute-start(bf16[4,96,1536]{2,1,0:T(8,128)(2,1)S(1)} %get-tuple-element.443), channel_id=1, source_target_pairs={{0,2},{1,5},{2,0},{3,7},{4,6},{5,1},{6,4},{7,3},{8,10},{9,13},{10,... | collective-permute-start | bytes 3538952 | tf_op jit(solution)/shard_map/ffn1_grad_1_far/ppermute | solution.py:57
  241.5 20.1 %collective-permute-start.45 = (bf16[2,4,96,768]{3,2,1,0:T(8,128)(2,1)S(1)}, bf16[2,4,96,768]{3,2,1,0:T(8,128)(2,1)S(1)}, u32[]{:S(2)}, u32[]{:S(2)}) collective-permute-start(bf16[2,4,96,768]{3,2,1,0:T(8,128)(2,1)S(1)} %pad_maximum_fusion.6), channel_id=1, source_target_pairs={{0,2},{1,5},{2,0},{3,7},{4,6},{5,1},{6,4},{7,3},{8,10},{9,13},{10,... | collective-permute-start | bytes 3538952 | tf_op jit(solution)/shard_map/attn1_grad_far/ppermute | solution.py:57
  252.2 42.7 %collective-permute-start.49 = (bf16[2,2,96,1536]{3,2,1,0:T(8,128)(2,1)S(1)}, bf16[2,2,96,1536]{3,2,1,0:T(8,128)(2,1)S(1)}, u32[]{:S(2)}, u32[]{:S(2)}) collective-permute-start(bf16[2,2,96,1536]{3,2,1,0:T(8,128)(2,1)S(1)} %fusion.1), channel_id=1, source_target_pairs={{0,8},{1,9},{2,10},{3,11},{4,12},{5,13},{6,14},{7,15},{8,0},{9,1},... | collective-permute-start | bytes 3538952 | tf_op jit(solution)/shard_map/ffn1_grad_z1/ppermute | solution.py:57
  261.6 33.3 %collective-permute-start.48 = (bf16[4,96,1536]{2,1,0:T(8,128)(2,1)S(1)}, bf16[4,96,1536]{2,1,0:T(8,128)(2,1)S(1)}, u32[]{:S(2)}, u32[]{:S(2)}) collective-permute-start(bf16[4,96,1536]{2,1,0:T(8,128)(2,1)S(1)} %get-tuple-element.509), channel_id=1, source_target_pairs={{0,2},{1,5},{2,0},{3,7},{4,6},{5,1},{6,4},{7,3},{8,10},{9,13},{10,... | collective-permute-start | bytes 3538952 | tf_op jit(solution)/shard_map/ffn0_grad_1_far/ppermute | solution.py:57
  263.5 31.4 %collective-permute-start.50 = (bf16[4,96,768]{2,1,0:T(8,128)(2,1)S(1)}, bf16[4,96,768]{2,1,0:T(8,128)(2,1)S(1)}, u32[]{:S(2)}, u32[]{:S(2)}) collective-permute-start(bf16[4,96,768]{2,1,0:T(8,128)(2,1)S(1)} %fusion.4), channel_id=1, source_target_pairs={{0,4},{1,3},{2,6},{3,1},{4,0},{5,7},{6,2},{7,5},{8,12},{9,11},{10,... | collective-permute-start | bytes 1769480 | tf_op jit(solution)/shard_map/attn1_grad_near/ppermute | solution.py:57
  271.5 23.4 %collective-permute-start.47 = (bf16[256,768]{1,0:T(8,128)(2,1)S(1)}, bf16[256,768]{1,0:T(8,128)(2,1)S(1)}, u32[]{:S(2)}, u32[]{:S(2)}) collective-permute-start(bf16[256,768]{1,0:T(8,128)(2,1)S(1)} %get-tuple-element.508), channel_id=1, source_target_pairs={{0,2},{1,3},{2,0},{3,1},{4,6},{5,7},{6,4},{7,5},{8,10},{9,11},{10,... | collective-permute-start | bytes 1179656 | tf_op jit(solution)/shard_map/keys_values_grad/ppermute | solution.py:57
  271.9 46.5 %collective-permute-start.57 = (bf16[4,96,1536]{2,1,0:T(8,128)(2,1)S(1)}, bf16[4,96,1536]{2,1,0:T(8,128)(2,1)S(1)}, u32[]{:S(2)}, u32[]{:S(2)}) collective-permute-start(bf16[4,96,1536]{2,1,0:T(8,128)(2,1)S(1)} %get-tuple-element.551), channel_id=1, source_target_pairs={{0,2},{1,5},{2,0},{3,7},{4,6},{5,1},{6,4},{7,3},{8,10},{9,13},{10,... | collective-permute-start | bytes 3538952 | tf_op jit(solution)/shard_map/ffn0_grad_0_far/ppermute | solution.py:57
  295.2 25.2 %collective-permute-start.58 = (bf16[4,96,1536]{2,1,0:T(8,128)(2,1)S(1)}, bf16[4,96,1536]{2,1,0:T(8,128)(2,1)S(1)}, u32[]{:S(2)}, u32[]{:S(2)}) collective-permute-start(bf16[4,96,1536]{2,1,0:T(8,128)(2,1)S(1)} %add_convert_fusion), channel_id=1, source_target_pairs={{0,4},{1,3},{2,6},{3,1},{4,0},{5,7},{6,2},{7,5},{8,12},{9,11},{10,... | collective-permute-start | bytes 3538952 | tf_op jit(solution)/shard_map/ffn0_grad_near/ppermute | solution.py:57
  305.9 29.9 %collective-permute-start.61 = (bf16[2,1,96,1536]{3,2,1,0:T(8,128)(2,1)S(1)}, bf16[2,1,96,1536]{3,2,1,0:T(8,128)(2,1)S(1)}, u32[]{:S(2)}, u32[]{:S(2)}) collective-permute-start(bf16[2,1,96,1536]{3,2,1,0:T(8,128)(2,1)S(1)} %slice.409), channel_id=1, source_target_pairs={{0,16},{1,17},{2,18},{3,19},{4,20},{5,21},{6,22},{7,23},{8,24},{9,... | collective-permute-start | bytes 1769480 | tf_op jit(solution)/shard_map/ffn1_grad_z2/ppermute | solution.py:57
  318.4 19.4 %collective-permute-start.54 = (bf16[4,96,768]{2,1,0:T(8,128)(2,1)S(1)}, bf16[4,96,768]{2,1,0:T(8,128)(2,1)S(1)}, u32[]{:S(2)}, u32[]{:S(2)}) collective-permute-start(bf16[4,96,768]{2,1,0:T(8,128)(2,1)S(1)} %get-tuple-element.540), channel_id=1, source_target_pairs={{0,2},{1,5},{2,0},{3,7},{4,6},{5,1},{6,4},{7,3},{8,10},{9,13},{10,... | collective-permute-start | bytes 1769480 | tf_op jit(solution)/shard_map/attn0_grad_1_far/ppermute | solution.py:57
  320.9 24.8 %collective-permute-start.60 = (bf16[2,96,1536]{2,1,0:T(8,128)(2,1)S(1)}, bf16[2,96,1536]{2,1,0:T(8,128)(2,1)S(1)}, u32[]{:S(2)}, u32[]{:S(2)}) collective-permute-start(bf16[2,96,1536]{2,1,0:T(8,128)(2,1)S(1)} %slice.410), channel_id=1, source_target_pairs={{0,8},{1,9},{2,10},{3,11},{4,12},{5,13},{6,14},{7,15},{8,0},{9,1},... | collective-permute-start | bytes 1769480 | tf_op jit(solution)/shard_map/ffn0_grad_z1/ppermute | solution.py:57
  324.5 29.7 %collective-permute-start.65 = (bf16[1,96,768]{2,1,0:T(8,128)(2,1)S(1)}, bf16[1,96,768]{2,1,0:T(8,128)(2,1)S(1)}, u32[]{:S(2)}, u32[]{:S(2)}) collective-permute-start(bf16[1,96,768]{2,1,0:T(8,128)(2,1)S(1)} %slice.415), channel_id=1, source_target_pairs={{0,16},{1,17},{2,18},{3,19},{4,20},{5,21},{6,22},{7,23},{8,24},{9,... | collective-permute-start | bytes 442376 | tf_op jit(solution)/shard_map/attn1_grad_z2/ppermute | solution.py:57
  335.8 18.3 %collective-permute-start.63 = (f32[16,768]{1,0:T(8,128)S(1)}, f32[16,768]{1,0:T(8,128)S(1)}, u32[]{:S(2)}, u32[]{:S(2)}) collective-permute-start(f32[16,768]{1,0:T(8,128)S(1)} %add.114), channel_id=1, source_target_pairs={{0,4},{1,5},{2,6},{3,7},{4,0},{5,1},{6,2},{7,3},{8,12},{9,13},{10,... | collective-permute-start | bytes 147464 | tf_op jit(solution)/shard_map/vectors_y/ppermute | solution.py:57
  354.1 20.5 %collective-permute-start.71 = (bf16[384,768]{1,0:T(8,128)(2,1)S(1)}, bf16[384,768]{1,0:T(8,128)(2,1)S(1)}, u32[]{:S(2)}, u32[]{:S(2)}) collective-permute-start(bf16[384,768]{1,0:T(8,128)(2,1)S(1)} %collective-permute-done.70.piece), channel_id=1, source_target_pairs={{0,1},{1,0},{2,3},{3,2},{4,5},{5,4},{6,7},{7,6},{8,9},{9,8},{10,11... | collective-permute-start | bytes 1769480 | tf_op jit(solution)/shard_map/rows_core/ppermute | solution.py:57
  (177 other events, 1020.1 us)

commit v7 on v6

--- a/solution.py
+++ b/solution.py
@@ -1030,16 +1030,16 @@
     states = [(params[i], moments[i], seconds[i]) for i in range(7)]
 
     order = links.places
-    grad_hidden, v_in, f0c0, f0near, a1_in, order = tie(
-        grad_hidden, v_in, f0c0, state["f0"], state["a1"][1], order
-    )
+    grad_hidden, v_in, f0c0, f0near, order = tie(grad_hidden, v_in, f0c0, state["f0"], order)
     f0s = scatter_z("ffn0_grad_z1", add(f0k0, f0c0, f0near), z_top)
-    a1s = scatter_z("attn1_grad_z2", add(state["a1"][0], a1_in), z_last)
     vector = vector + v_in
     v_in = links.swap_as("vectors_y", links.swap, vector, 4)
     encoded = all_rows(encoded_low, piece, state["twin"])
-    came, a0c0, f0_in, f1_in, encoded, order = tie(a0c1, a0c0, f0s[1], state["f1"][1], encoded, order)
+    came, a0c0, f0_in, f1_in, a1_in, encoded, order = tie(
+        a0c1, a0c0, f0s[1], state["f1"][1], state["a1"][1], encoded, order
+    )
     a0near = swap_near("attn0_grad", a0k1, came)
+    a1s = scatter_z("attn1_grad_z2", add(state["a1"][0], a1_in), z_last)
     f0s = scatter_z("ffn0_grad_z2", add(f0s[0], f0_in), z_last)
     f1s = add(state["f1"][0], f1_in)
     f1near = links.swap_as("ffn1_grad_near", links.swap_near, f1s[1].astype(BF16))

time: 388 us -> 403 us (1.039)
  waiting for transfers between devices: 120 us -> 138 us
    ppermute x73, waiting for transfers between devices: 120 us -> 138 us  [swap(): return lax.ppermute(array, AXES, pairs)]
  transfers between devices with their start and end apart: 73 -> 73, of which waited for: 30 -> 30; matrix products, arithmetic and copies ran while one was open for 7% -> 7% of each run, Pallas kernels for 31% -> 30%
where the time goes in v7:
time: 403 us; the launch traced here: 399 us
  waiting for transfers between devices  138 us (34%)
  Pallas kernels  135 us (33%)
  starting transfers between devices  58.9 us (15%)
  local copies, waits for them, and re-layouts  47.6 us (12%)
  other arithmetic  14.6 us (4%)
  between operations  5.79 us (1%)
    ppermute x73, waiting for transfers between devices, swap(): return lax.ppermute(array, AXES, pairs)  138 us
    pallas_call x45, Pallas kernels, call(): pl.pallas_call(kernel, out_shape=[jax.ShapeDtypeStruct(s, d) for s, d in...  129 us
    ppermute x73, starting transfers between devices, swap(): return lax.ppermute(array, AXES, pairs)  58.9 us
    unnamed x264, local copies, waits for them, and re-layouts  35.7 us
  transfers between devices with their start and end apart: 73, of which 30 were waited for; matrix products, arithmetic and copies ran while one was open for 7% of the time, Pallas kernels for 30%

profile of v7, /device:TPU:0, one launch (start us, length us, event | category | flops | bytes accessed | tf_op | source)
XLA Modules:
  0.0 399.1 jit_solution(8639422007622279993)
XLA Ops:
  2.1 4.1 %collective-permute-start = (bf16[1,96,768]{2,1,0:T(8,128)(2,1)S(1)}, bf16[1,96,768]{2,1,0:T(8,128)(2,1)S(1)}, u32[]{:S(2)}, u32[]{:S(2)}) collective-permute-start(bf16[1,96,768]{2,1,0:T(8,128)(2,1)S(1)} %maximum_bitcast_fusion.2), channel_id=1, source_target_pairs={{0,16},{1,17},{2,18},{3,19},{4,20},{5,21},{6,22},{7,23},{8,24},{9,... | collective-permute-start | bytes 442376 | tf_op jit(solution)/shard_map/attn0_z2/ppermute | solution.py:57
  9.4 3.8 collective-permute-done
  38.8 10.8 %collective-permute-done.5.refs_1_ = bf16[4,96,768]{2,1,0:T(8,128)(2,1)S(1)} collective-permute-done((bf16[4,96,768]{2,1,0:T(8,128)(2,1)S(1)}, bf16[4,96,768]{2,1,0:T(8,128)(2,1)S(1)}, u32[]{:S(2)}, u32[]{:S(2)}) %collective-permute-start.5) | collective-permute-done | bytes 589856 | tf_op jit(solution)/shard_map/attn0_near/ppermute | solution.py:57
  54.8 7.4 %collective-permute-done.9 = bf16[2,1,96,768]{3,2,1,0:T(8,128)(2,1)S(1)} collective-permute-done((bf16[2,1,96,768]{3,2,1,0:T(8,128)(2,1)S(1)}, bf16[2,1,96,768]{3,2,1,0:T(8,128)(2,1)S(1)}, u32[]{:S(2)}, u32[]{:S(2)}) %collective-permute-start.9) | collective-permute-done | bytes 294944 | tf_op jit(solution)/shard_map/attn1_z2/ppermute | solution.py:57
  78.9 6.6 %attend_full.2 = (bf16[512,192]{1,0:T(8,128)(2,1)S(1)}, bf16[512,192]{1,0:T(8,128)(2,1)S(1)}, f32[6,512]{1,0:T(8,128)S(1)}) custom-call(s32[3]{0:T(128)S(1)} %pad_add_fusion.limits, bf16[768,576]{1,0:T(8,128)(2,1)S(1)} %get-tuple-element.339.qkv0, bf16[768,576]{1,0:T(8,128)(2,1)S(1)} %get-tuple-element.340.qkv1), custom_call_target="tpu_custom_call" | custom-call | flops 1 | bytes 1 | tf_op jit(solution)/shard_map/attend_full/pallas_call | solution.py:306
  86.2 5.5 %collective-permute-done.11 = bf16[2,2,96,768]{3,2,1,0:T(8,128)(2,1)} collective-permute-done((bf16[2,2,96,768]{3,2,1,0:T(8,128)(2,1)}, bf16[2,2,96,768]{3,2,1,0:T(8,128)(2,1)}, u32[]{:S(2)}, u32[]{:S(2)}) %collective-permute-start.11) | collective-permute-done | bytes 589856 | tf_op jit(solution)/shard_map/attn1_z1/ppermute | solution.py:57
  116.4 6.4 %feed_forward.2 = (bf16[768,768]{1,0:T(8,128)(2,1)S(1)}, bf16[768,768]{1,0:T(8,128)(2,1)S(1)}, f32[768,768]{1,0:T(8,128)S(1)}, f32[768,768]{1,0:T(8,128)S(1)}, b...) custom-call(bf16[768,768]{1,0:T(8,128)(2,1)S(1)} %get-tuple-element.361.low.refs_0_, ...), custom_call_target="tpu_custom_call" | custom-call | flops 1 | bytes 1 | tf_op jit(solution)/shard_map/feed_forward/pallas_call | solution.py:306
  126.3 6.5 %collective-permute-done.19 = bf16[2,2,96,1536]{3,2,1,0:T(8,128)(2,1)S(1)} collective-permute-done((bf16[2,2,96,1536]{3,2,1,0:T(8,128)(2,1)S(1)}, bf16[2,2,96,1536]{3,2,1,0:T(8,128)(2,1)S(1)}, u32[]{:S(2)}, u32[]{:S(2)}) %collective-permute-start.19) | collective-permute-done | bytes 1179680 | tf_op jit(solution)/shard_map/ffn1_z1/ppermute | solution.py:57
  146.3 6.6 %attend_full.3 = (bf16[512,192]{1,0:T(8,128)(2,1)S(1)}, bf16[512,192]{1,0:T(8,128)(2,1)S(1)}, f32[6,512]{1,0:T(8,128)S(1)}) custom-call(s32[3]{0:T(128)S(1)} %pad_add_fusion.limits, bf16[768,576]{1,0:T(8,128)(2,1)S(1)} %get-tuple-element.379.qkv0, bf16[768,576]{1,0:T(8,128)(2,1)S(1)} %get-tuple-element.380.qkv1), custom_call_target="tpu_custom_call" | custom-call | flops 1 | bytes 1 | tf_op jit(solution)/shard_map/attend_full/pallas_call | solution.py:306
  164.7 3.7 attend_half.3
  179.2 6.5 %feed_forward.3 = (bf16[768,768]{1,0:T(8,128)(2,1)S(1)}, bf16[768,768]{1,0:T(8,128)(2,1)S(1)}, f32[768,768]{1,0:T(8,128)S(1)}, f32[768,768]{1,0:T(8,128)S(1)}, b...) custom-call(bf16[768,768]{1,0:T(8,128)(2,1)S(1)} %get-tuple-element.396.low.refs_0_, ...), custom_call_target="tpu_custom_call" | custom-call | flops 1 | bytes 1 | tf_op jit(solution)/shard_map/feed_forward/pallas_call | solution.py:306
  188.6 4.1 %add_norm.7 = (f32[768,768]{1,0:T(8,128)}, bf16[768,768]{1,0:T(8,128)(2,1)S(1)}, f32[768,768]{1,0:T(8,128)S(1)}, f32[768,1]{1,0:T(8,128)S(1)}) custom-call(bf16[256,768]{1,0:T(8,128)(2,1)S(1)} %get-tuple-element.401.refs_0_, bf16[256,768]{1,0:T(8,128)(2,1)S(1)} %get-tuple-element.402.refs_1_, bf16[256,768]{1,0:T(8,128)(2,1)S(1)} %get-tuple-element.403.refs_2_, ...), custom_call_target="tpu_custom_call" | custom-call | flops 1 | bytes 1 | tf_op jit(solution)/shard_map/add_norm/pallas_call | solution.py:306
  201.5 4.9 %weight_grads.4 = (bf16[4,96,1536]{2,1,0:T(8,128)(2,1)S(1)}, bf16[4,96,1536]{2,1,0:T(8,128)(2,1)S(1)}, bf16[4,96,1536]{2,1,0:T(8,128)(2,1)S(1)}, bf16[4,96,1536]{2,1,0:T(8,128)(2,1)S(1)}) custom-call(s32[4]{0:T(128)S(1)} %pad_add_fusion.1.places, bf16[768,768]{1,0:T(8,128)(2,1)S(1)} %get-tuple-element.396.low.refs_0_, ...), custom_call_target="tpu_custom_call" | custom-call | flops 1 | bytes 1 | tf_op jit(solution)/shard_map/weight_grads/pallas_call | solution.py:306
  218.3 6.9 %attend_full_back.2 = (bf16[512,576]{1,0:T(8,128)(2,1)S(1)}, bf16[512,576]{1,0:T(8,128)(2,1)S(1)}) custom-call(s32[3]{0:T(128)S(1)} %pad_add_fusion.limits, bf16[768,576]{1,0:T(8,128)(2,1)S(1)} %copy-done.14, bf16[768,576]{1,0:T(8,128)(2,1)S(1)} %copy-done.17, bf16[768,192]{1,0:T(8,128)(2,1)S(1)} %get-tuple-element.437.dctx0, ...), custom_call_target="tpu_custom_call" | custom-call | flops 1 | bytes 1 | tf_op jit(solution)/shard_map/attend_full_back/pallas_call | solution.py:306
  225.2 7.6 %collective-permute-done.36.came = bf16[256,768]{1,0:T(8,128)(2,1)S(1)} collective-permute-done((bf16[256,768]{1,0:T(8,128)(2,1)S(1)}, bf16[256,768]{1,0:T(8,128)(2,1)S(1)}, u32[]{:S(2)}, u32[]{:S(2)}) %collective-permute-start.36) | collective-permute-done | bytes 393248 | tf_op jit(solution)/shard_map/keys_values_grad/ppermute | solution.py:57
  237.5 3.9 weight_grads.5
  254.0 4.9 %weight_grads.6 = (bf16[4,96,1536]{2,1,0:T(8,128)(2,1)S(1)}, bf16[4,96,1536]{2,1,0:T(8,128)(2,1)S(1)}, bf16[4,96,1536]{2,1,0:T(8,128)(2,1)S(1)}, bf16[4,96,1536]{2,1,0:T(8,128)(2,1)S(1)}) custom-call(s32[4]{0:T(128)S(1)} %pad_add_fusion.1.places, bf16[768,768]{1,0:T(8,128)(2,1)S(1)} %copy-done.28, bf16[768,768]{1,0:T(8,128)(2,1)S(1)} %get-tuple-element.469.low.refs_1_, ...), custom_call_target="tpu_custom_call" | custom-call | flops 1 | bytes 1 | tf_op jit(solution)/shard_map/weight_grads/pallas_call | solution.py:306
  273.7 6.9 %attend_full_back.3 = (bf16[512,576]{1,0:T(8,128)(2,1)S(1)}, bf16[512,576]{1,0:T(8,128)(2,1)S(1)}) custom-call(s32[3]{0:T(128)S(1)} %pad_add_fusion.limits, bf16[768,576]{1,0:T(8,128)(2,1)S(1)} %copy-done.9, bf16[768,576]{1,0:T(8,128)(2,1)S(1)} %copy-done.11, bf16[768,192]{1,0:T(8,128)(2,1)S(1)} %get-tuple-element.503.dctx0, ...), custom_call_target="tpu_custom_call" | custom-call | flops 1 | bytes 1 | tf_op jit(solution)/shard_map/attend_full_back/pallas_call | solution.py:306
  280.6 14.3 %collective-permute-done.47.came = bf16[256,768]{1,0:T(8,128)(2,1)S(1)} collective-permute-done((bf16[256,768]{1,0:T(8,128)(2,1)S(1)}, bf16[256,768]{1,0:T(8,128)(2,1)S(1)}, u32[]{:S(2)}, u32[]{:S(2)}) %collective-permute-start.47) | collective-permute-done | bytes 393248 | tf_op jit(solution)/shard_map/keys_values_grad/ppermute | solution.py:57
  298.3 4.0 weight_grads.7
  307.0 11.4 %collective-permute-done.57 = bf16[4,96,1536]{2,1,0:T(8,128)(2,1)S(1)} collective-permute-done((bf16[4,96,1536]{2,1,0:T(8,128)(2,1)S(1)}, bf16[4,96,1536]{2,1,0:T(8,128)(2,1)S(1)}, u32[]{:S(2)}, u32[]{:S(2)}) %collective-permute-start.57) | collective-permute-done | bytes 1179680 | tf_op jit(solution)/shard_map/ffn0_grad_0_far/ppermute | solution.py:57
  326.2 26.0 %collective-permute-done.61 = bf16[2,96,768]{2,1,0:T(8,128)(2,1)S(1)} collective-permute-done((bf16[2,96,768]{2,1,0:T(8,128)(2,1)S(1)}, bf16[2,96,768]{2,1,0:T(8,128)(2,1)S(1)}, u32[]{:S(2)}, u32[]{:S(2)}) %collective-permute-start.61) | collective-permute-done | bytes 294944 | tf_op jit(solution)/shard_map/attn1_grad_z1/ppermute | solution.py:57
  355.9 12.6 %collective-permute-done.70.piece = bf16[384,768]{1,0:T(8,128)(2,1)S(1)} collective-permute-done((bf16[384,768]{1,0:T(8,128)(2,1)S(1)}, bf16[384,768]{1,0:T(8,128)(2,1)S(1)}, u32[]{:S(2)}, u32[]{:S(2)}) %collective-permute-start.70) | collective-permute-done | bytes 589856 | tf_op jit(solution)/shard_map/rows_x/ppermute | solution.py:57
  376.9 5.4 %collective-permute-done.67.refs_1_ = bf16[1,96,1536]{2,1,0:T(8,128)(2,1)S(1)} collective-permute-done((bf16[1,96,1536]{2,1,0:T(8,128)(2,1)S(1)}, bf16[1,96,1536]{2,1,0:T(8,128)(2,1)S(1)}, u32[]{:S(2)}, u32[]{:S(2)}) %collective-permute-start.67) | collective-permute-done | bytes 294944 | tf_op jit(solution)/shard_map/ffn0_grad_z2/ppermute | solution.py:57
  (535 shorter events, 212.3 us)
Async XLA Ops:
  13.2 19.4 %collective-permute-start.3 = (bf16[1,96,2304]{2,1,0:T(8,128)(2,1)S(1)}, bf16[1,96,2304]{2,1,0:T(8,128)(2,1)S(1)}, u32[]{:S(2)}, u32[]{:S(2)}) collective-permute-start(bf16[1,96,2304]{2,1,0:T(8,128)(2,1)S(1)} %pad_maximum_fusion.10), channel_id=1, source_target_pairs={{0,4},{1,3},{2,6},{3,1},{4,0},{5,7},{6,2},{7,5},{8,12},{9,11},{10,... | collective-permute-start | bytes 1327112 | tf_op jit(solution)/shard_map/layer1_near/ppermute | solution.py:57
  36.1 26.2 %collective-permute-start.6 = (bf16[4,96,768]{2,1,0:T(8,128)(2,1)S(1)}, bf16[4,96,768]{2,1,0:T(8,128)(2,1)S(1)}, u32[]{:S(2)}, u32[]{:S(2)}) collective-permute-start(bf16[4,96,768]{2,1,0:T(8,128)(2,1)S(1)} %pad_maximum_fusion.7.refs_0_), channel_id=1, source_target_pairs={{0,2},{1,5},{2,0},{3,7},{4,6},{5,1},{6,4},{7,3},{8,10},{9,13},{10,... | collective-permute-start | bytes 1769480 | tf_op jit(solution)/shard_map/attn0_far/ppermute | solution.py:57
  37.6 24.7 %collective-permute-start.8 = (bf16[2,96,1536]{2,1,0:T(8,128)(2,1)}, bf16[2,96,1536]{2,1,0:T(8,128)(2,1)}, u32[]{:S(2)}, u32[]{:S(2)}) collective-permute-start(bf16[2,96,1536]{2,1,0:T(8,128)(2,1)} %pad_maximum_fusion.8), channel_id=1, source_target_pairs={{0,8},{1,9},{2,10},{3,11},{4,12},{5,13},{6,14},{7,15},{8,0},{9,1},... | collective-permute-start | bytes 1769480 | tf_op jit(solution)/shard_map/ffn0_z1/ppermute | solution.py:57
  64.6 30.5 %collective-permute-start.10 = (bf16[4,96,1536]{2,1,0:T(8,128)(2,1)}, bf16[4,96,1536]{2,1,0:T(8,128)(2,1)}, u32[]{:S(2)}, u32[]{:S(2)}) collective-permute-start(bf16[4,96,1536]{2,1,0:T(8,128)(2,1)} %constant_dynamic-update-slice_fusion.refs_0_), channel_id=1, source_target_pairs={{0,4},{1,3},{2,6},{3,1},{4,0},{5,7},{6,2},{7,5},{8,12},{9,11},{10,... | collective-permute-start | bytes 3538952 | tf_op jit(solution)/shard_map/ffn0_near/ppermute | solution.py:57
  66.3 25.3 %collective-permute-start.11 = (bf16[2,2,96,768]{3,2,1,0:T(8,128)(2,1)}, bf16[2,2,96,768]{3,2,1,0:T(8,128)(2,1)}, u32[]{:S(2)}, u32[]{:S(2)}) collective-permute-start(bf16[2,2,96,768]{3,2,1,0:T(8,128)(2,1)} %pad_maximum_fusion.9), channel_id=1, source_target_pairs={{0,8},{1,9},{2,10},{3,11},{4,12},{5,13},{6,14},{7,15},{8,0},{9,1},... | collective-permute-start | bytes 1769480 | tf_op jit(solution)/shard_map/attn1_z1/ppermute | solution.py:57
  66.9 28.2 %collective-permute-start.12 = (bf16[2,1,96,1536]{3,2,1,0:T(8,128)(2,1)}, bf16[2,1,96,1536]{3,2,1,0:T(8,128)(2,1)}, u32[]{:S(2)}, u32[]{:S(2)}) collective-permute-start(bf16[2,1,96,1536]{3,2,1,0:T(8,128)(2,1)} %fusion.5), channel_id=1, source_target_pairs={{0,16},{1,17},{2,18},{3,19},{4,20},{5,21},{6,22},{7,23},{8,24},{9,... | collective-permute-start | bytes 1769480 | tf_op jit(solution)/shard_map/ffn1_z2/ppermute | solution.py:57
  71.0 31.6 %collective-permute-start.13 = (bf16[4,96,1536]{2,1,0:T(8,128)(2,1)}, bf16[4,96,1536]{2,1,0:T(8,128)(2,1)S(1)}, u32[]{:S(2)}, u32[]{:S(2)}) collective-permute-start(bf16[4,96,1536]{2,1,0:T(8,128)(2,1)} %constant_dynamic-update-slice_fusion.refs_0_), channel_id=1, source_target_pairs={{0,2},{1,5},{2,0},{3,7},{4,6},{5,1},{6,4},{7,3},{8,10},{9,13},{10,... | collective-permute-start | bytes 3538952 | tf_op jit(solution)/shard_map/ffn0_far/ppermute | solution.py:57
  104.5 28.4 %collective-permute-start.19 = (bf16[2,2,96,1536]{3,2,1,0:T(8,128)(2,1)S(1)}, bf16[2,2,96,1536]{3,2,1,0:T(8,128)(2,1)S(1)}, u32[]{:S(2)}, u32[]{:S(2)}) collective-permute-start(bf16[2,2,96,1536]{3,2,1,0:T(8,128)(2,1)S(1)} %pad_maximum_fusion.2), channel_id=1, source_target_pairs={{0,8},{1,9},{2,10},{3,11},{4,12},{5,13},{6,14},{7,15},{8,0},{9,1},... | collective-permute-start | bytes 3538952 | tf_op jit(solution)/shard_map/ffn1_z1/ppermute | solution.py:57
  111.5 21.4 %collective-permute-start.18 = (bf16[2,4,96,768]{3,2,1,0:T(8,128)(2,1)S(1)}, bf16[2,4,96,768]{3,2,1,0:T(8,128)(2,1)S(1)}, u32[]{:S(2)}, u32[]{:S(2)}) collective-permute-start(bf16[2,4,96,768]{3,2,1,0:T(8,128)(2,1)S(1)} %pad_maximum_fusion.3.refs_0_), channel_id=1, source_target_pairs={{0,2},{1,5},{2,0},{3,7},{4,6},{5,1},{6,4},{7,3},{8,10},{9,13},{10,... | collective-permute-start | bytes 3538952 | tf_op jit(solution)/shard_map/attn1_far/ppermute | solution.py:57
  133.1 25.4 %collective-permute-start.24 = (bf16[4,96,1536]{2,1,0:T(8,128)(2,1)S(1)}, bf16[4,96,1536]{2,1,0:T(8,128)(2,1)S(1)}, u32[]{:S(2)}, u32[]{:S(2)}) collective-permute-start(bf16[4,96,1536]{2,1,0:T(8,128)(2,1)S(1)} %pad_maximum_fusion.5.refs_0_), channel_id=1, source_target_pairs={{0,2},{1,5},{2,0},{3,7},{4,6},{5,1},{6,4},{7,3},{8,10},{9,13},{10,... | collective-permute-start | bytes 3538952 | tf_op jit(solution)/shard_map/ffn1_far/ppermute | solution.py:57
  208.1 24.6 %collective-permute-start.37 = (bf16[4,96,1536]{2,1,0:T(8,128)(2,1)S(1)}, bf16[4,96,1536]{2,1,0:T(8,128)(2,1)S(1)}, u32[]{:S(2)}, u32[]{:S(2)}) collective-permute-start(bf16[4,96,1536]{2,1,0:T(8,128)(2,1)S(1)} %get-tuple-element.443), channel_id=1, source_target_pairs={{0,2},{1,5},{2,0},{3,7},{4,6},{5,1},{6,4},{7,3},{8,10},{9,13},{10,... | collective-permute-start | bytes 3538952 | tf_op jit(solution)/shard_map/ffn1_grad_1_far/ppermute | solution.py:57
  241.5 20.1 %collective-permute-start.45 = (bf16[2,4,96,768]{3,2,1,0:T(8,128)(2,1)S(1)}, bf16[2,4,96,768]{3,2,1,0:T(8,128)(2,1)S(1)}, u32[]{:S(2)}, u32[]{:S(2)}) collective-permute-start(bf16[2,4,96,768]{3,2,1,0:T(8,128)(2,1)S(1)} %pad_maximum_fusion.6), channel_id=1, source_target_pairs={{0,2},{1,5},{2,0},{3,7},{4,6},{5,1},{6,4},{7,3},{8,10},{9,13},{10,... | collective-permute-start | bytes 3538952 | tf_op jit(solution)/shard_map/attn1_grad_far/ppermute | solution.py:57
  252.2 42.7 %collective-permute-start.49 = (bf16[2,2,96,1536]{3,2,1,0:T(8,128)(2,1)S(1)}, bf16[2,2,96,1536]{3,2,1,0:T(8,128)(2,1)S(1)}, u32[]{:S(2)}, u32[]{:S(2)}) collective-permute-start(bf16[2,2,96,1536]{3,2,1,0:T(8,128)(2,1)S(1)} %fusion.1), channel_id=1, source_target_pairs={{0,8},{1,9},{2,10},{3,11},{4,12},{5,13},{6,14},{7,15},{8,0},{9,1},... | collective-permute-start | bytes 3538952 | tf_op jit(solution)/shard_map/ffn1_grad_z1/ppermute | solution.py:57
  261.6 33.3 %collective-permute-start.48 = (bf16[4,96,1536]{2,1,0:T(8,128)(2,1)S(1)}, bf16[4,96,1536]{2,1,0:T(8,128)(2,1)S(1)}, u32[]{:S(2)}, u32[]{:S(2)}) collective-permute-start(bf16[4,96,1536]{2,1,0:T(8,128)(2,1)S(1)} %get-tuple-element.509), channel_id=1, source_target_pairs={{0,2},{1,5},{2,0},{3,7},{4,6},{5,1},{6,4},{7,3},{8,10},{9,13},{10,... | collective-permute-start | bytes 3538952 | tf_op jit(solution)/shard_map/ffn0_grad_1_far/ppermute | solution.py:57
  263.6 31.3 %collective-permute-start.50 = (bf16[4,96,768]{2,1,0:T(8,128)(2,1)S(1)}, bf16[4,96,768]{2,1,0:T(8,128)(2,1)S(1)}, u32[]{:S(2)}, u32[]{:S(2)}) collective-permute-start(bf16[4,96,768]{2,1,0:T(8,128)(2,1)S(1)} %fusion.4), channel_id=1, source_target_pairs={{0,4},{1,3},{2,6},{3,1},{4,0},{5,7},{6,2},{7,5},{8,12},{9,11},{10,... | collective-permute-start | bytes 1769480 | tf_op jit(solution)/shard_map/attn1_grad_near/ppermute | solution.py:57
  271.6 23.4 %collective-permute-start.47 = (bf16[256,768]{1,0:T(8,128)(2,1)S(1)}, bf16[256,768]{1,0:T(8,128)(2,1)S(1)}, u32[]{:S(2)}, u32[]{:S(2)}) collective-permute-start(bf16[256,768]{1,0:T(8,128)(2,1)S(1)} %get-tuple-element.508), channel_id=1, source_target_pairs={{0,2},{1,3},{2,0},{3,1},{4,6},{5,7},{6,4},{7,5},{8,10},{9,11},{10,... | collective-permute-start | bytes 1179656 | tf_op jit(solution)/shard_map/keys_values_grad/ppermute | solution.py:57
  271.9 46.5 %collective-permute-start.57 = (bf16[4,96,1536]{2,1,0:T(8,128)(2,1)S(1)}, bf16[4,96,1536]{2,1,0:T(8,128)(2,1)S(1)}, u32[]{:S(2)}, u32[]{:S(2)}) collective-permute-start(bf16[4,96,1536]{2,1,0:T(8,128)(2,1)S(1)} %get-tuple-element.551), channel_id=1, source_target_pairs={{0,2},{1,5},{2,0},{3,7},{4,6},{5,1},{6,4},{7,3},{8,10},{9,13},{10,... | collective-permute-start | bytes 3538952 | tf_op jit(solution)/shard_map/ffn0_grad_0_far/ppermute | solution.py:57
  295.3 24.9 %collective-permute-start.58 = (bf16[4,96,1536]{2,1,0:T(8,128)(2,1)S(1)}, bf16[4,96,1536]{2,1,0:T(8,128)(2,1)S(1)}, u32[]{:S(2)}, u32[]{:S(2)}) collective-permute-start(bf16[4,96,1536]{2,1,0:T(8,128)(2,1)S(1)} %add_convert_fusion), channel_id=1, source_target_pairs={{0,4},{1,3},{2,6},{3,1},{4,0},{5,7},{6,2},{7,5},{8,12},{9,11},{10,... | collective-permute-start | bytes 3538952 | tf_op jit(solution)/shard_map/ffn0_grad_near/ppermute | solution.py:57
  305.4 46.8 %collective-permute-start.60 = (bf16[2,1,96,1536]{3,2,1,0:T(8,128)(2,1)S(1)}, bf16[2,1,96,1536]{3,2,1,0:T(8,128)(2,1)S(1)}, u32[]{:S(2)}, u32[]{:S(2)}) collective-permute-start(bf16[2,1,96,1536]{3,2,1,0:T(8,128)(2,1)S(1)} %slice.409), channel_id=1, source_target_pairs={{0,16},{1,17},{2,18},{3,19},{4,20},{5,21},{6,22},{7,23},{8,24},{9,... | collective-permute-start | bytes 1769480 | tf_op jit(solution)/shard_map/ffn1_grad_z2/ppermute | solution.py:57
  306.7 45.8 %collective-permute-start.54 = (bf16[4,96,768]{2,1,0:T(8,128)(2,1)S(1)}, bf16[4,96,768]{2,1,0:T(8,128)(2,1)S(1)}, u32[]{:S(2)}, u32[]{:S(2)}) collective-permute-start(bf16[4,96,768]{2,1,0:T(8,128)(2,1)S(1)} %get-tuple-element.540), channel_id=1, source_target_pairs={{0,2},{1,5},{2,0},{3,7},{4,6},{5,1},{6,4},{7,3},{8,10},{9,13},{10,... | collective-permute-start | bytes 1769480 | tf_op jit(solution)/shard_map/attn0_grad_1_far/ppermute | solution.py:57
  318.5 34.0 %collective-permute-start.55 = (bf16[4,96,768]{2,1,0:T(8,128)(2,1)S(1)}, bf16[4,96,768]{2,1,0:T(8,128)(2,1)S(1)}, u32[]{:S(2)}, u32[]{:S(2)}) collective-permute-start(bf16[4,96,768]{2,1,0:T(8,128)(2,1)S(1)} %get-tuple-element.541), channel_id=1, source_target_pairs={{0,2},{1,5},{2,0},{3,7},{4,6},{5,1},{6,4},{7,3},{8,10},{9,13},{10,... | collective-permute-start | bytes 1769480 | tf_op jit(solution)/shard_map/attn0_grad_0_far/ppermute | solution.py:57
  320.7 31.8 %collective-permute-start.59 = (bf16[2,96,1536]{2,1,0:T(8,128)(2,1)S(1)}, bf16[2,96,1536]{2,1,0:T(8,128)(2,1)S(1)}, u32[]{:S(2)}, u32[]{:S(2)}) collective-permute-start(bf16[2,96,1536]{2,1,0:T(8,128)(2,1)S(1)} %slice.410), channel_id=1, source_target_pairs={{0,8},{1,9},{2,10},{3,11},{4,12},{5,13},{6,14},{7,15},{8,0},{9,1},... | collective-permute-start | bytes 1769480 | tf_op jit(solution)/shard_map/ffn0_grad_z1/ppermute | solution.py:57
  321.4 30.8 %collective-permute-start.61 = (bf16[2,96,768]{2,1,0:T(8,128)(2,1)S(1)}, bf16[2,96,768]{2,1,0:T(8,128)(2,1)S(1)}, u32[]{:S(2)}, u32[]{:S(2)}) collective-permute-start(bf16[2,96,768]{2,1,0:T(8,128)(2,1)S(1)} %slice.413), channel_id=1, source_target_pairs={{0,8},{1,9},{2,10},{3,11},{4,12},{5,13},{6,14},{7,15},{8,0},{9,1},... | collective-permute-start | bytes 884744 | tf_op jit(solution)/shard_map/attn1_grad_z1/ppermute | solution.py:57
  368.9 21.0 %collective-permute-start.71 = (bf16[384,768]{1,0:T(8,128)(2,1)S(1)}, bf16[384,768]{1,0:T(8,128)(2,1)S(1)}, u32[]{:S(2)}, u32[]{:S(2)}) collective-permute-start(bf16[384,768]{1,0:T(8,128)(2,1)S(1)} %collective-permute-done.70.piece), channel_id=1, source_target_pairs={{0,1},{1,0},{2,3},{3,2},{4,5},{5,4},{6,7},{7,6},{8,9},{9,8},{10,11... | collective-permute-start | bytes 1769480 | tf_op jit(solution)/shard_map/rows_core/ppermute | solution.py:57
  (177 other events, 1035.2 us)
